TPU v7x, 32 devices: a whole 2x2x4 slice. The times are simulated.
32 devices in a mesh: rep: 2 (over y), fsdp: 8 (over z, x), mp: 2 (over core).
Axes of the slice: x: 2, y: 2, z: 4, core: 2. Of those that a mesh axis runs over, the one named last changes fastest.
Arguments:
- noise_in: bfloat16 [1024, 3072], P(('rep', 'fsdp'), 'mp'), parts along dimension 0, may hold values from -6 to 6
- renoise: bfloat16 [1024, 3072], P(('rep', 'fsdp'), 'mp'), parts along dimension 0, may hold values from -6 to 6
- gen_step: int32 [16], P('rep'), parts along dimension 0, may hold values from 0 to 999
- noise_step: int32 [16], P('rep'), parts along dimension 0, may hold values from 0 to 999
- gen_weight: bfloat16 [3072, 3072], P('fsdp', 'mp'), may hold values from -0.109375 to 0.109375
- real_weight: bfloat16 [3072, 3072], P('fsdp', 'mp'), may hold values from -0.109375 to 0.109375
- fake_weight: bfloat16 [3072, 3072], P('fsdp', 'mp'), may hold values from -0.109375 to 0.109375
- gen_embed: bfloat16 [128, 3072], replicated, may hold values from -0.5 to 0.5
- real_embed: bfloat16 [128, 3072], replicated, may hold values from -0.5 to 0.5
- fake_embed: bfloat16 [128, 3072], replicated, may hold values from -0.5 to 0.5
- gen_gain: float32 [3072], replicated, may hold values from 0.1 to 1.9
- real_gain: float32 [3072], replicated, may hold values from 0.1 to 1.9
- fake_gain: float32 [3072], replicated, may hold values from 0.1 to 1.9
Outputs:
- noised: bfloat16 [1024, 3072], P(('rep', 'fsdp'), 'mp'), parts along dimension 0
- latent_grad: bfloat16 [1024, 3072], P(('rep', 'fsdp'), 'mp'), parts along dimension 0
- gain_grad: float32 [6144], P(('rep', 'fsdp', 'mp')), parts along dimension 0
There are 2 independent parts, one for each index of `rep`. A program takes and returns all parts, laid end to end along the dimension named above; an argument that names none is the same for every part. Nothing has to cross between parts.
All inputs are finite; a program needn't handle non-finite values.
Results may differ from a plain program's by a relative error of at most 0.0066.
Values may be sent and summed in bfloat16 or wider, within the bound.
No kernel may reach another device: no remote copies, remote signals or barrier semaphores. Data moves between devices by JAX's collectives and lax.ppermute only.
A program may use at most 128 MiB of HBM per device.

v0:
```python
import math

import jax
import jax.numpy as jnp
from jax import lax
from jax.sharding import PartitionSpec as P

NT = 1000


norm_epsilon = 1e-06


def from_behind(value, axis, by):
    size = lax.axis_size(axis)
    pairs = [(i, i + by) for i in range(size) if 0 <= i + by < size]
    return lax.ppermute(value, axis, pairs)


def shifted(value, axis, by):
    size = lax.axis_size(axis)
    return lax.ppermute(value, axis, [(i, (i + by) % size) for i in range(size)])


def step_features(step_ids, feature_width):
    half_width = feature_width // 2
    frequency = jnp.exp(-math.log(10000.0) * jnp.arange(half_width, dtype=jnp.float32) / half_width)
    angles = step_ids.astype(jnp.float32)[:, None] * frequency[None, :]
    return jnp.concatenate([jnp.cos(angles), jnp.sin(angles)], axis=1).astype(jnp.bfloat16)


def lookup(step_table, block_ids):
    matches = block_ids[:, None] == jnp.arange(step_table.shape[0], dtype=jnp.int32)[None, :]
    return jnp.sum(jnp.where(matches, step_table[None, :], 0), axis=1)


def block_shares(step_ids):
    return ((step_ids.astype(jnp.float32) + 1.0) / (NT + 1.0))[:, None, None]


def modulate(full_rows, gain_vec, modulation):
    blocks = modulation.shape[0]
    values = full_rows.astype(jnp.float32)
    normed = values * lax.rsqrt(jnp.mean(values * values, axis=1, keepdims=True) + norm_epsilon)
    lifted = normed.reshape(blocks, -1, values.shape[1]) * gain_vec * (1.0 + modulation[:, None, :])
    return (normed, lifted.reshape(values.shape).astype(jnp.bfloat16))


def on_device(
    noise_in,
    renoise,
    gen_step,
    noise_step,
    gen_weight,
    real_weight,
    fake_weight,
    gen_embed,
    real_embed,
    fake_embed,
    gen_gain,
    real_gain,
    fake_gain,
):
    devices = lax.axis_size("fsdp")
    quarter = devices // 4
    half = 2 * quarter
    position = lax.axis_index("fsdp")
    block_rows = noise_in.shape[0]
    half_width = noise_in.shape[1]
    model_width = gen_gain.shape[0]
    feature_width = gen_embed.shape[0]
    slice_rows = 4 * block_rows // devices
    group_role = (position >= quarter).astype(jnp.int32) + (position >= half).astype(jnp.int32)
    in_generator = group_role == 2
    slot_ids = jnp.arange(devices, dtype=jnp.int32)
    slot_role = (
        (slot_ids >= quarter).astype(jnp.int32) + (slot_ids >= half).astype(jnp.int32)
    ).reshape(devices, 1, 1)
    outgoing = jnp.where(
        slot_role == 2,
        gen_weight[None],
        jnp.where(slot_role == 0, real_weight[None], fake_weight[None]),
    )
    received = lax.all_to_all(outgoing, "fsdp", split_axis=0, concat_axis=0, tiled=True)
    weight_mine = received.reshape(model_width, half_width)
    embed_mine = jnp.where(
        group_role == 2, gen_embed, jnp.where(group_role == 0, real_embed, fake_embed)
    )
    gain_mine = jnp.where(
        group_role == 2, gen_gain, jnp.where(group_role == 0, real_gain, fake_gain)
    )
    partner_noise, partner_renoise = from_behind((noise_in, renoise), "fsdp", half)
    gen_ids = jnp.stack([position, (position + half) % devices])
    gen_mod = jnp.dot(
        step_features(lookup(gen_step, gen_ids), feature_width),
        embed_mine,
        preferred_element_type=jnp.float32,
    )
    gen_shares = block_shares(lookup(noise_step, gen_ids))
    gen_rows = jnp.concatenate([noise_in, partner_noise], axis=0)
    gen_noise = jnp.concatenate([renoise, partner_renoise], axis=0)
    gen_full = lax.all_gather(gen_rows, "mp", axis=1, tiled=True)

    def generate(operands):
        full_rows, own_rows, fresh_noise = operands
        normed, lifted = modulate(full_rows, gain_mine, gen_mod)
        latents = own_rows.astype(jnp.float32) + jnp.dot(
            lifted, weight_mine, preferred_element_type=jnp.float32
        )
        blended = (1.0 - gen_shares) * latents.reshape(
            2, block_rows, half_width
        ) + gen_shares * fresh_noise.astype(jnp.float32).reshape(2, block_rows, half_width)
        return (blended.reshape(2 * block_rows, half_width).astype(jnp.bfloat16), normed)

    def skip_generate(operands):
        return (
            jnp.zeros((2 * block_rows, half_width), jnp.bfloat16),
            jnp.zeros((2 * block_rows, model_width), jnp.float32),
        )

    gen_noised, gen_normed = lax.cond(
        in_generator, generate, skip_generate, (gen_full, gen_rows, gen_noise)
    )
    width_now = gen_noised.shape[1]
    pieces = (
        gen_noised.reshape(2, quarter, slice_rows, width_now)
        .transpose(1, 0, 2, 3)
        .reshape(quarter, 2 * slice_rows, width_now)
    )
    send_rows = jnp.concatenate(
        [pieces, pieces, jnp.zeros((half, 2 * slice_rows, width_now), jnp.bfloat16)], axis=0
    )
    arrived = lax.all_to_all(send_rows, "fsdp", split_axis=0, concat_axis=0, tiled=True)
    score_rows = arrived[half:].reshape(2 * half * slice_rows, width_now)
    gen_slots = jnp.arange(half, dtype=jnp.int32)
    score_ids = jnp.stack([gen_slots + half, gen_slots], axis=1).reshape(2 * half)
    score_mod = jnp.dot(
        step_features(lookup(noise_step, score_ids), feature_width),
        embed_mine,
        preferred_element_type=jnp.float32,
    )
    score_full = lax.all_gather(score_rows, "mp", axis=1, tiled=True)

    def assess(full_rows):
        normed, lifted = modulate(full_rows, gain_mine, score_mod)
        return jnp.dot(lifted, weight_mine, preferred_element_type=jnp.float32).astype(jnp.bfloat16)

    def skip_assess(full_rows):
        return jnp.zeros((2 * half * slice_rows, half_width), jnp.bfloat16)

    prediction = lax.cond(in_generator, skip_assess, assess, score_full)
    grouped = prediction.reshape(half, 2, slice_rows, half_width)
    by_owner = jnp.concatenate([grouped[:, 1], grouped[:, 0]], axis=0)
    returned = lax.all_to_all(by_owner, "fsdp", split_axis=0, concat_axis=0, tiled=True)
    real_block = returned[:quarter].reshape(block_rows, half_width).astype(jnp.float32)
    fake_block = returned[quarter:half].reshape(block_rows, half_width).astype(jnp.float32)
    own_share = block_shares(lookup(noise_step, position[None]))[0]
    own_grad = (own_share * (real_block - fake_block)).astype(jnp.bfloat16)
    handed = jnp.where(in_generator, gen_noised[block_rows:], own_grad)
    taken = shifted(handed, "fsdp", half)

    def reverse(operands):
        grad_rows, normed = operands
        backward = lax.dot_general(
            grad_rows, weight_mine, (((1,), (1,)), ((), ())), preferred_element_type=jnp.float32
        )
        scaled = backward.reshape(2, block_rows, model_width) * (1.0 + gen_mod[:, None, :])
        return jnp.sum(scaled.reshape(2 * block_rows, model_width) * normed, axis=0) / block_rows

    def skip_reverse(operands):
        return jnp.zeros((model_width,), jnp.float32)

    grad_rows = jnp.concatenate([own_grad, taken], axis=0)
    gain_term = lax.cond(in_generator, reverse, skip_reverse, (grad_rows, gen_normed))
    gain_grad = lax.psum_scatter(gain_term, ("fsdp", "mp"), scatter_dimension=0, tiled=True)
    noised_out = jnp.where(in_generator, gen_noised[:block_rows], taken)
    return (noised_out, own_grad, gain_grad)


def solution(mesh):
    return jax.shard_map(
        on_device,
        mesh=mesh,
        in_specs=(
            P(("rep", "fsdp"), "mp"),
            P(("rep", "fsdp"), "mp"),
            P("rep"),
            P("rep"),
            P("fsdp", "mp"),
            P("fsdp", "mp"),
            P("fsdp", "mp"),
            P(),
            P(),
            P(),
            P(),
            P(),
            P(),
        ),
        out_specs=(P(("rep", "fsdp"), "mp"), P(("rep", "fsdp"), "mp"), P(("rep", "fsdp", "mp"))),
        check_vma=False,
    )
```

profile of v0, /device:TPU:1, one launch (start us, length us, event | category | flops | bytes accessed | tf_op | source)
XLA Modules:
  0.0 424.8 jit_solution(14154333635152818002)
XLA Ops:
  7.2 7.0 %select_select_fusion = bf16[8,384,1536]{2,1,0:T(8,128)(2,1)} fusion(pred[8]{0:T(512)(128)(4,1)S(1)} %get-tuple-element.110, pred[8]{0:T(512)(128)(4,1)S(1)} %get-tuple-element.111, bf16[384,1536]{1,0:T(8,128)(2,1)} %param.25, bf16[384,1536]{1,0:T(8,128)(2,1)} %param.24, bf16[384,1536]{1,0:T(8,128)(2,1)} %param.23), kind=kLoop, calls=%fused_computation.28 | loop fusion | flops 9437184 | bytes 12976144 | tf_op jit(solution)/shard_map/jit(_where)/select_n | solution.py:79
  14.2 6.5 %all-to-all-start = ((bf16[8,384,1536]{2,1,0:T(8,128)(2,1)}), bf16[8,384,1536]{2,1,0:T(8,128)(2,1)}, u32[]{:S(2)}, u32[]{:S(2)}) async-start(bf16[8,384,1536]{2,1,0:T(8,128)(2,1)} %select_select_fusion), calls=%async_computation | async-start | bytes 18874368 | tf_op jit(solution)/shard_map/all_to_all | solution.py:84
  20.8 4.9 %collective-permute-start = (bf16[64,1536]{1,0:T(8,128)(2,1)}, bf16[64,1536]{1,0:T(8,128)(2,1)}, u32[]{:S(2)}, u32[]{:S(2)}) collective-permute-start(bf16[64,1536]{1,0:T(8,128)(2,1)} %param.19), channel_id=1, source_target_pairs={{0,8},{2,10},{4,12},{6,14},{1,9},{3,11},{5,13},{7,15},{16,24},{18,... | collective-permute-start | bytes 589832 | tf_op jit(solution)/shard_map/ppermute | solution.py:17
  25.7 2.0 collective-permute-start.1
  28.8 0.9 constant_dynamic-update-slice_fusion.1
  31.3 146.1 %collective-permute-done = bf16[64,1536]{1,0:T(8,128)(2,1)} collective-permute-done((bf16[64,1536]{1,0:T(8,128)(2,1)}, bf16[64,1536]{1,0:T(8,128)(2,1)}, u32[]{:S(2)}, u32[]{:S(2)}) %collective-permute-start) | collective-permute-done | bytes 196640 | tf_op jit(solution)/shard_map/ppermute | solution.py:17
  177.4 0.9 constant_dynamic-update-slice_fusion
  178.4 4.7 %all_gather.6 = bf16[128,3072]{1,0:T(8,128)(2,1)S(1)} all-gather(bf16[128,1536]{1,0:T(8,128)(2,1)S(1)} %constant_dynamic-update-slice_fusion), channel_id=1, replica_groups=mesh['rep'=2,'fsdp'=8,'mp'=2] {'mp'}, dimensions={1}, use_global_device_ids=true | all-gather | bytes 1179648 | tf_op jit(solution)/shard_map/all_gather | solution.py:102
  183.0 1.8 pad_maximum_fusion.1
  184.8 40.7 %all-to-all-done = bf16[8,384,1536]{2,1,0:T(8,128)(2,1)} async-done(((bf16[8,384,1536]{2,1,0:T(8,128)(2,1)}), bf16[8,384,1536]{2,1,0:T(8,128)(2,1)}, u32[]{:S(2)}, u32[]{:S(2)}) %all-to-all-start) | async-done | bytes 9437216 | tf_op jit(solution)/shard_map/all_to_all | solution.py:84
  225.5 2.3 conditional.3
  227.9 1.0 copy.25
  229.7 67.4 %all_to_all.15 = bf16[8,64,1536]{2,1,0:T(8,128)(2,1)S(1)} all-to-all(bf16[8,64,1536]{2,1,0:T(8,128)(2,1)S(1)} %maximum_maximum_fusion), channel_id=1, replica_groups=mesh['rep'=2,'fsdp'=8,'mp'=2] {'fsdp'}, dimensions={0} | all-to-all | bytes 3145728 | tf_op jit(solution)/shard_map/all_to_all | solution.py:133
  297.2 0.9 slice.34
  298.9 9.9 %all-gather.2.cloned.1.call-done = bf16[256,3072]{1,0:T(8,128)(2,1)} async-done(((bf16[256,1536]{1,0:T(8,128)(2,1)}), bf16[256,3072]{1,0:T(8,128)(2,1)}) %all-gather.2.cloned.1.call-update) | async-done | bytes 1572880 | tf_op jit(solution)/shard_map/all_gather | solution.py:142
  308.8 8.8 %conditional.4 = (bf16[256,1536]{1,0:T(8,128)(2,1)S(1)}) conditional(s32[]{:T(128)} %convert_element_type.111, (bf16[256,3072]{1,0:T(8,128)(2,1)}, f32[3072]{0:T(1024)S(1)}, f32[8,3072]{1,0:T(8,128)S(1)}, bf16[3072,1536]{1,0:T(8,128)(2,1)}) %tuple.42, () %tuple.43), branch_computations={%region_7.9_spmd, %region_9.10_spmd} | conditional | flops 2422628608 | bytes 23117860 | solution.py:151
  308.8 1.9 fusion.5
  311.4 6.3 %convolution_convert_fusion = bf16[256,1536]{1,0:T(8,128)(2,1)S(1)} fusion(bf16[256,3072]{1,0:T(8,128)(2,1)S(1)} %fusion.8, bf16[3072,1536]{1,0:T(8,128)(2,1)} %get-tuple-element.84), kind=kOutput, calls=%fused_computation.20 | convolution fusion | flops 2416312320 | bytes 11796480 | tf_op jit(solution)/shard_map/cond/branch_0_fun/dot_general | solution.py:146
  317.7 1.0 pad_maximum_fusion
  318.7 3.9 all-to-all-start.2
  323.9 18.5 %all-to-all-done.2 = bf16[8,32,1536]{2,1,0:T(8,128)(2,1)S(1)} async-done(((bf16[8,32,1536]{2,1,0:T(8,128)(2,1)}), bf16[8,32,1536]{2,1,0:T(8,128)(2,1)S(1)}, u32[]{:S(2)}, u32[]{:S(2)}) %all-to-all-start.2) | async-done | bytes 786464 | tf_op jit(solution)/shard_map/all_to_all | solution.py:154
  342.5 1.0 collective-permute-start.2
  344.7 9.1 %collective-permute-done.2 = bf16[64,1536]{1,0:T(8,128)(2,1)S(1)} collective-permute-done((bf16[64,1536]{1,0:T(8,128)(2,1)S(1)}, bf16[64,1536]{1,0:T(8,128)(2,1)S(1)}, u32[]{:S(2)}, u32[]{:S(2)}) %collective-permute-start.2) | collective-permute-done | bytes 196640 | tf_op jit(solution)/shard_map/ppermute | solution.py:22
  353.9 62.7 %all-reduce = f32[3072]{0:T(1024)S(1)} all-reduce(f32[3072]{0:T(1024)S(1)} %get-tuple-element.121), channel_id=2, replica_groups=mesh['rep'=2,'fsdp'=8,'mp'=2] {'fsdp','mp'}, use_global_device_ids=true, to_apply=%region_13.14.clone | all-reduce | flops 3072 | bytes 24576
  (70 shorter events, 10.1 us)
Async XLA Ops:
  14.2 13.5 %copy-start.12 = (s32[8]{0:T(128)S(1)}, s32[8]{0:T(128)}, u32[]{:S(2)}) copy-start(s32[8]{0:T(128)} %param.21) | copy-start | bytes 100
  14.2 14.5 %copy-start.6 = (f32[3072]{0:T(1024)S(1)}, f32[3072]{0:T(1024)}, u32[]{:S(2)}) copy-start(f32[3072]{0:T(1024)} %param.29) | copy-start | bytes 36868
  14.2 14.5 %copy-start.7 = (f32[3072]{0:T(1024)S(1)}, f32[3072]{0:T(1024)}, u32[]{:S(2)}) copy-start(f32[3072]{0:T(1024)} %param.30) | copy-start | bytes 36868
  14.2 14.5 %copy-start.8 = (f32[3072]{0:T(1024)S(1)}, f32[3072]{0:T(1024)}, u32[]{:S(2)}) copy-start(f32[3072]{0:T(1024)} %param.31) | copy-start | bytes 36868
  14.2 15.5 %copy-start.2 = (bf16[128,3072]{1,0:T(8,128)(2,1)S(1)}, bf16[128,3072]{1,0:T(8,128)(2,1)}, u32[]{:S(2)}) copy-start(bf16[128,3072]{1,0:T(8,128)(2,1)} %param.26) | copy-start | bytes 2359300
  14.2 15.5 %copy-start.3 = (bf16[128,3072]{1,0:T(8,128)(2,1)S(1)}, bf16[128,3072]{1,0:T(8,128)(2,1)}, u32[]{:S(2)}) copy-start(bf16[128,3072]{1,0:T(8,128)(2,1)} %param.27) | copy-start | bytes 2359300
  14.2 15.5 %copy-start.4 = (bf16[128,3072]{1,0:T(8,128)(2,1)S(1)}, bf16[128,3072]{1,0:T(8,128)(2,1)}, u32[]{:S(2)}) copy-start(bf16[128,3072]{1,0:T(8,128)(2,1)} %param.28) | copy-start | bytes 2359300
  14.2 211.3 %all-to-all-start = ((bf16[8,384,1536]{2,1,0:T(8,128)(2,1)}), bf16[8,384,1536]{2,1,0:T(8,128)(2,1)}, u32[]{:S(2)}, u32[]{:S(2)}) async-start(bf16[8,384,1536]{2,1,0:T(8,128)(2,1)} %select_select_fusion), calls=%async_computation | async-start | bytes 18874368 | tf_op jit(solution)/shard_map/all_to_all | solution.py:84
  20.7 288.1 %all-gather.2.cloned.1.call-start = ((), (), s32[]{:S(2)}) async-start(), calls=%async_computation.3 | async-start | bytes 2359296 | tf_op jit(solution)/shard_map/all_gather | solution.py:142
  20.8 156.6 %collective-permute-start = (bf16[64,1536]{1,0:T(8,128)(2,1)}, bf16[64,1536]{1,0:T(8,128)(2,1)}, u32[]{:S(2)}, u32[]{:S(2)}) collective-permute-start(bf16[64,1536]{1,0:T(8,128)(2,1)} %param.19), channel_id=1, source_target_pairs={{0,8},{2,10},{4,12},{6,14},{1,9},{3,11},{5,13},{7,15},{16,24},{18,... | collective-permute-start | bytes 589832 | tf_op jit(solution)/shard_map/ppermute | solution.py:17
  25.7 157.4 %collective-permute-start.1 = (bf16[64,1536]{1,0:T(8,128)(2,1)}, bf16[64,1536]{1,0:T(8,128)(2,1)}, u32[]{:S(2)}, u32[]{:S(2)}) collective-permute-start(bf16[64,1536]{1,0:T(8,128)(2,1)} %param.20), channel_id=1, source_target_pairs={{0,8},{2,10},{4,12},{6,14},{1,9},{3,11},{5,13},{7,15},{16,24},{18,... | collective-permute-start | bytes 589832 | tf_op jit(solution)/shard_map/ppermute | solution.py:17
  27.7 1.0 copy-start.14
  29.7 1.0 copy-start.15
  297.2 1.1 copy-start.9
  308.8 1.9 copy-start
  318.7 24.7 %copy-start.13 = (u32[32]{0:T(128)S(1)}, u32[32]{0:T(128)}, u32[]{:S(2)}) copy-start(u32[32]{0:T(128)} %constant.92) | copy-start | bytes 388
  318.7 35.1 %copy-start.5 = (f32[2,3072]{1,0:T(2,128)S(1)}, f32[2,3072]{1,0:T(2,128)}, u32[]{:S(2)}) copy-start(f32[2,3072]{1,0:T(2,128)} %fusion.21) | copy-start | bytes 73732
  318.7 23.6 %all-to-all-start.2 = ((bf16[8,32,1536]{2,1,0:T(8,128)(2,1)}), bf16[8,32,1536]{2,1,0:T(8,128)(2,1)S(1)}, u32[]{:S(2)}, u32[]{:S(2)}) async-start(bf16[8,32,1536]{2,1,0:T(8,128)(2,1)} %pad_maximum_fusion), calls=%async_computation.2 | async-start | bytes 1572864 | tf_op jit(solution)/shard_map/all_to_all | solution.py:154
  342.4 11.4 %copy-start.1 = (bf16[2,32,1536]{2,1,0:T(8,128)(2,1)}, bf16[2,32,1536]{2,1,0:T(8,128)(2,1)S(1)}, u32[]{:S(2)}) copy-start(bf16[2,32,1536]{2,1,0:T(8,128)(2,1)S(1)} %multiply_convert_fusion) | copy-start | bytes 589828
  342.5 11.3 %collective-permute-start.2 = (bf16[64,1536]{1,0:T(8,128)(2,1)S(1)}, bf16[64,1536]{1,0:T(8,128)(2,1)S(1)}, u32[]{:S(2)}, u32[]{:S(2)}) collective-permute-start(bf16[64,1536]{1,0:T(8,128)(2,1)S(1)} %broadcast_select_fusion.1), channel_id=1, source_target_pairs={{0,8},{2,10},{4,12},{6,14},{8,0},{10,2},{12,4},{14,6},{1,9},{3,11}... | collective-permute-start | bytes 589832 | tf_op jit(solution)/shard_map/ppermute | solution.py:22
Sparse Core Ops, SparseCore 0:
  298.3 10.5 all-gather.1
where the time goes:
time: 430 us; the launch traced here: 425 us
  waiting for transfers between devices  224 us (52%)
  blocking collectives  135 us (31%)
  starting transfers between devices  18.2 us (4%)
  other arithmetic  16.1 us (4%)
  between operations  15.6 us (4%)
  local copies, waits for them, and re-layouts  8.27 us (2%)
  matrix products  7.41 us (2%)
    ppermute x2, waiting for transfers between devices, from_behind(): return lax.ppermute(value, axis, pairs)  146 us
    all_to_all x1, blocking collectives, on_device(): lax.all_to_all(send_rows, 'fsdp', split_axis=0, concat_axis=0, tiled=True)  67.4 us
    unnamed x1, blocking collectives  62.7 us
    all_to_all x1, waiting for transfers between devices, on_device(): lax.all_to_all(outgoing, 'fsdp', split_axis=0, concat_axis=0, tiled=True)  40.7 us
    all_to_all x1, waiting for transfers between devices, on_device(): lax.all_to_all(by_owner, 'fsdp', split_axis=0, concat_axis=0, tiled=True)  18.5 us
    all_gather x1, waiting for transfers between devices, on_device(): score_full = lax.all_gather(score_rows, 'mp', axis=1, tiled=True)  9.93 us
    ppermute x1, waiting for transfers between devices, shifted(): lax.ppermute(value, axis, [(i, (i + by) % size) for i in range(size)])  9.09 us
  transfers between devices with their start and end apart: 6, of which 5 were waited for; matrix products, arithmetic and copies ran while one was open for 2% of the time, Pallas kernels for 0%

commit v1 on v0

--- a/solution.py
+++ b/solution.py
@@ -46,7 +46,7 @@
     return (normed, lifted.reshape(values.shape).astype(jnp.bfloat16))
 
 
-def on_device(
+def on_groups(
     noise_in,
     renoise,
     gen_step,
@@ -177,7 +177,154 @@
     return (noised_out, own_grad, gain_grad)
 
 
+def on_tiles(
+    noise_in,
+    renoise,
+    gen_step,
+    noise_step,
+    gen_weight,
+    real_weight,
+    fake_weight,
+    gen_embed,
+    real_embed,
+    fake_embed,
+    gen_gain,
+    real_gain,
+    fake_gain,
+):
+    g = lax.axis_size("fsdp") // 2
+    position, c = lax.axis_index("fsdp"), lax.axis_index("mp")
+    s, q = position // g, position % g
+    r, h = noise_in.shape
+    d = 2 * h
+    w = h // g
+    feature_width = gen_embed.shape[0]
+    f32, bf16 = jnp.float32, jnp.bfloat16
+    both = ("fsdp", "mp")
+    near = [q ^ k for k in range(g)]
+
+    def flat(s_, q_, c_):
+        return (s_ * g + q_) * 2 + c_
+
+    every = [(s_, q_, c_) for s_ in (0, 1) for q_ in range(g) for c_ in (0, 1)]
+
+    def in_square(value, k):
+        return lax.ppermute(value, "fsdp", [(i, i ^ k) for i in range(2 * g)])
+
+    def across(value):
+        return lax.ppermute(value, "fsdp", [(i, i ^ g) for i in range(2 * g)])
+
+    def cores(value):
+        return lax.ppermute(value, "mp", [(0, 1), (1, 0)])
+
+    def turned(value):
+        moved = lax.ppermute(value, both, [(flat(*i), flat(i[2], i[1], i[0])) for i in every if i[0] != i[2]])
+        return jnp.where(s == c, value, moved)
+
+    def piece(array, k):
+        return lax.dynamic_slice_in_dim(array, near[k] * w, w, 1)
+
+    def relative(array):
+        return jnp.concatenate([piece(array, k) for k in range(g)], axis=1)
+
+    def regroup(array, k, axis):
+        parts = jnp.split(array, g, axis)
+        return jnp.concatenate([parts[j ^ k] for j in range(g)], axis)
+
+    def mine(vector):
+        half = lax.dynamic_slice_in_dim(vector, s * h, h, vector.ndim - 1)
+        return relative(half.reshape(-1, h))
+
+    def spread(weight):
+        return jnp.concatenate([piece(weight, 0)] + [in_square(piece(weight, k), k) for k in range(1, g)], axis=0)
+
+    ids = c * g + jnp.stack(near)
+
+    def modulation(steps, embed):
+        return 1.0 + jnp.dot(step_features(lookup(steps, ids), feature_width), mine(embed), preferred_element_type=f32)
+
+    def lifted(values, scale):
+        return (values.astype(f32).reshape(g, r, -1) * scale[:, None, :]).astype(bf16).reshape(g * r, -1)
+
+    shares = jnp.repeat(block_shares(lookup(noise_step, ids)).reshape(g, 1), r, axis=0)
+
+    gen_own = spread(gen_weight)
+    x_turned = turned(relative(noise_in))
+    fresh_turned = turned(relative(renoise))
+    x = jnp.concatenate([x_turned] + [regroup(in_square(x_turned, k), k, 1) for k in range(1, g)], axis=0)
+    fresh = jnp.concatenate(
+        [fresh_turned[:, :w]] + [in_square(fresh_turned[:, k * w : (k + 1) * w], k) for k in range(1, g)], axis=0
+    )
+    gen_other = cores(gen_own)
+    gen_tile = jnp.concatenate([gen_own, gen_other], axis=1)
+
+    def row_sums(values):
+        wide = values.astype(f32)
+        return jnp.sum(wide * wide, axis=1, keepdims=True)
+
+    def row_scale(partial):
+        total = partial + across(partial.reshape(g, r)).reshape(g * r, 1)
+        return lax.rsqrt(total / d + norm_epsilon)
+
+    gen_scale = modulation(gen_step, gen_embed)
+    x_scale = row_scale(row_sums(x))
+    product = jnp.dot(lifted(x, gen_scale * mine(gen_gain)), gen_tile, preferred_element_type=f32)
+    keep = jnp.where(s == c, product[:, :w], product[:, w:])
+    away = jnp.where(s == c, product[:, w:], product[:, :w]).astype(bf16)
+    latents = x[:, :w].astype(f32) + x_scale * (keep + across(away).astype(f32))
+    noised_piece = ((1.0 - shares) * latents + shares * fresh.astype(f32)).astype(bf16)
+
+    real_own, fake_own = spread(real_weight), spread(fake_weight)
+    score_tile = jnp.concatenate([real_own, fake_own], axis=0)
+    score_other = cores(score_tile)
+    noised = jnp.concatenate(
+        [noised_piece] + [regroup(in_square(noised_piece, k), k, 0) for k in range(1, g)], axis=1
+    )
+    noised_scale = row_scale(row_sums(noised))
+    lifts = jnp.concatenate(
+        [
+            lifted(noised, modulation(noise_step, real_embed) * mine(real_gain)),
+            lifted(noised, -(modulation(noise_step, fake_embed) * mine(fake_gain))),
+        ],
+        axis=1,
+    )
+    gap = jnp.concatenate(
+        [
+            jnp.dot(lifts, score_tile, preferred_element_type=f32),
+            jnp.dot(lifts, score_other, preferred_element_type=f32),
+        ],
+        axis=1,
+    )
+    gap = gap + across(gap.astype(bf16)).astype(f32)
+    grad = (shares * noised_scale * gap).astype(bf16)
+
+    def absolute(array):
+        return relative(array)
+
+    def owners(value, k):
+        return lax.ppermute(value, both, [(flat(a, q_, a), flat(a, q_ ^ k, a)) for a in (0, 1) for q_ in range(g)])
+
+    owned = [grad[:r]] + [owners(grad[k * r : (k + 1) * r], k) for k in range(1, g)]
+    owned_here = jnp.concatenate([o[:, :w] for o in owned], axis=1)
+    owned_there = jnp.concatenate([o[:, w:] for o in owned], axis=1)
+    latent_grad = absolute(jnp.where(s == c, owned_here, cores(owned_there)))
+    noised_out = absolute(turned(noised[:r]))
+
+    backward = lax.dot_general(grad, gen_tile, (((1,), (1,)), ((), ())), preferred_element_type=f32)
+    terms = (backward.reshape(g, r, h) * gen_scale[:, None, :]).reshape(g * r, h) * (x.astype(f32) * x_scale)
+    sums = (jnp.sum(terms, axis=0) / r).reshape(g, 2, w // 2)
+    here = lax.dynamic_index_in_dim(sums, c, 1, False)
+    there = lax.dynamic_index_in_dim(sums, 1 - c, 1, False)
+    here = here + cores(there)
+    gain_grad = here[0]
+    for k in range(1, g):
+        gain_grad = gain_grad + in_square(here[k], k)
+    return (noised_out, latent_grad, gain_grad)
+
+
 def solution(mesh):
+    positions = mesh.shape["fsdp"]
+    on_device = on_tiles if positions in (4, 8, 16) and mesh.shape["mp"] == 2 else on_groups
     return jax.shard_map(
         on_device,
         mesh=mesh,

time: 430 us -> 155 us (0.36)
  waiting for transfers between devices: 224 us -> 55.9 us
  blocking collectives: 135 us -> 0 us
  starting transfers between devices: 18.2 us -> 49.7 us
  local copies, waits for them, and re-layouts: 8.27 us -> 23.3 us
  between operations: 15.6 us -> 1.55 us
  other arithmetic: 16.1 us -> 10.6 us
  matrix products: 7.41 us -> 12.8 us
    ppermute x3 -> x35, waiting for transfers between devices: 155 us -> 55.9 us  [the longest x4 37.7 us: across(): return lax.ppermute(value, 'fsdp', [(i, i ^ g) for i in range(2 * g)])]
    all_to_all x1 -> x0, blocking collectives: 67.4 us -> none  [on_device(): lax.all_to_all(send_rows, 'fsdp', split_axis=0, concat_axis=0, tiled=True)]
    unnamed x1 -> x0, blocking collectives: 62.7 us -> none
    all_to_all x2 -> x0, waiting for transfers between devices: 59.2 us -> none  [the longest x1 40.7 us: on_device(): lax.all_to_all(outgoing, 'fsdp', split_axis=0, concat_axis=0, tiled=True)]
    ppermute x3 -> x35, starting transfers between devices: 7.82 us -> 49.7 us  [the longest x21 21.3 us: in_square(): return lax.ppermute(value, 'fsdp', [(i, i ^ k) for i in range(2 * g)])]
    all_to_all x2 -> x0, starting transfers between devices: 10.4 us -> none  [the longest x1 6.5 us: on_device(): lax.all_to_all(outgoing, 'fsdp', split_axis=0, concat_axis=0, tiled=True)]
    all_gather x1 -> x0, waiting for transfers between devices: 9.93 us -> none  [on_device(): score_full = lax.all_gather(score_rows, 'mp', axis=1, tiled=True)]
    dynamic_slice x0 -> x21, local copies, waits for them, and re-layouts: none -> 9.86 us  [the longest x20 9.85 us: piece(): return lax.dynamic_slice_in_dim(array, near[k] * w, w, 1)]
  transfers between devices with their start and end apart: 6 -> 35, of which waited for: 5 -> 9; matrix products, arithmetic and copies ran while one was open for 2% -> 26% of each run, Pallas kernels for 0% -> 0%
where the time goes in v1:
time: 155 us; the launch traced here: 154 us
  waiting for transfers between devices  55.9 us (36%)
  starting transfers between devices  49.7 us (32%)
  local copies, waits for them, and re-layouts  23.3 us (15%)
  matrix products  12.8 us (8%)
  other arithmetic  10.6 us (7%)
  between operations  1.55 us (1%)
    ppermute x4, waiting for transfers between devices, across(): return lax.ppermute(value, 'fsdp', [(i, i ^ g) for i in range(2 * g)])  37.7 us
    ppermute x21, starting transfers between devices, in_square(): return lax.ppermute(value, 'fsdp', [(i, i ^ k) for i in range(2 * g)])  21.3 us
    ppermute x21, waiting for transfers between devices, in_square(): return lax.ppermute(value, 'fsdp', [(i, i ^ k) for i in range(2 * g)])  17.6 us
    ppermute x3, starting transfers between devices, turned(): lax.ppermute(value, both, [(flat(*i), flat(i[2], i[1], i[0])) for i in ev...  11.8 us
    ppermute x4, starting transfers between devices, cores(): return lax.ppermute(value, 'mp', [(0, 1), (1, 0)])  11 us
    dynamic_slice x20, local copies, waits for them, and re-layouts, piece(): return lax.dynamic_slice_in_dim(array, near[k] * w, w, 1)  9.85 us
    unnamed x82, local copies, waits for them, and re-layouts  8.07 us
    dot_general x1, matrix products, on_tiles(): jnp.dot(lifted(x, gen_scale * mine(gen_gain)), gen_tile, preferred_elemen...  4.86 us
  transfers between devices with their start and end apart: 35, of which 9 were waited for; matrix products, arithmetic and copies ran while one was open for 26% of the time, Pallas kernels for 0%

profile of v1, /device:TPU:1, one launch (start us, length us, event | category | flops | bytes accessed | tf_op | source)
XLA Modules:
  0.0 153.9 jit_solution(4236524398057986597)
XLA Ops:
  1.9 5.7 %collective-permute-start = (bf16[64,1536]{1,0:T(8,128)(2,1)S(1)}, bf16[64,1536]{1,0:T(8,128)(2,1)}, u32[]{:S(2)}, u32[]{:S(2)}) collective-permute-start(bf16[64,1536]{1,0:T(8,128)(2,1)S(1)} %pad_maximum_fusion.6), channel_id=1, source_target_pairs={{1,8},{3,10},{5,12},{7,14},{8,1},{10,3},{12,5},{14,7},{17,24},{19,... | collective-permute-start | bytes 589832 | tf_op jit(solution)/shard_map/ppermute | solution.py:221
  8.6 2.2 %collective-permute-start.7 = (bf16[384,384]{1,0:T(8,128)(2,1)}, bf16[384,384]{1,0:T(8,128)(2,1)S(1)}, u32[]{:S(2)}, u32[]{:S(2)}) collective-permute-start(bf16[384,384]{1,0:T(8,128)(2,1)} %get-tuple-element.19), channel_id=1, source_target_pairs={{0,6},{2,4},{4,2},{6,0},{8,14},{10,12},{12,10},{14,8},{1,7},{3,5},... | collective-permute-start | bytes 884744 | tf_op jit(solution)/shard_map/ppermute | solution.py:212
  11.2 2.8 %collective-permute-start.10 = (bf16[64,1536]{1,0:T(8,128)(2,1)S(1)}, bf16[64,1536]{1,0:T(8,128)(2,1)S(1)}, u32[]{:S(2)}, u32[]{:S(2)}) collective-permute-start(bf16[64,1536]{1,0:T(8,128)(2,1)S(1)} %pad_maximum_fusion.7), channel_id=1, source_target_pairs={{1,8},{3,10},{5,12},{7,14},{8,1},{10,3},{12,5},{14,7},{17,24},{19,... | collective-permute-start | bytes 589832 | tf_op jit(solution)/shard_map/ppermute | solution.py:221
  18.5 2.0 %constant_dynamic-slice_fusion.35 = (bf16[128,384]{1,0:T(8,128)(2,1)S(1)}, bf16[128,384]{1,0:T(8,128)(2,1)S(1)}, bf16[128,384]{1,0:T(8,128)(2,1)}, bf16[128,384]{1,0:T(8,128)(2,1)}) fusion(bf16[128,3072]{1,0:T(8,128)(2,1)} %param.20, s32[]{:T(128)S(6)} %dynamic_slice.193, s32[]{:T(128)S(6)} %dynamic_slice.195, s32[]{:T(128)S(6)} %dynamic_slice.199, ...), kind=kLoop, calls=%fused_computation.106 | loop fusion | bytes 786448 | tf_op jit(solution)/shard_map/dynamic_slice | solution.py:225
  23.8 2.4 %constant_dynamic-slice_fusion.15 = (bf16[128,384]{1,0:T(8,128)(2,1)}, bf16[128,384]{1,0:T(8,128)(2,1)}, bf16[128,384]{1,0:T(8,128)(2,1)}, bf16[128,384]{1,0:T(8...) fusion(bf16[128,3072]{1,0:T(8,128)(2,1)} %param.22, ...), kind=kLoop, calls=%fused_computation.86 | loop fusion | bytes 1572880 | tf_op jit(solution)/shard_map/dynamic_slice | solution.py:225
  32.6 2.2 %collective-permute-start.3 = (bf16[64,1536]{1,0:T(8,128)(2,1)S(1)}, bf16[64,1536]{1,0:T(8,128)(2,1)S(1)}, u32[]{:S(2)}, u32[]{:S(2)}) collective-permute-start(bf16[64,1536]{1,0:T(8,128)(2,1)S(1)} %broadcast_select_fusion.2), channel_id=1, source_target_pairs={{0,6},{2,4},{4,2},{6,0},{8,14},{10,12},{12,10},{14,8},{1,7},{3,5},... | collective-permute-start | bytes 589832 | tf_op jit(solution)/shard_map/ppermute | solution.py:212
  35.2 8.4 %collective-permute-done.19 = bf16[384,384]{1,0:T(8,128)(2,1)S(1)} collective-permute-done((bf16[384,384]{1,0:T(8,128)(2,1)}, bf16[384,384]{1,0:T(8,128)(2,1)S(1)}, u32[]{:S(2)}, u32[]{:S(2)}) %collective-permute-start.19) | collective-permute-done | bytes 294944 | tf_op jit(solution)/shard_map/ppermute | solution.py:212
  50.7 1.9 %collective-permute-start.24 = (bf16[384,384]{1,0:T(8,128)(2,1)}, bf16[384,384]{1,0:T(8,128)(2,1)}, u32[]{:S(2)}, u32[]{:S(2)}) collective-permute-start(bf16[384,384]{1,0:T(8,128)(2,1)} %get-tuple-element.9), channel_id=1, source_target_pairs={{0,6},{2,4},{4,2},{6,0},{8,14},{10,12},{12,10},{14,8},{1,7},{3,5},... | collective-permute-start | bytes 884744 | tf_op jit(solution)/shard_map/ppermute | solution.py:212
  53.8 9.7 %collective-permute-done.4 = f32[4,64]{1,0:T(4,128)S(1)} collective-permute-done((f32[4,64]{1,0:T(4,128)S(1)}, f32[4,64]{1,0:T(4,128)S(1)}, u32[]{:S(2)}, u32[]{:S(2)}) %collective-permute-start.4) | collective-permute-done | bytes 1056 | tf_op jit(solution)/shard_map/ppermute | solution.py:215
  64.1 1.8 %collective-permute-start.13 = (bf16[64,384]{1,0:T(8,128)(2,1)}, bf16[64,384]{1,0:T(8,128)(2,1)S(1)}, u32[]{:S(2)}, u32[]{:S(2)}) collective-permute-start(bf16[64,384]{1,0:T(8,128)(2,1)} %get-tuple-element.59), channel_id=1, source_target_pairs={{0,6},{2,4},{4,2},{6,0},{8,14},{10,12},{12,10},{14,8},{1,7},{3,5},... | collective-permute-start | bytes 147464 | tf_op jit(solution)/shard_map/ppermute | solution.py:212
  74.4 4.9 %fusion.46 = f32[256,768]{1,0:T(8,128)S(1)} fusion(bf16[256,1536]{1,0:T(8,128)(2,1)S(1)} %fusion.5, bf16[1536,384]{1,0:T(8,128)(2,1)} %collective-permute-done.8, bf16[384,384]{1,0:T(8,128)(2,1)S(1)} %collective-permute-done.7, bf16[384,384]{1,0:T(8,128)(2,1)S(1)} %copy-done.5, bf16[384,384]{1,0:T(8,128)(2,1)S(1)} %copy-done.8, ...), kind=kOutput, calls=%fused_computation.144 | convolution fusion | flops 615776256 | bytes 3932160 | tf_op jit(solution)/shard_map/dot_general | solution.py:271
  79.4 2.7 %collective-permute-start.9 = (bf16[256,384]{1,0:T(8,128)(2,1)S(1)}, bf16[256,384]{1,0:T(8,128)(2,1)S(1)}, u32[]{:S(2)}, u32[]{:S(2)}) collective-permute-start(bf16[256,384]{1,0:T(8,128)(2,1)S(1)} %select_convert_fusion), channel_id=1, source_target_pairs={{0,8},{2,10},{4,12},{6,14},{8,0},{10,2},{12,4},{14,6},{1,9},{3,11}... | collective-permute-start | bytes 589832 | tf_op jit(solution)/shard_map/ppermute | solution.py:215
  82.1 9.4 %collective-permute-done.9 = bf16[256,384]{1,0:T(8,128)(2,1)S(1)} collective-permute-done((bf16[256,384]{1,0:T(8,128)(2,1)S(1)}, bf16[256,384]{1,0:T(8,128)(2,1)S(1)}, u32[]{:S(2)}, u32[]{:S(2)}) %collective-permute-start.9) | collective-permute-done | bytes 196640 | tf_op jit(solution)/shard_map/ppermute | solution.py:215
  92.2 2.7 %collective-permute-start.15 = (bf16[256,384]{1,0:T(8,128)(2,1)S(1)}, bf16[256,384]{1,0:T(8,128)(2,1)S(1)}, u32[]{:S(2)}, u32[]{:S(2)}) collective-permute-start(bf16[256,384]{1,0:T(8,128)(2,1)S(1)} %add_convert_fusion), channel_id=1, source_target_pairs={{0,4},{2,6},{4,0},{6,2},{8,12},{10,14},{12,8},{14,10},{1,5},{3,7},... | collective-permute-start | bytes 589832 | tf_op jit(solution)/shard_map/ppermute | solution.py:212
  94.9 3.7 %collective-permute-done.16 = bf16[256,384]{1,0:T(8,128)(2,1)S(1)} collective-permute-done((bf16[256,384]{1,0:T(8,128)(2,1)S(1)}, bf16[256,384]{1,0:T(8,128)(2,1)S(1)}, u32[]{:S(2)}, u32[]{:S(2)}) %collective-permute-start.16) | collective-permute-done | bytes 196640 | tf_op jit(solution)/shard_map/ppermute | solution.py:212
  98.6 4.9 %collective-permute-done.14 = bf16[256,384]{1,0:T(8,128)(2,1)S(1)} collective-permute-done((bf16[256,384]{1,0:T(8,128)(2,1)S(1)}, bf16[256,384]{1,0:T(8,128)(2,1)S(1)}, u32[]{:S(2)}, u32[]{:S(2)}) %collective-permute-start.14) | collective-permute-done | bytes 196640 | tf_op jit(solution)/shard_map/ppermute | solution.py:212
  103.9 3.3 %collective-permute-start.17 = (bf16[64,1536]{1,0:T(8,128)(2,1)S(1)}, bf16[64,1536]{1,0:T(8,128)(2,1)}, u32[]{:S(2)}, u32[]{:S(2)}) collective-permute-start(bf16[64,1536]{1,0:T(8,128)(2,1)S(1)} %slice.108), channel_id=1, source_target_pairs={{1,8},{3,10},{5,12},{7,14},{8,1},{10,3},{12,5},{14,7},{17,24},{19,... | collective-permute-start | bytes 589832 | tf_op jit(solution)/shard_map/ppermute | solution.py:221
  110.3 2.0 %collective-permute-done.18 = f32[4,64]{1,0:T(4,128)S(1)} collective-permute-done((f32[4,64]{1,0:T(4,128)S(1)}, f32[4,64]{1,0:T(4,128)S(1)}, u32[]{:S(2)}, u32[]{:S(2)}) %collective-permute-start.18) | collective-permute-done | bytes 1056 | tf_op jit(solution)/shard_map/ppermute | solution.py:215
  112.3 2.9 %fusion.10 = f32[256,384]{1,0:T(8,128)S(1)} fusion(bf16[3072,384]{1,0:T(8,128)(2,1)} %collective-permute-done.25, bf16[256,1536]{1,0:T(8,128)(2,1)} %copy-done.3, bf16[256,1536]{1,0:T(8,128)(2,1)S(1)} %get-tuple-element.21), kind=kOutput, calls=%fused_computation.23 | convolution fusion | flops 607125504 | bytes 4325376 | tf_op jit(solution)/shard_map/dot_general | solution.py:294
  117.9 16.6 %collective-permute-done.26 = bf16[256,768]{1,0:T(8,128)(2,1)S(1)} collective-permute-done((bf16[256,768]{1,0:T(8,128)(2,1)S(1)}, bf16[256,768]{1,0:T(8,128)(2,1)S(1)}, u32[]{:S(2)}, u32[]{:S(2)}) %collective-permute-start.26) | collective-permute-done | bytes 393248 | tf_op jit(solution)/shard_map/ppermute | solution.py:215
  134.9 2.2 %fusion.9 = f32[1536]{0:T(1024)S(1)} fusion(bf16[256,1536]{1,0:T(8,128)(2,1)S(1)} %get-tuple-element.8, f32[256,1536]{1,0:T(8,128)S(1)} %bitcast.24, bf16[256,768]{1,0:T(8,128)(2,1)S(1)} %multiply_convert_fusion, f32[256]{0:T(256)S(1)} %copy-done.26, bf16[1536,384]{1,0:T(8,128)(2,1)} %collective-permute-done.8, ...), kind=kOutput, calls=%fused_computation.21 | convolution fusion | flops 617740800 | bytes 5118976 | tf_op jit(solution)/shard_map/dot_general | solution.py:313
  137.2 1.7 %collective-permute-start.31 = (f32[4,192]{1,0:T(4,128)S(1)}, f32[4,192]{1,0:T(4,128)S(1)}, u32[]{:S(2)}, u32[]{:S(2)}) collective-permute-start(f32[4,192]{1,0:T(4,128)S(1)} %bitcast.25), channel_id=1, source_target_pairs={{0,1},{1,0},{2,3},{3,2},{4,5},{5,4},{6,7},{7,6},{8,9},{9,8},{10,11... | collective-permute-start | bytes 9224 | tf_op jit(solution)/shard_map/ppermute | solution.py:218
  141.2 2.5 %collective-permute-start.32 = (f32[192]{0:T(256)S(1)}, f32[192]{0:T(256)S(1)}, u32[]{:S(2)}, u32[]{:S(2)}) collective-permute-start(f32[192]{0:T(256)S(1)} %bitcast.27), channel_id=1, source_target_pairs={{0,2},{2,0},{4,6},{6,4},{8,10},{10,8},{12,14},{14,12},{1,3},{3,1},... | collective-permute-start | bytes 2312 | tf_op jit(solution)/shard_map/ppermute | solution.py:212
  143.9 8.1 %collective-permute-start.30 = (bf16[64,1536]{1,0:T(8,128)(2,1)S(1)}, bf16[64,1536]{1,0:T(8,128)(2,1)S(1)}, u32[]{:S(2)}, u32[]{:S(2)}) collective-permute-start(bf16[64,1536]{1,0:T(8,128)(2,1)S(1)} %pad_maximum_fusion.9), channel_id=1, source_target_pairs={{0,1},{1,0},{2,3},{3,2},{4,5},{5,4},{6,7},{7,6},{8,9},{9,8},{10,11... | collective-permute-start | bytes 589832 | tf_op jit(solution)/shard_map/ppermute | solution.py:218
  (215 shorter events, 45.4 us)
Async XLA Ops:
  1.9 26.9 %collective-permute-start = (bf16[64,1536]{1,0:T(8,128)(2,1)S(1)}, bf16[64,1536]{1,0:T(8,128)(2,1)}, u32[]{:S(2)}, u32[]{:S(2)}) collective-permute-start(bf16[64,1536]{1,0:T(8,128)(2,1)S(1)} %pad_maximum_fusion.6), channel_id=1, source_target_pairs={{1,8},{3,10},{5,12},{7,14},{8,1},{10,3},{12,5},{14,7},{17,24},{19,... | collective-permute-start | bytes 589832 | tf_op jit(solution)/shard_map/ppermute | solution.py:221
  8.6 23.9 %collective-permute-start.7 = (bf16[384,384]{1,0:T(8,128)(2,1)}, bf16[384,384]{1,0:T(8,128)(2,1)S(1)}, u32[]{:S(2)}, u32[]{:S(2)}) collective-permute-start(bf16[384,384]{1,0:T(8,128)(2,1)} %get-tuple-element.19), channel_id=1, source_target_pairs={{0,6},{2,4},{4,2},{6,0},{8,14},{10,12},{12,10},{14,8},{1,7},{3,5},... | collective-permute-start | bytes 884744 | tf_op jit(solution)/shard_map/ppermute | solution.py:212
  10.8 21.8 %collective-permute-start.6 = (bf16[384,384]{1,0:T(8,128)(2,1)}, bf16[384,384]{1,0:T(8,128)(2,1)S(1)}, u32[]{:S(2)}, u32[]{:S(2)}) collective-permute-start(bf16[384,384]{1,0:T(8,128)(2,1)} %get-tuple-element.20), channel_id=1, source_target_pairs={{0,4},{2,6},{4,0},{6,2},{8,12},{10,14},{12,8},{14,10},{1,5},{3,7},... | collective-permute-start | bytes 884744 | tf_op jit(solution)/shard_map/ppermute | solution.py:212
  11.0 23.9 %collective-permute-start.5 = (bf16[384,384]{1,0:T(8,128)(2,1)}, bf16[384,384]{1,0:T(8,128)(2,1)S(1)}, u32[]{:S(2)}, u32[]{:S(2)}) collective-permute-start(bf16[384,384]{1,0:T(8,128)(2,1)} %get-tuple-element.18), channel_id=1, source_target_pairs={{0,2},{2,0},{4,6},{6,4},{8,10},{10,8},{12,14},{14,12},{1,3},{3,1},... | collective-permute-start | bytes 884744 | tf_op jit(solution)/shard_map/ppermute | solution.py:212
  11.2 19.8 %collective-permute-start.10 = (bf16[64,1536]{1,0:T(8,128)(2,1)S(1)}, bf16[64,1536]{1,0:T(8,128)(2,1)S(1)}, u32[]{:S(2)}, u32[]{:S(2)}) collective-permute-start(bf16[64,1536]{1,0:T(8,128)(2,1)S(1)} %pad_maximum_fusion.7), channel_id=1, source_target_pairs={{1,8},{3,10},{5,12},{7,14},{8,1},{10,3},{12,5},{14,7},{17,24},{19,... | collective-permute-start | bytes 589832 | tf_op jit(solution)/shard_map/ppermute | solution.py:221
  28.8 14.8 %collective-permute-start.19 = (bf16[384,384]{1,0:T(8,128)(2,1)}, bf16[384,384]{1,0:T(8,128)(2,1)S(1)}, u32[]{:S(2)}, u32[]{:S(2)}) collective-permute-start(bf16[384,384]{1,0:T(8,128)(2,1)} %get-tuple-element.14), channel_id=1, source_target_pairs={{0,2},{2,0},{4,6},{6,4},{8,10},{10,8},{12,14},{14,12},{1,3},{3,1},... | collective-permute-start | bytes 884744 | tf_op jit(solution)/shard_map/ppermute | solution.py:212
  31.0 13.7 %collective-permute-start.20 = (bf16[384,384]{1,0:T(8,128)(2,1)}, bf16[384,384]{1,0:T(8,128)(2,1)S(1)}, u32[]{:S(2)}, u32[]{:S(2)}) collective-permute-start(bf16[384,384]{1,0:T(8,128)(2,1)} %get-tuple-element.16), channel_id=1, source_target_pairs={{0,4},{2,6},{4,0},{6,2},{8,12},{10,14},{12,8},{14,10},{1,5},{3,7},... | collective-permute-start | bytes 884744 | tf_op jit(solution)/shard_map/ppermute | solution.py:212
  32.4 13.5 %collective-permute-start.21 = (bf16[384,384]{1,0:T(8,128)(2,1)}, bf16[384,384]{1,0:T(8,128)(2,1)S(1)}, u32[]{:S(2)}, u32[]{:S(2)}) collective-permute-start(bf16[384,384]{1,0:T(8,128)(2,1)} %get-tuple-element.13), channel_id=1, source_target_pairs={{0,6},{2,4},{4,2},{6,0},{8,14},{10,12},{12,10},{14,8},{1,7},{3,5},... | collective-permute-start | bytes 884744 | tf_op jit(solution)/shard_map/ppermute | solution.py:212
  32.6 16.7 %collective-permute-start.3 = (bf16[64,1536]{1,0:T(8,128)(2,1)S(1)}, bf16[64,1536]{1,0:T(8,128)(2,1)S(1)}, u32[]{:S(2)}, u32[]{:S(2)}) collective-permute-start(bf16[64,1536]{1,0:T(8,128)(2,1)S(1)} %broadcast_select_fusion.2), channel_id=1, source_target_pairs={{0,6},{2,4},{4,2},{6,0},{8,14},{10,12},{12,10},{14,8},{1,7},{3,5},... | collective-permute-start | bytes 589832 | tf_op jit(solution)/shard_map/ppermute | solution.py:212
  34.9 17.8 %collective-permute-start.2 = (bf16[64,1536]{1,0:T(8,128)(2,1)S(1)}, bf16[64,1536]{1,0:T(8,128)(2,1)S(1)}, u32[]{:S(2)}, u32[]{:S(2)}) collective-permute-start(bf16[64,1536]{1,0:T(8,128)(2,1)S(1)} %broadcast_select_fusion.2), channel_id=1, source_target_pairs={{0,4},{2,6},{4,0},{6,2},{8,12},{10,14},{12,8},{14,10},{1,5},{3,7},... | collective-permute-start | bytes 589832 | tf_op jit(solution)/shard_map/ppermute | solution.py:212
  44.7 29.7 %collective-permute-start.8 = (bf16[1536,384]{1,0:T(8,128)(2,1)S(1)}, bf16[1536,384]{1,0:T(8,128)(2,1)}, u32[]{:S(2)}, u32[]{:S(2)}) collective-permute-start(bf16[1536,384]{1,0:T(8,128)(2,1)S(1)} %pad_maximum_fusion.2), channel_id=1, source_target_pairs={{0,1},{1,0},{2,3},{3,2},{4,5},{5,4},{6,7},{7,6},{8,9},{9,8},{10,11... | collective-permute-start | bytes 3538952 | tf_op jit(solution)/shard_map/ppermute | solution.py:218
  47.7 19.5 %collective-permute-start.22 = (bf16[384,384]{1,0:T(8,128)(2,1)}, bf16[384,384]{1,0:T(8,128)(2,1)}, u32[]{:S(2)}, u32[]{:S(2)}) collective-permute-start(bf16[384,384]{1,0:T(8,128)(2,1)} %get-tuple-element.10), channel_id=1, source_target_pairs={{0,2},{2,0},{4,6},{6,4},{8,10},{10,8},{12,14},{14,12},{1,3},{3,1},... | collective-permute-start | bytes 884744 | tf_op jit(solution)/shard_map/ppermute | solution.py:212
  49.4 19.8 %collective-permute-start.23 = (bf16[384,384]{1,0:T(8,128)(2,1)}, bf16[384,384]{1,0:T(8,128)(2,1)}, u32[]{:S(2)}, u32[]{:S(2)}) collective-permute-start(bf16[384,384]{1,0:T(8,128)(2,1)} %get-tuple-element.12), channel_id=1, source_target_pairs={{0,4},{2,6},{4,0},{6,2},{8,12},{10,14},{12,8},{14,10},{1,5},{3,7},... | collective-permute-start | bytes 884744 | tf_op jit(solution)/shard_map/ppermute | solution.py:212
  50.7 20.9 %collective-permute-start.24 = (bf16[384,384]{1,0:T(8,128)(2,1)}, bf16[384,384]{1,0:T(8,128)(2,1)}, u32[]{:S(2)}, u32[]{:S(2)}) collective-permute-start(bf16[384,384]{1,0:T(8,128)(2,1)} %get-tuple-element.9), channel_id=1, source_target_pairs={{0,6},{2,4},{4,2},{6,0},{8,14},{10,12},{12,10},{14,8},{1,7},{3,5},... | collective-permute-start | bytes 884744 | tf_op jit(solution)/shard_map/ppermute | solution.py:212
  64.1 18.0 %collective-permute-start.13 = (bf16[64,384]{1,0:T(8,128)(2,1)}, bf16[64,384]{1,0:T(8,128)(2,1)S(1)}, u32[]{:S(2)}, u32[]{:S(2)}) collective-permute-start(bf16[64,384]{1,0:T(8,128)(2,1)} %get-tuple-element.59), channel_id=1, source_target_pairs={{0,6},{2,4},{4,2},{6,0},{8,14},{10,12},{12,10},{14,8},{1,7},{3,5},... | collective-permute-start | bytes 147464 | tf_op jit(solution)/shard_map/ppermute | solution.py:212
  67.3 14.9 %collective-permute-start.12 = (bf16[64,384]{1,0:T(8,128)(2,1)S(1)}, bf16[64,384]{1,0:T(8,128)(2,1)S(1)}, u32[]{:S(2)}, u32[]{:S(2)}) collective-permute-start(bf16[64,384]{1,0:T(8,128)(2,1)S(1)} %get-tuple-element.60), channel_id=1, source_target_pairs={{0,4},{2,6},{4,0},{6,2},{8,12},{10,14},{12,8},{14,10},{1,5},{3,7},... | collective-permute-start | bytes 147464 | tf_op jit(solution)/shard_map/ppermute | solution.py:212
  69.2 13.0 %collective-permute-start.11 = (bf16[64,384]{1,0:T(8,128)(2,1)S(1)}, bf16[64,384]{1,0:T(8,128)(2,1)S(1)}, u32[]{:S(2)}, u32[]{:S(2)}) collective-permute-start(bf16[64,384]{1,0:T(8,128)(2,1)S(1)} %get-tuple-element.61), channel_id=1, source_target_pairs={{0,2},{2,0},{4,6},{6,4},{8,10},{10,8},{12,14},{14,12},{1,3},{3,1},... | collective-permute-start | bytes 147464 | tf_op jit(solution)/shard_map/ppermute | solution.py:212
  73.3 39.0 %collective-permute-start.25 = (bf16[3072,384]{1,0:T(8,128)(2,1)}, bf16[3072,384]{1,0:T(8,128)(2,1)}, u32[]{:S(2)}, u32[]{:S(2)}) collective-permute-start(bf16[3072,384]{1,0:T(8,128)(2,1)} %constant_dynamic-update-slice_fusion), channel_id=1, source_target_pairs={{0,1},{1,0},{2,3},{3,2},{4,5},{5,4},{6,7},{7,6},{8,9},{9,8},{10,11... | collective-permute-start | bytes 7077896 | tf_op jit(solution)/shard_map/ppermute | solution.py:218
  79.4 12.2 %collective-permute-start.9 = (bf16[256,384]{1,0:T(8,128)(2,1)S(1)}, bf16[256,384]{1,0:T(8,128)(2,1)S(1)}, u32[]{:S(2)}, u32[]{:S(2)}) collective-permute-start(bf16[256,384]{1,0:T(8,128)(2,1)S(1)} %select_convert_fusion), channel_id=1, source_target_pairs={{0,8},{2,10},{4,12},{6,14},{8,0},{10,2},{12,4},{14,6},{1,9},{3,11}... | collective-permute-start | bytes 589832 | tf_op jit(solution)/shard_map/ppermute | solution.py:215
  92.2 11.4 %collective-permute-start.15 = (bf16[256,384]{1,0:T(8,128)(2,1)S(1)}, bf16[256,384]{1,0:T(8,128)(2,1)S(1)}, u32[]{:S(2)}, u32[]{:S(2)}) collective-permute-start(bf16[256,384]{1,0:T(8,128)(2,1)S(1)} %add_convert_fusion), channel_id=1, source_target_pairs={{0,4},{2,6},{4,0},{6,2},{8,12},{10,14},{12,8},{14,10},{1,5},{3,7},... | collective-permute-start | bytes 589832 | tf_op jit(solution)/shard_map/ppermute | solution.py:212
  103.9 12.3 %collective-permute-start.17 = (bf16[64,1536]{1,0:T(8,128)(2,1)S(1)}, bf16[64,1536]{1,0:T(8,128)(2,1)}, u32[]{:S(2)}, u32[]{:S(2)}) collective-permute-start(bf16[64,1536]{1,0:T(8,128)(2,1)S(1)} %slice.108), channel_id=1, source_target_pairs={{1,8},{3,10},{5,12},{7,14},{8,1},{10,3},{12,5},{14,7},{17,24},{19,... | collective-permute-start | bytes 589832 | tf_op jit(solution)/shard_map/ppermute | solution.py:221
  115.3 19.2 %collective-permute-start.26 = (bf16[256,768]{1,0:T(8,128)(2,1)S(1)}, bf16[256,768]{1,0:T(8,128)(2,1)S(1)}, u32[]{:S(2)}, u32[]{:S(2)}) collective-permute-start(bf16[256,768]{1,0:T(8,128)(2,1)S(1)} %fusion.12), channel_id=1, source_target_pairs={{0,8},{2,10},{4,12},{6,14},{8,0},{10,2},{12,4},{14,6},{1,9},{3,11}... | collective-permute-start | bytes 1179656 | tf_op jit(solution)/shard_map/ppermute | solution.py:215
  141.0 11.0 %collective-permute-start.34 = (f32[192]{0:T(256)S(1)}, f32[192]{0:T(256)S(1)}, u32[]{:S(2)}, u32[]{:S(2)}) collective-permute-start(f32[192]{0:T(256)S(1)} %bitcast.29), channel_id=1, source_target_pairs={{0,6},{2,4},{4,2},{6,0},{8,14},{10,12},{12,10},{14,8},{1,7},{3,5},... | collective-permute-start | bytes 2312 | tf_op jit(solution)/shard_map/ppermute | solution.py:212
  141.1 10.9 %collective-permute-start.33 = (f32[192]{0:T(256)S(1)}, f32[192]{0:T(256)S(1)}, u32[]{:S(2)}, u32[]{:S(2)}) collective-permute-start(f32[192]{0:T(256)S(1)} %bitcast.28), channel_id=1, source_target_pairs={{0,4},{2,6},{4,0},{6,2},{8,12},{10,14},{12,8},{14,10},{1,5},{3,7},... | collective-permute-start | bytes 2312 | tf_op jit(solution)/shard_map/ppermute | solution.py:212
  (49 other events, 429.3 us)

commit v2 on v0

--- a/solution.py
+++ b/solution.py
@@ -3,6 +3,8 @@
 import jax
 import jax.numpy as jnp
 from jax import lax
+from jax.experimental import pallas as pl
+from jax.experimental.pallas import tpu as pltpu
 from jax.sharding import PartitionSpec as P
 
 NT = 1000
@@ -46,7 +48,7 @@
     return (normed, lifted.reshape(values.shape).astype(jnp.bfloat16))
 
 
-def on_device(
+def on_groups(
     noise_in,
     renoise,
     gen_step,
@@ -177,7 +179,312 @@
     return (noised_out, own_grad, gain_grad)
 
 
+def on_tiles(
+    noise_in,
+    renoise,
+    gen_step,
+    noise_step,
+    gen_weight,
+    real_weight,
+    fake_weight,
+    gen_embed,
+    real_embed,
+    fake_embed,
+    gen_gain,
+    real_gain,
+    fake_gain,
+):
+    g = lax.axis_size("fsdp") // 2
+    r, h = noise_in.shape
+    d = 2 * h
+    w = h // g
+    t = g * r
+    blocks = gen_step.shape[0]
+    f32, bf16 = jnp.float32, jnp.bfloat16
+    tail = 16
+    span = range(g)
+
+    def place():
+        position, c = lax.axis_index("fsdp"), lax.axis_index("mp")
+        return lax.div(position, g), lax.rem(position, g), c
+
+    def flat(s_, q_, c_):
+        return (s_ * g + q_) * 2 + c_
+
+    every = [(s_, q_, c_) for s_ in (0, 1) for q_ in span for c_ in (0, 1)]
+
+    def in_square(value, k):
+        return lax.ppermute(value, "fsdp", [(i, i ^ k) for i in range(2 * g)])
+
+    def across(value):
+        return lax.ppermute(value, "fsdp", [(i, i ^ g) for i in range(2 * g)])
+
+    def cores(value):
+        return lax.ppermute(value, "mp", [(0, 1), (1, 0)])
+
+    def turned(value):
+        return lax.ppermute(value, ("fsdp", "mp"), [(flat(*i), flat(i[2], i[1], i[0])) for i in every])
+
+    s, q, c = place()
+
+    def piece(array, k):
+        return lax.dynamic_slice_in_dim(array, (q ^ k) * w, w, 1)
+
+    whole = pl.BlockSpec(memory_space=pltpu.VMEM)
+    scalars = pl.BlockSpec(memory_space=pltpu.SMEM)
+
+    def call(kernel, operands, outs, flops, scratch=(), in_scalars=0):
+        moved = sum(o.size * o.dtype.itemsize for o in operands)
+        return pl.pallas_call(
+            kernel,
+            in_specs=[scalars] * in_scalars + [whole] * (len(operands) - in_scalars),
+            out_specs=[whole] * len(outs),
+            out_shape=[jax.ShapeDtypeStruct(*o) for o in outs],
+            scratch_shapes=list(scratch),
+            compiler_params=pltpu.CompilerParams(vmem_limit_bytes=40 * 1024 * 1024),
+            cost_estimate=pl.CostEstimate(flops=flops, bytes_accessed=moved, transcendentals=0),
+        )(*operands)
+
+    def rows_of(columns):
+        return jnp.broadcast_to(columns, (t, 128)).T[:8]
+
+    def columns_of(rows):
+        return rows.T[:, :1]
+
+    def pack(rows, store):
+        high = rows.astype(bf16)
+        rest = rows - high.astype(f32)
+        middle = rest.astype(bf16)
+        low = (rest - middle.astype(f32)).astype(bf16)
+        line = lax.broadcasted_iota(jnp.int32, rows.shape, 0)
+        mixed = jnp.where(line == 0, high.astype(f32), jnp.where(line == 1, middle.astype(f32), low.astype(f32)))
+        mixed = jnp.where(line < 3, mixed, 0.0)
+        store(jnp.concatenate([mixed, jnp.zeros_like(mixed)], axis=0).astype(bf16))
+
+    def unpack(block):
+        return jnp.sum(block.astype(f32), axis=0, keepdims=True)
+
+    def share(steps, block):
+        return (steps[block].astype(f32) + 1.0) / (NT + 1.0)
+
+    def band(j):
+        return slice(j * r, (j + 1) * r)
+
+    def lanes(k):
+        return pl.ds(pl.multiple_of(k * w, w), w)
+
+    def scales_kernel(features, gen_e, real_e, fake_e, gen_g, real_g, fake_g, out):
+        s, _, _ = place()
+        mine = pl.ds(pl.multiple_of(s * h, h), h)
+        per = h // 128
+
+        def gain(ref):
+            return jnp.concatenate([ref[pl.ds(s * per + i, 1), :] for i in range(per)], axis=1)
+
+        for n, (embed, gains) in enumerate(((gen_e, gen_g), (real_e, real_g), (fake_e, fake_g))):
+            part = 0 if n == 0 else 1
+            mod = 1.0 + jnp.dot(
+                features[part], embed[:, mine], preferred_element_type=f32
+            )
+            if n == 0:
+                out[3] = mod
+            scale = mod * gain(gains)
+            out[n] = -scale if n == 2 else scale
+
+    features = jnp.stack(
+        [step_features(gen_step, gen_embed.shape[0]), step_features(noise_step, gen_embed.shape[0])]
+    )
+    (scales,) = call(
+        scales_kernel,
+        [features, gen_embed, real_embed, fake_embed]
+        + [v.reshape(-1, 128) for v in (gen_gain, real_gain, fake_gain)],
+        [((4, blocks, h), f32)],
+        2 * 3 * blocks * 128 * h,
+    )
+
+    x = [turned(noise_in)]
+    gen_mine = [piece(gen_weight, 0)] + [in_square(piece(gen_weight, k), k) for k in range(1, g)]
+    gen_other = [cores(v) for v in gen_mine]
+    fresh_turned = turned(renoise)
+    x = x + [in_square(x[0], k) for k in range(1, g)]
+    fresh = [piece(fresh_turned, 0)] + [in_square(piece(fresh_turned, k), k) for k in range(1, g)]
+    real_weight, fake_weight, _ = lax.optimization_barrier((real_weight, fake_weight, x[0]))
+    score_send = [jnp.stack([piece(real_weight, k), piece(fake_weight, k)]) for k in span]
+    score_mine = [score_send[0]] + [in_square(score_send[k], k) for k in range(1, g)]
+    score_other = [cores(v) for v in score_mine]
+
+    def generate_kernel(*refs):
+        xs, scale, own, other = refs[:g], refs[g], refs[g + 1 : 2 * g + 1], refs[2 * g + 1 : 3 * g + 1]
+        keep, away, sums, x_mine, lift = refs[3 * g + 1 :]
+        s, q, c = place()
+        totals = []
+        for j in span:
+            wide = xs[j][...].astype(f32)
+            totals.append(jnp.sum(wide * wide, axis=1, keepdims=True))
+            lift[band(j), :] = (wide * scale[0, pl.ds(c * g + (q ^ j), 1), :]).astype(bf16)
+            x_mine[band(j), :] = xs[j][:, lanes(q)]
+        here = jnp.zeros((t, w), f32)
+        there = jnp.zeros((t, w), f32)
+        for k in span:
+            part = lift[:, lanes(q ^ k)]
+            here = here + jnp.dot(part, own[k][...], preferred_element_type=f32)
+            there = there + jnp.dot(part, other[k][...], preferred_element_type=f32)
+        stays = s == c
+        keep[...] = jnp.where(stays, here, there)
+        away[0:t, :] = jnp.where(stays, there, here).astype(bf16)
+        rows = rows_of(jnp.concatenate(totals, axis=0))
+        sums[...] = rows
+
+        def store(value):
+            away[t : t + tail, 0:t] = value
+
+        if w > t:
+            away[t : t + tail, t:] = jnp.zeros((tail, w - t), bf16)
+        pack(rows, store)
+
+    keep, away, x_sums, x_mine = call(
+        generate_kernel,
+        x + [scales] + gen_mine + gen_other,
+        [((t, w), f32), ((t + tail, w), bf16), ((8, t), f32), ((t, w), bf16)],
+        4 * t * h * w,
+        [pltpu.VMEM((t, h), bf16)],
+    )
+
+    def inverse_rms(sums, came):
+        total = sums[...] + unpack(came[t : t + tail, 0:t])
+        return columns_of(lax.rsqrt(total / d + norm_epsilon))
+
+    def blend_kernel(steps, keep, came, sums, x_mine, *refs):
+        fresh, (noised, root) = refs[:g], refs[g:]
+        _, q, c = place()
+        inverse = inverse_rms(sums, came)
+        root[...] = jnp.broadcast_to(inverse, (t, 128))
+        for j in span:
+            part = share(steps, c * g + (q ^ j))
+            made = x_mine[band(j), :].astype(f32) + inverse[band(j), :] * (
+                keep[band(j), :] + came[band(j), :].astype(f32)
+            )
+            noised[band(j), :] = ((1.0 - part) * made + part * fresh[j][...].astype(f32)).astype(bf16)
+
+    noised_mine, x_root = call(
+        blend_kernel,
+        [noise_step, keep, across(away), x_sums, x_mine] + fresh,
+        [((t, w), bf16), ((t, 128), f32)],
+        10 * t * w,
+        in_scalars=1,
+    )
+    noised = [noised_mine] + [in_square(noised_mine, k) for k in range(1, g)]
+
+    def score_kernel(*refs):
+        ns, scale, own, other = refs[:g], refs[g], refs[g + 1 : 2 * g + 1], refs[2 * g + 1 : 3 * g + 1]
+        gap, away, sums, full, real_lift, fake_lift = refs[3 * g + 1 :]
+        _, q, c = place()
+        totals = [jnp.zeros((r, 1), f32) for _ in span]
+        here = jnp.zeros((t, w), f32)
+        there = jnp.zeros((t, w), f32)
+        for k in span:
+            for j in span:
+                block = pl.ds(c * g + (q ^ j), 1)
+                wide = ns[k][band(j ^ k), :].astype(f32)
+                totals[j] = totals[j] + jnp.sum(wide * wide, axis=1, keepdims=True)
+                real_lift[band(j), :] = (wide * scale[1, block, lanes(q ^ k)]).astype(bf16)
+                fake_lift[band(j), :] = (wide * scale[2, block, lanes(q ^ k)]).astype(bf16)
+            full[:, lanes(q ^ k)] = ns[k][band(k), :]
+            for n, lift in enumerate((real_lift, fake_lift)):
+                here = here + jnp.dot(lift[...], own[k][n], preferred_element_type=f32)
+                there = there + jnp.dot(lift[...], other[k][n], preferred_element_type=f32)
+        gap[:, :w] = here
+        gap[:, w:] = there
+        away[0:t, :w] = here.astype(bf16)
+        away[0:t, w:] = there.astype(bf16)
+        rows = rows_of(jnp.concatenate(totals, axis=0))
+        sums[...] = rows
+        away[t : t + tail, t:] = jnp.zeros((tail, 2 * w - t), bf16)
+
+        def store(value):
+            away[t : t + tail, 0:t] = value
+
+        pack(rows, store)
+
+    gap, gap_away, noised_sums, noised_full = call(
+        score_kernel,
+        noised + [scales] + score_mine + score_other,
+        [((t, 2 * w), f32), ((t + tail, 2 * w), bf16), ((8, t), f32), ((r, h), bf16)],
+        8 * t * h * w,
+        [pltpu.VMEM((t, w), bf16), pltpu.VMEM((t, w), bf16)],
+    )
+    gap_came = across(gap_away)
+    noised_out = turned(noised_full)
+
+    def backward_kernel(steps, gap, came, sums, root, scale, *refs):
+        xs, own, other = refs[:g], refs[g : 2 * g], refs[2 * g : 3 * g]
+        outs, grad = refs[3 * g : 4 * g], refs[4 * g]
+        _, q, c = place()
+        inverse = inverse_rms(sums, came)
+        for j in span:
+            part = share(steps, c * g + (q ^ j))
+            value = (part * inverse[band(j), :]) * (gap[band(j), :] + came[band(j), :].astype(f32))
+            grad[band(j), :] = value.astype(bf16)
+            outs[j][0:r, :] = value.astype(bf16)
+        contract = (((1,), (1,)), ((), ()))
+        for k in span:
+            back = lax.dot_general(grad[:, :w], own[k][...], contract, preferred_element_type=f32)
+            back = back + lax.dot_general(grad[:, w:], other[k][...], contract, preferred_element_type=f32)
+            total = jnp.zeros((1, w), f32)
+            for j in span:
+                normed = xs[j][:, lanes(q ^ k)].astype(f32) * root[band(j), :1]
+                summed = jnp.sum(back[band(j), :] * normed, axis=0, keepdims=True)
+                total = total + summed * scale[3, pl.ds(c * g + (q ^ j), 1), lanes(q ^ k)]
+
+            def store(value):
+                outs[k][r : r + tail, :w] = value
+
+            pack(jnp.broadcast_to(total / r, (8, w)), store)
+            outs[k][r : r + tail, w:] = jnp.zeros((tail, w), bf16)
+
+    sent = call(
+        backward_kernel,
+        [noise_step, gap, gap_came, noised_sums, x_root, scales] + x + gen_mine + gen_other,
+        [((r + tail, 2 * w), bf16)] * g,
+        4 * t * h * w,
+        [pltpu.VMEM((t, 2 * w), bf16)],
+        in_scalars=1,
+    )
+    arrived = [sent[0]] + [in_square(sent[k], k) for k in range(1, g)]
+
+    def gather_kernel(*refs):
+        parts, (here, there) = refs[:g], refs[g:]
+        _, q, _ = place()
+        total = jnp.zeros((1, w), f32)
+        for k in span:
+            here[0:r, lanes(q ^ k)] = parts[k][0:r, :w]
+            there[0:r, lanes(q ^ k)] = parts[k][0:r, w:]
+            total = total + unpack(parts[k][r : r + tail, :w])
+
+        for ref in (here, there):
+
+            def store(value):
+                ref[r : r + tail, :w] = value
+
+            pack(jnp.broadcast_to(total, (8, w)), store)
+            ref[r : r + tail, w:] = jnp.zeros((tail, h - w), bf16)
+
+    here, there = call(gather_kernel, arrived, [((r + tail, h), bf16)] * 2, t * h)
+    other_core = cores(there)
+
+    def finish_kernel(here, came, grad, gain):
+        s, _, c = place()
+        grad[...] = jnp.where(s == c, here[0:r, :], came[0:r, :])
+        gain[...] = unpack(here[r : r + tail, :w]) + unpack(came[r : r + tail, :w])
+
+    latent_grad, gain = call(finish_kernel, [here, other_core], [((r, h), bf16), ((1, w), f32)], r * h)
+    gain_grad = lax.dynamic_slice_in_dim(gain[0], c * (w // 2), w // 2, 0)
+    return (noised_out, latent_grad, gain_grad)
+
+
 def solution(mesh):
+    positions = mesh.shape["fsdp"]
+    on_device = on_tiles if positions in (4, 8) and mesh.shape["mp"] == 2 else on_groups
     return jax.shard_map(
         on_device,
         mesh=mesh,

time: 430 us -> 135 us (0.31); the launches traced: 425 us -> 135 us
  waiting for transfers between devices: 224 us -> 72.9 us
  blocking collectives: 135 us -> 0 us
  starting transfers between devices: 18.2 us -> 49.9 us
  other arithmetic: 16.1 us -> 0.49 us
  between operations: 15.6 us -> 0.93 us
  Pallas kernels: 0 us -> 7.45 us
  matrix products: 7.41 us -> 0 us
  local copies, waits for them, and re-layouts: 8.27 us -> 3.14 us
    ppermute x3 -> x32, waiting for transfers between devices: 155 us -> 72.9 us  [the longest x18 40.4 us: in_square(): return lax.ppermute(value, 'fsdp', [(i, i ^ k) for i in range(2 * g)])]
    all_to_all x1 -> x0, blocking collectives: 67.4 us -> none  [on_device(): lax.all_to_all(send_rows, 'fsdp', split_axis=0, concat_axis=0, tiled=True)]
    unnamed x1 -> x0, blocking collectives: 62.7 us -> none
    all_to_all x2 -> x0, waiting for transfers between devices: 59.2 us -> none  [the longest x1 40.7 us: on_device(): lax.all_to_all(outgoing, 'fsdp', split_axis=0, concat_axis=0, tiled=True)]
    ppermute x3 -> x32, starting transfers between devices: 7.82 us -> 49.9 us  [the longest x18 21.8 us: in_square(): return lax.ppermute(value, 'fsdp', [(i, i ^ k) for i in range(2 * g)])]
    all_to_all x2 -> x0, starting transfers between devices: 10.4 us -> none  [the longest x1 6.5 us: on_device(): lax.all_to_all(outgoing, 'fsdp', split_axis=0, concat_axis=0, tiled=True)]
    all_gather x1 -> x0, waiting for transfers between devices: 9.93 us -> none  [on_device(): score_full = lax.all_gather(score_rows, 'mp', axis=1, tiled=True)]
    select_n x5 -> x0, other arithmetic: 7.88 us -> none  [the longest x1 7.02 us: on_device(): jnp.where(slot_role == 2, gen_weight[None], jnp.where(slot_role == 0, rea...]
  transfers between devices with their start and end apart: 6 -> 32, of which waited for: 5 -> 16; matrix products, arithmetic and copies ran while one was open for 2% -> 2% of each run, Pallas kernels for 0% -> 2%
where the time goes in v2:
time: 135 us
  waiting for transfers between devices  72.9 us (54%)
  starting transfers between devices  49.9 us (37%)
  Pallas kernels  7.45 us (6%)
  local copies, waits for them, and re-layouts  3.14 us (2%)
    ppermute x18, waiting for transfers between devices, in_square(): return lax.ppermute(value, 'fsdp', [(i, i ^ k) for i in range(2 * g)])  40.4 us
    ppermute x18, starting transfers between devices, in_square(): return lax.ppermute(value, 'fsdp', [(i, i ^ k) for i in range(2 * g)])  21.8 us
    ppermute x2, waiting for transfers between devices, across(): return lax.ppermute(value, 'fsdp', [(i, i ^ g) for i in range(2 * g)])  19.9 us
    ppermute x9, starting transfers between devices, cores(): return lax.ppermute(value, 'mp', [(0, 1), (1, 0)])  15.2 us
    ppermute x3, waiting for transfers between devices, turned(): lax.ppermute(value, ('fsdp', 'mp'), [(flat(*i), flat(i[2], i[1], i[0])) f...  11.1 us
    ppermute x3, starting transfers between devices, turned(): lax.ppermute(value, ('fsdp', 'mp'), [(flat(*i), flat(i[2], i[1], i[0])) f...  9.44 us
    pallas_call x7, Pallas kernels, call(): pl.pallas_call(kernel, in_specs=[scalars] * in_scalars + [whole] * (len(o...  7.45 us
    ppermute x2, starting transfers between devices, across(): return lax.ppermute(value, 'fsdp', [(i, i ^ g) for i in range(2 * g)])  3.36 us
  transfers between devices with their start and end apart: 32, of which 16 were waited for; matrix products, arithmetic and copies ran while one was open for 2% of the time, Pallas kernels for 2%

profile of v2, /device:TPU:1, one launch (start us, length us, event | category | flops | bytes accessed | tf_op | source)
XLA Modules:
  0.0 134.8 jit_solution(11660039873787213599)
XLA Ops:
  0.6 5.6 %collective-permute-start = (bf16[64,1536]{1,0:T(8,128)(2,1)}, bf16[64,1536]{1,0:T(8,128)(2,1)S(1)}, u32[]{:S(2)}, u32[]{:S(2)}) collective-permute-start(bf16[64,1536]{1,0:T(8,128)(2,1)} %param.13), channel_id=1, source_target_pairs={{0,0},{1,8},{2,2},{3,10},{4,4},{5,12},{6,6},{7,14},{8,1},{9,9},{10... | collective-permute-start | bytes 589832 | tf_op jit(solution)/shard_map/ppermute | solution.py:226
  9.7 2.3 %collective-permute-start.6 = (bf16[384,384]{1,0:T(8,128)(2,1)S(1)}, bf16[384,384]{1,0:T(8,128)(2,1)S(1)}, u32[]{:S(2)}, u32[]{:S(2)}) collective-permute-start(bf16[384,384]{1,0:T(8,128)(2,1)S(1)} %get-tuple-element.51), channel_id=1, source_target_pairs={{0,6},{2,4},{4,2},{6,0},{8,14},{10,12},{12,10},{14,8},{1,7},{3,5},... | collective-permute-start | bytes 884744 | tf_op jit(solution)/shard_map/ppermute | solution.py:217
  12.5 3.2 %collective-permute-done.12 = bf16[64,1536]{1,0:T(8,128)(2,1)S(1)} collective-permute-done((bf16[64,1536]{1,0:T(8,128)(2,1)}, bf16[64,1536]{1,0:T(8,128)(2,1)S(1)}, u32[]{:S(2)}, u32[]{:S(2)}) %collective-permute-start.12) | collective-permute-done | bytes 196640 | tf_op jit(solution)/shard_map/ppermute | solution.py:226
  15.7 3.4 %collective-permute-start.15 = (bf16[64,384]{1,0:T(8,128)(2,1)S(1)}, bf16[64,384]{1,0:T(8,128)(2,1)S(1)}, u32[]{:S(2)}, u32[]{:S(2)}) collective-permute-start(bf16[64,384]{1,0:T(8,128)(2,1)S(1)} %get-tuple-element.55), channel_id=1, source_target_pairs={{0,6},{2,4},{4,2},{6,0},{8,14},{10,12},{12,10},{14,8},{1,7},{3,5},... | collective-permute-start | bytes 147464 | tf_op jit(solution)/shard_map/ppermute | solution.py:217
  19.4 7.7 %collective-permute-done.15.refs_3_ = bf16[64,384]{1,0:T(8,128)(2,1)S(1)} collective-permute-done((bf16[64,384]{1,0:T(8,128)(2,1)S(1)}, bf16[64,384]{1,0:T(8,128)(2,1)S(1)}, u32[]{:S(2)}, u32[]{:S(2)}) %collective-permute-start.15) | collective-permute-done | bytes 49184 | tf_op jit(solution)/shard_map/ppermute | solution.py:217
  27.8 2.2 %collective-permute-done.14.refs_2_ = bf16[64,384]{1,0:T(8,128)(2,1)S(1)} collective-permute-done((bf16[64,384]{1,0:T(8,128)(2,1)S(1)}, bf16[64,384]{1,0:T(8,128)(2,1)S(1)}, u32[]{:S(2)}, u32[]{:S(2)}) %collective-permute-start.14) | collective-permute-done | bytes 49184 | tf_op jit(solution)/shard_map/ppermute | solution.py:217
  30.0 1.9 %collective-permute-start.3 = (bf16[64,1536]{1,0:T(8,128)(2,1)S(1)}, bf16[64,1536]{1,0:T(8,128)(2,1)S(1)}, u32[]{:S(2)}, u32[]{:S(2)}) collective-permute-start(bf16[64,1536]{1,0:T(8,128)(2,1)S(1)} %collective-permute-done.refs_0_), channel_id=1, source_target_pairs={{0,6},{2,4},{4,2},{6,0},{8,14},{10,12},{12,10},{14,8},{1,7},{3,5},... | collective-permute-start | bytes 589832 | tf_op jit(solution)/shard_map/ppermute | solution.py:217
  35.0 2.6 %collective-permute-done.3.refs_3_ = bf16[64,1536]{1,0:T(8,128)(2,1)S(1)} collective-permute-done((bf16[64,1536]{1,0:T(8,128)(2,1)S(1)}, bf16[64,1536]{1,0:T(8,128)(2,1)S(1)}, u32[]{:S(2)}, u32[]{:S(2)}) %collective-permute-start.3) | collective-permute-done | bytes 196640 | tf_op jit(solution)/shard_map/ppermute | solution.py:217
  38.5 3.0 %collective-permute-done.2.refs_2_ = bf16[64,1536]{1,0:T(8,128)(2,1)S(1)} collective-permute-done((bf16[64,1536]{1,0:T(8,128)(2,1)S(1)}, bf16[64,1536]{1,0:T(8,128)(2,1)S(1)}, u32[]{:S(2)}, u32[]{:S(2)}) %collective-permute-start.2) | collective-permute-done | bytes 196640 | tf_op jit(solution)/shard_map/ppermute | solution.py:217
  50.2 5.2 %collective-permute-done.13.refs_1_ = bf16[64,384]{1,0:T(8,128)(2,1)S(1)} collective-permute-done((bf16[64,384]{1,0:T(8,128)(2,1)S(1)}, bf16[64,384]{1,0:T(8,128)(2,1)S(1)}, u32[]{:S(2)}, u32[]{:S(2)}) %collective-permute-start.13) | collective-permute-done | bytes 49184 | tf_op jit(solution)/shard_map/ppermute | solution.py:217
  55.4 3.3 %collective-permute-start.11 = (bf16[272,384]{1,0:T(8,128)(2,1)S(1)}, bf16[272,384]{1,0:T(8,128)(2,1)S(1)}, u32[]{:S(2)}, u32[]{:S(2)}) collective-permute-start(bf16[272,384]{1,0:T(8,128)(2,1)S(1)} %get-tuple-element.24), channel_id=1, source_target_pairs={{0,8},{2,10},{4,12},{6,14},{8,0},{10,2},{12,4},{14,6},{1,9},{3,11}... | collective-permute-start | bytes 626696 | tf_op jit(solution)/shard_map/ppermute | solution.py:220
  58.6 8.8 %collective-permute-start.23 = (bf16[2,384,384]{2,1,0:T(8,128)(2,1)S(1)}, bf16[2,384,384]{2,1,0:T(8,128)(2,1)S(1)}, u32[]{:S(2)}, u32[]{:S(2)}) collective-permute-start(bf16[2,384,384]{2,1,0:T(8,128)(2,1)S(1)} %collective-permute-done.19.refs_6_), channel_id=1, source_target_pairs={{0,1},{1,0},{2,3},{3,2},{4,5},{5,4},{6,7},{7,6},{8,9},{9,8},{10,11... | collective-permute-start | bytes 1769480 | tf_op jit(solution)/shard_map/ppermute | solution.py:223
  67.6 4.7 %collective-permute-done.21.refs_8_ = bf16[2,384,384]{2,1,0:T(8,128)(2,1)S(1)} collective-permute-done((bf16[2,384,384]{2,1,0:T(8,128)(2,1)S(1)}, bf16[2,384,384]{2,1,0:T(8,128)(2,1)S(1)}, u32[]{:S(2)}, u32[]{:S(2)}) %collective-permute-start.21) | collective-permute-done | bytes 589856 | tf_op jit(solution)/shard_map/ppermute | solution.py:217
  72.3 2.3 %collective-permute-start.25 = (bf16[2,384,384]{2,1,0:T(8,128)(2,1)S(1)}, bf16[2,384,384]{2,1,0:T(8,128)(2,1)S(1)}, u32[]{:S(2)}, u32[]{:S(2)}) collective-permute-start(bf16[2,384,384]{2,1,0:T(8,128)(2,1)S(1)} %collective-permute-done.21.refs_8_), channel_id=1, source_target_pairs={{0,1},{1,0},{2,3},{3,2},{4,5},{5,4},{6,7},{7,6},{8,9},{9,8},{10,11... | collective-permute-start | bytes 1769480 | tf_op jit(solution)/shard_map/ppermute | solution.py:223
  75.6 2.2 %collective-permute-start.17 = (bf16[256,384]{1,0:T(8,128)(2,1)S(1)}, bf16[256,384]{1,0:T(8,128)(2,1)S(1)}, u32[]{:S(2)}, u32[]{:S(2)}) collective-permute-start(bf16[256,384]{1,0:T(8,128)(2,1)S(1)} %get-tuple-element.27.refs_0_), channel_id=1, source_target_pairs={{0,4},{2,6},{4,0},{6,2},{8,12},{10,14},{12,8},{14,10},{1,5},{3,7},... | collective-permute-start | bytes 589832 | tf_op jit(solution)/shard_map/ppermute | solution.py:217
  77.7 5.3 %collective-permute-done.18.refs_3_ = bf16[256,384]{1,0:T(8,128)(2,1)S(1)} collective-permute-done((bf16[256,384]{1,0:T(8,128)(2,1)S(1)}, bf16[256,384]{1,0:T(8,128)(2,1)S(1)}, u32[]{:S(2)}, u32[]{:S(2)}) %collective-permute-start.18) | collective-permute-done | bytes 196640 | tf_op jit(solution)/shard_map/ppermute | solution.py:217
  84.0 3.0 %collective-permute-done.17.refs_2_ = bf16[256,384]{1,0:T(8,128)(2,1)S(1)} collective-permute-done((bf16[256,384]{1,0:T(8,128)(2,1)S(1)}, bf16[256,384]{1,0:T(8,128)(2,1)S(1)}, u32[]{:S(2)}, u32[]{:S(2)}) %collective-permute-start.17) | collective-permute-done | bytes 196640 | tf_op jit(solution)/shard_map/ppermute | solution.py:217
  88.2 2.2 %shard_map.151 = (f32[256,768]{1,0:T(8,128)S(1)}, bf16[272,768]{1,0:T(8,128)(2,1)S(1)}, f32[8,256]{1,0:T(8,128)S(1)}, bf16[64,1536]{1,0:T(8,128)(2,1)S(1)}) custom-call(bf16[256,384]{1,0:T(8,128)(2,1)S(1)} %get-tuple-element.27.refs_0_, bf16[256,384]{1,0:T(8,128)(2,1)S(1)} %collective-permute-done.16.refs_1_, ...), custom_call_target="tpu_custom_call" | custom-call | flops 1207959552 | bytes 5701632 | tf_op jit(solution)/shard_map/pallas_call | solution.py:238
  90.5 19.9 %collective-permute-done.27.came = bf16[272,768]{1,0:T(8,128)(2,1)S(1)} collective-permute-done((bf16[272,768]{1,0:T(8,128)(2,1)S(1)}, bf16[272,768]{1,0:T(8,128)(2,1)S(1)}, u32[]{:S(2)}, u32[]{:S(2)}) %collective-permute-start.27) | collective-permute-done | bytes 417824 | tf_op jit(solution)/shard_map/ppermute | solution.py:220
  110.3 2.0 %shard_map.152 = (bf16[80,768]{1,0:T(8,128)(2,1)S(1)}, bf16[80,768]{1,0:T(8,128)(2,1)S(1)}, bf16[80,768]{1,0:T(8,128)(2,1)S(1)}, bf16[80,768]{1,0:T(8,128)(2,1)S(1)}) custom-call(s32[8]{0:T(128)S(1)} %copy-done.6, f32[256,768]{1,0:T(8,128)S(1)} %get-tuple-element.31.gap, bf16[272,768]{1,0:T(8,128)(2,1)S(1)} %collective-permute-done.27.came, ...), custom_call_target="tpu_custom_call" | custom-call | flops 603979776 | bytes 4685856 | tf_op jit(solution)/shard_map/pallas_call | solution.py:238
  112.4 2.2 %collective-permute-start.28 = (bf16[80,768]{1,0:T(8,128)(2,1)S(1)}, bf16[80,768]{1,0:T(8,128)(2,1)S(1)}, u32[]{:S(2)}, u32[]{:S(2)}) collective-permute-start(bf16[80,768]{1,0:T(8,128)(2,1)S(1)} %get-tuple-element.36), channel_id=1, source_target_pairs={{0,2},{2,0},{4,6},{6,4},{8,10},{10,8},{12,14},{14,12},{1,3},{3,1},... | collective-permute-start | bytes 368648 | tf_op jit(solution)/shard_map/ppermute | solution.py:217
  115.9 2.0 %collective-permute-done.28.refs_1_ = bf16[80,768]{1,0:T(8,128)(2,1)S(1)} collective-permute-done((bf16[80,768]{1,0:T(8,128)(2,1)S(1)}, bf16[80,768]{1,0:T(8,128)(2,1)S(1)}, u32[]{:S(2)}, u32[]{:S(2)}) %collective-permute-start.28) | collective-permute-done | bytes 122912 | tf_op jit(solution)/shard_map/ppermute | solution.py:217
  118.7 2.8 %collective-permute-done.30.refs_3_ = bf16[80,768]{1,0:T(8,128)(2,1)S(1)} collective-permute-done((bf16[80,768]{1,0:T(8,128)(2,1)S(1)}, bf16[80,768]{1,0:T(8,128)(2,1)S(1)}, u32[]{:S(2)}, u32[]{:S(2)}) %collective-permute-start.30) | collective-permute-done | bytes 122912 | tf_op jit(solution)/shard_map/ppermute | solution.py:217
  124.8 7.9 %collective-permute-done.26 = bf16[64,1536]{1,0:T(8,128)(2,1)S(1)} collective-permute-done((bf16[64,1536]{1,0:T(8,128)(2,1)S(1)}, bf16[64,1536]{1,0:T(8,128)(2,1)S(1)}, u32[]{:S(2)}, u32[]{:S(2)}) %collective-permute-start.26) | collective-permute-done | bytes 196640 | tf_op jit(solution)/shard_map/ppermute | solution.py:226
  (81 shorter events, 28.1 us)
Async XLA Ops:
  0.6 11.8 %collective-permute-start = (bf16[64,1536]{1,0:T(8,128)(2,1)}, bf16[64,1536]{1,0:T(8,128)(2,1)S(1)}, u32[]{:S(2)}, u32[]{:S(2)}) collective-permute-start(bf16[64,1536]{1,0:T(8,128)(2,1)} %param.13), channel_id=1, source_target_pairs={{0,0},{1,8},{2,2},{3,10},{4,4},{5,12},{6,6},{7,14},{8,1},{9,9},{10... | collective-permute-start | bytes 589832 | tf_op jit(solution)/shard_map/ppermute | solution.py:226
  6.2 9.4 %collective-permute-start.12 = (bf16[64,1536]{1,0:T(8,128)(2,1)}, bf16[64,1536]{1,0:T(8,128)(2,1)S(1)}, u32[]{:S(2)}, u32[]{:S(2)}) collective-permute-start(bf16[64,1536]{1,0:T(8,128)(2,1)} %param.14), channel_id=1, source_target_pairs={{0,0},{1,8},{2,2},{3,10},{4,4},{5,12},{6,6},{7,14},{8,1},{9,9},{10... | collective-permute-start | bytes 589832 | tf_op jit(solution)/shard_map/ppermute | solution.py:226
  9.7 22.2 %collective-permute-start.6 = (bf16[384,384]{1,0:T(8,128)(2,1)S(1)}, bf16[384,384]{1,0:T(8,128)(2,1)S(1)}, u32[]{:S(2)}, u32[]{:S(2)}) collective-permute-start(bf16[384,384]{1,0:T(8,128)(2,1)S(1)} %get-tuple-element.51), channel_id=1, source_target_pairs={{0,6},{2,4},{4,2},{6,0},{8,14},{10,12},{12,10},{14,8},{1,7},{3,5},... | collective-permute-start | bytes 884744 | tf_op jit(solution)/shard_map/ppermute | solution.py:217
  12.0 21.2 %collective-permute-start.4 = (bf16[384,384]{1,0:T(8,128)(2,1)S(1)}, bf16[384,384]{1,0:T(8,128)(2,1)S(1)}, u32[]{:S(2)}, u32[]{:S(2)}) collective-permute-start(bf16[384,384]{1,0:T(8,128)(2,1)S(1)} %get-tuple-element.52), channel_id=1, source_target_pairs={{0,2},{2,0},{4,6},{6,4},{8,10},{10,8},{12,14},{14,12},{1,3},{3,1},... | collective-permute-start | bytes 884744 | tf_op jit(solution)/shard_map/ppermute | solution.py:217
  12.3 21.0 %collective-permute-start.5 = (bf16[384,384]{1,0:T(8,128)(2,1)S(1)}, bf16[384,384]{1,0:T(8,128)(2,1)S(1)}, u32[]{:S(2)}, u32[]{:S(2)}) collective-permute-start(bf16[384,384]{1,0:T(8,128)(2,1)S(1)} %get-tuple-element.54), channel_id=1, source_target_pairs={{0,4},{2,6},{4,0},{6,2},{8,12},{10,14},{12,8},{14,10},{1,5},{3,7},... | collective-permute-start | bytes 884744 | tf_op jit(solution)/shard_map/ppermute | solution.py:217
  12.5 22.3 %collective-permute-start.7 = (bf16[384,384]{1,0:T(8,128)(2,1)S(1)}, bf16[384,384]{1,0:T(8,128)(2,1)S(1)}, u32[]{:S(2)}, u32[]{:S(2)}) collective-permute-start(bf16[384,384]{1,0:T(8,128)(2,1)S(1)} %get-tuple-element.53.refs_5_.refs_4_), channel_id=1, source_target_pairs={{0,1},{1,0},{2,3},{3,2},{4,5},{5,4},{6,7},{7,6},{8,9},{9,8},{10,11... | collective-permute-start | bytes 884744 | tf_op jit(solution)/shard_map/ppermute | solution.py:223
  15.7 11.4 %collective-permute-start.15 = (bf16[64,384]{1,0:T(8,128)(2,1)S(1)}, bf16[64,384]{1,0:T(8,128)(2,1)S(1)}, u32[]{:S(2)}, u32[]{:S(2)}) collective-permute-start(bf16[64,384]{1,0:T(8,128)(2,1)S(1)} %get-tuple-element.55), channel_id=1, source_target_pairs={{0,6},{2,4},{4,2},{6,0},{8,14},{10,12},{12,10},{14,8},{1,7},{3,5},... | collective-permute-start | bytes 147464 | tf_op jit(solution)/shard_map/ppermute | solution.py:217
  31.9 9.6 %collective-permute-start.2 = (bf16[64,1536]{1,0:T(8,128)(2,1)S(1)}, bf16[64,1536]{1,0:T(8,128)(2,1)S(1)}, u32[]{:S(2)}, u32[]{:S(2)}) collective-permute-start(bf16[64,1536]{1,0:T(8,128)(2,1)S(1)} %collective-permute-done.refs_0_), channel_id=1, source_target_pairs={{0,4},{2,6},{4,0},{6,2},{8,12},{10,14},{12,8},{14,10},{1,5},{3,7},... | collective-permute-start | bytes 589832 | tf_op jit(solution)/shard_map/ppermute | solution.py:217
  33.2 8.8 %collective-permute-start.1 = (bf16[64,1536]{1,0:T(8,128)(2,1)S(1)}, bf16[64,1536]{1,0:T(8,128)(2,1)S(1)}, u32[]{:S(2)}, u32[]{:S(2)}) collective-permute-start(bf16[64,1536]{1,0:T(8,128)(2,1)S(1)} %collective-permute-done.refs_0_), channel_id=1, source_target_pairs={{0,2},{2,0},{4,6},{6,4},{8,10},{10,8},{12,14},{14,12},{1,3},{3,1},... | collective-permute-start | bytes 589832 | tf_op jit(solution)/shard_map/ppermute | solution.py:217
  33.3 10.7 %collective-permute-start.10 = (bf16[384,384]{1,0:T(8,128)(2,1)S(1)}, bf16[384,384]{1,0:T(8,128)(2,1)S(1)}, u32[]{:S(2)}, u32[]{:S(2)}) collective-permute-start(bf16[384,384]{1,0:T(8,128)(2,1)S(1)} %collective-permute-done.6.refs_8_.refs_7_), channel_id=1, source_target_pairs={{0,1},{1,0},{2,3},{3,2},{4,5},{5,4},{6,7},{7,6},{8,9},{9,8},{10,11... | collective-permute-start | bytes 884744 | tf_op jit(solution)/shard_map/ppermute | solution.py:223
  34.8 10.2 %collective-permute-start.8 = (bf16[384,384]{1,0:T(8,128)(2,1)S(1)}, bf16[384,384]{1,0:T(8,128)(2,1)S(1)}, u32[]{:S(2)}, u32[]{:S(2)}) collective-permute-start(bf16[384,384]{1,0:T(8,128)(2,1)S(1)} %collective-permute-done.4.refs_6_.refs_5_), channel_id=1, source_target_pairs={{0,1},{1,0},{2,3},{3,2},{4,5},{5,4},{6,7},{7,6},{8,9},{9,8},{10,11... | collective-permute-start | bytes 884744 | tf_op jit(solution)/shard_map/ppermute | solution.py:223
  37.6 21.1 %collective-permute-start.19 = (bf16[2,384,384]{2,1,0:T(8,128)(2,1)S(1)}, bf16[2,384,384]{2,1,0:T(8,128)(2,1)S(1)}, u32[]{:S(2)}, u32[]{:S(2)}) collective-permute-start(bf16[2,384,384]{2,1,0:T(8,128)(2,1)S(1)} %pad_maximum_fusion.1), channel_id=1, source_target_pairs={{0,2},{2,0},{4,6},{6,4},{8,10},{10,8},{12,14},{14,12},{1,3},{3,1},... | collective-permute-start | bytes 1769480 | tf_op jit(solution)/shard_map/ppermute | solution.py:217
  41.6 25.9 %collective-permute-start.20 = (bf16[2,384,384]{2,1,0:T(8,128)(2,1)S(1)}, bf16[2,384,384]{2,1,0:T(8,128)(2,1)S(1)}, u32[]{:S(2)}, u32[]{:S(2)}) collective-permute-start(bf16[2,384,384]{2,1,0:T(8,128)(2,1)S(1)} %pad_maximum_fusion.2), channel_id=1, source_target_pairs={{0,4},{2,6},{4,0},{6,2},{8,12},{10,14},{12,8},{14,10},{1,5},{3,7},... | collective-permute-start | bytes 1769480 | tf_op jit(solution)/shard_map/ppermute | solution.py:217
  42.0 30.3 %collective-permute-start.21 = (bf16[2,384,384]{2,1,0:T(8,128)(2,1)S(1)}, bf16[2,384,384]{2,1,0:T(8,128)(2,1)S(1)}, u32[]{:S(2)}, u32[]{:S(2)}) collective-permute-start(bf16[2,384,384]{2,1,0:T(8,128)(2,1)S(1)} %pad_maximum_fusion.3), channel_id=1, source_target_pairs={{0,6},{2,4},{4,2},{6,0},{8,14},{10,12},{12,10},{14,8},{1,7},{3,5},... | collective-permute-start | bytes 1769480 | tf_op jit(solution)/shard_map/ppermute | solution.py:217
  44.0 31.5 %collective-permute-start.22 = (bf16[2,384,384]{2,1,0:T(8,128)(2,1)S(1)}, bf16[2,384,384]{2,1,0:T(8,128)(2,1)S(1)}, u32[]{:S(2)}, u32[]{:S(2)}) collective-permute-start(bf16[2,384,384]{2,1,0:T(8,128)(2,1)S(1)} %pad_maximum_fusion.refs_5_), channel_id=1, source_target_pairs={{0,1},{1,0},{2,3},{3,2},{4,5},{5,4},{6,7},{7,6},{8,9},{9,8},{10,11... | collective-permute-start | bytes 1769480 | tf_op jit(solution)/shard_map/ppermute | solution.py:223
  47.0 8.4 %collective-permute-start.13 = (bf16[64,384]{1,0:T(8,128)(2,1)S(1)}, bf16[64,384]{1,0:T(8,128)(2,1)S(1)}, u32[]{:S(2)}, u32[]{:S(2)}) collective-permute-start(bf16[64,384]{1,0:T(8,128)(2,1)S(1)} %get-tuple-element.57), channel_id=1, source_target_pairs={{0,2},{2,0},{4,6},{6,4},{8,10},{10,8},{12,14},{14,12},{1,3},{3,1},... | collective-permute-start | bytes 147464 | tf_op jit(solution)/shard_map/ppermute | solution.py:217
  55.4 19.3 %collective-permute-start.11 = (bf16[272,384]{1,0:T(8,128)(2,1)S(1)}, bf16[272,384]{1,0:T(8,128)(2,1)S(1)}, u32[]{:S(2)}, u32[]{:S(2)}) collective-permute-start(bf16[272,384]{1,0:T(8,128)(2,1)S(1)} %get-tuple-element.24), channel_id=1, source_target_pairs={{0,8},{2,10},{4,12},{6,14},{8,0},{10,2},{12,4},{14,6},{1,9},{3,11}... | collective-permute-start | bytes 626696 | tf_op jit(solution)/shard_map/ppermute | solution.py:220
  58.6 29.6 %collective-permute-start.23 = (bf16[2,384,384]{2,1,0:T(8,128)(2,1)S(1)}, bf16[2,384,384]{2,1,0:T(8,128)(2,1)S(1)}, u32[]{:S(2)}, u32[]{:S(2)}) collective-permute-start(bf16[2,384,384]{2,1,0:T(8,128)(2,1)S(1)} %collective-permute-done.19.refs_6_), channel_id=1, source_target_pairs={{0,1},{1,0},{2,3},{3,2},{4,5},{5,4},{6,7},{7,6},{8,9},{9,8},{10,11... | collective-permute-start | bytes 1769480 | tf_op jit(solution)/shard_map/ppermute | solution.py:223
  67.5 20.7 %collective-permute-start.24 = (bf16[2,384,384]{2,1,0:T(8,128)(2,1)S(1)}, bf16[2,384,384]{2,1,0:T(8,128)(2,1)S(1)}, u32[]{:S(2)}, u32[]{:S(2)}) collective-permute-start(bf16[2,384,384]{2,1,0:T(8,128)(2,1)S(1)} %collective-permute-done.20.refs_7_), channel_id=1, source_target_pairs={{0,1},{1,0},{2,3},{3,2},{4,5},{5,4},{6,7},{7,6},{8,9},{9,8},{10,11... | collective-permute-start | bytes 1769480 | tf_op jit(solution)/shard_map/ppermute | solution.py:223
  72.3 15.9 %collective-permute-start.25 = (bf16[2,384,384]{2,1,0:T(8,128)(2,1)S(1)}, bf16[2,384,384]{2,1,0:T(8,128)(2,1)S(1)}, u32[]{:S(2)}, u32[]{:S(2)}) collective-permute-start(bf16[2,384,384]{2,1,0:T(8,128)(2,1)S(1)} %collective-permute-done.21.refs_8_), channel_id=1, source_target_pairs={{0,1},{1,0},{2,3},{3,2},{4,5},{5,4},{6,7},{7,6},{8,9},{9,8},{10,11... | collective-permute-start | bytes 1769480 | tf_op jit(solution)/shard_map/ppermute | solution.py:223
  75.6 11.4 %collective-permute-start.17 = (bf16[256,384]{1,0:T(8,128)(2,1)S(1)}, bf16[256,384]{1,0:T(8,128)(2,1)S(1)}, u32[]{:S(2)}, u32[]{:S(2)}) collective-permute-start(bf16[256,384]{1,0:T(8,128)(2,1)S(1)} %get-tuple-element.27.refs_0_), channel_id=1, source_target_pairs={{0,4},{2,6},{4,0},{6,2},{8,12},{10,14},{12,8},{14,10},{1,5},{3,7},... | collective-permute-start | bytes 589832 | tf_op jit(solution)/shard_map/ppermute | solution.py:217
  90.4 20.0 %collective-permute-start.27 = (bf16[272,768]{1,0:T(8,128)(2,1)S(1)}, bf16[272,768]{1,0:T(8,128)(2,1)S(1)}, u32[]{:S(2)}, u32[]{:S(2)}) collective-permute-start(bf16[272,768]{1,0:T(8,128)(2,1)S(1)} %get-tuple-element.32), channel_id=1, source_target_pairs={{0,8},{2,10},{4,12},{6,14},{8,0},{10,2},{12,4},{14,6},{1,9},{3,11}... | collective-permute-start | bytes 1253384 | tf_op jit(solution)/shard_map/ppermute | solution.py:220
  121.5 11.2 %collective-permute-start.31 = (bf16[80,1536]{1,0:T(8,128)(2,1)S(1)}, bf16[80,1536]{1,0:T(8,128)(2,1)S(1)}, u32[]{:S(2)}, u32[]{:S(2)}) collective-permute-start(bf16[80,1536]{1,0:T(8,128)(2,1)S(1)} %get-tuple-element.40), channel_id=1, source_target_pairs={{0,1},{1,0},{2,3},{3,2},{4,5},{5,4},{6,7},{7,6},{8,9},{9,8},{10,11... | collective-permute-start | bytes 737288 | tf_op jit(solution)/shard_map/ppermute | solution.py:223
  122.9 9.8 %collective-permute-start.26 = (bf16[64,1536]{1,0:T(8,128)(2,1)S(1)}, bf16[64,1536]{1,0:T(8,128)(2,1)S(1)}, u32[]{:S(2)}, u32[]{:S(2)}) collective-permute-start(bf16[64,1536]{1,0:T(8,128)(2,1)S(1)} %get-tuple-element.30), channel_id=1, source_target_pairs={{0,0},{1,8},{2,2},{3,10},{4,4},{5,12},{6,6},{7,14},{8,1},{9,9},{10... | collective-permute-start | bytes 589832 | tf_op jit(solution)/shard_map/ppermute | solution.py:226
  (18 other events, 147.1 us)

commit v3 on v2

--- a/solution.py
+++ b/solution.py
@@ -225,11 +225,6 @@
     def turned(value):
         return lax.ppermute(value, ("fsdp", "mp"), [(flat(*i), flat(i[2], i[1], i[0])) for i in every])
 
-    s, q, c = place()
-
-    def piece(array, k):
-        return lax.dynamic_slice_in_dim(array, (q ^ k) * w, w, 1)
-
     whole = pl.BlockSpec(memory_space=pltpu.VMEM)
     scalars = pl.BlockSpec(memory_space=pltpu.SMEM)
 
@@ -302,15 +297,30 @@
         2 * 3 * blocks * 128 * h,
     )
 
+    depth = gen_weight.shape[0]
+
+    def cut_gen_kernel(weight, fresh, *outs):
+        _, q, _ = place()
+        for k in span:
+            outs[k][0:depth, :] = weight[:, lanes(q ^ k)]
+            outs[k][depth : depth + r, :] = fresh[:, lanes(q ^ k)]
+
+    def cut_score_kernel(real, fake, *outs):
+        _, q, _ = place()
+        for k in span:
+            outs[k][0] = real[:, lanes(q ^ k)]
+            outs[k][1] = fake[:, lanes(q ^ k)]
+
     x = [turned(noise_in)]
-    gen_mine = [piece(gen_weight, 0)] + [in_square(piece(gen_weight, k), k) for k in range(1, g)]
+    gen_sent = call(cut_gen_kernel, [gen_weight, renoise], [((depth + r, w), bf16)] * g, depth * h)
+    gen_mine = [gen_sent[0]] + [in_square(gen_sent[k], k) for k in range(1, g)]
     gen_other = [cores(v) for v in gen_mine]
-    fresh_turned = turned(renoise)
+    x[0], scales = lax.optimization_barrier((x[0], scales))
     x = x + [in_square(x[0], k) for k in range(1, g)]
-    fresh = [piece(fresh_turned, 0)] + [in_square(piece(fresh_turned, k), k) for k in range(1, g)]
+    fresh = turned(jnp.concatenate([v[depth:] for v in gen_mine], axis=0))
     real_weight, fake_weight, _ = lax.optimization_barrier((real_weight, fake_weight, x[0]))
-    score_send = [jnp.stack([piece(real_weight, k), piece(fake_weight, k)]) for k in span]
-    score_mine = [score_send[0]] + [in_square(score_send[k], k) for k in range(1, g)]
+    score_sent = call(cut_score_kernel, [real_weight, fake_weight], [((2, depth, w), bf16)] * g, 2 * depth * h)
+    score_mine = [score_sent[0]] + [in_square(score_sent[k], k) for k in range(1, g)]
     score_other = [cores(v) for v in score_mine]
 
     def generate_kernel(*refs):
@@ -327,8 +337,8 @@
         there = jnp.zeros((t, w), f32)
         for k in span:
             part = lift[:, lanes(q ^ k)]
-            here = here + jnp.dot(part, own[k][...], preferred_element_type=f32)
-            there = there + jnp.dot(part, other[k][...], preferred_element_type=f32)
+            here = here + jnp.dot(part, own[k][0:depth, :], preferred_element_type=f32)
+            there = there + jnp.dot(part, other[k][0:depth, :], preferred_element_type=f32)
         stays = s == c
         keep[...] = jnp.where(stays, here, there)
         away[0:t, :] = jnp.where(stays, there, here).astype(bf16)
@@ -354,8 +364,7 @@
         total = sums[...] + unpack(came[t : t + tail, 0:t])
         return columns_of(lax.rsqrt(total / d + norm_epsilon))
 
-    def blend_kernel(steps, keep, came, sums, x_mine, *refs):
-        fresh, (noised, root) = refs[:g], refs[g:]
+    def blend_kernel(steps, keep, came, sums, x_mine, fresh, noised, root):
         _, q, c = place()
         inverse = inverse_rms(sums, came)
         root[...] = jnp.broadcast_to(inverse, (t, 128))
@@ -364,20 +373,21 @@
             made = x_mine[band(j), :].astype(f32) + inverse[band(j), :] * (
                 keep[band(j), :] + came[band(j), :].astype(f32)
             )
-            noised[band(j), :] = ((1.0 - part) * made + part * fresh[j][...].astype(f32)).astype(bf16)
+            noised[band(j), :] = ((1.0 - part) * made + part * fresh[band(j), :].astype(f32)).astype(bf16)
 
     noised_mine, x_root = call(
         blend_kernel,
-        [noise_step, keep, across(away), x_sums, x_mine] + fresh,
+        [noise_step, keep, across(away), x_sums, x_mine, fresh],
         [((t, w), bf16), ((t, 128), f32)],
         10 * t * w,
         in_scalars=1,
     )
+    noised_owned = turned(noised_mine)
     noised = [noised_mine] + [in_square(noised_mine, k) for k in range(1, g)]
 
     def score_kernel(*refs):
         ns, scale, own, other = refs[:g], refs[g], refs[g + 1 : 2 * g + 1], refs[2 * g + 1 : 3 * g + 1]
-        gap, away, sums, full, real_lift, fake_lift = refs[3 * g + 1 :]
+        gap, away, sums, real_lift, fake_lift = refs[3 * g + 1 :]
         _, q, c = place()
         totals = [jnp.zeros((r, 1), f32) for _ in span]
         here = jnp.zeros((t, w), f32)
@@ -389,7 +399,6 @@
                 totals[j] = totals[j] + jnp.sum(wide * wide, axis=1, keepdims=True)
                 real_lift[band(j), :] = (wide * scale[1, block, lanes(q ^ k)]).astype(bf16)
                 fake_lift[band(j), :] = (wide * scale[2, block, lanes(q ^ k)]).astype(bf16)
-            full[:, lanes(q ^ k)] = ns[k][band(k), :]
             for n, lift in enumerate((real_lift, fake_lift)):
                 here = here + jnp.dot(lift[...], own[k][n], preferred_element_type=f32)
                 there = there + jnp.dot(lift[...], other[k][n], preferred_element_type=f32)
@@ -406,17 +415,16 @@
 
         pack(rows, store)
 
-    gap, gap_away, noised_sums, noised_full = call(
+    gap, gap_away, noised_sums = call(
         score_kernel,
         noised + [scales] + score_mine + score_other,
-        [((t, 2 * w), f32), ((t + tail, 2 * w), bf16), ((8, t), f32), ((r, h), bf16)],
+        [((t, 2 * w), f32), ((t + tail, 2 * w), bf16), ((8, t), f32)],
         8 * t * h * w,
         [pltpu.VMEM((t, w), bf16), pltpu.VMEM((t, w), bf16)],
     )
     gap_came = across(gap_away)
-    noised_out = turned(noised_full)
-
-    def backward_kernel(steps, gap, came, sums, root, scale, *refs):
+
+    def backward_kernel(steps, gap, came, sums, root, scale, owned, *refs):
         xs, own, other = refs[:g], refs[g : 2 * g], refs[2 * g : 3 * g]
         outs, grad = refs[3 * g : 4 * g], refs[4 * g]
         _, q, c = place()
@@ -426,10 +434,13 @@
             value = (part * inverse[band(j), :]) * (gap[band(j), :] + came[band(j), :].astype(f32))
             grad[band(j), :] = value.astype(bf16)
             outs[j][0:r, :] = value.astype(bf16)
+            for n in (0, 1):
+                half = slice(j * r + n * (r // 2), j * r + (n + 1) * (r // 2))
+                outs[j][r + tail : r + tail + r // 2, n * w : (n + 1) * w] = owned[half, :]
         contract = (((1,), (1,)), ((), ()))
         for k in span:
-            back = lax.dot_general(grad[:, :w], own[k][...], contract, preferred_element_type=f32)
-            back = back + lax.dot_general(grad[:, w:], other[k][...], contract, preferred_element_type=f32)
+            back = lax.dot_general(grad[:, :w], own[k][0:depth, :], contract, preferred_element_type=f32)
+            back = back + lax.dot_general(grad[:, w:], other[k][0:depth, :], contract, preferred_element_type=f32)
             total = jnp.zeros((1, w), f32)
             for j in span:
                 normed = xs[j][:, lanes(q ^ k)].astype(f32) * root[band(j), :1]
@@ -444,8 +455,8 @@
 
     sent = call(
         backward_kernel,
-        [noise_step, gap, gap_came, noised_sums, x_root, scales] + x + gen_mine + gen_other,
-        [((r + tail, 2 * w), bf16)] * g,
+        [noise_step, gap, gap_came, noised_sums, x_root, scales, noised_owned] + x + gen_mine + gen_other,
+        [((r + tail + r // 2, 2 * w), bf16)] * g,
         4 * t * h * w,
         [pltpu.VMEM((t, 2 * w), bf16)],
         in_scalars=1,
@@ -453,13 +464,15 @@
     arrived = [sent[0]] + [in_square(sent[k], k) for k in range(1, g)]
 
     def gather_kernel(*refs):
-        parts, (here, there) = refs[:g], refs[g:]
+        parts, (here, there, noised) = refs[:g], refs[g:]
         _, q, _ = place()
         total = jnp.zeros((1, w), f32)
         for k in span:
             here[0:r, lanes(q ^ k)] = parts[k][0:r, :w]
             there[0:r, lanes(q ^ k)] = parts[k][0:r, w:]
             total = total + unpack(parts[k][r : r + tail, :w])
+            for n in (0, 1):
+                noised[n * (r // 2) : (n + 1) * (r // 2), lanes(q ^ k)] = parts[k][r + tail :, n * w : (n + 1) * w]
 
         for ref in (here, there):
 
@@ -469,17 +482,19 @@
             pack(jnp.broadcast_to(total, (8, w)), store)
             ref[r : r + tail, w:] = jnp.zeros((tail, h - w), bf16)
 
-    here, there = call(gather_kernel, arrived, [((r + tail, h), bf16)] * 2, t * h)
+    here, there, noised_out = call(
+        gather_kernel, arrived, [((r + tail, h), bf16)] * 2 + [((r, h), bf16)], t * h
+    )
     other_core = cores(there)
 
     def finish_kernel(here, came, grad, gain):
         s, _, c = place()
         grad[...] = jnp.where(s == c, here[0:r, :], came[0:r, :])
-        gain[...] = unpack(here[r : r + tail, :w]) + unpack(came[r : r + tail, :w])
-
-    latent_grad, gain = call(finish_kernel, [here, other_core], [((r, h), bf16), ((1, w), f32)], r * h)
-    gain_grad = lax.dynamic_slice_in_dim(gain[0], c * (w // 2), w // 2, 0)
-    return (noised_out, latent_grad, gain_grad)
+        both = unpack(here[r : r + tail, :w]) + unpack(came[r : r + tail, :w])
+        gain[...] = jnp.where(c == 0, both[:, : w // 2], both[:, w // 2 :])
+
+    latent_grad, gain = call(finish_kernel, [here, other_core], [((r, h), bf16), ((1, w // 2), f32)], r * h)
+    return (noised_out, latent_grad, gain[0])
 
 
 def solution(mesh):

time: 135 us -> 127 us (0.941)
  starting transfers between devices: 49.9 us -> 42.4 us
  waiting for transfers between devices: 72.9 us -> 70 us
  local copies, waits for them, and re-layouts: 3.14 us -> 4.51 us
    ppermute x3, waiting for transfers between devices: 11.1 us -> 35 us  [turned(): lax.ppermute(value, ('fsdp', 'mp'), [(flat(*i), flat(i[2], i[1], i[0])) f...]
    ppermute x18 -> x15, waiting for transfers between devices: 40.4 us -> 24.8 us  [in_square(): return lax.ppermute(value, 'fsdp', [(i, i ^ k) for i in range(2 * g)])]
    ppermute x2, waiting for transfers between devices: 19.9 us -> 7.6 us  [across(): return lax.ppermute(value, 'fsdp', [(i, i ^ g) for i in range(2 * g)])]
    ppermute x9, starting transfers between devices: 15.2 us -> 7.92 us  [cores(): return lax.ppermute(value, 'mp', [(0, 1), (1, 0)])]
    ppermute x3, starting transfers between devices: 9.44 us -> 15.4 us  [turned(): lax.ppermute(value, ('fsdp', 'mp'), [(flat(*i), flat(i[2], i[1], i[0])) f...]
    ppermute x18 -> x15, starting transfers between devices: 21.8 us -> 17 us  [in_square(): return lax.ppermute(value, 'fsdp', [(i, i ^ k) for i in range(2 * g)])]
    unnamed x21 -> x26, local copies, waits for them, and re-layouts: 0.72 us -> 4.49 us
    dynamic_slice x3 -> x0, local copies, waits for them, and re-layouts: 2.17 us -> none  [the longest x2 1.54 us: piece(): return lax.dynamic_slice_in_dim(array, (q ^ k) * w, w, 1)]
  transfers between devices with their start and end apart: 32 -> 29, of which waited for: 16 -> 15; matrix products, arithmetic and copies ran while one was open for 2% -> 0% of each run, Pallas kernels for 2% -> 2%
where the time goes in v3:
time: 127 us; the launch traced here: 126 us
  waiting for transfers between devices  70 us (55%)
  starting transfers between devices  42.4 us (33%)
  Pallas kernels  8.43 us (7%)
  local copies, waits for them, and re-layouts  4.51 us (4%)
    ppermute x3, waiting for transfers between devices, turned(): lax.ppermute(value, ('fsdp', 'mp'), [(flat(*i), flat(i[2], i[1], i[0])) f...  35 us
    ppermute x15, waiting for transfers between devices, in_square(): return lax.ppermute(value, 'fsdp', [(i, i ^ k) for i in range(2 * g)])  24.8 us
    ppermute x15, starting transfers between devices, in_square(): return lax.ppermute(value, 'fsdp', [(i, i ^ k) for i in range(2 * g)])  17 us
    ppermute x3, starting transfers between devices, turned(): lax.ppermute(value, ('fsdp', 'mp'), [(flat(*i), flat(i[2], i[1], i[0])) f...  15.4 us
    pallas_call x9, Pallas kernels, call(): pl.pallas_call(kernel, in_specs=[scalars] * in_scalars + [whole] * (len(o...  8.43 us
    ppermute x9, starting transfers between devices, cores(): return lax.ppermute(value, 'mp', [(0, 1), (1, 0)])  7.92 us
    ppermute x2, waiting for transfers between devices, across(): return lax.ppermute(value, 'fsdp', [(i, i ^ g) for i in range(2 * g)])  7.6 us
    unnamed x26, local copies, waits for them, and re-layouts  4.49 us
  transfers between devices with their start and end apart: 29, of which 15 were waited for; matrix products, arithmetic and copies ran while one was open for 0% of the time, Pallas kernels for 2%

profile of v3, /device:TPU:1, one launch (start us, length us, event | category | flops | bytes accessed | tf_op | source)
XLA Modules:
  0.0 126.5 jit_solution(14377066444716415977)
XLA Ops:
  3.0 3.1 %collective-permute-start.6 = (bf16[448,384]{1,0:T(8,128)(2,1)S(1)}, bf16[448,384]{1,0:T(8,128)(2,1)S(1)}, u32[]{:S(2)}, u32[]{:S(2)}) collective-permute-start(bf16[448,384]{1,0:T(8,128)(2,1)S(1)} %get-tuple-element.38), channel_id=1, source_target_pairs={{0,6},{2,4},{4,2},{6,0},{8,14},{10,12},{12,10},{14,8},{1,7},{3,5},... | collective-permute-start | bytes 1032200 | tf_op jit(solution)/shard_map/ppermute | solution.py:217
  6.1 5.0 %collective-permute-start = (bf16[64,1536]{1,0:T(8,128)(2,1)S(1)}, bf16[64,1536]{1,0:T(8,128)(2,1)S(1)}, u32[]{:S(2)}, u32[]{:S(2)}) collective-permute-start(bf16[64,1536]{1,0:T(8,128)(2,1)S(1)} %copy-done.11), channel_id=1, source_target_pairs={{0,0},{1,8},{2,2},{3,10},{4,4},{5,12},{6,6},{7,14},{8,1},{9,9},{10... | collective-permute-start | bytes 589832 | tf_op jit(solution)/shard_map/ppermute | solution.py:226
  12.1 4.0 %collective-permute-done.6.refs_8_.refs_7_ = bf16[448,384]{1,0:T(8,128)(2,1)S(1)} collective-permute-done((bf16[448,384]{1,0:T(8,128)(2,1)S(1)}, bf16[448,384]{1,0:T(8,128)(2,1)S(1)}, u32[]{:S(2)}, u32[]{:S(2)}) %collective-permute-start.6) | collective-permute-done | bytes 344096 | tf_op jit(solution)/shard_map/ppermute | solution.py:217
  16.1 2.1 %collective-permute-start.10 = (bf16[448,384]{1,0:T(8,128)(2,1)S(1)}, bf16[448,384]{1,0:T(8,128)(2,1)S(1)}, u32[]{:S(2)}, u32[]{:S(2)}) collective-permute-start(bf16[448,384]{1,0:T(8,128)(2,1)S(1)} %collective-permute-done.6.refs_8_.refs_7_), channel_id=1, source_target_pairs={{0,1},{1,0},{2,3},{3,2},{4,5},{5,4},{6,7},{7,6},{8,9},{9,8},{10,11... | collective-permute-start | bytes 1032200 | tf_op jit(solution)/shard_map/ppermute | solution.py:223
  20.8 1.8 %collective-permute-start.1 = (bf16[64,1536]{1,0:T(8,128)(2,1)S(1)}, bf16[64,1536]{1,0:T(8,128)(2,1)S(1)}, u32[]{:S(2)}, u32[]{:S(2)}) collective-permute-start(bf16[64,1536]{1,0:T(8,128)(2,1)S(1)} %collective-permute-done.refs_0_), channel_id=1, source_target_pairs={{0,2},{2,0},{4,6},{6,4},{8,10},{10,8},{12,14},{14,12},{1,3},{3,1},... | collective-permute-start | bytes 589832 | tf_op jit(solution)/shard_map/ppermute | solution.py:217
  23.6 2.1 %collective-permute-start.3 = (bf16[64,1536]{1,0:T(8,128)(2,1)S(1)}, bf16[64,1536]{1,0:T(8,128)(2,1)S(1)}, u32[]{:S(2)}, u32[]{:S(2)}) collective-permute-start(bf16[64,1536]{1,0:T(8,128)(2,1)S(1)} %collective-permute-done.refs_0_), channel_id=1, source_target_pairs={{0,6},{2,4},{4,2},{6,0},{8,14},{10,12},{12,10},{14,8},{1,7},{3,5},... | collective-permute-start | bytes 589832 | tf_op jit(solution)/shard_map/ppermute | solution.py:217
  28.8 1.9 %collective-permute-start.18 = (bf16[2,384,384]{2,1,0:T(8,128)(2,1)S(1)}, bf16[2,384,384]{2,1,0:T(8,128)(2,1)S(1)}, u32[]{:S(2)}, u32[]{:S(2)}) collective-permute-start(bf16[2,384,384]{2,1,0:T(8,128)(2,1)S(1)} %get-tuple-element.49), channel_id=1, source_target_pairs={{0,6},{2,4},{4,2},{6,0},{8,14},{10,12},{12,10},{14,8},{1,7},{3,5},... | collective-permute-start | bytes 1769480 | tf_op jit(solution)/shard_map/ppermute | solution.py:217
  30.7 3.1 %collective-permute-done.3.refs_3_ = bf16[64,1536]{1,0:T(8,128)(2,1)S(1)} collective-permute-done((bf16[64,1536]{1,0:T(8,128)(2,1)S(1)}, bf16[64,1536]{1,0:T(8,128)(2,1)S(1)}, u32[]{:S(2)}, u32[]{:S(2)}) %collective-permute-start.3) | collective-permute-done | bytes 196640 | tf_op jit(solution)/shard_map/ppermute | solution.py:217
  36.6 4.8 %collective-permute-start.12 = (bf16[256,384]{1,0:T(8,128)(2,1)S(1)}, bf16[256,384]{1,0:T(8,128)(2,1)S(1)}, u32[]{:S(2)}, u32[]{:S(2)}) collective-permute-start(bf16[256,384]{1,0:T(8,128)(2,1)S(1)} %pad_maximum_fusion), channel_id=1, source_target_pairs={{0,0},{1,8},{2,2},{3,10},{4,4},{5,12},{6,6},{7,14},{8,1},{9,9},{10... | collective-permute-start | bytes 589832 | tf_op jit(solution)/shard_map/ppermute | solution.py:226
  42.8 17.1 %collective-permute-done.12.fresh = bf16[256,384]{1,0:T(8,128)(2,1)S(1)} collective-permute-done((bf16[256,384]{1,0:T(8,128)(2,1)S(1)}, bf16[256,384]{1,0:T(8,128)(2,1)S(1)}, u32[]{:S(2)}, u32[]{:S(2)}) %collective-permute-start.12) | collective-permute-done | bytes 196640 | tf_op jit(solution)/shard_map/ppermute | solution.py:226
  59.9 3.8 %collective-permute-start.20 = (bf16[2,384,384]{2,1,0:T(8,128)(2,1)S(1)}, bf16[2,384,384]{2,1,0:T(8,128)(2,1)S(1)}, u32[]{:S(2)}, u32[]{:S(2)}) collective-permute-start(bf16[2,384,384]{2,1,0:T(8,128)(2,1)S(1)} %collective-permute-done.16.refs_6_), channel_id=1, source_target_pairs={{0,1},{1,0},{2,3},{3,2},{4,5},{5,4},{6,7},{7,6},{8,9},{9,8},{10,11... | collective-permute-start | bytes 1769480 | tf_op jit(solution)/shard_map/ppermute | solution.py:223
  64.2 7.6 %collective-permute-done.11.came = bf16[272,384]{1,0:T(8,128)(2,1)S(1)} collective-permute-done((bf16[272,384]{1,0:T(8,128)(2,1)S(1)}, bf16[272,384]{1,0:T(8,128)(2,1)S(1)}, u32[]{:S(2)}, u32[]{:S(2)}) %collective-permute-start.11) | collective-permute-done | bytes 208928 | tf_op jit(solution)/shard_map/ppermute | solution.py:220
  74.2 3.9 %collective-permute-done.13.refs_1_ = bf16[256,384]{1,0:T(8,128)(2,1)S(1)} collective-permute-done((bf16[256,384]{1,0:T(8,128)(2,1)S(1)}, bf16[256,384]{1,0:T(8,128)(2,1)S(1)}, u32[]{:S(2)}, u32[]{:S(2)}) %collective-permute-start.13) | collective-permute-done | bytes 196640 | tf_op jit(solution)/shard_map/ppermute | solution.py:217
  79.4 4.0 %collective-permute-done.15.refs_3_ = bf16[256,384]{1,0:T(8,128)(2,1)S(1)} collective-permute-done((bf16[256,384]{1,0:T(8,128)(2,1)S(1)}, bf16[256,384]{1,0:T(8,128)(2,1)S(1)}, u32[]{:S(2)}, u32[]{:S(2)}) %collective-permute-start.15) | collective-permute-done | bytes 196640 | tf_op jit(solution)/shard_map/ppermute | solution.py:217
  83.5 2.1 %shard_map.153 = (f32[256,768]{1,0:T(8,128)S(1)}, bf16[272,768]{1,0:T(8,128)(2,1)S(1)}, f32[8,256]{1,0:T(8,128)S(1)}) custom-call(bf16[256,384]{1,0:T(8,128)(2,1)S(1)} %get-tuple-element.43.refs_0_, bf16[256,384]{1,0:T(8,128)(2,1)S(1)} %collective-permute-done.13.refs_1_, bf16[256,384]{1,0:T(8,128)(2,1)S(1)} %collective-permute-done.14.refs_2_, ...), custom_call_target="tpu_custom_call" | custom-call | flops 1207959552 | bytes 5701632 | tf_op jit(solution)/shard_map/pallas_call | solution.py:233
  85.6 2.0 %collective-permute-start.23 = (bf16[272,768]{1,0:T(8,128)(2,1)S(1)}, bf16[272,768]{1,0:T(8,128)(2,1)S(1)}, u32[]{:S(2)}, u32[]{:S(2)}) collective-permute-start(bf16[272,768]{1,0:T(8,128)(2,1)S(1)} %get-tuple-element.51), channel_id=1, source_target_pairs={{0,8},{2,10},{4,12},{6,14},{8,0},{10,2},{12,4},{14,6},{1,9},{3,11}... | collective-permute-start | bytes 1253384 | tf_op jit(solution)/shard_map/ppermute | solution.py:220
  87.7 5.6 %collective-permute-start.24 = (bf16[256,384]{1,0:T(8,128)(2,1)S(1)}, bf16[256,384]{1,0:T(8,128)(2,1)S(1)}, u32[]{:S(2)}, u32[]{:S(2)}) collective-permute-start(bf16[256,384]{1,0:T(8,128)(2,1)S(1)} %get-tuple-element.43.refs_0_), channel_id=1, source_target_pairs={{0,0},{1,8},{2,2},{3,10},{4,4},{5,12},{6,6},{7,14},{8,1},{9,9},{10... | collective-permute-start | bytes 589832 | tf_op jit(solution)/shard_map/ppermute | solution.py:226
  93.3 17.9 %collective-permute-done.24.owned = bf16[256,384]{1,0:T(8,128)(2,1)S(1)} collective-permute-done((bf16[256,384]{1,0:T(8,128)(2,1)S(1)}, bf16[256,384]{1,0:T(8,128)(2,1)S(1)}, u32[]{:S(2)}, u32[]{:S(2)}) %collective-permute-start.24) | collective-permute-done | bytes 196640 | tf_op jit(solution)/shard_map/ppermute | solution.py:226
  111.1 2.0 %shard_map.154 = (bf16[112,768]{1,0:T(8,128)(2,1)S(1)}, bf16[112,768]{1,0:T(8,128)(2,1)S(1)}, bf16[112,768]{1,0:T(8,128)(2,1)S(1)}, bf16[112,768]{1,0:T(8,128)(2,1)S(1)}) custom-call(s32[8]{0:T(128)S(1)} %copy-done.10, f32[256,768]{1,0:T(8,128)S(1)} %get-tuple-element.50.gap, bf16[272,768]{1,0:T(8,128)(2,1)S(1)} %collective-permute-done.23.came, ...), custom_call_target="tpu_custom_call" | custom-call | flops 603979776 | bytes 5275680 | tf_op jit(solution)/shard_map/pallas_call | solution.py:233
  113.2 1.7 %collective-permute-start.25 = (bf16[112,768]{1,0:T(8,128)(2,1)S(1)}, bf16[112,768]{1,0:T(8,128)(2,1)S(1)}, u32[]{:S(2)}, u32[]{:S(2)}) collective-permute-start(bf16[112,768]{1,0:T(8,128)(2,1)S(1)} %get-tuple-element.55), channel_id=1, source_target_pairs={{0,2},{2,0},{4,6},{6,4},{8,10},{10,8},{12,14},{14,12},{1,3},{3,1},... | collective-permute-start | bytes 516104 | tf_op jit(solution)/shard_map/ppermute | solution.py:217
  116.2 2.5 %collective-permute-done.25.refs_1_ = bf16[112,768]{1,0:T(8,128)(2,1)S(1)} collective-permute-done((bf16[112,768]{1,0:T(8,128)(2,1)S(1)}, bf16[112,768]{1,0:T(8,128)(2,1)S(1)}, u32[]{:S(2)}, u32[]{:S(2)}) %collective-permute-start.25) | collective-permute-done | bytes 172064 | tf_op jit(solution)/shard_map/ppermute | solution.py:217
  118.7 2.6 %collective-permute-done.26.refs_2_ = bf16[112,768]{1,0:T(8,128)(2,1)S(1)} collective-permute-done((bf16[112,768]{1,0:T(8,128)(2,1)S(1)}, bf16[112,768]{1,0:T(8,128)(2,1)S(1)}, u32[]{:S(2)}, u32[]{:S(2)}) %collective-permute-start.26) | collective-permute-done | bytes 172064 | tf_op jit(solution)/shard_map/ppermute | solution.py:217
  121.3 2.3 %collective-permute-done.27.refs_3_ = bf16[112,768]{1,0:T(8,128)(2,1)S(1)} collective-permute-done((bf16[112,768]{1,0:T(8,128)(2,1)S(1)}, bf16[112,768]{1,0:T(8,128)(2,1)S(1)}, u32[]{:S(2)}, u32[]{:S(2)}) %collective-permute-start.27) | collective-permute-done | bytes 172064 | tf_op jit(solution)/shard_map/ppermute | solution.py:217
  124.3 1.5 %collective-permute-done.28.came = bf16[80,1536]{1,0:T(8,128)(2,1)S(1)} collective-permute-done((bf16[80,1536]{1,0:T(8,128)(2,1)S(1)}, bf16[80,1536]{1,0:T(8,128)(2,1)S(1)}, u32[]{:S(2)}, u32[]{:S(2)}) %collective-permute-start.28) | collective-permute-done | bytes 245792 | tf_op jit(solution)/shard_map/ppermute | solution.py:223
  (79 shorter events, 21.1 us)
Async XLA Ops:
  3.0 13.1 %collective-permute-start.6 = (bf16[448,384]{1,0:T(8,128)(2,1)S(1)}, bf16[448,384]{1,0:T(8,128)(2,1)S(1)}, u32[]{:S(2)}, u32[]{:S(2)}) collective-permute-start(bf16[448,384]{1,0:T(8,128)(2,1)S(1)} %get-tuple-element.38), channel_id=1, source_target_pairs={{0,6},{2,4},{4,2},{6,0},{8,14},{10,12},{12,10},{14,8},{1,7},{3,5},... | collective-permute-start | bytes 1032200 | tf_op jit(solution)/shard_map/ppermute | solution.py:217
  6.1 14.7 %collective-permute-start = (bf16[64,1536]{1,0:T(8,128)(2,1)S(1)}, bf16[64,1536]{1,0:T(8,128)(2,1)S(1)}, u32[]{:S(2)}, u32[]{:S(2)}) collective-permute-start(bf16[64,1536]{1,0:T(8,128)(2,1)S(1)} %copy-done.11), channel_id=1, source_target_pairs={{0,0},{1,8},{2,2},{3,10},{4,4},{5,12},{6,6},{7,14},{8,1},{9,9},{10... | collective-permute-start | bytes 589832 | tf_op jit(solution)/shard_map/ppermute | solution.py:226
  11.2 11.4 %collective-permute-start.4 = (bf16[448,384]{1,0:T(8,128)(2,1)S(1)}, bf16[448,384]{1,0:T(8,128)(2,1)S(1)}, u32[]{:S(2)}, u32[]{:S(2)}) collective-permute-start(bf16[448,384]{1,0:T(8,128)(2,1)S(1)} %get-tuple-element.36), channel_id=1, source_target_pairs={{0,2},{2,0},{4,6},{6,4},{8,10},{10,8},{12,14},{14,12},{1,3},{3,1},... | collective-permute-start | bytes 1032200 | tf_op jit(solution)/shard_map/ppermute | solution.py:217
  11.5 12.1 %collective-permute-start.5 = (bf16[448,384]{1,0:T(8,128)(2,1)S(1)}, bf16[448,384]{1,0:T(8,128)(2,1)S(1)}, u32[]{:S(2)}, u32[]{:S(2)}) collective-permute-start(bf16[448,384]{1,0:T(8,128)(2,1)S(1)} %get-tuple-element.37), channel_id=1, source_target_pairs={{0,4},{2,6},{4,0},{6,2},{8,12},{10,14},{12,8},{14,10},{1,5},{3,7},... | collective-permute-start | bytes 1032200 | tf_op jit(solution)/shard_map/ppermute | solution.py:217
  11.9 14.0 %collective-permute-start.7 = (bf16[448,384]{1,0:T(8,128)(2,1)S(1)}, bf16[448,384]{1,0:T(8,128)(2,1)S(1)}, u32[]{:S(2)}, u32[]{:S(2)}) collective-permute-start(bf16[448,384]{1,0:T(8,128)(2,1)S(1)} %get-tuple-element.35.refs_5_.refs_4_), channel_id=1, source_target_pairs={{0,1},{1,0},{2,3},{3,2},{4,5},{5,4},{6,7},{7,6},{8,9},{9,8},{10,11... | collective-permute-start | bytes 1032200 | tf_op jit(solution)/shard_map/ppermute | solution.py:223
  16.1 19.2 %collective-permute-start.10 = (bf16[448,384]{1,0:T(8,128)(2,1)S(1)}, bf16[448,384]{1,0:T(8,128)(2,1)S(1)}, u32[]{:S(2)}, u32[]{:S(2)}) collective-permute-start(bf16[448,384]{1,0:T(8,128)(2,1)S(1)} %collective-permute-done.6.refs_8_.refs_7_), channel_id=1, source_target_pairs={{0,1},{1,0},{2,3},{3,2},{4,5},{5,4},{6,7},{7,6},{8,9},{9,8},{10,11... | collective-permute-start | bytes 1032200 | tf_op jit(solution)/shard_map/ppermute | solution.py:223
  20.8 7.0 %collective-permute-start.1 = (bf16[64,1536]{1,0:T(8,128)(2,1)S(1)}, bf16[64,1536]{1,0:T(8,128)(2,1)S(1)}, u32[]{:S(2)}, u32[]{:S(2)}) collective-permute-start(bf16[64,1536]{1,0:T(8,128)(2,1)S(1)} %collective-permute-done.refs_0_), channel_id=1, source_target_pairs={{0,2},{2,0},{4,6},{6,4},{8,10},{10,8},{12,14},{14,12},{1,3},{3,1},... | collective-permute-start | bytes 589832 | tf_op jit(solution)/shard_map/ppermute | solution.py:217
  22.6 6.2 %collective-permute-start.2 = (bf16[64,1536]{1,0:T(8,128)(2,1)S(1)}, bf16[64,1536]{1,0:T(8,128)(2,1)S(1)}, u32[]{:S(2)}, u32[]{:S(2)}) collective-permute-start(bf16[64,1536]{1,0:T(8,128)(2,1)S(1)} %collective-permute-done.refs_0_), channel_id=1, source_target_pairs={{0,4},{2,6},{4,0},{6,2},{8,12},{10,14},{12,8},{14,10},{1,5},{3,7},... | collective-permute-start | bytes 589832 | tf_op jit(solution)/shard_map/ppermute | solution.py:217
  23.6 10.3 %collective-permute-start.3 = (bf16[64,1536]{1,0:T(8,128)(2,1)S(1)}, bf16[64,1536]{1,0:T(8,128)(2,1)S(1)}, u32[]{:S(2)}, u32[]{:S(2)}) collective-permute-start(bf16[64,1536]{1,0:T(8,128)(2,1)S(1)} %collective-permute-done.refs_0_), channel_id=1, source_target_pairs={{0,6},{2,4},{4,2},{6,0},{8,14},{10,12},{12,10},{14,8},{1,7},{3,5},... | collective-permute-start | bytes 589832 | tf_op jit(solution)/shard_map/ppermute | solution.py:217
  25.9 34.0 %collective-permute-start.16 = (bf16[2,384,384]{2,1,0:T(8,128)(2,1)S(1)}, bf16[2,384,384]{2,1,0:T(8,128)(2,1)S(1)}, u32[]{:S(2)}, u32[]{:S(2)}) collective-permute-start(bf16[2,384,384]{2,1,0:T(8,128)(2,1)S(1)} %get-tuple-element.47), channel_id=1, source_target_pairs={{0,2},{2,0},{4,6},{6,4},{8,10},{10,8},{12,14},{14,12},{1,3},{3,1},... | collective-permute-start | bytes 1769480 | tf_op jit(solution)/shard_map/ppermute | solution.py:217
  27.8 35.9 %collective-permute-start.17 = (bf16[2,384,384]{2,1,0:T(8,128)(2,1)S(1)}, bf16[2,384,384]{2,1,0:T(8,128)(2,1)S(1)}, u32[]{:S(2)}, u32[]{:S(2)}) collective-permute-start(bf16[2,384,384]{2,1,0:T(8,128)(2,1)S(1)} %get-tuple-element.48), channel_id=1, source_target_pairs={{0,4},{2,6},{4,0},{6,2},{8,12},{10,14},{12,8},{14,10},{1,5},{3,7},... | collective-permute-start | bytes 1769480 | tf_op jit(solution)/shard_map/ppermute | solution.py:217
  28.8 35.0 %collective-permute-start.18 = (bf16[2,384,384]{2,1,0:T(8,128)(2,1)S(1)}, bf16[2,384,384]{2,1,0:T(8,128)(2,1)S(1)}, u32[]{:S(2)}, u32[]{:S(2)}) collective-permute-start(bf16[2,384,384]{2,1,0:T(8,128)(2,1)S(1)} %get-tuple-element.49), channel_id=1, source_target_pairs={{0,6},{2,4},{4,2},{6,0},{8,14},{10,12},{12,10},{14,8},{1,7},{3,5},... | collective-permute-start | bytes 1769480 | tf_op jit(solution)/shard_map/ppermute | solution.py:217
  35.3 6.0 %collective-permute-start.9 = (bf16[448,384]{1,0:T(8,128)(2,1)S(1)}, bf16[448,384]{1,0:T(8,128)(2,1)S(1)}, u32[]{:S(2)}, u32[]{:S(2)}) collective-permute-start(bf16[448,384]{1,0:T(8,128)(2,1)S(1)} %collective-permute-done.5.refs_7_.refs_6_), channel_id=1, source_target_pairs={{0,1},{1,0},{2,3},{3,2},{4,5},{5,4},{6,7},{7,6},{8,9},{9,8},{10,11... | collective-permute-start | bytes 1032200 | tf_op jit(solution)/shard_map/ppermute | solution.py:223
  36.6 23.3 %collective-permute-start.12 = (bf16[256,384]{1,0:T(8,128)(2,1)S(1)}, bf16[256,384]{1,0:T(8,128)(2,1)S(1)}, u32[]{:S(2)}, u32[]{:S(2)}) collective-permute-start(bf16[256,384]{1,0:T(8,128)(2,1)S(1)} %pad_maximum_fusion), channel_id=1, source_target_pairs={{0,0},{1,8},{2,2},{3,10},{4,4},{5,12},{6,6},{7,14},{8,1},{9,9},{10... | collective-permute-start | bytes 589832 | tf_op jit(solution)/shard_map/ppermute | solution.py:226
  41.4 32.8 %collective-permute-start.19 = (bf16[2,384,384]{2,1,0:T(8,128)(2,1)S(1)}, bf16[2,384,384]{2,1,0:T(8,128)(2,1)S(1)}, u32[]{:S(2)}, u32[]{:S(2)}) collective-permute-start(bf16[2,384,384]{2,1,0:T(8,128)(2,1)S(1)} %get-tuple-element.46.refs_5_), channel_id=1, source_target_pairs={{0,1},{1,0},{2,3},{3,2},{4,5},{5,4},{6,7},{7,6},{8,9},{9,8},{10,11... | collective-permute-start | bytes 1769480 | tf_op jit(solution)/shard_map/ppermute | solution.py:223
  59.9 11.9 %collective-permute-start.11 = (bf16[272,384]{1,0:T(8,128)(2,1)S(1)}, bf16[272,384]{1,0:T(8,128)(2,1)S(1)}, u32[]{:S(2)}, u32[]{:S(2)}) collective-permute-start(bf16[272,384]{1,0:T(8,128)(2,1)S(1)} %get-tuple-element.40), channel_id=1, source_target_pairs={{0,8},{2,10},{4,12},{6,14},{8,0},{10,2},{12,4},{14,6},{1,9},{3,11}... | collective-permute-start | bytes 626696 | tf_op jit(solution)/shard_map/ppermute | solution.py:220
  59.9 23.6 %collective-permute-start.20 = (bf16[2,384,384]{2,1,0:T(8,128)(2,1)S(1)}, bf16[2,384,384]{2,1,0:T(8,128)(2,1)S(1)}, u32[]{:S(2)}, u32[]{:S(2)}) collective-permute-start(bf16[2,384,384]{2,1,0:T(8,128)(2,1)S(1)} %collective-permute-done.16.refs_6_), channel_id=1, source_target_pairs={{0,1},{1,0},{2,3},{3,2},{4,5},{5,4},{6,7},{7,6},{8,9},{9,8},{10,11... | collective-permute-start | bytes 1769480 | tf_op jit(solution)/shard_map/ppermute | solution.py:223
  63.7 19.8 %collective-permute-start.21 = (bf16[2,384,384]{2,1,0:T(8,128)(2,1)S(1)}, bf16[2,384,384]{2,1,0:T(8,128)(2,1)S(1)}, u32[]{:S(2)}, u32[]{:S(2)}) collective-permute-start(bf16[2,384,384]{2,1,0:T(8,128)(2,1)S(1)} %collective-permute-done.17.refs_7_), channel_id=1, source_target_pairs={{0,1},{1,0},{2,3},{3,2},{4,5},{5,4},{6,7},{7,6},{8,9},{9,8},{10,11... | collective-permute-start | bytes 1769480 | tf_op jit(solution)/shard_map/ppermute | solution.py:223
  63.8 19.7 %collective-permute-start.22 = (bf16[2,384,384]{2,1,0:T(8,128)(2,1)S(1)}, bf16[2,384,384]{2,1,0:T(8,128)(2,1)S(1)}, u32[]{:S(2)}, u32[]{:S(2)}) collective-permute-start(bf16[2,384,384]{2,1,0:T(8,128)(2,1)S(1)} %collective-permute-done.18.refs_8_), channel_id=1, source_target_pairs={{0,1},{1,0},{2,3},{3,2},{4,5},{5,4},{6,7},{7,6},{8,9},{9,8},{10,11... | collective-permute-start | bytes 1769480 | tf_op jit(solution)/shard_map/ppermute | solution.py:223
  85.6 25.5 %collective-permute-start.23 = (bf16[272,768]{1,0:T(8,128)(2,1)S(1)}, bf16[272,768]{1,0:T(8,128)(2,1)S(1)}, u32[]{:S(2)}, u32[]{:S(2)}) collective-permute-start(bf16[272,768]{1,0:T(8,128)(2,1)S(1)} %get-tuple-element.51), channel_id=1, source_target_pairs={{0,8},{2,10},{4,12},{6,14},{8,0},{10,2},{12,4},{14,6},{1,9},{3,11}... | collective-permute-start | bytes 1253384 | tf_op jit(solution)/shard_map/ppermute | solution.py:220
  87.7 23.5 %collective-permute-start.24 = (bf16[256,384]{1,0:T(8,128)(2,1)S(1)}, bf16[256,384]{1,0:T(8,128)(2,1)S(1)}, u32[]{:S(2)}, u32[]{:S(2)}) collective-permute-start(bf16[256,384]{1,0:T(8,128)(2,1)S(1)} %get-tuple-element.43.refs_0_), channel_id=1, source_target_pairs={{0,0},{1,8},{2,2},{3,10},{4,4},{5,12},{6,6},{7,14},{8,1},{9,9},{10... | collective-permute-start | bytes 589832 | tf_op jit(solution)/shard_map/ppermute | solution.py:226
  113.2 5.5 %collective-permute-start.25 = (bf16[112,768]{1,0:T(8,128)(2,1)S(1)}, bf16[112,768]{1,0:T(8,128)(2,1)S(1)}, u32[]{:S(2)}, u32[]{:S(2)}) collective-permute-start(bf16[112,768]{1,0:T(8,128)(2,1)S(1)} %get-tuple-element.55), channel_id=1, source_target_pairs={{0,2},{2,0},{4,6},{6,4},{8,10},{10,8},{12,14},{14,12},{1,3},{3,1},... | collective-permute-start | bytes 516104 | tf_op jit(solution)/shard_map/ppermute | solution.py:217
  114.9 6.3 %collective-permute-start.26 = (bf16[112,768]{1,0:T(8,128)(2,1)S(1)}, bf16[112,768]{1,0:T(8,128)(2,1)S(1)}, u32[]{:S(2)}, u32[]{:S(2)}) collective-permute-start(bf16[112,768]{1,0:T(8,128)(2,1)S(1)} %get-tuple-element.56), channel_id=1, source_target_pairs={{0,4},{2,6},{4,0},{6,2},{8,12},{10,14},{12,8},{14,10},{1,5},{3,7},... | collective-permute-start | bytes 516104 | tf_op jit(solution)/shard_map/ppermute | solution.py:217
  114.9 8.6 %collective-permute-start.27 = (bf16[112,768]{1,0:T(8,128)(2,1)S(1)}, bf16[112,768]{1,0:T(8,128)(2,1)S(1)}, u32[]{:S(2)}, u32[]{:S(2)}) collective-permute-start(bf16[112,768]{1,0:T(8,128)(2,1)S(1)} %get-tuple-element.57), channel_id=1, source_target_pairs={{0,6},{2,4},{4,2},{6,0},{8,14},{10,12},{12,10},{14,8},{1,7},{3,5},... | collective-permute-start | bytes 516104 | tf_op jit(solution)/shard_map/ppermute | solution.py:217
  (18 other events, 118.3 us)

commit v4 on v3

--- a/solution.py
+++ b/solution.py
@@ -298,12 +298,12 @@
     )
 
     depth = gen_weight.shape[0]
-
-    def cut_gen_kernel(weight, fresh, *outs):
+    fold = r // g
+
+    def cut_gen_kernel(weight, *outs):
         _, q, _ = place()
         for k in span:
-            outs[k][0:depth, :] = weight[:, lanes(q ^ k)]
-            outs[k][depth : depth + r, :] = fresh[:, lanes(q ^ k)]
+            outs[k][...] = weight[:, lanes(q ^ k)]
 
     def cut_score_kernel(real, fake, *outs):
         _, q, _ = place()
@@ -311,34 +311,46 @@
             outs[k][0] = real[:, lanes(q ^ k)]
             outs[k][1] = fake[:, lanes(q ^ k)]
 
-    x = [turned(noise_in)]
-    gen_sent = call(cut_gen_kernel, [gen_weight, renoise], [((depth + r, w), bf16)] * g, depth * h)
+    def cut_rows_kernel(rows, fresh, *outs):
+        _, q, _ = place()
+        for k in span:
+            outs[k][0:r, :] = rows[...]
+            for i in span:
+                outs[k][r : r + fold, i * w : (i + 1) * w] = fresh[i * fold : (i + 1) * fold, lanes(q ^ k)]
+
+    x_turned, fresh_turned = turned(noise_in), turned(renoise)
+    gen_sent = call(cut_gen_kernel, [gen_weight], [((depth, w), bf16)] * g, depth * h)
     gen_mine = [gen_sent[0]] + [in_square(gen_sent[k], k) for k in range(1, g)]
     gen_other = [cores(v) for v in gen_mine]
-    x[0], scales = lax.optimization_barrier((x[0], scales))
-    x = x + [in_square(x[0], k) for k in range(1, g)]
-    fresh = turned(jnp.concatenate([v[depth:] for v in gen_mine], axis=0))
-    real_weight, fake_weight, _ = lax.optimization_barrier((real_weight, fake_weight, x[0]))
+    x_turned, scales = lax.optimization_barrier((x_turned, scales))
+    x_sent = call(cut_rows_kernel, [x_turned, fresh_turned], [((r + fold, h), bf16)] * g, r * h)
+    x = [x_sent[0]] + [in_square(x_sent[k], k) for k in range(1, g)]
+    real_weight, fake_weight, _ = lax.optimization_barrier((real_weight, fake_weight, x_turned))
     score_sent = call(cut_score_kernel, [real_weight, fake_weight], [((2, depth, w), bf16)] * g, 2 * depth * h)
     score_mine = [score_sent[0]] + [in_square(score_sent[k], k) for k in range(1, g)]
     score_other = [cores(v) for v in score_mine]
 
-    def generate_kernel(*refs):
+    def generate_kernel(steps, *refs):
         xs, scale, own, other = refs[:g], refs[g], refs[g + 1 : 2 * g + 1], refs[2 * g + 1 : 3 * g + 1]
-        keep, away, sums, x_mine, lift = refs[3 * g + 1 :]
+        keep, away, sums, base, lift = refs[3 * g + 1 :]
         s, q, c = place()
         totals = []
         for j in span:
-            wide = xs[j][...].astype(f32)
+            wide = xs[j][0:r, :].astype(f32)
             totals.append(jnp.sum(wide * wide, axis=1, keepdims=True))
             lift[band(j), :] = (wide * scale[0, pl.ds(c * g + (q ^ j), 1), :]).astype(bf16)
-            x_mine[band(j), :] = xs[j][:, lanes(q)]
+            part = share(steps, c * g + (q ^ j))
+            for i in span:
+                some = slice(i * fold, (i + 1) * fold)
+                base[j * r + i * fold : j * r + (i + 1) * fold, :] = (1.0 - part) * xs[j][some, lanes(q)].astype(
+                    f32
+                ) + part * xs[j][r : r + fold, i * w : (i + 1) * w].astype(f32)
         here = jnp.zeros((t, w), f32)
         there = jnp.zeros((t, w), f32)
         for k in span:
             part = lift[:, lanes(q ^ k)]
-            here = here + jnp.dot(part, own[k][0:depth, :], preferred_element_type=f32)
-            there = there + jnp.dot(part, other[k][0:depth, :], preferred_element_type=f32)
+            here = here + jnp.dot(part, own[k][...], preferred_element_type=f32)
+            there = there + jnp.dot(part, other[k][...], preferred_element_type=f32)
         stays = s == c
         keep[...] = jnp.where(stays, here, there)
         away[0:t, :] = jnp.where(stays, there, here).astype(bf16)
@@ -352,38 +364,38 @@
             away[t : t + tail, t:] = jnp.zeros((tail, w - t), bf16)
         pack(rows, store)
 
-    keep, away, x_sums, x_mine = call(
+    keep, away, x_sums, base = call(
         generate_kernel,
-        x + [scales] + gen_mine + gen_other,
-        [((t, w), f32), ((t + tail, w), bf16), ((8, t), f32), ((t, w), bf16)],
+        [noise_step] + x + [scales] + gen_mine + gen_other,
+        [((t, w), f32), ((t + tail, w), bf16), ((8, t), f32), ((t, w), f32)],
         4 * t * h * w,
         [pltpu.VMEM((t, h), bf16)],
+        in_scalars=1,
     )
 
     def inverse_rms(sums, came):
         total = sums[...] + unpack(came[t : t + tail, 0:t])
         return columns_of(lax.rsqrt(total / d + norm_epsilon))
 
-    def blend_kernel(steps, keep, came, sums, x_mine, fresh, noised, root):
+    def blend_kernel(steps, keep, came, sums, base, noised, root):
         _, q, c = place()
         inverse = inverse_rms(sums, came)
         root[...] = jnp.broadcast_to(inverse, (t, 128))
         for j in span:
-            part = share(steps, c * g + (q ^ j))
-            made = x_mine[band(j), :].astype(f32) + inverse[band(j), :] * (
-                keep[band(j), :] + came[band(j), :].astype(f32)
-            )
-            noised[band(j), :] = ((1.0 - part) * made + part * fresh[band(j), :].astype(f32)).astype(bf16)
+            stay = 1.0 - share(steps, c * g + (q ^ j))
+            made = keep[band(j), :] + came[band(j), :].astype(f32)
+            noised[band(j), :] = (base[band(j), :] + (stay * inverse[band(j), :]) * made).astype(bf16)
 
     noised_mine, x_root = call(
         blend_kernel,
-        [noise_step, keep, across(away), x_sums, x_mine, fresh],
+        [noise_step, keep, across(away), x_sums, base],
         [((t, w), bf16), ((t, 128), f32)],
         10 * t * w,
         in_scalars=1,
     )
     noised_owned = turned(noised_mine)
     noised = [noised_mine] + [in_square(noised_mine, k) for k in range(1, g)]
+    noised_owned, score_scales = lax.optimization_barrier((noised_owned, scales))
 
     def score_kernel(*refs):
         ns, scale, own, other = refs[:g], refs[g], refs[g + 1 : 2 * g + 1], refs[2 * g + 1 : 3 * g + 1]
@@ -417,7 +429,7 @@
 
     gap, gap_away, noised_sums = call(
         score_kernel,
-        noised + [scales] + score_mine + score_other,
+        noised + [score_scales] + score_mine + score_other,
         [((t, 2 * w), f32), ((t + tail, 2 * w), bf16), ((8, t), f32)],
         8 * t * h * w,
         [pltpu.VMEM((t, w), bf16), pltpu.VMEM((t, w), bf16)],
@@ -439,11 +451,11 @@
                 outs[j][r + tail : r + tail + r // 2, n * w : (n + 1) * w] = owned[half, :]
         contract = (((1,), (1,)), ((), ()))
         for k in span:
-            back = lax.dot_general(grad[:, :w], own[k][0:depth, :], contract, preferred_element_type=f32)
-            back = back + lax.dot_general(grad[:, w:], other[k][0:depth, :], contract, preferred_element_type=f32)
+            back = lax.dot_general(grad[:, :w], own[k][...], contract, preferred_element_type=f32)
+            back = back + lax.dot_general(grad[:, w:], other[k][...], contract, preferred_element_type=f32)
             total = jnp.zeros((1, w), f32)
             for j in span:
-                normed = xs[j][:, lanes(q ^ k)].astype(f32) * root[band(j), :1]
+                normed = xs[j][0:r, lanes(q ^ k)].astype(f32) * root[band(j), :1]
                 summed = jnp.sum(back[band(j), :] * normed, axis=0, keepdims=True)
                 total = total + summed * scale[3, pl.ds(c * g + (q ^ j), 1), lanes(q ^ k)]
 

time: 127 us -> 126 us (level)
  starting transfers between devices: 42.4 us -> 39 us
  waiting for transfers between devices: 70 us -> 72.9 us
    ppermute x3, waiting for transfers between devices: 35 us -> 1.86 us  [turned(): lax.ppermute(value, ('fsdp', 'mp'), [(flat(*i), flat(i[2], i[1], i[0])) f...]
    ppermute x15, waiting for transfers between devices: 24.8 us -> 46.7 us  [in_square(): return lax.ppermute(value, 'fsdp', [(i, i ^ k) for i in range(2 * g)])]
    ppermute x2, waiting for transfers between devices: 7.6 us -> 21.2 us  [across(): return lax.ppermute(value, 'fsdp', [(i, i ^ g) for i in range(2 * g)])]
    ppermute x3, starting transfers between devices: 15.4 us -> 11.5 us  [turned(): lax.ppermute(value, ('fsdp', 'mp'), [(flat(*i), flat(i[2], i[1], i[0])) f...]
    ppermute x2, starting transfers between devices: 2.05 us -> 5.8 us  [across(): return lax.ppermute(value, 'fsdp', [(i, i ^ g) for i in range(2 * g)])]
    ppermute x9, starting transfers between devices: 7.92 us -> 4.27 us  [cores(): return lax.ppermute(value, 'mp', [(0, 1), (1, 0)])]
    unnamed x26 -> x22, local copies, waits for them, and re-layouts: 4.49 us -> 3.56 us
    pallas_call x9 -> x10, Pallas kernels: 8.43 us -> 9.06 us  [call(): pl.pallas_call(kernel, in_specs=[scalars] * in_scalars + [whole] * (len(o...]
  transfers between devices with their start and end apart: 29 -> 29, of which waited for: 15 -> 18; matrix products, arithmetic and copies ran while one was open for 0% -> 0% of each run, Pallas kernels for 2% -> 3%
where the time goes in v4:
time: 126 us
  waiting for transfers between devices  72.9 us (58%)
  starting transfers between devices  39 us (31%)
  Pallas kernels  9.06 us (7%)
  local copies, waits for them, and re-layouts  3.56 us (3%)
    ppermute x15, waiting for transfers between devices, in_square(): return lax.ppermute(value, 'fsdp', [(i, i ^ k) for i in range(2 * g)])  46.7 us
    ppermute x2, waiting for transfers between devices, across(): return lax.ppermute(value, 'fsdp', [(i, i ^ g) for i in range(2 * g)])  21.2 us
    ppermute x15, starting transfers between devices, in_square(): return lax.ppermute(value, 'fsdp', [(i, i ^ k) for i in range(2 * g)])  17.4 us
    ppermute x3, starting transfers between devices, turned(): lax.ppermute(value, ('fsdp', 'mp'), [(flat(*i), flat(i[2], i[1], i[0])) f...  11.5 us
    pallas_call x10, Pallas kernels, call(): pl.pallas_call(kernel, in_specs=[scalars] * in_scalars + [whole] * (len(o...  9.06 us
    ppermute x2, starting transfers between devices, across(): return lax.ppermute(value, 'fsdp', [(i, i ^ g) for i in range(2 * g)])  5.8 us
    ppermute x9, starting transfers between devices, cores(): return lax.ppermute(value, 'mp', [(0, 1), (1, 0)])  4.27 us
    unnamed x22, local copies, waits for them, and re-layouts  3.56 us
  transfers between devices with their start and end apart: 29, of which 18 were waited for; matrix products, arithmetic and copies ran while one was open for 0% of the time, Pallas kernels for 3%

profile of v4, /device:TPU:1, one launch (start us, length us, event | category | flops | bytes accessed | tf_op | source)
XLA Modules:
  0.0 125.6 jit_solution(1449263078520159675)
XLA Ops:
  0.6 5.6 %collective-permute-start = (bf16[64,1536]{1,0:T(8,128)(2,1)}, bf16[64,1536]{1,0:T(8,128)(2,1)S(1)}, u32[]{:S(2)}, u32[]{:S(2)}) collective-permute-start(bf16[64,1536]{1,0:T(8,128)(2,1)} %param.13), channel_id=1, source_target_pairs={{0,0},{1,8},{2,2},{3,10},{4,4},{5,12},{6,6},{7,14},{8,1},{9,9},{10... | collective-permute-start | bytes 589832 | tf_op jit(solution)/shard_map/ppermute | solution.py:226
  6.2 1.9 %collective-permute-start.1 = (bf16[64,1536]{1,0:T(8,128)(2,1)}, bf16[64,1536]{1,0:T(8,128)(2,1)S(1)}, u32[]{:S(2)}, u32[]{:S(2)}) collective-permute-start(bf16[64,1536]{1,0:T(8,128)(2,1)} %param.14), channel_id=1, source_target_pairs={{0,0},{1,8},{2,2},{3,10},{4,4},{5,12},{6,6},{7,14},{8,1},{9,9},{10... | collective-permute-start | bytes 589832 | tf_op jit(solution)/shard_map/ppermute | solution.py:226
  16.7 2.4 %collective-permute-start.3 = (bf16[80,1536]{1,0:T(8,128)(2,1)S(1)}, bf16[80,1536]{1,0:T(8,128)(2,1)S(1)}, u32[]{:S(2)}, u32[]{:S(2)}) collective-permute-start(bf16[80,1536]{1,0:T(8,128)(2,1)S(1)} %get-tuple-element.42), channel_id=1, source_target_pairs={{0,4},{2,6},{4,0},{6,2},{8,12},{10,14},{12,8},{14,10},{1,5},{3,7},... | collective-permute-start | bytes 737288 | tf_op jit(solution)/shard_map/ppermute | solution.py:217
  19.2 1.9 %collective-permute-done.6.refs_7_.refs_6_ = bf16[384,384]{1,0:T(8,128)(2,1)S(1)} collective-permute-done((bf16[384,384]{1,0:T(8,128)(2,1)S(1)}, bf16[384,384]{1,0:T(8,128)(2,1)S(1)}, u32[]{:S(2)}, u32[]{:S(2)}) %collective-permute-start.6) | collective-permute-done | bytes 294944 | tf_op jit(solution)/shard_map/ppermute | solution.py:217
  22.2 5.8 %collective-permute-done.7.refs_8_.refs_7_ = bf16[384,384]{1,0:T(8,128)(2,1)S(1)} collective-permute-done((bf16[384,384]{1,0:T(8,128)(2,1)S(1)}, bf16[384,384]{1,0:T(8,128)(2,1)S(1)}, u32[]{:S(2)}, u32[]{:S(2)}) %collective-permute-start.7) | collective-permute-done | bytes 294944 | tf_op jit(solution)/shard_map/ppermute | solution.py:217
  30.2 2.5 %collective-permute-done.3.refs_2_ = bf16[80,1536]{1,0:T(8,128)(2,1)S(1)} collective-permute-done((bf16[80,1536]{1,0:T(8,128)(2,1)S(1)}, bf16[80,1536]{1,0:T(8,128)(2,1)S(1)}, u32[]{:S(2)}, u32[]{:S(2)}) %collective-permute-start.3) | collective-permute-done | bytes 245792 | tf_op jit(solution)/shard_map/ppermute | solution.py:217
  32.9 5.7 %collective-permute-done.4.refs_3_ = bf16[80,1536]{1,0:T(8,128)(2,1)S(1)} collective-permute-done((bf16[80,1536]{1,0:T(8,128)(2,1)S(1)}, bf16[80,1536]{1,0:T(8,128)(2,1)S(1)}, u32[]{:S(2)}, u32[]{:S(2)}) %collective-permute-start.4) | collective-permute-done | bytes 245792 | tf_op jit(solution)/shard_map/ppermute | solution.py:217
  39.1 1.9 %collective-permute-done.11.refs_12_.refs_11_ = bf16[384,384]{1,0:T(8,128)(2,1)S(1)} collective-permute-done((bf16[384,384]{1,0:T(8,128)(2,1)S(1)}, bf16[384,384]{1,0:T(8,128)(2,1)S(1)}, u32[]{:S(2)}, u32[]{:S(2)}) %collective-permute-start.11) | collective-permute-done | bytes 294944 | tf_op jit(solution)/shard_map/ppermute | solution.py:223
  41.0 2.0 %shard_map.151 = (f32[256,384]{1,0:T(8,128)S(1)}, bf16[272,384]{1,0:T(8,128)(2,1)S(1)}, f32[8,256]{1,0:T(8,128)S(1)}, f32[256,384]{1,0:T(8,128)S(1)}) custom-call(s32[8]{0:T(128)S(1)} %copy-done.9, bf16[80,1536]{1,0:T(8,128)(2,1)S(1)} %get-tuple-element.40.refs_0_, bf16[80,1536]{1,0:T(8,128)(2,1)S(1)} %collective-permute-done.2.refs_1_, ...), custom_call_target="tpu_custom_call" | custom-call | flops 603979776 | bytes 3538976 | tf_op jit(solution)/shard_map/pallas_call | solution.py:233
  43.0 5.7 %collective-permute-start.12 = (bf16[272,384]{1,0:T(8,128)(2,1)S(1)}, bf16[272,384]{1,0:T(8,128)(2,1)S(1)}, u32[]{:S(2)}, u32[]{:S(2)}) collective-permute-start(bf16[272,384]{1,0:T(8,128)(2,1)S(1)} %get-tuple-element.50), channel_id=1, source_target_pairs={{0,8},{2,10},{4,12},{6,14},{8,0},{10,2},{12,4},{14,6},{1,9},{3,11}... | collective-permute-start | bytes 626696 | tf_op jit(solution)/shard_map/ppermute | solution.py:220
  50.1 5.0 %collective-permute-done.18.refs_7_ = bf16[2,384,384]{2,1,0:T(8,128)(2,1)S(1)} collective-permute-done((bf16[2,384,384]{2,1,0:T(8,128)(2,1)S(1)}, bf16[2,384,384]{2,1,0:T(8,128)(2,1)S(1)}, u32[]{:S(2)}, u32[]{:S(2)}) %collective-permute-start.18) | collective-permute-done | bytes 589856 | tf_op jit(solution)/shard_map/ppermute | solution.py:217
  55.1 11.7 %collective-permute-done.19.refs_8_ = bf16[2,384,384]{2,1,0:T(8,128)(2,1)S(1)} collective-permute-done((bf16[2,384,384]{2,1,0:T(8,128)(2,1)S(1)}, bf16[2,384,384]{2,1,0:T(8,128)(2,1)S(1)}, u32[]{:S(2)}, u32[]{:S(2)}) %collective-permute-start.19) | collective-permute-done | bytes 589856 | tf_op jit(solution)/shard_map/ppermute | solution.py:217
  67.7 4.0 %collective-permute-start.16 = (bf16[256,384]{1,0:T(8,128)(2,1)S(1)}, bf16[256,384]{1,0:T(8,128)(2,1)S(1)}, u32[]{:S(2)}, u32[]{:S(2)}) collective-permute-start(bf16[256,384]{1,0:T(8,128)(2,1)S(1)} %get-tuple-element.53.refs_0_), channel_id=1, source_target_pairs={{0,0},{1,8},{2,2},{3,10},{4,4},{5,12},{6,6},{7,14},{8,1},{9,9},{10... | collective-permute-start | bytes 589832 | tf_op jit(solution)/shard_map/ppermute | solution.py:226
  71.7 3.2 %collective-permute-start.15 = (bf16[256,384]{1,0:T(8,128)(2,1)S(1)}, bf16[256,384]{1,0:T(8,128)(2,1)S(1)}, u32[]{:S(2)}, u32[]{:S(2)}) collective-permute-start(bf16[256,384]{1,0:T(8,128)(2,1)S(1)} %get-tuple-element.53.refs_0_), channel_id=1, source_target_pairs={{0,6},{2,4},{4,2},{6,0},{8,14},{10,12},{12,10},{14,8},{1,7},{3,5},... | collective-permute-start | bytes 589832 | tf_op jit(solution)/shard_map/ppermute | solution.py:217
  76.5 2.7 %collective-permute-start.14 = (bf16[256,384]{1,0:T(8,128)(2,1)S(1)}, bf16[256,384]{1,0:T(8,128)(2,1)S(1)}, u32[]{:S(2)}, u32[]{:S(2)}) collective-permute-start(bf16[256,384]{1,0:T(8,128)(2,1)S(1)} %get-tuple-element.53.refs_0_), channel_id=1, source_target_pairs={{0,4},{2,6},{4,0},{6,2},{8,12},{10,14},{12,8},{14,10},{1,5},{3,7},... | collective-permute-start | bytes 589832 | tf_op jit(solution)/shard_map/ppermute | solution.py:217
  79.2 1.9 %collective-permute-done.15.refs_3_ = bf16[256,384]{1,0:T(8,128)(2,1)S(1)} collective-permute-done((bf16[256,384]{1,0:T(8,128)(2,1)S(1)}, bf16[256,384]{1,0:T(8,128)(2,1)S(1)}, u32[]{:S(2)}, u32[]{:S(2)}) %collective-permute-start.15) | collective-permute-done | bytes 196640 | tf_op jit(solution)/shard_map/ppermute | solution.py:217
  81.2 2.6 %collective-permute-done.14.refs_2_ = bf16[256,384]{1,0:T(8,128)(2,1)S(1)} collective-permute-done((bf16[256,384]{1,0:T(8,128)(2,1)S(1)}, bf16[256,384]{1,0:T(8,128)(2,1)S(1)}, u32[]{:S(2)}, u32[]{:S(2)}) %collective-permute-start.14) | collective-permute-done | bytes 196640 | tf_op jit(solution)/shard_map/ppermute | solution.py:217
  83.8 2.0 %collective-permute-done.13.refs_1_ = bf16[256,384]{1,0:T(8,128)(2,1)S(1)} collective-permute-done((bf16[256,384]{1,0:T(8,128)(2,1)S(1)}, bf16[256,384]{1,0:T(8,128)(2,1)S(1)}, u32[]{:S(2)}, u32[]{:S(2)}) %collective-permute-start.13) | collective-permute-done | bytes 196640 | tf_op jit(solution)/shard_map/ppermute | solution.py:217
  85.8 2.1 %shard_map.154 = (f32[256,768]{1,0:T(8,128)S(1)}, bf16[272,768]{1,0:T(8,128)(2,1)S(1)}, f32[8,256]{1,0:T(8,128)S(1)}) custom-call(bf16[256,384]{1,0:T(8,128)(2,1)S(1)} %get-tuple-element.53.refs_0_, bf16[256,384]{1,0:T(8,128)(2,1)S(1)} %collective-permute-done.13.refs_1_, bf16[256,384]{1,0:T(8,128)(2,1)S(1)} %collective-permute-done.14.refs_2_, ...), custom_call_target="tpu_custom_call" | custom-call | flops 1207959552 | bytes 5701632 | tf_op jit(solution)/shard_map/pallas_call | solution.py:233
  88.0 21.2 %collective-permute-done.24.came = bf16[272,768]{1,0:T(8,128)(2,1)S(1)} collective-permute-done((bf16[272,768]{1,0:T(8,128)(2,1)S(1)}, bf16[272,768]{1,0:T(8,128)(2,1)S(1)}, u32[]{:S(2)}, u32[]{:S(2)}) %collective-permute-start.24) | collective-permute-done | bytes 417824 | tf_op jit(solution)/shard_map/ppermute | solution.py:220
  109.3 2.0 %shard_map.155 = (bf16[112,768]{1,0:T(8,128)(2,1)S(1)}, bf16[112,768]{1,0:T(8,128)(2,1)S(1)}, bf16[112,768]{1,0:T(8,128)(2,1)S(1)}, bf16[112,768]{1,0:T(8,128)(2,1)S(1)}) custom-call(s32[8]{0:T(128)S(1)} %copy-done.9, f32[256,768]{1,0:T(8,128)S(1)} %get-tuple-element.61.gap, bf16[272,768]{1,0:T(8,128)(2,1)S(1)} %collective-permute-done.24.came, ...), custom_call_target="tpu_custom_call" | custom-call | flops 603979776 | bytes 5079072 | tf_op jit(solution)/shard_map/pallas_call | solution.py:233
  112.0 1.9 %collective-permute-start.27 = (bf16[112,768]{1,0:T(8,128)(2,1)S(1)}, bf16[112,768]{1,0:T(8,128)(2,1)S(1)}, u32[]{:S(2)}, u32[]{:S(2)}) collective-permute-start(bf16[112,768]{1,0:T(8,128)(2,1)S(1)} %get-tuple-element.69), channel_id=1, source_target_pairs={{0,6},{2,4},{4,2},{6,0},{8,14},{10,12},{12,10},{14,8},{1,7},{3,5},... | collective-permute-start | bytes 516104 | tf_op jit(solution)/shard_map/ppermute | solution.py:217
  114.0 2.6 %collective-permute-done.25.refs_1_ = bf16[112,768]{1,0:T(8,128)(2,1)S(1)} collective-permute-done((bf16[112,768]{1,0:T(8,128)(2,1)S(1)}, bf16[112,768]{1,0:T(8,128)(2,1)S(1)}, u32[]{:S(2)}, u32[]{:S(2)}) %collective-permute-start.25) | collective-permute-done | bytes 172064 | tf_op jit(solution)/shard_map/ppermute | solution.py:217
  117.2 4.0 %collective-permute-done.27.refs_3_ = bf16[112,768]{1,0:T(8,128)(2,1)S(1)} collective-permute-done((bf16[112,768]{1,0:T(8,128)(2,1)S(1)}, bf16[112,768]{1,0:T(8,128)(2,1)S(1)}, u32[]{:S(2)}, u32[]{:S(2)}) %collective-permute-start.27) | collective-permute-done | bytes 172064 | tf_op jit(solution)/shard_map/ppermute | solution.py:217
  (71 shorter events, 22.3 us)
Async XLA Ops:
  0.6 11.7 %collective-permute-start = (bf16[64,1536]{1,0:T(8,128)(2,1)}, bf16[64,1536]{1,0:T(8,128)(2,1)S(1)}, u32[]{:S(2)}, u32[]{:S(2)}) collective-permute-start(bf16[64,1536]{1,0:T(8,128)(2,1)} %param.13), channel_id=1, source_target_pairs={{0,0},{1,8},{2,2},{3,10},{4,4},{5,12},{6,6},{7,14},{8,1},{9,9},{10... | collective-permute-start | bytes 589832 | tf_op jit(solution)/shard_map/ppermute | solution.py:226
  6.2 9.1 %collective-permute-start.1 = (bf16[64,1536]{1,0:T(8,128)(2,1)}, bf16[64,1536]{1,0:T(8,128)(2,1)S(1)}, u32[]{:S(2)}, u32[]{:S(2)}) collective-permute-start(bf16[64,1536]{1,0:T(8,128)(2,1)} %param.14), channel_id=1, source_target_pairs={{0,0},{1,8},{2,2},{3,10},{4,4},{5,12},{6,6},{7,14},{8,1},{9,9},{10... | collective-permute-start | bytes 589832 | tf_op jit(solution)/shard_map/ppermute | solution.py:226
  9.6 7.1 %collective-permute-start.5 = (bf16[384,384]{1,0:T(8,128)(2,1)S(1)}, bf16[384,384]{1,0:T(8,128)(2,1)S(1)}, u32[]{:S(2)}, u32[]{:S(2)}) collective-permute-start(bf16[384,384]{1,0:T(8,128)(2,1)S(1)} %get-tuple-element.46), channel_id=1, source_target_pairs={{0,2},{2,0},{4,6},{6,4},{8,10},{10,8},{12,14},{14,12},{1,3},{3,1},... | collective-permute-start | bytes 884744 | tf_op jit(solution)/shard_map/ppermute | solution.py:217
  10.9 10.2 %collective-permute-start.6 = (bf16[384,384]{1,0:T(8,128)(2,1)S(1)}, bf16[384,384]{1,0:T(8,128)(2,1)S(1)}, u32[]{:S(2)}, u32[]{:S(2)}) collective-permute-start(bf16[384,384]{1,0:T(8,128)(2,1)S(1)} %get-tuple-element.47), channel_id=1, source_target_pairs={{0,4},{2,6},{4,0},{6,2},{8,12},{10,14},{12,8},{14,10},{1,5},{3,7},... | collective-permute-start | bytes 884744 | tf_op jit(solution)/shard_map/ppermute | solution.py:217
  12.2 15.8 %collective-permute-start.7 = (bf16[384,384]{1,0:T(8,128)(2,1)S(1)}, bf16[384,384]{1,0:T(8,128)(2,1)S(1)}, u32[]{:S(2)}, u32[]{:S(2)}) collective-permute-start(bf16[384,384]{1,0:T(8,128)(2,1)S(1)} %get-tuple-element.48), channel_id=1, source_target_pairs={{0,6},{2,4},{4,2},{6,0},{8,14},{10,12},{12,10},{14,8},{1,7},{3,5},... | collective-permute-start | bytes 884744 | tf_op jit(solution)/shard_map/ppermute | solution.py:217
  12.4 15.7 %collective-permute-start.8 = (bf16[384,384]{1,0:T(8,128)(2,1)S(1)}, bf16[384,384]{1,0:T(8,128)(2,1)S(1)}, u32[]{:S(2)}, u32[]{:S(2)}) collective-permute-start(bf16[384,384]{1,0:T(8,128)(2,1)S(1)} %get-tuple-element.45.refs_5_.refs_4_), channel_id=1, source_target_pairs={{0,1},{1,0},{2,3},{3,2},{4,5},{5,4},{6,7},{7,6},{8,9},{9,8},{10,11... | collective-permute-start | bytes 884744 | tf_op jit(solution)/shard_map/ppermute | solution.py:223
  15.4 13.7 %collective-permute-start.2 = (bf16[80,1536]{1,0:T(8,128)(2,1)S(1)}, bf16[80,1536]{1,0:T(8,128)(2,1)S(1)}, u32[]{:S(2)}, u32[]{:S(2)}) collective-permute-start(bf16[80,1536]{1,0:T(8,128)(2,1)S(1)} %get-tuple-element.41), channel_id=1, source_target_pairs={{0,2},{2,0},{4,6},{6,4},{8,10},{10,8},{12,14},{14,12},{1,3},{3,1},... | collective-permute-start | bytes 737288 | tf_op jit(solution)/shard_map/ppermute | solution.py:217
  16.7 16.0 %collective-permute-start.3 = (bf16[80,1536]{1,0:T(8,128)(2,1)S(1)}, bf16[80,1536]{1,0:T(8,128)(2,1)S(1)}, u32[]{:S(2)}, u32[]{:S(2)}) collective-permute-start(bf16[80,1536]{1,0:T(8,128)(2,1)S(1)} %get-tuple-element.42), channel_id=1, source_target_pairs={{0,4},{2,6},{4,0},{6,2},{8,12},{10,14},{12,8},{14,10},{1,5},{3,7},... | collective-permute-start | bytes 737288 | tf_op jit(solution)/shard_map/ppermute | solution.py:217
  21.1 17.5 %collective-permute-start.4 = (bf16[80,1536]{1,0:T(8,128)(2,1)S(1)}, bf16[80,1536]{1,0:T(8,128)(2,1)S(1)}, u32[]{:S(2)}, u32[]{:S(2)}) collective-permute-start(bf16[80,1536]{1,0:T(8,128)(2,1)S(1)} %get-tuple-element.43), channel_id=1, source_target_pairs={{0,6},{2,4},{4,2},{6,0},{8,14},{10,12},{12,10},{14,8},{1,7},{3,5},... | collective-permute-start | bytes 737288 | tf_op jit(solution)/shard_map/ppermute | solution.py:217
  28.0 10.6 %collective-permute-start.9 = (bf16[384,384]{1,0:T(8,128)(2,1)S(1)}, bf16[384,384]{1,0:T(8,128)(2,1)S(1)}, u32[]{:S(2)}, u32[]{:S(2)}) collective-permute-start(bf16[384,384]{1,0:T(8,128)(2,1)S(1)} %collective-permute-done.5.refs_6_.refs_5_), channel_id=1, source_target_pairs={{0,1},{1,0},{2,3},{3,2},{4,5},{5,4},{6,7},{7,6},{8,9},{9,8},{10,11... | collective-permute-start | bytes 884744 | tf_op jit(solution)/shard_map/ppermute | solution.py:223
  28.0 10.6 %collective-permute-start.10 = (bf16[384,384]{1,0:T(8,128)(2,1)S(1)}, bf16[384,384]{1,0:T(8,128)(2,1)S(1)}, u32[]{:S(2)}, u32[]{:S(2)}) collective-permute-start(bf16[384,384]{1,0:T(8,128)(2,1)S(1)} %collective-permute-done.6.refs_7_.refs_6_), channel_id=1, source_target_pairs={{0,1},{1,0},{2,3},{3,2},{4,5},{5,4},{6,7},{7,6},{8,9},{9,8},{10,11... | collective-permute-start | bytes 884744 | tf_op jit(solution)/shard_map/ppermute | solution.py:223
  29.1 19.6 %collective-permute-start.17 = (bf16[2,384,384]{2,1,0:T(8,128)(2,1)S(1)}, bf16[2,384,384]{2,1,0:T(8,128)(2,1)S(1)}, u32[]{:S(2)}, u32[]{:S(2)}) collective-permute-start(bf16[2,384,384]{2,1,0:T(8,128)(2,1)S(1)} %get-tuple-element.58), channel_id=1, source_target_pairs={{0,2},{2,0},{4,6},{6,4},{8,10},{10,8},{12,14},{14,12},{1,3},{3,1},... | collective-permute-start | bytes 1769480 | tf_op jit(solution)/shard_map/ppermute | solution.py:217
  32.7 22.4 %collective-permute-start.18 = (bf16[2,384,384]{2,1,0:T(8,128)(2,1)S(1)}, bf16[2,384,384]{2,1,0:T(8,128)(2,1)S(1)}, u32[]{:S(2)}, u32[]{:S(2)}) collective-permute-start(bf16[2,384,384]{2,1,0:T(8,128)(2,1)S(1)} %get-tuple-element.59), channel_id=1, source_target_pairs={{0,4},{2,6},{4,0},{6,2},{8,12},{10,14},{12,8},{14,10},{1,5},{3,7},... | collective-permute-start | bytes 1769480 | tf_op jit(solution)/shard_map/ppermute | solution.py:217
  38.6 28.2 %collective-permute-start.19 = (bf16[2,384,384]{2,1,0:T(8,128)(2,1)S(1)}, bf16[2,384,384]{2,1,0:T(8,128)(2,1)S(1)}, u32[]{:S(2)}, u32[]{:S(2)}) collective-permute-start(bf16[2,384,384]{2,1,0:T(8,128)(2,1)S(1)} %get-tuple-element.60), channel_id=1, source_target_pairs={{0,6},{2,4},{4,2},{6,0},{8,14},{10,12},{12,10},{14,8},{1,7},{3,5},... | collective-permute-start | bytes 1769480 | tf_op jit(solution)/shard_map/ppermute | solution.py:217
  38.6 33.0 %collective-permute-start.20 = (bf16[2,384,384]{2,1,0:T(8,128)(2,1)S(1)}, bf16[2,384,384]{2,1,0:T(8,128)(2,1)S(1)}, u32[]{:S(2)}, u32[]{:S(2)}) collective-permute-start(bf16[2,384,384]{2,1,0:T(8,128)(2,1)S(1)} %get-tuple-element.57.refs_5_), channel_id=1, source_target_pairs={{0,1},{1,0},{2,3},{3,2},{4,5},{5,4},{6,7},{7,6},{8,9},{9,8},{10,11... | collective-permute-start | bytes 1769480 | tf_op jit(solution)/shard_map/ppermute | solution.py:223
  43.0 23.8 %collective-permute-start.12 = (bf16[272,384]{1,0:T(8,128)(2,1)S(1)}, bf16[272,384]{1,0:T(8,128)(2,1)S(1)}, u32[]{:S(2)}, u32[]{:S(2)}) collective-permute-start(bf16[272,384]{1,0:T(8,128)(2,1)S(1)} %get-tuple-element.50), channel_id=1, source_target_pairs={{0,8},{2,10},{4,12},{6,14},{8,0},{10,2},{12,4},{14,6},{1,9},{3,11}... | collective-permute-start | bytes 626696 | tf_op jit(solution)/shard_map/ppermute | solution.py:220
  48.7 37.1 %collective-permute-start.21 = (bf16[2,384,384]{2,1,0:T(8,128)(2,1)S(1)}, bf16[2,384,384]{2,1,0:T(8,128)(2,1)S(1)}, u32[]{:S(2)}, u32[]{:S(2)}) collective-permute-start(bf16[2,384,384]{2,1,0:T(8,128)(2,1)S(1)} %collective-permute-done.17.refs_6_), channel_id=1, source_target_pairs={{0,1},{1,0},{2,3},{3,2},{4,5},{5,4},{6,7},{7,6},{8,9},{9,8},{10,11... | collective-permute-start | bytes 1769480 | tf_op jit(solution)/shard_map/ppermute | solution.py:223
  55.1 30.7 %collective-permute-start.22 = (bf16[2,384,384]{2,1,0:T(8,128)(2,1)S(1)}, bf16[2,384,384]{2,1,0:T(8,128)(2,1)S(1)}, u32[]{:S(2)}, u32[]{:S(2)}) collective-permute-start(bf16[2,384,384]{2,1,0:T(8,128)(2,1)S(1)} %collective-permute-done.18.refs_7_), channel_id=1, source_target_pairs={{0,1},{1,0},{2,3},{3,2},{4,5},{5,4},{6,7},{7,6},{8,9},{9,8},{10,11... | collective-permute-start | bytes 1769480 | tf_op jit(solution)/shard_map/ppermute | solution.py:223
  66.8 19.0 %collective-permute-start.23 = (bf16[2,384,384]{2,1,0:T(8,128)(2,1)S(1)}, bf16[2,384,384]{2,1,0:T(8,128)(2,1)S(1)}, u32[]{:S(2)}, u32[]{:S(2)}) collective-permute-start(bf16[2,384,384]{2,1,0:T(8,128)(2,1)S(1)} %collective-permute-done.19.refs_8_), channel_id=1, source_target_pairs={{0,1},{1,0},{2,3},{3,2},{4,5},{5,4},{6,7},{7,6},{8,9},{9,8},{10,11... | collective-permute-start | bytes 1769480 | tf_op jit(solution)/shard_map/ppermute | solution.py:223
  67.7 8.8 %collective-permute-start.16 = (bf16[256,384]{1,0:T(8,128)(2,1)S(1)}, bf16[256,384]{1,0:T(8,128)(2,1)S(1)}, u32[]{:S(2)}, u32[]{:S(2)}) collective-permute-start(bf16[256,384]{1,0:T(8,128)(2,1)S(1)} %get-tuple-element.53.refs_0_), channel_id=1, source_target_pairs={{0,0},{1,8},{2,2},{3,10},{4,4},{5,12},{6,6},{7,14},{8,1},{9,9},{10... | collective-permute-start | bytes 589832 | tf_op jit(solution)/shard_map/ppermute | solution.py:226
  71.7 9.5 %collective-permute-start.15 = (bf16[256,384]{1,0:T(8,128)(2,1)S(1)}, bf16[256,384]{1,0:T(8,128)(2,1)S(1)}, u32[]{:S(2)}, u32[]{:S(2)}) collective-permute-start(bf16[256,384]{1,0:T(8,128)(2,1)S(1)} %get-tuple-element.53.refs_0_), channel_id=1, source_target_pairs={{0,6},{2,4},{4,2},{6,0},{8,14},{10,12},{12,10},{14,8},{1,7},{3,5},... | collective-permute-start | bytes 589832 | tf_op jit(solution)/shard_map/ppermute | solution.py:217
  76.5 7.3 %collective-permute-start.14 = (bf16[256,384]{1,0:T(8,128)(2,1)S(1)}, bf16[256,384]{1,0:T(8,128)(2,1)S(1)}, u32[]{:S(2)}, u32[]{:S(2)}) collective-permute-start(bf16[256,384]{1,0:T(8,128)(2,1)S(1)} %get-tuple-element.53.refs_0_), channel_id=1, source_target_pairs={{0,4},{2,6},{4,0},{6,2},{8,12},{10,14},{12,8},{14,10},{1,5},{3,7},... | collective-permute-start | bytes 589832 | tf_op jit(solution)/shard_map/ppermute | solution.py:217
  87.9 21.3 %collective-permute-start.24 = (bf16[272,768]{1,0:T(8,128)(2,1)S(1)}, bf16[272,768]{1,0:T(8,128)(2,1)S(1)}, u32[]{:S(2)}, u32[]{:S(2)}) collective-permute-start(bf16[272,768]{1,0:T(8,128)(2,1)S(1)} %get-tuple-element.62), channel_id=1, source_target_pairs={{0,8},{2,10},{4,12},{6,14},{8,0},{10,2},{12,4},{14,6},{1,9},{3,11}... | collective-permute-start | bytes 1253384 | tf_op jit(solution)/shard_map/ppermute | solution.py:220
  112.0 9.1 %collective-permute-start.27 = (bf16[112,768]{1,0:T(8,128)(2,1)S(1)}, bf16[112,768]{1,0:T(8,128)(2,1)S(1)}, u32[]{:S(2)}, u32[]{:S(2)}) collective-permute-start(bf16[112,768]{1,0:T(8,128)(2,1)S(1)} %get-tuple-element.69), channel_id=1, source_target_pairs={{0,6},{2,4},{4,2},{6,0},{8,14},{10,12},{12,10},{14,8},{1,7},{3,5},... | collective-permute-start | bytes 516104 | tf_op jit(solution)/shard_map/ppermute | solution.py:217
  (16 other events, 69.8 us)

commit v5 on v4

--- a/solution.py
+++ b/solution.py
@@ -321,14 +321,14 @@
     x_turned, fresh_turned = turned(noise_in), turned(renoise)
     gen_sent = call(cut_gen_kernel, [gen_weight], [((depth, w), bf16)] * g, depth * h)
     gen_mine = [gen_sent[0]] + [in_square(gen_sent[k], k) for k in range(1, g)]
-    gen_other = [cores(v) for v in gen_mine]
     x_turned, scales = lax.optimization_barrier((x_turned, scales))
     x_sent = call(cut_rows_kernel, [x_turned, fresh_turned], [((r + fold, h), bf16)] * g, r * h)
     x = [x_sent[0]] + [in_square(x_sent[k], k) for k in range(1, g)]
+    gen_swap, x[1] = lax.optimization_barrier((gen_mine, x[1]))
+    gen_other = [cores(v) for v in gen_swap]
     real_weight, fake_weight, _ = lax.optimization_barrier((real_weight, fake_weight, x_turned))
     score_sent = call(cut_score_kernel, [real_weight, fake_weight], [((2, depth, w), bf16)] * g, 2 * depth * h)
     score_mine = [score_sent[0]] + [in_square(score_sent[k], k) for k in range(1, g)]
-    score_other = [cores(v) for v in score_mine]
 
     def generate_kernel(steps, *refs):
         xs, scale, own, other = refs[:g], refs[g], refs[g + 1 : 2 * g + 1], refs[2 * g + 1 : 3 * g + 1]
@@ -398,114 +398,153 @@
     noised_owned, score_scales = lax.optimization_barrier((noised_owned, scales))
 
     def score_kernel(*refs):
-        ns, scale, own, other = refs[:g], refs[g], refs[g + 1 : 2 * g + 1], refs[2 * g + 1 : 3 * g + 1]
-        gap, away, sums, real_lift, fake_lift = refs[3 * g + 1 :]
+        ns, scale, own = refs[:g], refs[g], refs[g + 1 : 2 * g + 1]
+        gap, away, sums, lifts = refs[2 * g + 1 :]
         _, q, c = place()
         totals = [jnp.zeros((r, 1), f32) for _ in span]
         here = jnp.zeros((t, w), f32)
-        there = jnp.zeros((t, w), f32)
-        for k in span:
+        for k in span:
+            columns = slice(k * w, (k + 1) * w)
             for j in span:
                 block = pl.ds(c * g + (q ^ j), 1)
                 wide = ns[k][band(j ^ k), :].astype(f32)
                 totals[j] = totals[j] + jnp.sum(wide * wide, axis=1, keepdims=True)
-                real_lift[band(j), :] = (wide * scale[1, block, lanes(q ^ k)]).astype(bf16)
-                fake_lift[band(j), :] = (wide * scale[2, block, lanes(q ^ k)]).astype(bf16)
-            for n, lift in enumerate((real_lift, fake_lift)):
-                here = here + jnp.dot(lift[...], own[k][n], preferred_element_type=f32)
-                there = there + jnp.dot(lift[...], other[k][n], preferred_element_type=f32)
-        gap[:, :w] = here
-        gap[:, w:] = there
-        away[0:t, :w] = here.astype(bf16)
-        away[0:t, w:] = there.astype(bf16)
+                for n in (0, 1):
+                    lifts[n, band(j), columns] = (wide * scale[1 + n, block, lanes(q ^ k)]).astype(bf16)
+            for n in (0, 1):
+                here = here + jnp.dot(lifts[n, :, columns], own[k][n], preferred_element_type=f32)
+        gap[...] = here
+        away[0:t, :] = here.astype(bf16)
         rows = rows_of(jnp.concatenate(totals, axis=0))
         sums[...] = rows
-        away[t : t + tail, t:] = jnp.zeros((tail, 2 * w - t), bf16)
+        if w > t:
+            away[t : t + tail, t:] = jnp.zeros((tail, w - t), bf16)
 
         def store(value):
             away[t : t + tail, 0:t] = value
 
         pack(rows, store)
 
-    gap, gap_away, noised_sums = call(
+    gap_here, away_here, noised_sums, lifts = call(
         score_kernel,
-        noised + [score_scales] + score_mine + score_other,
-        [((t, 2 * w), f32), ((t + tail, 2 * w), bf16), ((8, t), f32)],
-        8 * t * h * w,
-        [pltpu.VMEM((t, w), bf16), pltpu.VMEM((t, w), bf16)],
-    )
-    gap_came = across(gap_away)
-
-    def backward_kernel(steps, gap, came, sums, root, scale, owned, *refs):
-        xs, own, other = refs[:g], refs[g : 2 * g], refs[2 * g : 3 * g]
-        outs, grad = refs[3 * g : 4 * g], refs[4 * g]
+        noised + [score_scales] + score_mine,
+        [((t, w), f32), ((t + tail, w), bf16), ((8, t), f32), ((2, t, h), bf16)],
+        4 * t * h * w,
+    )
+    came_here = across(away_here)
+    score_mine, away_here = lax.optimization_barrier((score_mine, away_here))
+    score_other = [cores(v) for v in score_mine]
+
+    def score_rest_kernel(lifts, *refs):
+        other, (gap, away) = refs[:g], refs[g:]
+        there = jnp.zeros((t, w), f32)
+        for k in span:
+            for n in (0, 1):
+                there = there + jnp.dot(
+                    lifts[n, :, k * w : (k + 1) * w], other[k][n], preferred_element_type=f32
+                )
+        gap[...] = there
+        away[...] = there.astype(bf16)
+
+    gap_there, away_there = call(
+        score_rest_kernel, [lifts] + score_other, [((t, w), f32), ((t, w), bf16)], 4 * t * h * w
+    )
+    came_there = across(away_there)
+
+    def gradient(steps, gap, came, inverse, grad, outs):
         _, q, c = place()
-        inverse = inverse_rms(sums, came)
         for j in span:
             part = share(steps, c * g + (q ^ j))
             value = (part * inverse[band(j), :]) * (gap[band(j), :] + came[band(j), :].astype(f32))
             grad[band(j), :] = value.astype(bf16)
             outs[j][0:r, :] = value.astype(bf16)
-            for n in (0, 1):
-                half = slice(j * r + n * (r // 2), j * r + (n + 1) * (r // 2))
-                outs[j][r + tail : r + tail + r // 2, n * w : (n + 1) * w] = owned[half, :]
-        contract = (((1,), (1,)), ((), ()))
-        for k in span:
-            back = lax.dot_general(grad[:, :w], own[k][...], contract, preferred_element_type=f32)
-            back = back + lax.dot_general(grad[:, w:], other[k][...], contract, preferred_element_type=f32)
+
+    def gain_sums(grad, tile, xs, root, scale):
+        _, q, c = place()
+        sums = []
+        for k in span:
+            back = lax.dot_general(grad[...], tile[k][...], (((1,), (1,)), ((), ())), preferred_element_type=f32)
             total = jnp.zeros((1, w), f32)
             for j in span:
                 normed = xs[j][0:r, lanes(q ^ k)].astype(f32) * root[band(j), :1]
                 summed = jnp.sum(back[band(j), :] * normed, axis=0, keepdims=True)
                 total = total + summed * scale[3, pl.ds(c * g + (q ^ j), 1), lanes(q ^ k)]
+            sums.append(total)
+        return sums
+
+    def backward_kernel(steps, gap, came, sums, root, scale, owned, *refs):
+        xs, own, outs, (noised_root, partial, grad) = refs[:g], refs[g : 2 * g], refs[2 * g : 3 * g], refs[3 * g :]
+        inverse = inverse_rms(sums, came)
+        noised_root[...] = jnp.broadcast_to(inverse, (t, 128))
+        gradient(steps, gap, came, inverse, grad, outs)
+        for k, total in enumerate(gain_sums(grad, own, xs, root, scale)):
+            partial[k : k + 1, :] = total
+            outs[k][r : 2 * r, :] = owned[band(k), :]
+
+    *sent_here, noised_root, partial = call(
+        backward_kernel,
+        [noise_step, gap_here, came_here, noised_sums, x_root, scales, noised_owned] + x + gen_mine,
+        [((2 * r, w), bf16)] * g + [((t, 128), f32), ((8, w), f32)],
+        2 * t * h * w,
+        [pltpu.VMEM((t, w), bf16)],
+        in_scalars=1,
+    )
+    arrived_here = [sent_here[0]] + [in_square(sent_here[k], k) for k in range(1, g)]
+
+    def backward_rest_kernel(steps, gap, came, noised_root, partial, root, scale, *refs):
+        xs, other, outs, (grad,) = refs[:g], refs[g : 2 * g], refs[2 * g : 3 * g], refs[3 * g :]
+        gradient(steps, gap, came, noised_root[:, :1], grad, outs)
+        for k, total in enumerate(gain_sums(grad, other, xs, root, scale)):
 
             def store(value):
-                outs[k][r : r + tail, :w] = value
-
-            pack(jnp.broadcast_to(total / r, (8, w)), store)
-            outs[k][r : r + tail, w:] = jnp.zeros((tail, w), bf16)
-
-    sent = call(
-        backward_kernel,
-        [noise_step, gap, gap_came, noised_sums, x_root, scales, noised_owned] + x + gen_mine + gen_other,
-        [((r + tail + r // 2, 2 * w), bf16)] * g,
-        4 * t * h * w,
-        [pltpu.VMEM((t, 2 * w), bf16)],
+                outs[k][r : r + tail, :] = value
+
+            pack(jnp.broadcast_to((total + partial[k : k + 1, :]) / r, (8, w)), store)
+
+    sent_there = call(
+        backward_rest_kernel,
+        [noise_step, gap_there, came_there, noised_root, partial, x_root, scales] + x + gen_other,
+        [((r + tail, w), bf16)] * g,
+        2 * t * h * w,
+        [pltpu.VMEM((t, w), bf16)],
         in_scalars=1,
     )
-    arrived = [sent[0]] + [in_square(sent[k], k) for k in range(1, g)]
+    arrived_there = [sent_there[0]] + [in_square(sent_there[k], k) for k in range(1, g)]
 
     def gather_kernel(*refs):
-        parts, (here, there, noised) = refs[:g], refs[g:]
+        a, b, (here, there, gains, noised) = refs[:g], refs[g : 2 * g], refs[2 * g :]
         _, q, _ = place()
         total = jnp.zeros((1, w), f32)
         for k in span:
-            here[0:r, lanes(q ^ k)] = parts[k][0:r, :w]
-            there[0:r, lanes(q ^ k)] = parts[k][0:r, w:]
-            total = total + unpack(parts[k][r : r + tail, :w])
-            for n in (0, 1):
-                noised[n * (r // 2) : (n + 1) * (r // 2), lanes(q ^ k)] = parts[k][r + tail :, n * w : (n + 1) * w]
-
-        for ref in (here, there):
-
-            def store(value):
-                ref[r : r + tail, :w] = value
-
-            pack(jnp.broadcast_to(total, (8, w)), store)
-            ref[r : r + tail, w:] = jnp.zeros((tail, h - w), bf16)
-
-    here, there, noised_out = call(
-        gather_kernel, arrived, [((r + tail, h), bf16)] * 2 + [((r, h), bf16)], t * h
+            here[:, lanes(q ^ k)] = a[k][0:r, :]
+            noised[:, lanes(q ^ k)] = a[k][r : 2 * r, :]
+            there[0:r, lanes(q ^ k)] = b[k][0:r, :]
+            total = total + unpack(b[k][r : r + tail, :])
+        gains[...] = total
+
+        def store(value):
+            there[r : r + tail, :w] = value
+
+        pack(jnp.broadcast_to(total, (8, w)), store)
+        there[r : r + tail, w:] = jnp.zeros((tail, h - w), bf16)
+
+    here, there, gains, noised_out = call(
+        gather_kernel,
+        arrived_here + arrived_there,
+        [((r, h), bf16), ((r + tail, h), bf16), ((1, w), f32), ((r, h), bf16)],
+        t * h,
     )
     other_core = cores(there)
 
-    def finish_kernel(here, came, grad, gain):
+    def finish_kernel(here, gains, came, grad, gain):
         s, _, c = place()
-        grad[...] = jnp.where(s == c, here[0:r, :], came[0:r, :])
-        both = unpack(here[r : r + tail, :w]) + unpack(came[r : r + tail, :w])
+        grad[...] = jnp.where(s == c, here[...], came[0:r, :])
+        both = gains[...] + unpack(came[r : r + tail, :w])
         gain[...] = jnp.where(c == 0, both[:, : w // 2], both[:, w // 2 :])
 
-    latent_grad, gain = call(finish_kernel, [here, other_core], [((r, h), bf16), ((1, w // 2), f32)], r * h)
+    latent_grad, gain = call(
+        finish_kernel, [here, gains, other_core], [((r, h), bf16), ((1, w // 2), f32)], r * h
+    )
     return (noised_out, latent_grad, gain[0])
 
 

time: 126 us -> 119 us (0.944)
  starting transfers between devices: 39 us -> 34.7 us
  waiting for transfers between devices: 72.9 us -> 69.3 us
    ppermute x15 -> x18, waiting for transfers between devices: 46.7 us -> 27.7 us  [in_square(): return lax.ppermute(value, 'fsdp', [(i, i ^ k) for i in range(2 * g)])]
    ppermute x3, waiting for transfers between devices: 1.86 us -> 16 us  [turned(): lax.ppermute(value, ('fsdp', 'mp'), [(flat(*i), flat(i[2], i[1], i[0])) f...]
    ppermute x2 -> x3, starting transfers between devices: 5.8 us -> 0.95 us  [across(): return lax.ppermute(value, 'fsdp', [(i, i ^ g) for i in range(2 * g)])]
    ppermute x9, starting transfers between devices: 4.27 us -> 6.57 us  [cores(): return lax.ppermute(value, 'mp', [(0, 1), (1, 0)])]
    ppermute x3, starting transfers between devices: 11.5 us -> 9.45 us  [turned(): lax.ppermute(value, ('fsdp', 'mp'), [(flat(*i), flat(i[2], i[1], i[0])) f...]
    pallas_call x10 -> x12, Pallas kernels: 9.06 us -> 10.1 us  [call(): pl.pallas_call(kernel, in_specs=[scalars] * in_scalars + [whole] * (len(o...]
    ppermute x15 -> x18, starting transfers between devices: 17.4 us -> 17.7 us  [in_square(): return lax.ppermute(value, 'fsdp', [(i, i ^ k) for i in range(2 * g)])]
    ppermute x2 -> x3, waiting for transfers between devices: 21.2 us -> 21.3 us  [across(): return lax.ppermute(value, 'fsdp', [(i, i ^ g) for i in range(2 * g)])]
  transfers between devices with their start and end apart: 29 -> 33, of which waited for: 18 -> 17; matrix products, arithmetic and copies ran while one was open for 0% -> 0% of each run, Pallas kernels for 3% -> 6%
where the time goes in v5:
time: 119 us
  waiting for transfers between devices  69.3 us (58%)
  starting transfers between devices  34.7 us (29%)
  Pallas kernels  10.1 us (8%)
  local copies, waits for them, and re-layouts  3.56 us (3%)
    ppermute x18, waiting for transfers between devices, in_square(): return lax.ppermute(value, 'fsdp', [(i, i ^ k) for i in range(2 * g)])  27.7 us
    ppermute x3, waiting for transfers between devices, across(): return lax.ppermute(value, 'fsdp', [(i, i ^ g) for i in range(2 * g)])  21.3 us
    ppermute x18, starting transfers between devices, in_square(): return lax.ppermute(value, 'fsdp', [(i, i ^ k) for i in range(2 * g)])  17.7 us
    ppermute x3, waiting for transfers between devices, turned(): lax.ppermute(value, ('fsdp', 'mp'), [(flat(*i), flat(i[2], i[1], i[0])) f...  16 us
    pallas_call x12, Pallas kernels, call(): pl.pallas_call(kernel, in_specs=[scalars] * in_scalars + [whole] * (len(o...  10.1 us
    ppermute x3, starting transfers between devices, turned(): lax.ppermute(value, ('fsdp', 'mp'), [(flat(*i), flat(i[2], i[1], i[0])) f...  9.45 us
    ppermute x9, starting transfers between devices, cores(): return lax.ppermute(value, 'mp', [(0, 1), (1, 0)])  6.57 us
    ppermute x9, waiting for transfers between devices, cores(): return lax.ppermute(value, 'mp', [(0, 1), (1, 0)])  4.31 us
  transfers between devices with their start and end apart: 33, of which 17 were waited for; matrix products, arithmetic and copies ran while one was open for 0% of the time, Pallas kernels for 6%

profile of v5, /device:TPU:1, one launch (start us, length us, event | category | flops | bytes accessed | tf_op | source)
XLA Modules:
  0.0 118.7 jit_solution(137664754494090170)
XLA Ops:
  0.6 5.6 %collective-permute-start = (bf16[64,1536]{1,0:T(8,128)(2,1)}, bf16[64,1536]{1,0:T(8,128)(2,1)S(1)}, u32[]{:S(2)}, u32[]{:S(2)}) collective-permute-start(bf16[64,1536]{1,0:T(8,128)(2,1)} %param.13), channel_id=1, source_target_pairs={{0,0},{1,8},{2,2},{3,10},{4,4},{5,12},{6,6},{7,14},{8,1},{9,9},{10... | collective-permute-start | bytes 589832 | tf_op jit(solution)/shard_map/ppermute | solution.py:226
  6.2 1.9 %collective-permute-start.1 = (bf16[64,1536]{1,0:T(8,128)(2,1)}, bf16[64,1536]{1,0:T(8,128)(2,1)S(1)}, u32[]{:S(2)}, u32[]{:S(2)}) collective-permute-start(bf16[64,1536]{1,0:T(8,128)(2,1)} %param.14), channel_id=1, source_target_pairs={{0,0},{1,8},{2,2},{3,10},{4,4},{5,12},{6,6},{7,14},{8,1},{9,9},{10... | collective-permute-start | bytes 589832 | tf_op jit(solution)/shard_map/ppermute | solution.py:226
  16.7 2.4 %collective-permute-start.6 = (bf16[80,1536]{1,0:T(8,128)(2,1)S(1)}, bf16[80,1536]{1,0:T(8,128)(2,1)S(1)}, u32[]{:S(2)}, u32[]{:S(2)}) collective-permute-start(bf16[80,1536]{1,0:T(8,128)(2,1)S(1)} %get-tuple-element.66), channel_id=1, source_target_pairs={{0,4},{2,6},{4,0},{6,2},{8,12},{10,14},{12,8},{14,10},{1,5},{3,7},... | collective-permute-start | bytes 737288 | tf_op jit(solution)/shard_map/ppermute | solution.py:217
  19.2 1.9 %collective-permute-done.3.refs_7_.refs_6_ = bf16[384,384]{1,0:T(8,128)(2,1)S(1)} collective-permute-done((bf16[384,384]{1,0:T(8,128)(2,1)S(1)}, bf16[384,384]{1,0:T(8,128)(2,1)S(1)}, u32[]{:S(2)}, u32[]{:S(2)}) %collective-permute-start.3) | collective-permute-done | bytes 294944 | tf_op jit(solution)/shard_map/ppermute | solution.py:217
  21.1 6.9 %collective-permute-done.4.refs_8_.refs_7_ = bf16[384,384]{1,0:T(8,128)(2,1)S(1)} collective-permute-done((bf16[384,384]{1,0:T(8,128)(2,1)S(1)}, bf16[384,384]{1,0:T(8,128)(2,1)S(1)}, u32[]{:S(2)}, u32[]{:S(2)}) %collective-permute-start.4) | collective-permute-done | bytes 294944 | tf_op jit(solution)/shard_map/ppermute | solution.py:217
  28.5 4.2 %collective-permute-done.6.refs_2_ = bf16[80,1536]{1,0:T(8,128)(2,1)S(1)} collective-permute-done((bf16[80,1536]{1,0:T(8,128)(2,1)S(1)}, bf16[80,1536]{1,0:T(8,128)(2,1)S(1)}, u32[]{:S(2)}, u32[]{:S(2)}) %collective-permute-start.6) | collective-permute-done | bytes 245792 | tf_op jit(solution)/shard_map/ppermute | solution.py:217
  32.9 4.1 %collective-permute-done.7.refs_3_ = bf16[80,1536]{1,0:T(8,128)(2,1)S(1)} collective-permute-done((bf16[80,1536]{1,0:T(8,128)(2,1)S(1)}, bf16[80,1536]{1,0:T(8,128)(2,1)S(1)}, u32[]{:S(2)}, u32[]{:S(2)}) %collective-permute-start.7) | collective-permute-done | bytes 245792 | tf_op jit(solution)/shard_map/ppermute | solution.py:217
  37.0 1.4 %collective-permute-start.17 = (bf16[2,384,384]{2,1,0:T(8,128)(2,1)S(1)}, bf16[2,384,384]{2,1,0:T(8,128)(2,1)S(1)}, u32[]{:S(2)}, u32[]{:S(2)}) collective-permute-start(bf16[2,384,384]{2,1,0:T(8,128)(2,1)S(1)} %get-tuple-element.82), channel_id=1, source_target_pairs={{0,2},{2,0},{4,6},{6,4},{8,10},{10,8},{12,14},{14,12},{1,3},{3,1},... | collective-permute-start | bytes 1769480 | tf_op jit(solution)/shard_map/ppermute | solution.py:217
  38.4 2.0 %shard_map.151 = (f32[256,384]{1,0:T(8,128)S(1)}, bf16[272,384]{1,0:T(8,128)(2,1)S(1)}, f32[8,256]{1,0:T(8,128)S(1)}, f32[256,384]{1,0:T(8,128)S(1)}) custom-call(s32[8]{0:T(128)S(1)} %copy-done.9, bf16[80,1536]{1,0:T(8,128)(2,1)S(1)} %get-tuple-element.59.refs_0_, bf16[80,1536]{1,0:T(8,128)(2,1)S(1)} %collective-permute-done.5.refs_1_, ...), custom_call_target="tpu_custom_call" | custom-call | flops 603979776 | bytes 3538976 | tf_op jit(solution)/shard_map/pallas_call | solution.py:233
  40.5 1.7 %collective-permute-start.18 = (bf16[2,384,384]{2,1,0:T(8,128)(2,1)S(1)}, bf16[2,384,384]{2,1,0:T(8,128)(2,1)S(1)}, u32[]{:S(2)}, u32[]{:S(2)}) collective-permute-start(bf16[2,384,384]{2,1,0:T(8,128)(2,1)S(1)} %get-tuple-element.83), channel_id=1, source_target_pairs={{0,4},{2,6},{4,0},{6,2},{8,12},{10,14},{12,8},{14,10},{1,5},{3,7},... | collective-permute-start | bytes 1769480 | tf_op jit(solution)/shard_map/ppermute | solution.py:217
  42.2 9.8 %collective-permute-done.12.came = bf16[272,384]{1,0:T(8,128)(2,1)S(1)} collective-permute-done((bf16[272,384]{1,0:T(8,128)(2,1)S(1)}, bf16[272,384]{1,0:T(8,128)(2,1)S(1)}, u32[]{:S(2)}, u32[]{:S(2)}) %collective-permute-start.12) | collective-permute-done | bytes 208928 | tf_op jit(solution)/shard_map/ppermute | solution.py:220
  52.9 1.9 %collective-permute-start.16 = (bf16[256,384]{1,0:T(8,128)(2,1)S(1)}, bf16[256,384]{1,0:T(8,128)(2,1)S(1)}, u32[]{:S(2)}, u32[]{:S(2)}) collective-permute-start(bf16[256,384]{1,0:T(8,128)(2,1)S(1)} %get-tuple-element.77.refs_0_), channel_id=1, source_target_pairs={{0,0},{1,8},{2,2},{3,10},{4,4},{5,12},{6,6},{7,14},{8,1},{9,9},{10... | collective-permute-start | bytes 589832 | tf_op jit(solution)/shard_map/ppermute | solution.py:226
  54.8 2.4 %collective-permute-start.15 = (bf16[256,384]{1,0:T(8,128)(2,1)S(1)}, bf16[256,384]{1,0:T(8,128)(2,1)S(1)}, u32[]{:S(2)}, u32[]{:S(2)}) collective-permute-start(bf16[256,384]{1,0:T(8,128)(2,1)S(1)} %get-tuple-element.77.refs_0_), channel_id=1, source_target_pairs={{0,6},{2,4},{4,2},{6,0},{8,14},{10,12},{12,10},{14,8},{1,7},{3,5},... | collective-permute-start | bytes 589832 | tf_op jit(solution)/shard_map/ppermute | solution.py:217
  57.6 15.7 %collective-permute-done.16.owned = bf16[256,384]{1,0:T(8,128)(2,1)S(1)} collective-permute-done((bf16[256,384]{1,0:T(8,128)(2,1)S(1)}, bf16[256,384]{1,0:T(8,128)(2,1)S(1)}, u32[]{:S(2)}, u32[]{:S(2)}) %collective-permute-start.16) | collective-permute-done | bytes 196640 | tf_op jit(solution)/shard_map/ppermute | solution.py:226
  73.3 4.2 %collective-permute-done.15.refs_3_ = bf16[256,384]{1,0:T(8,128)(2,1)S(1)} collective-permute-done((bf16[256,384]{1,0:T(8,128)(2,1)S(1)}, bf16[256,384]{1,0:T(8,128)(2,1)S(1)}, u32[]{:S(2)}, u32[]{:S(2)}) %collective-permute-start.15) | collective-permute-done | bytes 196640 | tf_op jit(solution)/shard_map/ppermute | solution.py:217
  77.5 3.9 %collective-permute-done.14.refs_2_ = bf16[256,384]{1,0:T(8,128)(2,1)S(1)} collective-permute-done((bf16[256,384]{1,0:T(8,128)(2,1)S(1)}, bf16[256,384]{1,0:T(8,128)(2,1)S(1)}, u32[]{:S(2)}, u32[]{:S(2)}) %collective-permute-start.14) | collective-permute-done | bytes 196640 | tf_op jit(solution)/shard_map/ppermute | solution.py:217
  82.6 2.8 %collective-permute-start.24 = (bf16[2,384,384]{2,1,0:T(8,128)(2,1)S(1)}, bf16[2,384,384]{2,1,0:T(8,128)(2,1)S(1)}, u32[]{:S(2)}, u32[]{:S(2)}) collective-permute-start(bf16[2,384,384]{2,1,0:T(8,128)(2,1)S(1)} %get-tuple-element.95.refs_5_), channel_id=1, source_target_pairs={{0,1},{1,0},{2,3},{3,2},{4,5},{5,4},{6,7},{7,6},{8,9},{9,8},{10,11... | collective-permute-start | bytes 1769480 | tf_op jit(solution)/shard_map/ppermute | solution.py:223
  91.2 11.5 %collective-permute-done.20.came = bf16[272,384]{1,0:T(8,128)(2,1)S(1)} collective-permute-done((bf16[272,384]{1,0:T(8,128)(2,1)S(1)}, bf16[272,384]{1,0:T(8,128)(2,1)S(1)}, u32[]{:S(2)}, u32[]{:S(2)}) %collective-permute-start.20) | collective-permute-done | bytes 208928 | tf_op jit(solution)/shard_map/ppermute | solution.py:220
  102.6 1.5 %shard_map.155 = (bf16[128,384]{1,0:T(8,128)(2,1)S(1)}, bf16[128,384]{1,0:T(8,128)(2,1)S(1)}, bf16[128,384]{1,0:T(8,128)(2,1)S(1)}, bf16[128,384]{1,0:T(8,128)(2...) custom-call(s32[8]{0:T(128)S(1)} %copy-done.9, f32[256,384]{1,0:T(8,128)S(1)} %get-tuple-element.85.gap, ...), custom_call_target="tpu_custom_call" | custom-call | flops 301989888 | bytes 3297312 | tf_op jit(solution)/shard_map/pallas_call | solution.py:233
  104.3 2.6 %collective-permute-start.23 = (bf16[128,384]{1,0:T(8,128)(2,1)S(1)}, bf16[128,384]{1,0:T(8,128)(2,1)S(1)}, u32[]{:S(2)}, u32[]{:S(2)}) collective-permute-start(bf16[128,384]{1,0:T(8,128)(2,1)S(1)} %get-tuple-element.93), channel_id=1, source_target_pairs={{0,6},{2,4},{4,2},{6,0},{8,14},{10,12},{12,10},{14,8},{1,7},{3,5},... | collective-permute-start | bytes 294920 | tf_op jit(solution)/shard_map/ppermute | solution.py:217
  106.9 1.3 %shard_map.157 = (bf16[80,384]{1,0:T(8,128)(2,1)S(1)}, bf16[80,384]{1,0:T(8,128)(2,1)S(1)}, bf16[80,384]{1,0:T(8,128)(2,1)S(1)}, bf16[80,384]{1,0:T(8,128)(2,1)S(1)}) custom-call(s32[8]{0:T(128)S(1)} %copy-done.9, f32[256,384]{1,0:T(8,128)S(1)} %get-tuple-element.99.gap, bf16[256,384]{1,0:T(8,128)(2,1)S(1)} %collective-permute-done.28.came, ...), custom_call_target="tpu_custom_call" | custom-call | flops 301989888 | bytes 3223584 | tf_op jit(solution)/shard_map/pallas_call | solution.py:233
  108.6 2.4 %collective-permute-start.31 = (bf16[80,384]{1,0:T(8,128)(2,1)S(1)}, bf16[80,384]{1,0:T(8,128)(2,1)S(1)}, u32[]{:S(2)}, u32[]{:S(2)}) collective-permute-start(bf16[80,384]{1,0:T(8,128)(2,1)S(1)} %get-tuple-element.106), channel_id=1, source_target_pairs={{0,6},{2,4},{4,2},{6,0},{8,14},{10,12},{12,10},{14,8},{1,7},{3,5},... | collective-permute-start | bytes 184328 | tf_op jit(solution)/shard_map/ppermute | solution.py:217
  111.0 1.5 %collective-permute-done.29.refs_5_ = bf16[80,384]{1,0:T(8,128)(2,1)S(1)} collective-permute-done((bf16[80,384]{1,0:T(8,128)(2,1)S(1)}, bf16[80,384]{1,0:T(8,128)(2,1)S(1)}, u32[]{:S(2)}, u32[]{:S(2)}) %collective-permute-start.29) | collective-permute-done | bytes 61472 | tf_op jit(solution)/shard_map/ppermute | solution.py:217
  114.3 2.6 %collective-permute-start.32 = (bf16[80,1536]{1,0:T(8,128)(2,1)S(1)}, bf16[80,1536]{1,0:T(8,128)(2,1)S(1)}, u32[]{:S(2)}, u32[]{:S(2)}) collective-permute-start(bf16[80,1536]{1,0:T(8,128)(2,1)S(1)} %get-tuple-element.110), channel_id=1, source_target_pairs={{0,1},{1,0},{2,3},{3,2},{4,5},{5,4},{6,7},{7,6},{8,9},{9,8},{10,11... | collective-permute-start | bytes 737288 | tf_op jit(solution)/shard_map/ppermute | solution.py:223
  (81 shorter events, 21.6 us)
Async XLA Ops:
  0.6 14.5 %collective-permute-start = (bf16[64,1536]{1,0:T(8,128)(2,1)}, bf16[64,1536]{1,0:T(8,128)(2,1)S(1)}, u32[]{:S(2)}, u32[]{:S(2)}) collective-permute-start(bf16[64,1536]{1,0:T(8,128)(2,1)} %param.13), channel_id=1, source_target_pairs={{0,0},{1,8},{2,2},{3,10},{4,4},{5,12},{6,6},{7,14},{8,1},{9,9},{10... | collective-permute-start | bytes 589832 | tf_op jit(solution)/shard_map/ppermute | solution.py:226
  6.2 9.1 %collective-permute-start.1 = (bf16[64,1536]{1,0:T(8,128)(2,1)}, bf16[64,1536]{1,0:T(8,128)(2,1)S(1)}, u32[]{:S(2)}, u32[]{:S(2)}) collective-permute-start(bf16[64,1536]{1,0:T(8,128)(2,1)} %param.14), channel_id=1, source_target_pairs={{0,0},{1,8},{2,2},{3,10},{4,4},{5,12},{6,6},{7,14},{8,1},{9,9},{10... | collective-permute-start | bytes 589832 | tf_op jit(solution)/shard_map/ppermute | solution.py:226
  9.6 9.6 %collective-permute-start.2 = (bf16[384,384]{1,0:T(8,128)(2,1)S(1)}, bf16[384,384]{1,0:T(8,128)(2,1)S(1)}, u32[]{:S(2)}, u32[]{:S(2)}) collective-permute-start(bf16[384,384]{1,0:T(8,128)(2,1)S(1)} %get-tuple-element.61), channel_id=1, source_target_pairs={{0,2},{2,0},{4,6},{6,4},{8,10},{10,8},{12,14},{14,12},{1,3},{3,1},... | collective-permute-start | bytes 884744 | tf_op jit(solution)/shard_map/ppermute | solution.py:217
  10.9 10.2 %collective-permute-start.3 = (bf16[384,384]{1,0:T(8,128)(2,1)S(1)}, bf16[384,384]{1,0:T(8,128)(2,1)S(1)}, u32[]{:S(2)}, u32[]{:S(2)}) collective-permute-start(bf16[384,384]{1,0:T(8,128)(2,1)S(1)} %get-tuple-element.62), channel_id=1, source_target_pairs={{0,4},{2,6},{4,0},{6,2},{8,12},{10,14},{12,8},{14,10},{1,5},{3,7},... | collective-permute-start | bytes 884744 | tf_op jit(solution)/shard_map/ppermute | solution.py:217
  12.2 15.8 %collective-permute-start.4 = (bf16[384,384]{1,0:T(8,128)(2,1)S(1)}, bf16[384,384]{1,0:T(8,128)(2,1)S(1)}, u32[]{:S(2)}, u32[]{:S(2)}) collective-permute-start(bf16[384,384]{1,0:T(8,128)(2,1)S(1)} %get-tuple-element.63), channel_id=1, source_target_pairs={{0,6},{2,4},{4,2},{6,0},{8,14},{10,12},{12,10},{14,8},{1,7},{3,5},... | collective-permute-start | bytes 884744 | tf_op jit(solution)/shard_map/ppermute | solution.py:217
  15.4 12.6 %collective-permute-start.5 = (bf16[80,1536]{1,0:T(8,128)(2,1)S(1)}, bf16[80,1536]{1,0:T(8,128)(2,1)S(1)}, u32[]{:S(2)}, u32[]{:S(2)}) collective-permute-start(bf16[80,1536]{1,0:T(8,128)(2,1)S(1)} %get-tuple-element.64), channel_id=1, source_target_pairs={{0,2},{2,0},{4,6},{6,4},{8,10},{10,8},{12,14},{14,12},{1,3},{3,1},... | collective-permute-start | bytes 737288 | tf_op jit(solution)/shard_map/ppermute | solution.py:217
  16.7 16.0 %collective-permute-start.6 = (bf16[80,1536]{1,0:T(8,128)(2,1)S(1)}, bf16[80,1536]{1,0:T(8,128)(2,1)S(1)}, u32[]{:S(2)}, u32[]{:S(2)}) collective-permute-start(bf16[80,1536]{1,0:T(8,128)(2,1)S(1)} %get-tuple-element.66), channel_id=1, source_target_pairs={{0,4},{2,6},{4,0},{6,2},{8,12},{10,14},{12,8},{14,10},{1,5},{3,7},... | collective-permute-start | bytes 737288 | tf_op jit(solution)/shard_map/ppermute | solution.py:217
  19.2 17.8 %collective-permute-start.7 = (bf16[80,1536]{1,0:T(8,128)(2,1)S(1)}, bf16[80,1536]{1,0:T(8,128)(2,1)S(1)}, u32[]{:S(2)}, u32[]{:S(2)}) collective-permute-start(bf16[80,1536]{1,0:T(8,128)(2,1)S(1)} %get-tuple-element.67), channel_id=1, source_target_pairs={{0,6},{2,4},{4,2},{6,0},{8,14},{10,12},{12,10},{14,8},{1,7},{3,5},... | collective-permute-start | bytes 737288 | tf_op jit(solution)/shard_map/ppermute | solution.py:217
  28.0 10.4 %collective-permute-start.8 = (bf16[384,384]{1,0:T(8,128)(2,1)S(1)}, bf16[384,384]{1,0:T(8,128)(2,1)S(1)}, u32[]{:S(2)}, u32[]{:S(2)}) collective-permute-start(bf16[384,384]{1,0:T(8,128)(2,1)S(1)} %get-tuple-element.69.refs_5_.refs_4_), channel_id=1, source_target_pairs={{0,1},{1,0},{2,3},{3,2},{4,5},{5,4},{6,7},{7,6},{8,9},{9,8},{10,11... | collective-permute-start | bytes 884744 | tf_op jit(solution)/shard_map/ppermute | solution.py:223
  28.0 10.4 %collective-permute-start.9 = (bf16[384,384]{1,0:T(8,128)(2,1)S(1)}, bf16[384,384]{1,0:T(8,128)(2,1)S(1)}, u32[]{:S(2)}, u32[]{:S(2)}) collective-permute-start(bf16[384,384]{1,0:T(8,128)(2,1)S(1)} %collective-permute-done.2.refs_6_.refs_5_), channel_id=1, source_target_pairs={{0,1},{1,0},{2,3},{3,2},{4,5},{5,4},{6,7},{7,6},{8,9},{9,8},{10,11... | collective-permute-start | bytes 884744 | tf_op jit(solution)/shard_map/ppermute | solution.py:223
  28.5 9.9 %collective-permute-start.10 = (bf16[384,384]{1,0:T(8,128)(2,1)S(1)}, bf16[384,384]{1,0:T(8,128)(2,1)S(1)}, u32[]{:S(2)}, u32[]{:S(2)}) collective-permute-start(bf16[384,384]{1,0:T(8,128)(2,1)S(1)} %collective-permute-done.3.refs_7_.refs_6_), channel_id=1, source_target_pairs={{0,1},{1,0},{2,3},{3,2},{4,5},{5,4},{6,7},{7,6},{8,9},{9,8},{10,11... | collective-permute-start | bytes 884744 | tf_op jit(solution)/shard_map/ppermute | solution.py:223
  32.7 5.7 %collective-permute-start.11 = (bf16[384,384]{1,0:T(8,128)(2,1)S(1)}, bf16[384,384]{1,0:T(8,128)(2,1)S(1)}, u32[]{:S(2)}, u32[]{:S(2)}) collective-permute-start(bf16[384,384]{1,0:T(8,128)(2,1)S(1)} %collective-permute-done.4.refs_8_.refs_7_), channel_id=1, source_target_pairs={{0,1},{1,0},{2,3},{3,2},{4,5},{5,4},{6,7},{7,6},{8,9},{9,8},{10,11... | collective-permute-start | bytes 884744 | tf_op jit(solution)/shard_map/ppermute | solution.py:223
  37.0 20.2 %collective-permute-start.17 = (bf16[2,384,384]{2,1,0:T(8,128)(2,1)S(1)}, bf16[2,384,384]{2,1,0:T(8,128)(2,1)S(1)}, u32[]{:S(2)}, u32[]{:S(2)}) collective-permute-start(bf16[2,384,384]{2,1,0:T(8,128)(2,1)S(1)} %get-tuple-element.82), channel_id=1, source_target_pairs={{0,2},{2,0},{4,6},{6,4},{8,10},{10,8},{12,14},{14,12},{1,3},{3,1},... | collective-permute-start | bytes 1769480 | tf_op jit(solution)/shard_map/ppermute | solution.py:217
  40.4 11.6 %collective-permute-start.12 = (bf16[272,384]{1,0:T(8,128)(2,1)S(1)}, bf16[272,384]{1,0:T(8,128)(2,1)S(1)}, u32[]{:S(2)}, u32[]{:S(2)}) collective-permute-start(bf16[272,384]{1,0:T(8,128)(2,1)S(1)} %get-tuple-element.74), channel_id=1, source_target_pairs={{0,8},{2,10},{4,12},{6,14},{8,0},{10,2},{12,4},{14,6},{1,9},{3,11}... | collective-permute-start | bytes 626696 | tf_op jit(solution)/shard_map/ppermute | solution.py:220
  40.5 32.8 %collective-permute-start.18 = (bf16[2,384,384]{2,1,0:T(8,128)(2,1)S(1)}, bf16[2,384,384]{2,1,0:T(8,128)(2,1)S(1)}, u32[]{:S(2)}, u32[]{:S(2)}) collective-permute-start(bf16[2,384,384]{2,1,0:T(8,128)(2,1)S(1)} %get-tuple-element.83), channel_id=1, source_target_pairs={{0,4},{2,6},{4,0},{6,2},{8,12},{10,14},{12,8},{14,10},{1,5},{3,7},... | collective-permute-start | bytes 1769480 | tf_op jit(solution)/shard_map/ppermute | solution.py:217
  42.2 31.1 %collective-permute-start.19 = (bf16[2,384,384]{2,1,0:T(8,128)(2,1)S(1)}, bf16[2,384,384]{2,1,0:T(8,128)(2,1)S(1)}, u32[]{:S(2)}, u32[]{:S(2)}) collective-permute-start(bf16[2,384,384]{2,1,0:T(8,128)(2,1)S(1)} %get-tuple-element.84), channel_id=1, source_target_pairs={{0,6},{2,4},{4,2},{6,0},{8,14},{10,12},{12,10},{14,8},{1,7},{3,5},... | collective-permute-start | bytes 1769480 | tf_op jit(solution)/shard_map/ppermute | solution.py:217
  52.9 20.4 %collective-permute-start.16 = (bf16[256,384]{1,0:T(8,128)(2,1)S(1)}, bf16[256,384]{1,0:T(8,128)(2,1)S(1)}, u32[]{:S(2)}, u32[]{:S(2)}) collective-permute-start(bf16[256,384]{1,0:T(8,128)(2,1)S(1)} %get-tuple-element.77.refs_0_), channel_id=1, source_target_pairs={{0,0},{1,8},{2,2},{3,10},{4,4},{5,12},{6,6},{7,14},{8,1},{9,9},{10... | collective-permute-start | bytes 589832 | tf_op jit(solution)/shard_map/ppermute | solution.py:226
  54.8 22.7 %collective-permute-start.15 = (bf16[256,384]{1,0:T(8,128)(2,1)S(1)}, bf16[256,384]{1,0:T(8,128)(2,1)S(1)}, u32[]{:S(2)}, u32[]{:S(2)}) collective-permute-start(bf16[256,384]{1,0:T(8,128)(2,1)S(1)} %get-tuple-element.77.refs_0_), channel_id=1, source_target_pairs={{0,6},{2,4},{4,2},{6,0},{8,14},{10,12},{12,10},{14,8},{1,7},{3,5},... | collective-permute-start | bytes 589832 | tf_op jit(solution)/shard_map/ppermute | solution.py:217
  57.2 24.2 %collective-permute-start.14 = (bf16[256,384]{1,0:T(8,128)(2,1)S(1)}, bf16[256,384]{1,0:T(8,128)(2,1)S(1)}, u32[]{:S(2)}, u32[]{:S(2)}) collective-permute-start(bf16[256,384]{1,0:T(8,128)(2,1)S(1)} %get-tuple-element.77.refs_0_), channel_id=1, source_target_pairs={{0,4},{2,6},{4,0},{6,2},{8,12},{10,14},{12,8},{14,10},{1,5},{3,7},... | collective-permute-start | bytes 589832 | tf_op jit(solution)/shard_map/ppermute | solution.py:217
  73.3 8.1 %collective-permute-start.13 = (bf16[256,384]{1,0:T(8,128)(2,1)S(1)}, bf16[256,384]{1,0:T(8,128)(2,1)S(1)}, u32[]{:S(2)}, u32[]{:S(2)}) collective-permute-start(bf16[256,384]{1,0:T(8,128)(2,1)S(1)} %get-tuple-element.77.refs_0_), channel_id=1, source_target_pairs={{0,2},{2,0},{4,6},{6,4},{8,10},{10,8},{12,14},{14,12},{1,3},{3,1},... | collective-permute-start | bytes 589832 | tf_op jit(solution)/shard_map/ppermute | solution.py:217
  86.0 16.6 %collective-permute-start.20 = (bf16[272,384]{1,0:T(8,128)(2,1)S(1)}, bf16[272,384]{1,0:T(8,128)(2,1)S(1)}, u32[]{:S(2)}, u32[]{:S(2)}) collective-permute-start(bf16[272,384]{1,0:T(8,128)(2,1)S(1)} %get-tuple-element.86), channel_id=1, source_target_pairs={{0,8},{2,10},{4,12},{6,14},{8,0},{10,2},{12,4},{14,6},{1,9},{3,11}... | collective-permute-start | bytes 626696 | tf_op jit(solution)/shard_map/ppermute | solution.py:220
  90.7 16.2 %collective-permute-start.28 = (bf16[256,384]{1,0:T(8,128)(2,1)S(1)}, bf16[256,384]{1,0:T(8,128)(2,1)S(1)}, u32[]{:S(2)}, u32[]{:S(2)}) collective-permute-start(bf16[256,384]{1,0:T(8,128)(2,1)S(1)} %get-tuple-element.100), channel_id=1, source_target_pairs={{0,8},{2,10},{4,12},{6,14},{8,0},{10,2},{12,4},{14,6},{1,9},{3,11}... | collective-permute-start | bytes 589832 | tf_op jit(solution)/shard_map/ppermute | solution.py:220
  104.2 6.7 %collective-permute-start.22 = (bf16[128,384]{1,0:T(8,128)(2,1)S(1)}, bf16[128,384]{1,0:T(8,128)(2,1)S(1)}, u32[]{:S(2)}, u32[]{:S(2)}) collective-permute-start(bf16[128,384]{1,0:T(8,128)(2,1)S(1)} %get-tuple-element.92), channel_id=1, source_target_pairs={{0,4},{2,6},{4,0},{6,2},{8,12},{10,14},{12,8},{14,10},{1,5},{3,7},... | collective-permute-start | bytes 294920 | tf_op jit(solution)/shard_map/ppermute | solution.py:217
  104.3 6.6 %collective-permute-start.23 = (bf16[128,384]{1,0:T(8,128)(2,1)S(1)}, bf16[128,384]{1,0:T(8,128)(2,1)S(1)}, u32[]{:S(2)}, u32[]{:S(2)}) collective-permute-start(bf16[128,384]{1,0:T(8,128)(2,1)S(1)} %get-tuple-element.93), channel_id=1, source_target_pairs={{0,6},{2,4},{4,2},{6,0},{8,14},{10,12},{12,10},{14,8},{1,7},{3,5},... | collective-permute-start | bytes 294920 | tf_op jit(solution)/shard_map/ppermute | solution.py:217
  (20 other events, 92.7 us)

commit v6 on v5

--- a/solution.py
+++ b/solution.py
@@ -299,6 +299,7 @@
 
     depth = gen_weight.shape[0]
     fold = r // g
+    shared = g // 2
 
     def cut_gen_kernel(weight, *outs):
         _, q, _ = place()
@@ -308,8 +309,15 @@
     def cut_score_kernel(real, fake, *outs):
         _, q, _ = place()
         for k in span:
-            outs[k][0] = real[:, lanes(q ^ k)]
-            outs[k][1] = fake[:, lanes(q ^ k)]
+            if k < shared:
+                outs[k][0] = real[:, lanes(q ^ k)]
+                outs[k][1] = fake[:, lanes(q ^ k)]
+            else:
+                for n, weight in enumerate((real, fake)):
+
+                    @pl.when(lax.axis_index("rep") == n)
+                    def _():
+                        outs[k][...] = weight[:, lanes(q ^ k)]
 
     def cut_rows_kernel(rows, fresh, *outs):
         _, q, _ = place()
@@ -317,6 +325,19 @@
             outs[k][0:r, :] = rows[...]
             for i in span:
                 outs[k][r : r + fold, i * w : (i + 1) * w] = fresh[i * fold : (i + 1) * fold, lanes(q ^ k)]
+
+    def swap_all(tile):
+        counts = [v.size // (depth * w) for v in tile]
+
+        def join_kernel(*refs):
+            out, at = refs[-1], 0
+            for ref, n in zip(refs[:-1], counts):
+                for i in range(n):
+                    out[at] = ref[i] if n > 1 else ref[...]
+                    at += 1
+
+        (joined,) = call(join_kernel, tile, [((sum(counts), depth, w), bf16)], depth * w)
+        return cores(joined)
 
     x_turned, fresh_turned = turned(noise_in), turned(renoise)
     gen_sent = call(cut_gen_kernel, [gen_weight], [((depth, w), bf16)] * g, depth * h)
@@ -327,7 +348,12 @@
     gen_swap, x[1] = lax.optimization_barrier((gen_mine, x[1]))
     gen_other = [cores(v) for v in gen_swap]
     real_weight, fake_weight, _ = lax.optimization_barrier((real_weight, fake_weight, x_turned))
-    score_sent = call(cut_score_kernel, [real_weight, fake_weight], [((2, depth, w), bf16)] * g, 2 * depth * h)
+    score_sent = call(
+        cut_score_kernel,
+        [real_weight, fake_weight],
+        [((2, depth, w), bf16)] * shared + [((depth, w), bf16)] * (g - shared),
+        2 * depth * h,
+    )
     score_mine = [score_sent[0]] + [in_square(score_sent[k], k) for k in range(1, g)]
 
     def generate_kernel(steps, *refs):
@@ -386,23 +412,40 @@
             made = keep[band(j), :] + came[band(j), :].astype(f32)
             noised[band(j), :] = (base[band(j), :] + (stay * inverse[band(j), :]) * made).astype(bf16)
 
+    came, *fetched = lax.optimization_barrier((across(away), *score_mine[shared:g]))
+    score_mine[shared:g] = fetched
+    for k in range(shared, g):
+        score_mine.append(lax.ppermute(score_mine[k], "rep", [(0, 1), (1, 0)]))
     noised_mine, x_root = call(
         blend_kernel,
-        [noise_step, keep, across(away), x_sums, base],
+        [noise_step, keep, came, x_sums, base],
         [((t, w), bf16), ((t, 128), f32)],
         10 * t * w,
         in_scalars=1,
     )
-    noised_owned = turned(noised_mine)
-    noised = [noised_mine] + [in_square(noised_mine, k) for k in range(1, g)]
-    noised_owned, score_scales = lax.optimization_barrier((noised_owned, scales))
+    noised_last, score_mine[1] = lax.optimization_barrier((noised_mine, score_mine[1]))
+    noised = [noised_mine, in_square(noised_last, 1)] + [in_square(noised_mine, k) for k in range(2, g)]
+
+    tiles = len(score_mine)
+
+    def score_product(lifts, tile):
+        copy = lax.axis_index("rep")
+        total = jnp.zeros((t, w), f32)
+        for k in span:
+            columns = slice(k * w, (k + 1) * w)
+            if k < shared:
+                pairs = [(tile[k][0], 0), (tile[k][1], 1)]
+            else:
+                pairs = [(tile[k][...], copy), (tile[k + g - shared][...], 1 - copy)]
+            for part, n in pairs:
+                total = total + jnp.dot(lifts[n, :, columns], part, preferred_element_type=f32)
+        return total
 
     def score_kernel(*refs):
-        ns, scale, own = refs[:g], refs[g], refs[g + 1 : 2 * g + 1]
-        gap, away, sums, lifts = refs[2 * g + 1 :]
+        ns, scale, own = refs[:g], refs[g], refs[g + 1 : g + 1 + tiles]
+        gap, away, sums, lifts = refs[g + 1 + tiles :]
         _, q, c = place()
         totals = [jnp.zeros((r, 1), f32) for _ in span]
-        here = jnp.zeros((t, w), f32)
         for k in span:
             columns = slice(k * w, (k + 1) * w)
             for j in span:
@@ -411,8 +454,7 @@
                 totals[j] = totals[j] + jnp.sum(wide * wide, axis=1, keepdims=True)
                 for n in (0, 1):
                     lifts[n, band(j), columns] = (wide * scale[1 + n, block, lanes(q ^ k)]).astype(bf16)
-            for n in (0, 1):
-                here = here + jnp.dot(lifts[n, :, columns], own[k][n], preferred_element_type=f32)
+        here = score_product(lifts, own)
         gap[...] = here
         away[0:t, :] = here.astype(bf16)
         rows = rows_of(jnp.concatenate(totals, axis=0))
@@ -427,27 +469,26 @@
 
     gap_here, away_here, noised_sums, lifts = call(
         score_kernel,
-        noised + [score_scales] + score_mine,
+        noised + [scales] + score_mine,
         [((t, w), f32), ((t + tail, w), bf16), ((8, t), f32), ((2, t, h), bf16)],
         4 * t * h * w,
     )
     came_here = across(away_here)
-    score_mine, away_here = lax.optimization_barrier((score_mine, away_here))
-    score_other = [cores(v) for v in score_mine]
-
-    def score_rest_kernel(lifts, *refs):
-        other, (gap, away) = refs[:g], refs[g:]
-        there = jnp.zeros((t, w), f32)
-        for k in span:
-            for n in (0, 1):
-                there = there + jnp.dot(
-                    lifts[n, :, k * w : (k + 1) * w], other[k][n], preferred_element_type=f32
-                )
+    score_mine, noised_home, away_here = lax.optimization_barrier((score_mine, noised_mine, away_here))
+    noised_owned = turned(noised_home)
+    score_other = swap_all(score_mine)
+
+    def score_rest_kernel(lifts, other, gap, away):
+        there = score_product(
+            lifts,
+            [(other[2 * k], other[2 * k + 1]) for k in range(shared)]
+            + [other[shared + k] for k in range(shared, tiles)],
+        )
         gap[...] = there
         away[...] = there.astype(bf16)
 
     gap_there, away_there = call(
-        score_rest_kernel, [lifts] + score_other, [((t, w), f32), ((t, w), bf16)], 4 * t * h * w
+        score_rest_kernel, [lifts, score_other], [((t, w), f32), ((t, w), bf16)], 4 * t * h * w
     )
     came_there = across(away_there)
 
@@ -550,7 +591,7 @@
 
 def solution(mesh):
     positions = mesh.shape["fsdp"]
-    on_device = on_tiles if positions in (4, 8) and mesh.shape["mp"] == 2 else on_groups
+    on_device = on_tiles if (positions, mesh.shape["rep"], mesh.shape["mp"]) == (8, 2, 2) else on_groups
     return jax.shard_map(
         on_device,
         mesh=mesh,

time: 119 us -> 111 us (0.933)
  waiting for transfers between devices: 69.3 us -> 59.2 us
  local copies, waits for them, and re-layouts: 3.56 us -> 5.67 us
  starting transfers between devices: 34.7 us -> 33 us
  other arithmetic: 0.21 us -> 1.53 us
    ppermute x3, waiting for transfers between devices: 21.3 us -> 0.01 us  [across(): return lax.ppermute(value, 'fsdp', [(i, i ^ g) for i in range(2 * g)])]
    ppermute x18, waiting for transfers between devices: 27.7 us -> 41.8 us  [in_square(): return lax.ppermute(value, 'fsdp', [(i, i ^ k) for i in range(2 * g)])]
    ppermute x9 -> x6, starting transfers between devices: 6.57 us -> 1.95 us  [cores(): return lax.ppermute(value, 'mp', [(0, 1), (1, 0)])]
    ppermute x9 -> x6, waiting for transfers between devices: 4.31 us -> 1.52 us  [cores(): return lax.ppermute(value, 'mp', [(0, 1), (1, 0)])]
    unnamed x22 -> x20, local copies, waits for them, and re-layouts: 3.56 us -> 5.67 us
    ppermute x0 -> x2, starting transfers between devices: none -> 2.06 us  [on_tiles(): score_mine.append(lax.ppermute(score_mine[k], 'rep', [(0, 1), (1, 0)]))]
    ppermute x3, starting transfers between devices: 9.45 us -> 11.4 us  [turned(): lax.ppermute(value, ('fsdp', 'mp'), [(flat(*i), flat(i[2], i[1], i[0])) f...]
    ppermute x18, starting transfers between devices: 17.7 us -> 16.2 us  [in_square(): return lax.ppermute(value, 'fsdp', [(i, i ^ k) for i in range(2 * g)])]
  transfers between devices with their start and end apart: 33 -> 32, of which waited for: 17 -> 15; matrix products, arithmetic and copies ran while one was open for 0% -> 1% of each run, Pallas kernels for 6% -> 7%
where the time goes in v6:
time: 111 us
  waiting for transfers between devices  59.2 us (53%)
  starting transfers between devices  33 us (30%)
  Pallas kernels  10.4 us (9%)
  local copies, waits for them, and re-layouts  5.67 us (5%)
  other arithmetic  1.53 us (1%)
    ppermute x18, waiting for transfers between devices, in_square(): return lax.ppermute(value, 'fsdp', [(i, i ^ k) for i in range(2 * g)])  41.8 us
    ppermute x18, starting transfers between devices, in_square(): return lax.ppermute(value, 'fsdp', [(i, i ^ k) for i in range(2 * g)])  16.2 us
    ppermute x3, waiting for transfers between devices, turned(): lax.ppermute(value, ('fsdp', 'mp'), [(flat(*i), flat(i[2], i[1], i[0])) f...  15.2 us
    ppermute x3, starting transfers between devices, turned(): lax.ppermute(value, ('fsdp', 'mp'), [(flat(*i), flat(i[2], i[1], i[0])) f...  11.4 us
    pallas_call x13, Pallas kernels, call(): pl.pallas_call(kernel, in_specs=[scalars] * in_scalars + [whole] * (len(o...  10.4 us
    unnamed x20, local copies, waits for them, and re-layouts  5.67 us
  transfers between devices with their start and end apart: 32, of which 15 were waited for; matrix products, arithmetic and copies ran while one was open for 1% of the time, Pallas kernels for 7%

profile of v6, /device:TPU:1, one launch (start us, length us, event | category | flops | bytes accessed | tf_op | source)
XLA Modules:
  0.0 110.6 jit_solution(339482558768055330)
XLA Ops:
  0.6 5.6 %collective-permute-start = (bf16[64,1536]{1,0:T(8,128)(2,1)}, bf16[64,1536]{1,0:T(8,128)(2,1)S(1)}, u32[]{:S(2)}, u32[]{:S(2)}) collective-permute-start(bf16[64,1536]{1,0:T(8,128)(2,1)} %param.13), channel_id=1, source_target_pairs={{0,0},{1,8},{2,2},{3,10},{4,4},{5,12},{6,6},{7,14},{8,1},{9,9},{10... | collective-permute-start | bytes 589832 | tf_op jit(solution)/shard_map/ppermute | solution.py:226
  6.2 1.9 %collective-permute-start.1 = (bf16[64,1536]{1,0:T(8,128)(2,1)}, bf16[64,1536]{1,0:T(8,128)(2,1)S(1)}, u32[]{:S(2)}, u32[]{:S(2)}) collective-permute-start(bf16[64,1536]{1,0:T(8,128)(2,1)} %param.14), channel_id=1, source_target_pairs={{0,0},{1,8},{2,2},{3,10},{4,4},{5,12},{6,6},{7,14},{8,1},{9,9},{10... | collective-permute-start | bytes 589832 | tf_op jit(solution)/shard_map/ppermute | solution.py:226
  21.3 6.7 %collective-permute-done.4.refs_8_.refs_7_ = bf16[384,384]{1,0:T(8,128)(2,1)S(1)} collective-permute-done((bf16[384,384]{1,0:T(8,128)(2,1)S(1)}, bf16[384,384]{1,0:T(8,128)(2,1)S(1)}, u32[]{:S(2)}, u32[]{:S(2)}) %collective-permute-start.4) | collective-permute-done | bytes 294944 | tf_op jit(solution)/shard_map/ppermute | solution.py:217
  28.0 2.9 %collective-permute-done.5.refs_1_ = bf16[80,1536]{1,0:T(8,128)(2,1)S(1)} collective-permute-done((bf16[80,1536]{1,0:T(8,128)(2,1)S(1)}, bf16[80,1536]{1,0:T(8,128)(2,1)S(1)}, u32[]{:S(2)}, u32[]{:S(2)}) %collective-permute-start.5) | collective-permute-done | bytes 245792 | tf_op jit(solution)/shard_map/ppermute | solution.py:217
  32.9 4.1 %collective-permute-done.7.refs_3_ = bf16[80,1536]{1,0:T(8,128)(2,1)S(1)} collective-permute-done((bf16[80,1536]{1,0:T(8,128)(2,1)S(1)}, bf16[80,1536]{1,0:T(8,128)(2,1)S(1)}, u32[]{:S(2)}, u32[]{:S(2)}) %collective-permute-start.7) | collective-permute-done | bytes 245792 | tf_op jit(solution)/shard_map/ppermute | solution.py:217
  37.0 1.4 %collective-permute-start.15 = (bf16[2,384,384]{2,1,0:T(8,128)(2,1)S(1)}, bf16[2,384,384]{2,1,0:T(8,128)(2,1)S(1)}, u32[]{:S(2)}, u32[]{:S(2)}) collective-permute-start(bf16[2,384,384]{2,1,0:T(8,128)(2,1)S(1)} %get-tuple-element.89), channel_id=1, source_target_pairs={{0,2},{2,0},{4,6},{6,4},{8,10},{10,8},{12,14},{14,12},{1,3},{3,1},... | collective-permute-start | bytes 1769480 | tf_op jit(solution)/shard_map/ppermute | solution.py:217
  39.6 2.0 %shard_map.151 = (f32[256,384]{1,0:T(8,128)S(1)}, bf16[272,384]{1,0:T(8,128)(2,1)S(1)}, f32[8,256]{1,0:T(8,128)S(1)}, f32[256,384]{1,0:T(8,128)S(1)}) custom-call(s32[8]{0:T(128)S(1)} %copy-done.9, bf16[80,1536]{1,0:T(8,128)(2,1)S(1)} %get-tuple-element.65.refs_0_, bf16[80,1536]{1,0:T(8,128)(2,1)S(1)} %collective-permute-done.5.refs_1_, ...), custom_call_target="tpu_custom_call" | custom-call | flops 603979776 | bytes 3538976 | tf_op jit(solution)/shard_map/pallas_call | solution.py:233
  42.1 8.8 %collective-permute-done.13.refs_7_.refs_2_ = bf16[384,384]{1,0:T(8,128)(2,1)S(1)} collective-permute-done((bf16[384,384]{1,0:T(8,128)(2,1)S(1)}, bf16[384,384]{1,0:T(8,128)(2,1)S(1)}, u32[]{:S(2)}, u32[]{:S(2)}) %collective-permute-start.13) | collective-permute-done | bytes 294944 | tf_op jit(solution)/shard_map/ppermute | solution.py:217
  50.9 6.5 %collective-permute-done.14.refs_8_.refs_3_ = bf16[384,384]{1,0:T(8,128)(2,1)S(1)} collective-permute-done((bf16[384,384]{1,0:T(8,128)(2,1)S(1)}, bf16[384,384]{1,0:T(8,128)(2,1)S(1)}, u32[]{:S(2)}, u32[]{:S(2)}) %collective-permute-start.14) | collective-permute-done | bytes 294944 | tf_op jit(solution)/shard_map/ppermute | solution.py:217
  57.4 2.0 %collective-permute-start.19 = (bf16[384,384]{1,0:T(8,128)(2,1)S(1)}, bf16[384,384]{1,0:T(8,128)(2,1)S(1)}, u32[]{:S(2)}, u32[]{:S(2)}) collective-permute-start(bf16[384,384]{1,0:T(8,128)(2,1)S(1)} %collective-permute-done.13.refs_7_.refs_2_), channel_id=1, source_target_pairs={{0,16},{16,0},{1,17},{17,1},{2,18},{18,2},{3,19},{19,3},{4,20},{20... | collective-permute-start | bytes 884744 | tf_op jit(solution)/shard_map/ppermute | solution.py:418
  60.4 1.7 %collective-permute-start.17 = (bf16[256,384]{1,0:T(8,128)(2,1)S(1)}, bf16[256,384]{1,0:T(8,128)(2,1)S(1)}, u32[]{:S(2)}, u32[]{:S(2)}) collective-permute-start(bf16[256,384]{1,0:T(8,128)(2,1)S(1)} %get-tuple-element.99.refs_0_), channel_id=1, source_target_pairs={{0,4},{2,6},{4,0},{6,2},{8,12},{10,14},{12,8},{14,10},{1,5},{3,7},... | collective-permute-start | bytes 589832 | tf_op jit(solution)/shard_map/ppermute | solution.py:217
  63.1 3.6 %collective-permute-done.18.refs_3_ = bf16[256,384]{1,0:T(8,128)(2,1)S(1)} collective-permute-done((bf16[256,384]{1,0:T(8,128)(2,1)S(1)}, bf16[256,384]{1,0:T(8,128)(2,1)S(1)}, u32[]{:S(2)}, u32[]{:S(2)}) %collective-permute-start.18) | collective-permute-done | bytes 196640 | tf_op jit(solution)/shard_map/ppermute | solution.py:217
  66.7 2.6 %collective-permute-done.17.refs_2_ = bf16[256,384]{1,0:T(8,128)(2,1)S(1)} collective-permute-done((bf16[256,384]{1,0:T(8,128)(2,1)S(1)}, bf16[256,384]{1,0:T(8,128)(2,1)S(1)}, u32[]{:S(2)}, u32[]{:S(2)}) %collective-permute-start.17) | collective-permute-done | bytes 196640 | tf_op jit(solution)/shard_map/ppermute | solution.py:217
  69.2 2.5 %collective-permute-done.16.refs_1_ = bf16[256,384]{1,0:T(8,128)(2,1)S(1)} collective-permute-done((bf16[256,384]{1,0:T(8,128)(2,1)S(1)}, bf16[256,384]{1,0:T(8,128)(2,1)S(1)}, u32[]{:S(2)}, u32[]{:S(2)}) %collective-permute-start.16) | collective-permute-done | bytes 196640 | tf_op jit(solution)/shard_map/ppermute | solution.py:217
  72.3 1.3 %shard_map.154 = (f32[256,384]{1,0:T(8,128)S(1)}, bf16[272,384]{1,0:T(8,128)(2,1)S(1)}, f32[8,256]{1,0:T(8,128)S(1)}, bf16[2,256,1536]{2,1,0:T(8,128)(2,1)S(1)}) custom-call(bf16[256,384]{1,0:T(8,128)(2,1)S(1)} %get-tuple-element.99.refs_0_, bf16[256,384]{1,0:T(8,128)(2,1)S(1)} %collective-permute-done.16.refs_1_, ...), custom_call_target="tpu_custom_call" | custom-call | flops 603979776 | bytes 3342336 | tf_op jit(solution)/shard_map/pallas_call | solution.py:233
  73.9 1.4 %collective-permute-start.26 = (bf16[8,384,384]{2,1,0:T(8,128)(2,1)S(1)}, bf16[8,384,384]{2,1,0:T(8,128)(2,1)S(1)}, u32[]{:S(2)}, u32[]{:S(2)}) collective-permute-start(bf16[8,384,384]{2,1,0:T(8,128)(2,1)S(1)} %shard_map.156), channel_id=1, source_target_pairs={{0,1},{1,0},{2,3},{3,2},{4,5},{5,4},{6,7},{7,6},{8,9},{9,8},{10,11... | collective-permute-start | bytes 7077896 | tf_op jit(solution)/shard_map/ppermute | solution.py:223
  75.9 3.9 %collective-permute-start.22 = (bf16[256,384]{1,0:T(8,128)(2,1)S(1)}, bf16[256,384]{1,0:T(8,128)(2,1)S(1)}, u32[]{:S(2)}, u32[]{:S(2)}) collective-permute-start(bf16[256,384]{1,0:T(8,128)(2,1)S(1)} %get-tuple-element.99.refs_0_), channel_id=1, source_target_pairs={{0,0},{1,8},{2,2},{3,10},{4,4},{5,12},{6,6},{7,14},{8,1},{9,9},{10... | collective-permute-start | bytes 589832 | tf_op jit(solution)/shard_map/ppermute | solution.py:226
  81.2 15.2 %collective-permute-done.22.owned = bf16[256,384]{1,0:T(8,128)(2,1)S(1)} collective-permute-done((bf16[256,384]{1,0:T(8,128)(2,1)S(1)}, bf16[256,384]{1,0:T(8,128)(2,1)S(1)}, u32[]{:S(2)}, u32[]{:S(2)}) %collective-permute-start.22) | collective-permute-done | bytes 196640 | tf_op jit(solution)/shard_map/ppermute | solution.py:226
  96.4 1.5 %shard_map.155 = (bf16[128,384]{1,0:T(8,128)(2,1)S(1)}, bf16[128,384]{1,0:T(8,128)(2,1)S(1)}, bf16[128,384]{1,0:T(8,128)(2,1)S(1)}, bf16[128,384]{1,0:T(8,128)(2...) custom-call(s32[8]{0:T(128)S(1)} %copy-done.9, f32[256,384]{1,0:T(8,128)S(1)} %get-tuple-element.95.gap, ...), custom_call_target="tpu_custom_call" | custom-call | flops 301989888 | bytes 3297312 | tf_op jit(solution)/shard_map/pallas_call | solution.py:233
  99.0 1.7 %collective-permute-start.25 = (bf16[128,384]{1,0:T(8,128)(2,1)S(1)}, bf16[128,384]{1,0:T(8,128)(2,1)S(1)}, u32[]{:S(2)}, u32[]{:S(2)}) collective-permute-start(bf16[128,384]{1,0:T(8,128)(2,1)S(1)} %get-tuple-element.103), channel_id=1, source_target_pairs={{0,6},{2,4},{4,2},{6,0},{8,14},{10,12},{12,10},{14,8},{1,7},{3,5},... | collective-permute-start | bytes 294920 | tf_op jit(solution)/shard_map/ppermute | solution.py:217
  100.7 1.3 %shard_map.158 = (bf16[80,384]{1,0:T(8,128)(2,1)S(1)}, bf16[80,384]{1,0:T(8,128)(2,1)S(1)}, bf16[80,384]{1,0:T(8,128)(2,1)S(1)}, bf16[80,384]{1,0:T(8,128)(2,1)S(1)}) custom-call(s32[8]{0:T(128)S(1)} %copy-done.9, f32[256,384]{1,0:T(8,128)S(1)} %get-tuple-element.111.gap, bf16[256,384]{1,0:T(8,128)(2,1)S(1)} %collective-permute-done.27.came, ...), custom_call_target="tpu_custom_call" | custom-call | flops 301989888 | bytes 3223584 | tf_op jit(solution)/shard_map/pallas_call | solution.py:233
  103.0 1.7 %collective-permute-start.30 = (bf16[80,384]{1,0:T(8,128)(2,1)S(1)}, bf16[80,384]{1,0:T(8,128)(2,1)S(1)}, u32[]{:S(2)}, u32[]{:S(2)}) collective-permute-start(bf16[80,384]{1,0:T(8,128)(2,1)S(1)} %get-tuple-element.118), channel_id=1, source_target_pairs={{0,6},{2,4},{4,2},{6,0},{8,14},{10,12},{12,10},{14,8},{1,7},{3,5},... | collective-permute-start | bytes 184328 | tf_op jit(solution)/shard_map/ppermute | solution.py:217
  105.5 1.5 %collective-permute-done.29.refs_6_ = bf16[80,384]{1,0:T(8,128)(2,1)S(1)} collective-permute-done((bf16[80,384]{1,0:T(8,128)(2,1)S(1)}, bf16[80,384]{1,0:T(8,128)(2,1)S(1)}, u32[]{:S(2)}, u32[]{:S(2)}) %collective-permute-start.29) | collective-permute-done | bytes 61472 | tf_op jit(solution)/shard_map/ppermute | solution.py:217
  108.4 1.5 %collective-permute-done.31.came = bf16[80,1536]{1,0:T(8,128)(2,1)S(1)} collective-permute-done((bf16[80,1536]{1,0:T(8,128)(2,1)S(1)}, bf16[80,1536]{1,0:T(8,128)(2,1)S(1)}, u32[]{:S(2)}, u32[]{:S(2)}) %collective-permute-start.31) | collective-permute-done | bytes 245792 | tf_op jit(solution)/shard_map/ppermute | solution.py:223
  (78 shorter events, 26.2 us)
Async XLA Ops:
  0.6 17.9 %collective-permute-start = (bf16[64,1536]{1,0:T(8,128)(2,1)}, bf16[64,1536]{1,0:T(8,128)(2,1)S(1)}, u32[]{:S(2)}, u32[]{:S(2)}) collective-permute-start(bf16[64,1536]{1,0:T(8,128)(2,1)} %param.13), channel_id=1, source_target_pairs={{0,0},{1,8},{2,2},{3,10},{4,4},{5,12},{6,6},{7,14},{8,1},{9,9},{10... | collective-permute-start | bytes 589832 | tf_op jit(solution)/shard_map/ppermute | solution.py:226
  6.2 12.3 %collective-permute-start.1 = (bf16[64,1536]{1,0:T(8,128)(2,1)}, bf16[64,1536]{1,0:T(8,128)(2,1)S(1)}, u32[]{:S(2)}, u32[]{:S(2)}) collective-permute-start(bf16[64,1536]{1,0:T(8,128)(2,1)} %param.14), channel_id=1, source_target_pairs={{0,0},{1,8},{2,2},{3,10},{4,4},{5,12},{6,6},{7,14},{8,1},{9,9},{10... | collective-permute-start | bytes 589832 | tf_op jit(solution)/shard_map/ppermute | solution.py:226
  9.6 11.6 %collective-permute-start.2 = (bf16[384,384]{1,0:T(8,128)(2,1)S(1)}, bf16[384,384]{1,0:T(8,128)(2,1)S(1)}, u32[]{:S(2)}, u32[]{:S(2)}) collective-permute-start(bf16[384,384]{1,0:T(8,128)(2,1)S(1)} %get-tuple-element.67), channel_id=1, source_target_pairs={{0,2},{2,0},{4,6},{6,4},{8,10},{10,8},{12,14},{14,12},{1,3},{3,1},... | collective-permute-start | bytes 884744 | tf_op jit(solution)/shard_map/ppermute | solution.py:217
  10.9 10.5 %collective-permute-start.3 = (bf16[384,384]{1,0:T(8,128)(2,1)S(1)}, bf16[384,384]{1,0:T(8,128)(2,1)S(1)}, u32[]{:S(2)}, u32[]{:S(2)}) collective-permute-start(bf16[384,384]{1,0:T(8,128)(2,1)S(1)} %get-tuple-element.68), channel_id=1, source_target_pairs={{0,4},{2,6},{4,0},{6,2},{8,12},{10,14},{12,8},{14,10},{1,5},{3,7},... | collective-permute-start | bytes 884744 | tf_op jit(solution)/shard_map/ppermute | solution.py:217
  12.2 15.9 %collective-permute-start.4 = (bf16[384,384]{1,0:T(8,128)(2,1)S(1)}, bf16[384,384]{1,0:T(8,128)(2,1)S(1)}, u32[]{:S(2)}, u32[]{:S(2)}) collective-permute-start(bf16[384,384]{1,0:T(8,128)(2,1)S(1)} %get-tuple-element.69), channel_id=1, source_target_pairs={{0,6},{2,4},{4,2},{6,0},{8,14},{10,12},{12,10},{14,8},{1,7},{3,5},... | collective-permute-start | bytes 884744 | tf_op jit(solution)/shard_map/ppermute | solution.py:217
  18.6 12.3 %collective-permute-start.5 = (bf16[80,1536]{1,0:T(8,128)(2,1)S(1)}, bf16[80,1536]{1,0:T(8,128)(2,1)S(1)}, u32[]{:S(2)}, u32[]{:S(2)}) collective-permute-start(bf16[80,1536]{1,0:T(8,128)(2,1)S(1)} %get-tuple-element.70), channel_id=1, source_target_pairs={{0,2},{2,0},{4,6},{6,4},{8,10},{10,8},{12,14},{14,12},{1,3},{3,1},... | collective-permute-start | bytes 737288 | tf_op jit(solution)/shard_map/ppermute | solution.py:217
  19.9 12.8 %collective-permute-start.6 = (bf16[80,1536]{1,0:T(8,128)(2,1)S(1)}, bf16[80,1536]{1,0:T(8,128)(2,1)S(1)}, u32[]{:S(2)}, u32[]{:S(2)}) collective-permute-start(bf16[80,1536]{1,0:T(8,128)(2,1)S(1)} %get-tuple-element.72), channel_id=1, source_target_pairs={{0,4},{2,6},{4,0},{6,2},{8,12},{10,14},{12,8},{14,10},{1,5},{3,7},... | collective-permute-start | bytes 737288 | tf_op jit(solution)/shard_map/ppermute | solution.py:217
  21.2 15.8 %collective-permute-start.7 = (bf16[80,1536]{1,0:T(8,128)(2,1)S(1)}, bf16[80,1536]{1,0:T(8,128)(2,1)S(1)}, u32[]{:S(2)}, u32[]{:S(2)}) collective-permute-start(bf16[80,1536]{1,0:T(8,128)(2,1)S(1)} %get-tuple-element.73), channel_id=1, source_target_pairs={{0,6},{2,4},{4,2},{6,0},{8,14},{10,12},{12,10},{14,8},{1,7},{3,5},... | collective-permute-start | bytes 737288 | tf_op jit(solution)/shard_map/ppermute | solution.py:217
  30.9 7.5 %collective-permute-start.8 = (bf16[384,384]{1,0:T(8,128)(2,1)S(1)}, bf16[384,384]{1,0:T(8,128)(2,1)S(1)}, u32[]{:S(2)}, u32[]{:S(2)}) collective-permute-start(bf16[384,384]{1,0:T(8,128)(2,1)S(1)} %get-tuple-element.75.refs_5_.refs_4_), channel_id=1, source_target_pairs={{0,1},{1,0},{2,3},{3,2},{4,5},{5,4},{6,7},{7,6},{8,9},{9,8},{10,11... | collective-permute-start | bytes 884744 | tf_op jit(solution)/shard_map/ppermute | solution.py:223
  30.9 7.5 %collective-permute-start.9 = (bf16[384,384]{1,0:T(8,128)(2,1)S(1)}, bf16[384,384]{1,0:T(8,128)(2,1)S(1)}, u32[]{:S(2)}, u32[]{:S(2)}) collective-permute-start(bf16[384,384]{1,0:T(8,128)(2,1)S(1)} %collective-permute-done.2.refs_6_.refs_5_), channel_id=1, source_target_pairs={{0,1},{1,0},{2,3},{3,2},{4,5},{5,4},{6,7},{7,6},{8,9},{9,8},{10,11... | collective-permute-start | bytes 884744 | tf_op jit(solution)/shard_map/ppermute | solution.py:223
  31.4 8.2 %collective-permute-start.10 = (bf16[384,384]{1,0:T(8,128)(2,1)S(1)}, bf16[384,384]{1,0:T(8,128)(2,1)S(1)}, u32[]{:S(2)}, u32[]{:S(2)}) collective-permute-start(bf16[384,384]{1,0:T(8,128)(2,1)S(1)} %collective-permute-done.3.refs_7_.refs_6_), channel_id=1, source_target_pairs={{0,1},{1,0},{2,3},{3,2},{4,5},{5,4},{6,7},{7,6},{8,9},{9,8},{10,11... | collective-permute-start | bytes 884744 | tf_op jit(solution)/shard_map/ppermute | solution.py:223
  32.7 6.9 %collective-permute-start.11 = (bf16[384,384]{1,0:T(8,128)(2,1)S(1)}, bf16[384,384]{1,0:T(8,128)(2,1)S(1)}, u32[]{:S(2)}, u32[]{:S(2)}) collective-permute-start(bf16[384,384]{1,0:T(8,128)(2,1)S(1)} %collective-permute-done.4.refs_8_.refs_7_), channel_id=1, source_target_pairs={{0,1},{1,0},{2,3},{3,2},{4,5},{5,4},{6,7},{7,6},{8,9},{9,8},{10,11... | collective-permute-start | bytes 884744 | tf_op jit(solution)/shard_map/ppermute | solution.py:223
  37.0 25.1 %collective-permute-start.15 = (bf16[2,384,384]{2,1,0:T(8,128)(2,1)S(1)}, bf16[2,384,384]{2,1,0:T(8,128)(2,1)S(1)}, u32[]{:S(2)}, u32[]{:S(2)}) collective-permute-start(bf16[2,384,384]{2,1,0:T(8,128)(2,1)S(1)} %get-tuple-element.89), channel_id=1, source_target_pairs={{0,2},{2,0},{4,6},{6,4},{8,10},{10,8},{12,14},{14,12},{1,3},{3,1},... | collective-permute-start | bytes 1769480 | tf_op jit(solution)/shard_map/ppermute | solution.py:217
  38.4 12.5 %collective-permute-start.13 = (bf16[384,384]{1,0:T(8,128)(2,1)S(1)}, bf16[384,384]{1,0:T(8,128)(2,1)S(1)}, u32[]{:S(2)}, u32[]{:S(2)}) collective-permute-start(bf16[384,384]{1,0:T(8,128)(2,1)S(1)} %get-tuple-element.83), channel_id=1, source_target_pairs={{0,4},{2,6},{4,0},{6,2},{8,12},{10,14},{12,8},{14,10},{1,5},{3,7},... | collective-permute-start | bytes 884744 | tf_op jit(solution)/shard_map/ppermute | solution.py:217
  38.4 19.0 %collective-permute-start.14 = (bf16[384,384]{1,0:T(8,128)(2,1)S(1)}, bf16[384,384]{1,0:T(8,128)(2,1)S(1)}, u32[]{:S(2)}, u32[]{:S(2)}) collective-permute-start(bf16[384,384]{1,0:T(8,128)(2,1)S(1)} %get-tuple-element.84), channel_id=1, source_target_pairs={{0,6},{2,4},{4,2},{6,0},{8,14},{10,12},{12,10},{14,8},{1,7},{3,5},... | collective-permute-start | bytes 884744 | tf_op jit(solution)/shard_map/ppermute | solution.py:217
  41.6 15.8 %collective-permute-start.12 = (bf16[272,384]{1,0:T(8,128)(2,1)S(1)}, bf16[272,384]{1,0:T(8,128)(2,1)S(1)}, u32[]{:S(2)}, u32[]{:S(2)}) collective-permute-start(bf16[272,384]{1,0:T(8,128)(2,1)S(1)} %get-tuple-element.80), channel_id=1, source_target_pairs={{0,8},{2,10},{4,12},{6,14},{8,0},{10,2},{12,4},{14,6},{1,9},{3,11}... | collective-permute-start | bytes 626696 | tf_op jit(solution)/shard_map/ppermute | solution.py:220
  57.4 14.4 %collective-permute-start.19 = (bf16[384,384]{1,0:T(8,128)(2,1)S(1)}, bf16[384,384]{1,0:T(8,128)(2,1)S(1)}, u32[]{:S(2)}, u32[]{:S(2)}) collective-permute-start(bf16[384,384]{1,0:T(8,128)(2,1)S(1)} %collective-permute-done.13.refs_7_.refs_2_), channel_id=1, source_target_pairs={{0,16},{16,0},{1,17},{17,1},{2,18},{18,2},{3,19},{19,3},{4,20},{20... | collective-permute-start | bytes 884744 | tf_op jit(solution)/shard_map/ppermute | solution.py:418
  59.4 12.9 %collective-permute-start.20 = (bf16[384,384]{1,0:T(8,128)(2,1)S(1)}, bf16[384,384]{1,0:T(8,128)(2,1)S(1)}, u32[]{:S(2)}, u32[]{:S(2)}) collective-permute-start(bf16[384,384]{1,0:T(8,128)(2,1)S(1)} %collective-permute-done.14.refs_8_.refs_3_), channel_id=1, source_target_pairs={{0,16},{16,0},{1,17},{17,1},{2,18},{18,2},{3,19},{19,3},{4,20},{20... | collective-permute-start | bytes 884744 | tf_op jit(solution)/shard_map/ppermute | solution.py:418
  60.3 6.3 %collective-permute-start.18 = (bf16[256,384]{1,0:T(8,128)(2,1)S(1)}, bf16[256,384]{1,0:T(8,128)(2,1)S(1)}, u32[]{:S(2)}, u32[]{:S(2)}) collective-permute-start(bf16[256,384]{1,0:T(8,128)(2,1)S(1)} %get-tuple-element.99.refs_0_), channel_id=1, source_target_pairs={{0,6},{2,4},{4,2},{6,0},{8,14},{10,12},{12,10},{14,8},{1,7},{3,5},... | collective-permute-start | bytes 589832 | tf_op jit(solution)/shard_map/ppermute | solution.py:217
  60.4 8.8 %collective-permute-start.17 = (bf16[256,384]{1,0:T(8,128)(2,1)S(1)}, bf16[256,384]{1,0:T(8,128)(2,1)S(1)}, u32[]{:S(2)}, u32[]{:S(2)}) collective-permute-start(bf16[256,384]{1,0:T(8,128)(2,1)S(1)} %get-tuple-element.99.refs_0_), channel_id=1, source_target_pairs={{0,4},{2,6},{4,0},{6,2},{8,12},{10,14},{12,8},{14,10},{1,5},{3,7},... | collective-permute-start | bytes 589832 | tf_op jit(solution)/shard_map/ppermute | solution.py:217
  62.1 9.7 %collective-permute-start.16 = (bf16[256,384]{1,0:T(8,128)(2,1)S(1)}, bf16[256,384]{1,0:T(8,128)(2,1)S(1)}, u32[]{:S(2)}, u32[]{:S(2)}) collective-permute-start(bf16[256,384]{1,0:T(8,128)(2,1)S(1)} %get-tuple-element.99.refs_0_), channel_id=1, source_target_pairs={{0,2},{2,0},{4,6},{6,4},{8,10},{10,8},{12,14},{14,12},{1,3},{3,1},... | collective-permute-start | bytes 589832 | tf_op jit(solution)/shard_map/ppermute | solution.py:217
  75.3 21.1 %collective-permute-start.21 = (bf16[272,384]{1,0:T(8,128)(2,1)S(1)}, bf16[272,384]{1,0:T(8,128)(2,1)S(1)}, u32[]{:S(2)}, u32[]{:S(2)}) collective-permute-start(bf16[272,384]{1,0:T(8,128)(2,1)S(1)} %get-tuple-element.96), channel_id=1, source_target_pairs={{0,8},{2,10},{4,12},{6,14},{8,0},{10,2},{12,4},{14,6},{1,9},{3,11}... | collective-permute-start | bytes 626696 | tf_op jit(solution)/shard_map/ppermute | solution.py:220
  75.9 20.6 %collective-permute-start.22 = (bf16[256,384]{1,0:T(8,128)(2,1)S(1)}, bf16[256,384]{1,0:T(8,128)(2,1)S(1)}, u32[]{:S(2)}, u32[]{:S(2)}) collective-permute-start(bf16[256,384]{1,0:T(8,128)(2,1)S(1)} %get-tuple-element.99.refs_0_), channel_id=1, source_target_pairs={{0,0},{1,8},{2,2},{3,10},{4,4},{5,12},{6,6},{7,14},{8,1},{9,9},{10... | collective-permute-start | bytes 589832 | tf_op jit(solution)/shard_map/ppermute | solution.py:226
  80.9 19.8 %collective-permute-start.27 = (bf16[256,384]{1,0:T(8,128)(2,1)S(1)}, bf16[256,384]{1,0:T(8,128)(2,1)S(1)}, u32[]{:S(2)}, u32[]{:S(2)}) collective-permute-start(bf16[256,384]{1,0:T(8,128)(2,1)S(1)} %get-tuple-element.112), channel_id=1, source_target_pairs={{0,8},{2,10},{4,12},{6,14},{8,0},{10,2},{12,4},{14,6},{1,9},{3,11}... | collective-permute-start | bytes 589832 | tf_op jit(solution)/shard_map/ppermute | solution.py:220
  (18 other events, 113.6 us)

commit v7 on v6

--- a/solution.py
+++ b/solution.py
@@ -268,43 +268,74 @@
     def lanes(k):
         return pl.ds(pl.multiple_of(k * w, w), w)
 
-    def scales_kernel(features, gen_e, real_e, fake_e, gen_g, real_g, fake_g, out):
+    def scales_kernel(features, *refs):
+        sources, out, held, sems = refs[:6], refs[6], refs[7:13], refs[13]
         s, _, _ = place()
         mine = pl.ds(pl.multiple_of(s * h, h), h)
         per = h // 128
+        copies = [
+            pltpu.make_async_copy(source.at[:, mine] if n < 3 else source, here, sems.at[n])
+            for n, (source, here) in enumerate(zip(sources, held))
+        ]
+        for copy in copies:
+            copy.start()
+        for copy in copies:
+            copy.wait()
 
         def gain(ref):
             return jnp.concatenate([ref[pl.ds(s * per + i, 1), :] for i in range(per)], axis=1)
 
-        for n, (embed, gains) in enumerate(((gen_e, gen_g), (real_e, real_g), (fake_e, fake_g))):
-            part = 0 if n == 0 else 1
-            mod = 1.0 + jnp.dot(
-                features[part], embed[:, mine], preferred_element_type=f32
-            )
+        for n in range(3):
+            steps = slice(0, blocks) if n == 0 else slice(blocks, 2 * blocks)
+            mod = 1.0 + jnp.dot(features[steps, :], held[n][...], preferred_element_type=f32)
             if n == 0:
                 out[3] = mod
-            scale = mod * gain(gains)
+            scale = mod * gain(held[3 + n])
             out[n] = -scale if n == 2 else scale
 
-    features = jnp.stack(
-        [step_features(gen_step, gen_embed.shape[0]), step_features(noise_step, gen_embed.shape[0])]
-    )
-    (scales,) = call(
+    gains = [v.reshape(-1, 128) for v in (gen_gain, real_gain, fake_gain)]
+    scales = pl.pallas_call(
         scales_kernel,
-        [features, gen_embed, real_embed, fake_embed]
-        + [v.reshape(-1, 128) for v in (gen_gain, real_gain, fake_gain)],
-        [((4, blocks, h), f32)],
-        2 * 3 * blocks * 128 * h,
+        in_specs=[whole] + [pl.BlockSpec(memory_space=pltpu.HBM)] * 6,
+        out_specs=whole,
+        out_shape=jax.ShapeDtypeStruct((4, blocks, h), f32),
+        scratch_shapes=[pltpu.VMEM((gen_embed.shape[0], h), bf16)] * 3
+        + [pltpu.VMEM(v.shape, f32) for v in gains]
+        + [pltpu.SemaphoreType.DMA((6,))],
+        compiler_params=pltpu.CompilerParams(vmem_limit_bytes=40 * 1024 * 1024),
+        cost_estimate=pl.CostEstimate(flops=6 * blocks * 128 * h, bytes_accessed=6 * 128 * h, transcendentals=0),
+    )(
+        step_features(jnp.concatenate([gen_step, noise_step]), gen_embed.shape[0]),
+        gen_embed,
+        real_embed,
+        fake_embed,
+        *gains,
     )
 
     depth = gen_weight.shape[0]
     fold = r // g
     shared = g // 2
 
+    part_rows = depth // 2
+
+    def rows_half(n):
+        return pl.ds(pl.multiple_of(n * part_rows, 16), part_rows)
+
     def cut_gen_kernel(weight, *outs):
         _, q, _ = place()
-        for k in span:
-            outs[k][...] = weight[:, lanes(q ^ k)]
+        copy = lax.axis_index("rep")
+        for k in span:
+            if k < shared:
+                outs[k][...] = weight[:, lanes(q ^ k)]
+            else:
+                outs[k][...] = weight[rows_half(copy), lanes(q ^ k)]
+
+    def join_gen_kernel(*refs):
+        copy = lax.axis_index("rep")
+        n = g - shared
+        for fetched, given, out in zip(refs[:n], refs[n : 2 * n], refs[2 * n :]):
+            out[rows_half(copy), :] = fetched[...]
+            out[rows_half(1 - copy), :] = given[...]
 
     def cut_score_kernel(real, fake, *outs):
         _, q, _ = place()
@@ -340,12 +371,14 @@
         return cores(joined)
 
     x_turned, fresh_turned = turned(noise_in), turned(renoise)
-    gen_sent = call(cut_gen_kernel, [gen_weight], [((depth, w), bf16)] * g, depth * h)
+    gen_sent = call(cut_gen_kernel, [gen_weight], [((depth, w), bf16)] * shared + [((part_rows, w), bf16)] * (g - shared), depth * h)
     gen_mine = [gen_sent[0]] + [in_square(gen_sent[k], k) for k in range(1, g)]
-    x_turned, scales = lax.optimization_barrier((x_turned, scales))
+    fetched = gen_mine[shared:]
+    given = [lax.ppermute(v, "rep", [(0, 1), (1, 0)]) for v in fetched]
+    gen_mine[shared:] = call(join_gen_kernel, fetched + given, [((depth, w), bf16)] * (g - shared), depth * w)
     x_sent = call(cut_rows_kernel, [x_turned, fresh_turned], [((r + fold, h), bf16)] * g, r * h)
     x = [x_sent[0]] + [in_square(x_sent[k], k) for k in range(1, g)]
-    gen_swap, x[1] = lax.optimization_barrier((gen_mine, x[1]))
+    gen_swap, x[1], scales = lax.optimization_barrier((gen_mine, x[1], scales))
     gen_other = [cores(v) for v in gen_swap]
     real_weight, fake_weight, _ = lax.optimization_barrier((real_weight, fake_weight, x_turned))
     score_sent = call(

time: 111 us -> 108 us (0.973)
  starting transfers between devices: 33 us -> 39.2 us
  waiting for transfers between devices: 59.2 us -> 53.8 us
  local copies, waits for them, and re-layouts: 5.67 us -> 2.42 us
    ppermute x18, waiting for transfers between devices: 41.8 us -> 34.9 us  [in_square(): return lax.ppermute(value, 'fsdp', [(i, i ^ k) for i in range(2 * g)])]
    unnamed x20, local copies, waits for them, and re-layouts: 5.67 us -> 2.42 us
    ppermute x0 -> x2, starting transfers between devices: none -> 2.48 us  [on_tiles(): given = [lax.ppermute(v, 'rep', [(0, 1), (1, 0)]) for v in fetched]]
    ppermute x3, starting transfers between devices: 1.35 us -> 3.63 us  [across(): return lax.ppermute(value, 'fsdp', [(i, i ^ g) for i in range(2 * g)])]
    ppermute x6, starting transfers between devices: 1.95 us -> 3.92 us  [cores(): return lax.ppermute(value, 'mp', [(0, 1), (1, 0)])]
    ppermute x3, waiting for transfers between devices: 15.2 us -> 17 us  [turned(): lax.ppermute(value, ('fsdp', 'mp'), [(flat(*i), flat(i[2], i[1], i[0])) f...]
    ppermute x18, starting transfers between devices: 16.2 us -> 17.4 us  [in_square(): return lax.ppermute(value, 'fsdp', [(i, i ^ k) for i in range(2 * g)])]
    ppermute x3, starting transfers between devices: 11.4 us -> 10.3 us  [turned(): lax.ppermute(value, ('fsdp', 'mp'), [(flat(*i), flat(i[2], i[1], i[0])) f...]
  transfers between devices with their start and end apart: 32 -> 34, of which waited for: 15 -> 16; matrix products, arithmetic and copies ran while one was open for 1% -> 1% of each run, Pallas kernels for 7% -> 7%
where the time goes in v7:
time: 108 us
  waiting for transfers between devices  53.8 us (50%)
  starting transfers between devices  39.2 us (36%)
  Pallas kernels  10.7 us (10%)
  local copies, waits for them, and re-layouts  2.42 us (2%)
    ppermute x18, waiting for transfers between devices, in_square(): return lax.ppermute(value, 'fsdp', [(i, i ^ k) for i in range(2 * g)])  34.9 us
    ppermute x18, starting transfers between devices, in_square(): return lax.ppermute(value, 'fsdp', [(i, i ^ k) for i in range(2 * g)])  17.4 us
    ppermute x3, waiting for transfers between devices, turned(): lax.ppermute(value, ('fsdp', 'mp'), [(flat(*i), flat(i[2], i[1], i[0])) f...  17 us
    ppermute x3, starting transfers between devices, turned(): lax.ppermute(value, ('fsdp', 'mp'), [(flat(*i), flat(i[2], i[1], i[0])) f...  10.3 us
    pallas_call x13, Pallas kernels, call(): pl.pallas_call(kernel, in_specs=[scalars] * in_scalars + [whole] * (len(o...  10.2 us
    ppermute x6, starting transfers between devices, cores(): return lax.ppermute(value, 'mp', [(0, 1), (1, 0)])  3.92 us
    ppermute x3, starting transfers between devices, across(): return lax.ppermute(value, 'fsdp', [(i, i ^ g) for i in range(2 * g)])  3.63 us
    ppermute x2, starting transfers between devices, on_tiles(): given = [lax.ppermute(v, 'rep', [(0, 1), (1, 0)]) for v in fetched]  2.48 us
  transfers between devices with their start and end apart: 34, of which 16 were waited for; matrix products, arithmetic and copies ran while one was open for 1% of the time, Pallas kernels for 7%

profile of v7, /device:TPU:1, one launch (start us, length us, event | category | flops | bytes accessed | tf_op | source)
XLA Modules:
  0.0 107.9 jit_solution(4037844215184827278)
XLA Ops:
  2.0 2.2 %collective-permute-start.3 = (bf16[192,384]{1,0:T(8,128)(2,1)S(1)}, bf16[192,384]{1,0:T(8,128)(2,1)S(1)}, u32[]{:S(2)}, u32[]{:S(2)}) collective-permute-start(bf16[192,384]{1,0:T(8,128)(2,1)S(1)} %get-tuple-element.68), channel_id=1, source_target_pairs={{0,4},{2,6},{4,0},{6,2},{8,12},{10,14},{12,8},{14,10},{1,5},{3,7},... | collective-permute-start | bytes 442376 | tf_op jit(solution)/shard_map/ppermute | solution.py:217
  4.2 5.0 %collective-permute-start = (bf16[64,1536]{1,0:T(8,128)(2,1)}, bf16[64,1536]{1,0:T(8,128)(2,1)S(1)}, u32[]{:S(2)}, u32[]{:S(2)}) collective-permute-start(bf16[64,1536]{1,0:T(8,128)(2,1)} %param.13), channel_id=1, source_target_pairs={{0,0},{1,8},{2,2},{3,10},{4,4},{5,12},{6,6},{7,14},{8,1},{9,9},{10... | collective-permute-start | bytes 589832 | tf_op jit(solution)/shard_map/ppermute | solution.py:226
  9.3 1.9 %collective-permute-start.1 = (bf16[64,1536]{1,0:T(8,128)(2,1)}, bf16[64,1536]{1,0:T(8,128)(2,1)S(1)}, u32[]{:S(2)}, u32[]{:S(2)}) collective-permute-start(bf16[64,1536]{1,0:T(8,128)(2,1)} %param.14), channel_id=1, source_target_pairs={{0,0},{1,8},{2,2},{3,10},{4,4},{5,12},{6,6},{7,14},{8,1},{9,9},{10... | collective-permute-start | bytes 589832 | tf_op jit(solution)/shard_map/ppermute | solution.py:226
  14.6 2.9 %collective-permute-done.4.refs_1_ = bf16[192,384]{1,0:T(8,128)(2,1)S(1)} collective-permute-done((bf16[192,384]{1,0:T(8,128)(2,1)S(1)}, bf16[192,384]{1,0:T(8,128)(2,1)S(1)}, u32[]{:S(2)}, u32[]{:S(2)}) %collective-permute-start.4) | collective-permute-done | bytes 147488 | tf_op jit(solution)/shard_map/ppermute | solution.py:217
  24.3 2.9 %collective-permute-done.7.refs_1_ = bf16[80,1536]{1,0:T(8,128)(2,1)S(1)} collective-permute-done((bf16[80,1536]{1,0:T(8,128)(2,1)S(1)}, bf16[80,1536]{1,0:T(8,128)(2,1)S(1)}, u32[]{:S(2)}, u32[]{:S(2)}) %collective-permute-start.7) | collective-permute-done | bytes 245792 | tf_op jit(solution)/shard_map/ppermute | solution.py:217
  29.4 3.9 %collective-permute-done.9.refs_3_ = bf16[80,1536]{1,0:T(8,128)(2,1)S(1)} collective-permute-done((bf16[80,1536]{1,0:T(8,128)(2,1)S(1)}, bf16[80,1536]{1,0:T(8,128)(2,1)S(1)}, u32[]{:S(2)}, u32[]{:S(2)}) %collective-permute-start.9) | collective-permute-done | bytes 245792 | tf_op jit(solution)/shard_map/ppermute | solution.py:217
  33.3 1.7 %collective-permute-start.17 = (bf16[2,384,384]{2,1,0:T(8,128)(2,1)S(1)}, bf16[2,384,384]{2,1,0:T(8,128)(2,1)S(1)}, u32[]{:S(2)}, u32[]{:S(2)}) collective-permute-start(bf16[2,384,384]{2,1,0:T(8,128)(2,1)S(1)} %get-tuple-element.91), channel_id=1, source_target_pairs={{0,2},{2,0},{4,6},{6,4},{8,10},{10,8},{12,14},{14,12},{1,3},{3,1},... | collective-permute-start | bytes 1769480 | tf_op jit(solution)/shard_map/ppermute | solution.py:217
  36.2 2.0 %shard_map.152 = (f32[256,384]{1,0:T(8,128)S(1)}, bf16[272,384]{1,0:T(8,128)(2,1)S(1)}, f32[8,256]{1,0:T(8,128)S(1)}, f32[256,384]{1,0:T(8,128)S(1)}) custom-call(s32[8]{0:T(128)S(1)} %copy-done.9, bf16[80,1536]{1,0:T(8,128)(2,1)S(1)} %get-tuple-element.65.refs_0_, bf16[80,1536]{1,0:T(8,128)(2,1)S(1)} %collective-permute-done.7.refs_1_, ...), custom_call_target="tpu_custom_call" | custom-call | flops 603979776 | bytes 3538976 | tf_op jit(solution)/shard_map/pallas_call | solution.py:233
  38.2 1.6 %collective-permute-start.14 = (bf16[272,384]{1,0:T(8,128)(2,1)S(1)}, bf16[272,384]{1,0:T(8,128)(2,1)S(1)}, u32[]{:S(2)}, u32[]{:S(2)}) collective-permute-start(bf16[272,384]{1,0:T(8,128)(2,1)S(1)} %get-tuple-element.82), channel_id=1, source_target_pairs={{0,8},{2,10},{4,12},{6,14},{8,0},{10,2},{12,4},{14,6},{1,9},{3,11}... | collective-permute-start | bytes 626696 | tf_op jit(solution)/shard_map/ppermute | solution.py:220
  39.8 7.4 %collective-permute-done.15.refs_7_.refs_2_ = bf16[384,384]{1,0:T(8,128)(2,1)S(1)} collective-permute-done((bf16[384,384]{1,0:T(8,128)(2,1)S(1)}, bf16[384,384]{1,0:T(8,128)(2,1)S(1)}, u32[]{:S(2)}, u32[]{:S(2)}) %collective-permute-start.15) | collective-permute-done | bytes 294944 | tf_op jit(solution)/shard_map/ppermute | solution.py:217
  47.2 6.4 %collective-permute-done.16.refs_8_.refs_3_ = bf16[384,384]{1,0:T(8,128)(2,1)S(1)} collective-permute-done((bf16[384,384]{1,0:T(8,128)(2,1)S(1)}, bf16[384,384]{1,0:T(8,128)(2,1)S(1)}, u32[]{:S(2)}, u32[]{:S(2)}) %collective-permute-start.16) | collective-permute-done | bytes 294944 | tf_op jit(solution)/shard_map/ppermute | solution.py:217
  55.9 1.3 %collective-permute-start.20 = (bf16[256,384]{1,0:T(8,128)(2,1)S(1)}, bf16[256,384]{1,0:T(8,128)(2,1)S(1)}, u32[]{:S(2)}, u32[]{:S(2)}) collective-permute-start(bf16[256,384]{1,0:T(8,128)(2,1)S(1)} %get-tuple-element.101.refs_0_), channel_id=1, source_target_pairs={{0,6},{2,4},{4,2},{6,0},{8,14},{10,12},{12,10},{14,8},{1,7},{3,5},... | collective-permute-start | bytes 589832 | tf_op jit(solution)/shard_map/ppermute | solution.py:217
  58.6 2.8 %collective-permute-done.20.refs_3_ = bf16[256,384]{1,0:T(8,128)(2,1)S(1)} collective-permute-done((bf16[256,384]{1,0:T(8,128)(2,1)S(1)}, bf16[256,384]{1,0:T(8,128)(2,1)S(1)}, u32[]{:S(2)}, u32[]{:S(2)}) %collective-permute-start.20) | collective-permute-done | bytes 196640 | tf_op jit(solution)/shard_map/ppermute | solution.py:217
  61.5 3.6 %collective-permute-done.19.refs_2_ = bf16[256,384]{1,0:T(8,128)(2,1)S(1)} collective-permute-done((bf16[256,384]{1,0:T(8,128)(2,1)S(1)}, bf16[256,384]{1,0:T(8,128)(2,1)S(1)}, u32[]{:S(2)}, u32[]{:S(2)}) %collective-permute-start.19) | collective-permute-done | bytes 196640 | tf_op jit(solution)/shard_map/ppermute | solution.py:217
  66.9 1.3 %shard_map.155 = (f32[256,384]{1,0:T(8,128)S(1)}, bf16[272,384]{1,0:T(8,128)(2,1)S(1)}, f32[8,256]{1,0:T(8,128)S(1)}, bf16[2,256,1536]{2,1,0:T(8,128)(2,1)S(1)}) custom-call(bf16[256,384]{1,0:T(8,128)(2,1)S(1)} %get-tuple-element.101.refs_0_, bf16[256,384]{1,0:T(8,128)(2,1)S(1)} %collective-permute-done.18.refs_1_, ...), custom_call_target="tpu_custom_call" | custom-call | flops 603979776 | bytes 3342336 | tf_op jit(solution)/shard_map/pallas_call | solution.py:233
  68.5 2.5 %collective-permute-start.28 = (bf16[8,384,384]{2,1,0:T(8,128)(2,1)S(1)}, bf16[8,384,384]{2,1,0:T(8,128)(2,1)S(1)}, u32[]{:S(2)}, u32[]{:S(2)}) collective-permute-start(bf16[8,384,384]{2,1,0:T(8,128)(2,1)S(1)} %shard_map.157), channel_id=1, source_target_pairs={{0,1},{1,0},{2,3},{3,2},{4,5},{5,4},{6,7},{7,6},{8,9},{9,8},{10,11... | collective-permute-start | bytes 7077896 | tf_op jit(solution)/shard_map/ppermute | solution.py:223
  72.1 3.3 %collective-permute-start.24 = (bf16[256,384]{1,0:T(8,128)(2,1)S(1)}, bf16[256,384]{1,0:T(8,128)(2,1)S(1)}, u32[]{:S(2)}, u32[]{:S(2)}) collective-permute-start(bf16[256,384]{1,0:T(8,128)(2,1)S(1)} %get-tuple-element.101.refs_0_), channel_id=1, source_target_pairs={{0,0},{1,8},{2,2},{3,10},{4,4},{5,12},{6,6},{7,14},{8,1},{9,9},{10... | collective-permute-start | bytes 589832 | tf_op jit(solution)/shard_map/ppermute | solution.py:226
  77.4 16.3 %collective-permute-done.24.owned = bf16[256,384]{1,0:T(8,128)(2,1)S(1)} collective-permute-done((bf16[256,384]{1,0:T(8,128)(2,1)S(1)}, bf16[256,384]{1,0:T(8,128)(2,1)S(1)}, u32[]{:S(2)}, u32[]{:S(2)}) %collective-permute-start.24) | collective-permute-done | bytes 196640 | tf_op jit(solution)/shard_map/ppermute | solution.py:226
  93.7 1.5 %shard_map.156 = (bf16[128,384]{1,0:T(8,128)(2,1)S(1)}, bf16[128,384]{1,0:T(8,128)(2,1)S(1)}, bf16[128,384]{1,0:T(8,128)(2,1)S(1)}, bf16[128,384]{1,0:T(8,128)(2...) custom-call(s32[8]{0:T(128)S(1)} %copy-done.9, f32[256,384]{1,0:T(8,128)S(1)} %get-tuple-element.97.gap, ...), custom_call_target="tpu_custom_call" | custom-call | flops 301989888 | bytes 3297312 | tf_op jit(solution)/shard_map/pallas_call | solution.py:233
  96.5 1.5 %collective-permute-start.27 = (bf16[128,384]{1,0:T(8,128)(2,1)S(1)}, bf16[128,384]{1,0:T(8,128)(2,1)S(1)}, u32[]{:S(2)}, u32[]{:S(2)}) collective-permute-start(bf16[128,384]{1,0:T(8,128)(2,1)S(1)} %get-tuple-element.105), channel_id=1, source_target_pairs={{0,6},{2,4},{4,2},{6,0},{8,14},{10,12},{12,10},{14,8},{1,7},{3,5},... | collective-permute-start | bytes 294920 | tf_op jit(solution)/shard_map/ppermute | solution.py:217
  98.0 1.3 %shard_map.159 = (bf16[80,384]{1,0:T(8,128)(2,1)S(1)}, bf16[80,384]{1,0:T(8,128)(2,1)S(1)}, bf16[80,384]{1,0:T(8,128)(2,1)S(1)}, bf16[80,384]{1,0:T(8,128)(2,1)S(1)}) custom-call(s32[8]{0:T(128)S(1)} %copy-done.9, f32[256,384]{1,0:T(8,128)S(1)} %get-tuple-element.113.gap, bf16[256,384]{1,0:T(8,128)(2,1)S(1)} %collective-permute-done.29.came, ...), custom_call_target="tpu_custom_call" | custom-call | flops 301989888 | bytes 3223584 | tf_op jit(solution)/shard_map/pallas_call | solution.py:233
  100.5 1.5 %collective-permute-start.32 = (bf16[80,384]{1,0:T(8,128)(2,1)S(1)}, bf16[80,384]{1,0:T(8,128)(2,1)S(1)}, u32[]{:S(2)}, u32[]{:S(2)}) collective-permute-start(bf16[80,384]{1,0:T(8,128)(2,1)S(1)} %get-tuple-element.120), channel_id=1, source_target_pairs={{0,6},{2,4},{4,2},{6,0},{8,14},{10,12},{12,10},{14,8},{1,7},{3,5},... | collective-permute-start | bytes 184328 | tf_op jit(solution)/shard_map/ppermute | solution.py:217
  102.7 1.8 %collective-permute-done.31.refs_6_ = bf16[80,384]{1,0:T(8,128)(2,1)S(1)} collective-permute-done((bf16[80,384]{1,0:T(8,128)(2,1)S(1)}, bf16[80,384]{1,0:T(8,128)(2,1)S(1)}, u32[]{:S(2)}, u32[]{:S(2)}) %collective-permute-start.31) | collective-permute-done | bytes 61472 | tf_op jit(solution)/shard_map/ppermute | solution.py:217
  105.9 1.3 %collective-permute-done.33.came = bf16[80,1536]{1,0:T(8,128)(2,1)S(1)} collective-permute-done((bf16[80,1536]{1,0:T(8,128)(2,1)S(1)}, bf16[80,1536]{1,0:T(8,128)(2,1)S(1)}, u32[]{:S(2)}, u32[]{:S(2)}) %collective-permute-start.33) | collective-permute-done | bytes 245792 | tf_op jit(solution)/shard_map/ppermute | solution.py:223
  (82 shorter events, 29.1 us)
Async XLA Ops:
  2.0 10.6 %collective-permute-start.3 = (bf16[192,384]{1,0:T(8,128)(2,1)S(1)}, bf16[192,384]{1,0:T(8,128)(2,1)S(1)}, u32[]{:S(2)}, u32[]{:S(2)}) collective-permute-start(bf16[192,384]{1,0:T(8,128)(2,1)S(1)} %get-tuple-element.68), channel_id=1, source_target_pairs={{0,4},{2,6},{4,0},{6,2},{8,12},{10,14},{12,8},{14,10},{1,5},{3,7},... | collective-permute-start | bytes 442376 | tf_op jit(solution)/shard_map/ppermute | solution.py:217
  4.2 14.5 %collective-permute-start = (bf16[64,1536]{1,0:T(8,128)(2,1)}, bf16[64,1536]{1,0:T(8,128)(2,1)S(1)}, u32[]{:S(2)}, u32[]{:S(2)}) collective-permute-start(bf16[64,1536]{1,0:T(8,128)(2,1)} %param.13), channel_id=1, source_target_pairs={{0,0},{1,8},{2,2},{3,10},{4,4},{5,12},{6,6},{7,14},{8,1},{9,9},{10... | collective-permute-start | bytes 589832 | tf_op jit(solution)/shard_map/ppermute | solution.py:226
  9.3 10.1 %collective-permute-start.1 = (bf16[64,1536]{1,0:T(8,128)(2,1)}, bf16[64,1536]{1,0:T(8,128)(2,1)S(1)}, u32[]{:S(2)}, u32[]{:S(2)}) collective-permute-start(bf16[64,1536]{1,0:T(8,128)(2,1)} %param.14), channel_id=1, source_target_pairs={{0,0},{1,8},{2,2},{3,10},{4,4},{5,12},{6,6},{7,14},{8,1},{9,9},{10... | collective-permute-start | bytes 589832 | tf_op jit(solution)/shard_map/ppermute | solution.py:226
  12.4 11.9 %collective-permute-start.2 = (bf16[384,384]{1,0:T(8,128)(2,1)S(1)}, bf16[384,384]{1,0:T(8,128)(2,1)S(1)}, u32[]{:S(2)}, u32[]{:S(2)}) collective-permute-start(bf16[384,384]{1,0:T(8,128)(2,1)S(1)} %get-tuple-element.67), channel_id=1, source_target_pairs={{0,2},{2,0},{4,6},{6,4},{8,10},{10,8},{12,14},{14,12},{1,3},{3,1},... | collective-permute-start | bytes 884744 | tf_op jit(solution)/shard_map/ppermute | solution.py:217
  12.6 9.3 %collective-permute-start.5 = (bf16[192,384]{1,0:T(8,128)(2,1)S(1)}, bf16[192,384]{1,0:T(8,128)(2,1)S(1)}, u32[]{:S(2)}, u32[]{:S(2)}) collective-permute-start(bf16[192,384]{1,0:T(8,128)(2,1)S(1)} %collective-permute-done.3.refs_0_), channel_id=1, source_target_pairs={{0,16},{16,0},{1,17},{17,1},{2,18},{18,2},{3,19},{19,3},{4,20},{20... | collective-permute-start | bytes 442376 | tf_op jit(solution)/shard_map/ppermute | solution.py:377
  19.5 7.7 %collective-permute-start.7 = (bf16[80,1536]{1,0:T(8,128)(2,1)S(1)}, bf16[80,1536]{1,0:T(8,128)(2,1)S(1)}, u32[]{:S(2)}, u32[]{:S(2)}) collective-permute-start(bf16[80,1536]{1,0:T(8,128)(2,1)S(1)} %get-tuple-element.72), channel_id=1, source_target_pairs={{0,2},{2,0},{4,6},{6,4},{8,10},{10,8},{12,14},{14,12},{1,3},{3,1},... | collective-permute-start | bytes 737288 | tf_op jit(solution)/shard_map/ppermute | solution.py:217
  20.7 7.8 %collective-permute-start.8 = (bf16[80,1536]{1,0:T(8,128)(2,1)S(1)}, bf16[80,1536]{1,0:T(8,128)(2,1)S(1)}, u32[]{:S(2)}, u32[]{:S(2)}) collective-permute-start(bf16[80,1536]{1,0:T(8,128)(2,1)S(1)} %get-tuple-element.74), channel_id=1, source_target_pairs={{0,4},{2,6},{4,0},{6,2},{8,12},{10,14},{12,8},{14,10},{1,5},{3,7},... | collective-permute-start | bytes 737288 | tf_op jit(solution)/shard_map/ppermute | solution.py:217
  21.9 11.4 %collective-permute-start.9 = (bf16[80,1536]{1,0:T(8,128)(2,1)S(1)}, bf16[80,1536]{1,0:T(8,128)(2,1)S(1)}, u32[]{:S(2)}, u32[]{:S(2)}) collective-permute-start(bf16[80,1536]{1,0:T(8,128)(2,1)S(1)} %get-tuple-element.75), channel_id=1, source_target_pairs={{0,6},{2,4},{4,2},{6,0},{8,14},{10,12},{12,10},{14,8},{1,7},{3,5},... | collective-permute-start | bytes 737288 | tf_op jit(solution)/shard_map/ppermute | solution.py:217
  27.2 7.8 %collective-permute-start.10 = (bf16[384,384]{1,0:T(8,128)(2,1)S(1)}, bf16[384,384]{1,0:T(8,128)(2,1)S(1)}, u32[]{:S(2)}, u32[]{:S(2)}) collective-permute-start(bf16[384,384]{1,0:T(8,128)(2,1)S(1)} %get-tuple-element.77.refs_5_.refs_4_), channel_id=1, source_target_pairs={{0,1},{1,0},{2,3},{3,2},{4,5},{5,4},{6,7},{7,6},{8,9},{9,8},{10,11... | collective-permute-start | bytes 884744 | tf_op jit(solution)/shard_map/ppermute | solution.py:223
  27.2 7.8 %collective-permute-start.11 = (bf16[384,384]{1,0:T(8,128)(2,1)S(1)}, bf16[384,384]{1,0:T(8,128)(2,1)S(1)}, u32[]{:S(2)}, u32[]{:S(2)}) collective-permute-start(bf16[384,384]{1,0:T(8,128)(2,1)S(1)} %collective-permute-done.2.refs_6_.refs_5_), channel_id=1, source_target_pairs={{0,1},{1,0},{2,3},{3,2},{4,5},{5,4},{6,7},{7,6},{8,9},{9,8},{10,11... | collective-permute-start | bytes 884744 | tf_op jit(solution)/shard_map/ppermute | solution.py:223
  27.7 8.5 %collective-permute-start.12 = (bf16[384,384]{1,0:T(8,128)(2,1)S(1)}, bf16[384,384]{1,0:T(8,128)(2,1)S(1)}, u32[]{:S(2)}, u32[]{:S(2)}) collective-permute-start(bf16[384,384]{1,0:T(8,128)(2,1)S(1)} %get-tuple-element.79.refs_7_.refs_6_), channel_id=1, source_target_pairs={{0,1},{1,0},{2,3},{3,2},{4,5},{5,4},{6,7},{7,6},{8,9},{9,8},{10,11... | collective-permute-start | bytes 884744 | tf_op jit(solution)/shard_map/ppermute | solution.py:223
  28.5 7.7 %collective-permute-start.13 = (bf16[384,384]{1,0:T(8,128)(2,1)S(1)}, bf16[384,384]{1,0:T(8,128)(2,1)S(1)}, u32[]{:S(2)}, u32[]{:S(2)}) collective-permute-start(bf16[384,384]{1,0:T(8,128)(2,1)S(1)} %get-tuple-element.80.refs_8_.refs_7_), channel_id=1, source_target_pairs={{0,1},{1,0},{2,3},{3,2},{4,5},{5,4},{6,7},{7,6},{8,9},{9,8},{10,11... | collective-permute-start | bytes 884744 | tf_op jit(solution)/shard_map/ppermute | solution.py:223
  33.3 25.0 %collective-permute-start.17 = (bf16[2,384,384]{2,1,0:T(8,128)(2,1)S(1)}, bf16[2,384,384]{2,1,0:T(8,128)(2,1)S(1)}, u32[]{:S(2)}, u32[]{:S(2)}) collective-permute-start(bf16[2,384,384]{2,1,0:T(8,128)(2,1)S(1)} %get-tuple-element.91), channel_id=1, source_target_pairs={{0,2},{2,0},{4,6},{6,4},{8,10},{10,8},{12,14},{14,12},{1,3},{3,1},... | collective-permute-start | bytes 1769480 | tf_op jit(solution)/shard_map/ppermute | solution.py:217
  35.0 12.2 %collective-permute-start.15 = (bf16[384,384]{1,0:T(8,128)(2,1)S(1)}, bf16[384,384]{1,0:T(8,128)(2,1)S(1)}, u32[]{:S(2)}, u32[]{:S(2)}) collective-permute-start(bf16[384,384]{1,0:T(8,128)(2,1)S(1)} %get-tuple-element.85), channel_id=1, source_target_pairs={{0,4},{2,6},{4,0},{6,2},{8,12},{10,14},{12,8},{14,10},{1,5},{3,7},... | collective-permute-start | bytes 884744 | tf_op jit(solution)/shard_map/ppermute | solution.py:217
  35.0 18.6 %collective-permute-start.16 = (bf16[384,384]{1,0:T(8,128)(2,1)S(1)}, bf16[384,384]{1,0:T(8,128)(2,1)S(1)}, u32[]{:S(2)}, u32[]{:S(2)}) collective-permute-start(bf16[384,384]{1,0:T(8,128)(2,1)S(1)} %get-tuple-element.86), channel_id=1, source_target_pairs={{0,6},{2,4},{4,2},{6,0},{8,14},{10,12},{12,10},{14,8},{1,7},{3,5},... | collective-permute-start | bytes 884744 | tf_op jit(solution)/shard_map/ppermute | solution.py:217
  38.2 15.4 %collective-permute-start.14 = (bf16[272,384]{1,0:T(8,128)(2,1)S(1)}, bf16[272,384]{1,0:T(8,128)(2,1)S(1)}, u32[]{:S(2)}, u32[]{:S(2)}) collective-permute-start(bf16[272,384]{1,0:T(8,128)(2,1)S(1)} %get-tuple-element.82), channel_id=1, source_target_pairs={{0,8},{2,10},{4,12},{6,14},{8,0},{10,2},{12,4},{14,6},{1,9},{3,11}... | collective-permute-start | bytes 626696 | tf_op jit(solution)/shard_map/ppermute | solution.py:220
  53.6 12.8 %collective-permute-start.21 = (bf16[384,384]{1,0:T(8,128)(2,1)S(1)}, bf16[384,384]{1,0:T(8,128)(2,1)S(1)}, u32[]{:S(2)}, u32[]{:S(2)}) collective-permute-start(bf16[384,384]{1,0:T(8,128)(2,1)S(1)} %collective-permute-done.15.refs_7_.refs_2_), channel_id=1, source_target_pairs={{0,16},{16,0},{1,17},{17,1},{2,18},{18,2},{3,19},{19,3},{4,20},{20... | collective-permute-start | bytes 884744 | tf_op jit(solution)/shard_map/ppermute | solution.py:451
  54.5 12.4 %collective-permute-start.22 = (bf16[384,384]{1,0:T(8,128)(2,1)S(1)}, bf16[384,384]{1,0:T(8,128)(2,1)S(1)}, u32[]{:S(2)}, u32[]{:S(2)}) collective-permute-start(bf16[384,384]{1,0:T(8,128)(2,1)S(1)} %collective-permute-done.16.refs_8_.refs_3_), channel_id=1, source_target_pairs={{0,16},{16,0},{1,17},{17,1},{2,18},{18,2},{3,19},{19,3},{4,20},{20... | collective-permute-start | bytes 884744 | tf_op jit(solution)/shard_map/ppermute | solution.py:451
  57.3 7.9 %collective-permute-start.19 = (bf16[256,384]{1,0:T(8,128)(2,1)S(1)}, bf16[256,384]{1,0:T(8,128)(2,1)S(1)}, u32[]{:S(2)}, u32[]{:S(2)}) collective-permute-start(bf16[256,384]{1,0:T(8,128)(2,1)S(1)} %get-tuple-element.101.refs_0_), channel_id=1, source_target_pairs={{0,4},{2,6},{4,0},{6,2},{8,12},{10,14},{12,8},{14,10},{1,5},{3,7},... | collective-permute-start | bytes 589832 | tf_op jit(solution)/shard_map/ppermute | solution.py:217
  58.3 8.1 %collective-permute-start.18 = (bf16[256,384]{1,0:T(8,128)(2,1)S(1)}, bf16[256,384]{1,0:T(8,128)(2,1)S(1)}, u32[]{:S(2)}, u32[]{:S(2)}) collective-permute-start(bf16[256,384]{1,0:T(8,128)(2,1)S(1)} %get-tuple-element.101.refs_0_), channel_id=1, source_target_pairs={{0,2},{2,0},{4,6},{6,4},{8,10},{10,8},{12,14},{14,12},{1,3},{3,1},... | collective-permute-start | bytes 589832 | tf_op jit(solution)/shard_map/ppermute | solution.py:217
  68.5 7.0 %collective-permute-start.28 = (bf16[8,384,384]{2,1,0:T(8,128)(2,1)S(1)}, bf16[8,384,384]{2,1,0:T(8,128)(2,1)S(1)}, u32[]{:S(2)}, u32[]{:S(2)}) collective-permute-start(bf16[8,384,384]{2,1,0:T(8,128)(2,1)S(1)} %shard_map.157), channel_id=1, source_target_pairs={{0,1},{1,0},{2,3},{3,2},{4,5},{5,4},{6,7},{7,6},{8,9},{9,8},{10,11... | collective-permute-start | bytes 7077896 | tf_op jit(solution)/shard_map/ppermute | solution.py:223
  70.9 22.8 %collective-permute-start.23 = (bf16[272,384]{1,0:T(8,128)(2,1)S(1)}, bf16[272,384]{1,0:T(8,128)(2,1)S(1)}, u32[]{:S(2)}, u32[]{:S(2)}) collective-permute-start(bf16[272,384]{1,0:T(8,128)(2,1)S(1)} %get-tuple-element.98), channel_id=1, source_target_pairs={{0,8},{2,10},{4,12},{6,14},{8,0},{10,2},{12,4},{14,6},{1,9},{3,11}... | collective-permute-start | bytes 626696 | tf_op jit(solution)/shard_map/ppermute | solution.py:220
  72.1 21.6 %collective-permute-start.24 = (bf16[256,384]{1,0:T(8,128)(2,1)S(1)}, bf16[256,384]{1,0:T(8,128)(2,1)S(1)}, u32[]{:S(2)}, u32[]{:S(2)}) collective-permute-start(bf16[256,384]{1,0:T(8,128)(2,1)S(1)} %get-tuple-element.101.refs_0_), channel_id=1, source_target_pairs={{0,0},{1,8},{2,2},{3,10},{4,4},{5,12},{6,6},{7,14},{8,1},{9,9},{10... | collective-permute-start | bytes 589832 | tf_op jit(solution)/shard_map/ppermute | solution.py:226
  76.5 21.4 %collective-permute-start.29 = (bf16[256,384]{1,0:T(8,128)(2,1)S(1)}, bf16[256,384]{1,0:T(8,128)(2,1)S(1)}, u32[]{:S(2)}, u32[]{:S(2)}) collective-permute-start(bf16[256,384]{1,0:T(8,128)(2,1)S(1)} %get-tuple-element.114), channel_id=1, source_target_pairs={{0,8},{2,10},{4,12},{6,14},{8,0},{10,2},{12,4},{14,6},{1,9},{3,11}... | collective-permute-start | bytes 589832 | tf_op jit(solution)/shard_map/ppermute | solution.py:220
  (20 other events, 177.0 us)

commit v8 on v7

--- a/solution.py
+++ b/solution.py
@@ -373,10 +373,11 @@
     x_turned, fresh_turned = turned(noise_in), turned(renoise)
     gen_sent = call(cut_gen_kernel, [gen_weight], [((depth, w), bf16)] * shared + [((part_rows, w), bf16)] * (g - shared), depth * h)
     gen_mine = [gen_sent[0]] + [in_square(gen_sent[k], k) for k in range(1, g)]
-    fetched = gen_mine[shared:]
+    x_sent = call(cut_rows_kernel, [x_turned, fresh_turned], [((r + fold, h), bf16)] * g, r * h)
+    x_sent = list(x_sent)
+    *fetched, x_sent[0] = lax.optimization_barrier((*gen_mine[shared:], x_sent[0]))
     given = [lax.ppermute(v, "rep", [(0, 1), (1, 0)]) for v in fetched]
     gen_mine[shared:] = call(join_gen_kernel, fetched + given, [((depth, w), bf16)] * (g - shared), depth * w)
-    x_sent = call(cut_rows_kernel, [x_turned, fresh_turned], [((r + fold, h), bf16)] * g, r * h)
     x = [x_sent[0]] + [in_square(x_sent[k], k) for k in range(1, g)]
     gen_swap, x[1], scales = lax.optimization_barrier((gen_mine, x[1], scales))
     gen_other = [cores(v) for v in gen_swap]
@@ -500,6 +501,7 @@
 
         pack(rows, store)
 
+    noised_home, noised[3] = lax.optimization_barrier((noised_mine, noised[3]))
     gap_here, away_here, noised_sums, lifts = call(
         score_kernel,
         noised + [scales] + score_mine,
@@ -507,8 +509,8 @@
         4 * t * h * w,
     )
     came_here = across(away_here)
-    score_mine, noised_home, away_here = lax.optimization_barrier((score_mine, noised_mine, away_here))
-    noised_owned = turned(noised_home)
+    noised_owned, score_mine, gap_here = lax.optimization_barrier((turned(noised_home), score_mine, gap_here))
+    score_mine, _ = lax.optimization_barrier((score_mine, cores(noised_sums)))
     score_other = swap_all(score_mine)
 
     def score_rest_kernel(lifts, other, gap, away):

time: 108 us -> 105 us (0.972)
  starting transfers between devices: 39.2 us -> 37.1 us
  waiting for transfers between devices: 53.8 us -> 52.6 us
    ppermute x3, waiting for transfers between devices: 0.01 us -> 10.3 us  [across(): return lax.ppermute(value, 'fsdp', [(i, i ^ g) for i in range(2 * g)])]
    ppermute x18, waiting for transfers between devices: 34.9 us -> 25.3 us  [in_square(): return lax.ppermute(value, 'fsdp', [(i, i ^ k) for i in range(2 * g)])]
    ppermute x3, waiting for transfers between devices: 17 us -> 10.1 us  [turned(): lax.ppermute(value, ('fsdp', 'mp'), [(flat(*i), flat(i[2], i[1], i[0])) f...]
    ppermute x6, waiting for transfers between devices: 1.32 us -> 5.35 us  [cores(): return lax.ppermute(value, 'mp', [(0, 1), (1, 0)])]
    ppermute x3, starting transfers between devices: 3.63 us -> 1.01 us  [across(): return lax.ppermute(value, 'fsdp', [(i, i ^ g) for i in range(2 * g)])]
  transfers between devices with their start and end apart: 34 -> 34, of which waited for: 16 -> 17; matrix products, arithmetic and copies ran while one was open for 1% -> 1% of each run, Pallas kernels for 7% -> 8%
where the time goes in v8:
time: 105 us
  waiting for transfers between devices  52.6 us (50%)
  starting transfers between devices  37.1 us (35%)
  Pallas kernels  10.6 us (10%)
  local copies, waits for them, and re-layouts  2.42 us (2%)
    ppermute x18, waiting for transfers between devices, in_square(): return lax.ppermute(value, 'fsdp', [(i, i ^ k) for i in range(2 * g)])  25.3 us
    ppermute x18, starting transfers between devices, in_square(): return lax.ppermute(value, 'fsdp', [(i, i ^ k) for i in range(2 * g)])  17.1 us
    ppermute x3, starting transfers between devices, turned(): lax.ppermute(value, ('fsdp', 'mp'), [(flat(*i), flat(i[2], i[1], i[0])) f...  11.4 us
    ppermute x3, waiting for transfers between devices, across(): return lax.ppermute(value, 'fsdp', [(i, i ^ g) for i in range(2 * g)])  10.3 us
    pallas_call x13, Pallas kernels, call(): pl.pallas_call(kernel, in_specs=[scalars] * in_scalars + [whole] * (len(o...  10.1 us
    ppermute x3, waiting for transfers between devices, turned(): lax.ppermute(value, ('fsdp', 'mp'), [(flat(*i), flat(i[2], i[1], i[0])) f...  10.1 us
    ppermute x6, waiting for transfers between devices, cores(): return lax.ppermute(value, 'mp', [(0, 1), (1, 0)])  5.35 us
    ppermute x6, starting transfers between devices, cores(): return lax.ppermute(value, 'mp', [(0, 1), (1, 0)])  4.58 us
  transfers between devices with their start and end apart: 34, of which 17 were waited for; matrix products, arithmetic and copies ran while one was open for 1% of the time, Pallas kernels for 8%

profile of v8, /device:TPU:1, one launch (start us, length us, event | category | flops | bytes accessed | tf_op | source)
XLA Modules:
  0.0 104.7 jit_solution(16340289527009849992)
XLA Ops:
  2.0 2.2 %collective-permute-start = (bf16[192,384]{1,0:T(8,128)(2,1)S(1)}, bf16[192,384]{1,0:T(8,128)(2,1)S(1)}, u32[]{:S(2)}, u32[]{:S(2)}) collective-permute-start(bf16[192,384]{1,0:T(8,128)(2,1)S(1)} %get-tuple-element.77), channel_id=1, source_target_pairs={{0,4},{2,6},{4,0},{6,2},{8,12},{10,14},{12,8},{14,10},{1,5},{3,7},... | collective-permute-start | bytes 442376 | tf_op jit(solution)/shard_map/ppermute | solution.py:217
  5.3 5.3 %collective-permute-start.2 = (bf16[64,1536]{1,0:T(8,128)(2,1)}, bf16[64,1536]{1,0:T(8,128)(2,1)S(1)}, u32[]{:S(2)}, u32[]{:S(2)}) collective-permute-start(bf16[64,1536]{1,0:T(8,128)(2,1)} %param.13), channel_id=1, source_target_pairs={{0,0},{1,8},{2,2},{3,10},{4,4},{5,12},{6,6},{7,14},{8,1},{9,9},{10... | collective-permute-start | bytes 589832 | tf_op jit(solution)/shard_map/ppermute | solution.py:226
  10.7 1.9 %collective-permute-start.3 = (bf16[64,1536]{1,0:T(8,128)(2,1)}, bf16[64,1536]{1,0:T(8,128)(2,1)S(1)}, u32[]{:S(2)}, u32[]{:S(2)}) collective-permute-start(bf16[64,1536]{1,0:T(8,128)(2,1)} %param.14), channel_id=1, source_target_pairs={{0,0},{1,8},{2,2},{3,10},{4,4},{5,12},{6,6},{7,14},{8,1},{9,9},{10... | collective-permute-start | bytes 589832 | tf_op jit(solution)/shard_map/ppermute | solution.py:226
  13.7 2.6 %collective-permute-done.2.rows = bf16[64,1536]{1,0:T(8,128)(2,1)S(1)} collective-permute-done((bf16[64,1536]{1,0:T(8,128)(2,1)}, bf16[64,1536]{1,0:T(8,128)(2,1)S(1)}, u32[]{:S(2)}, u32[]{:S(2)}) %collective-permute-start.2) | collective-permute-done | bytes 196640 | tf_op jit(solution)/shard_map/ppermute | solution.py:226
  16.3 3.9 %collective-permute-done.3.fresh = bf16[64,1536]{1,0:T(8,128)(2,1)S(1)} collective-permute-done((bf16[64,1536]{1,0:T(8,128)(2,1)}, bf16[64,1536]{1,0:T(8,128)(2,1)S(1)}, u32[]{:S(2)}, u32[]{:S(2)}) %collective-permute-start.3) | collective-permute-done | bytes 196640 | tf_op jit(solution)/shard_map/ppermute | solution.py:226
  20.3 1.3 %collective-permute-start.5 = (bf16[192,384]{1,0:T(8,128)(2,1)S(1)}, bf16[192,384]{1,0:T(8,128)(2,1)S(1)}, u32[]{:S(2)}, u32[]{:S(2)}) collective-permute-start(bf16[192,384]{1,0:T(8,128)(2,1)S(1)} %collective-permute-done.refs_0_), channel_id=1, source_target_pairs={{0,16},{16,0},{1,17},{17,1},{2,18},{18,2},{3,19},{19,3},{4,20},{20... | collective-permute-start | bytes 442376 | tf_op jit(solution)/shard_map/ppermute | solution.py:379
  27.5 2.1 %collective-permute-done.7.refs_1_ = bf16[80,1536]{1,0:T(8,128)(2,1)S(1)} collective-permute-done((bf16[80,1536]{1,0:T(8,128)(2,1)S(1)}, bf16[80,1536]{1,0:T(8,128)(2,1)S(1)}, u32[]{:S(2)}, u32[]{:S(2)}) %collective-permute-start.7) | collective-permute-done | bytes 245792 | tf_op jit(solution)/shard_map/ppermute | solution.py:217
  30.7 1.7 %collective-permute-done.9.refs_3_ = bf16[80,1536]{1,0:T(8,128)(2,1)S(1)} collective-permute-done((bf16[80,1536]{1,0:T(8,128)(2,1)S(1)}, bf16[80,1536]{1,0:T(8,128)(2,1)S(1)}, u32[]{:S(2)}, u32[]{:S(2)}) %collective-permute-start.9) | collective-permute-done | bytes 245792 | tf_op jit(solution)/shard_map/ppermute | solution.py:217
  32.9 2.2 %collective-permute-start.16 = (bf16[384,384]{1,0:T(8,128)(2,1)S(1)}, bf16[384,384]{1,0:T(8,128)(2,1)S(1)}, u32[]{:S(2)}, u32[]{:S(2)}) collective-permute-start(bf16[384,384]{1,0:T(8,128)(2,1)S(1)} %get-tuple-element.101), channel_id=1, source_target_pairs={{0,6},{2,4},{4,2},{6,0},{8,14},{10,12},{12,10},{14,8},{1,7},{3,5},... | collective-permute-start | bytes 884744 | tf_op jit(solution)/shard_map/ppermute | solution.py:217
  35.1 2.0 %shard_map.152 = (f32[256,384]{1,0:T(8,128)S(1)}, bf16[272,384]{1,0:T(8,128)(2,1)S(1)}, f32[8,256]{1,0:T(8,128)S(1)}, f32[256,384]{1,0:T(8,128)S(1)}) custom-call(s32[8]{0:T(128)S(1)} %copy-done.9, bf16[80,1536]{1,0:T(8,128)(2,1)S(1)} %get-tuple-element.80.refs_0_, bf16[80,1536]{1,0:T(8,128)(2,1)S(1)} %collective-permute-done.7.refs_1_, ...), custom_call_target="tpu_custom_call" | custom-call | flops 603979776 | bytes 3538976 | tf_op jit(solution)/shard_map/pallas_call | solution.py:233
  37.7 8.2 %collective-permute-done.15.refs_7_.refs_2_ = bf16[384,384]{1,0:T(8,128)(2,1)S(1)} collective-permute-done((bf16[384,384]{1,0:T(8,128)(2,1)S(1)}, bf16[384,384]{1,0:T(8,128)(2,1)S(1)}, u32[]{:S(2)}, u32[]{:S(2)}) %collective-permute-start.15) | collective-permute-done | bytes 294944 | tf_op jit(solution)/shard_map/ppermute | solution.py:217
  45.9 6.5 %collective-permute-done.16.refs_8_.refs_3_ = bf16[384,384]{1,0:T(8,128)(2,1)S(1)} collective-permute-done((bf16[384,384]{1,0:T(8,128)(2,1)S(1)}, bf16[384,384]{1,0:T(8,128)(2,1)S(1)}, u32[]{:S(2)}, u32[]{:S(2)}) %collective-permute-start.16) | collective-permute-done | bytes 294944 | tf_op jit(solution)/shard_map/ppermute | solution.py:217
  55.0 2.4 %collective-permute-start.23 = (bf16[256,384]{1,0:T(8,128)(2,1)S(1)}, bf16[256,384]{1,0:T(8,128)(2,1)S(1)}, u32[]{:S(2)}, u32[]{:S(2)}) collective-permute-start(bf16[256,384]{1,0:T(8,128)(2,1)S(1)} %get-tuple-element.112.refs_0_), channel_id=1, source_target_pairs={{0,4},{2,6},{4,0},{6,2},{8,12},{10,14},{12,8},{14,10},{1,5},{3,7},... | collective-permute-start | bytes 589832 | tf_op jit(solution)/shard_map/ppermute | solution.py:217
  57.5 3.4 %collective-permute-done.17.refs_3_ = bf16[256,384]{1,0:T(8,128)(2,1)S(1)} collective-permute-done((bf16[256,384]{1,0:T(8,128)(2,1)S(1)}, bf16[256,384]{1,0:T(8,128)(2,1)S(1)}, u32[]{:S(2)}, u32[]{:S(2)}) %collective-permute-start.17) | collective-permute-done | bytes 196640 | tf_op jit(solution)/shard_map/ppermute | solution.py:217
  60.9 4.1 %collective-permute-start.18 = (bf16[256,384]{1,0:T(8,128)(2,1)S(1)}, bf16[256,384]{1,0:T(8,128)(2,1)S(1)}, u32[]{:S(2)}, u32[]{:S(2)}) collective-permute-start(bf16[256,384]{1,0:T(8,128)(2,1)S(1)} %get-tuple-element.112.refs_0_), channel_id=1, source_target_pairs={{0,0},{1,8},{2,2},{3,10},{4,4},{5,12},{6,6},{7,14},{8,1},{9,9},{10... | collective-permute-start | bytes 589832 | tf_op jit(solution)/shard_map/ppermute | solution.py:226
  67.3 3.5 %collective-permute-done.18.owned = bf16[256,384]{1,0:T(8,128)(2,1)S(1)} collective-permute-done((bf16[256,384]{1,0:T(8,128)(2,1)S(1)}, bf16[256,384]{1,0:T(8,128)(2,1)S(1)}, u32[]{:S(2)}, u32[]{:S(2)}) %collective-permute-start.18) | collective-permute-done | bytes 196640 | tf_op jit(solution)/shard_map/ppermute | solution.py:226
  71.5 4.2 %collective-permute-done.28.other = bf16[8,384,384]{2,1,0:T(8,128)(2,1)S(1)} collective-permute-done((bf16[8,384,384]{2,1,0:T(8,128)(2,1)S(1)}, bf16[8,384,384]{2,1,0:T(8,128)(2,1)S(1)}, u32[]{:S(2)}, u32[]{:S(2)}) %collective-permute-start.28) | collective-permute-done | bytes 2359328 | tf_op jit(solution)/shard_map/ppermute | solution.py:223
  76.9 10.3 %collective-permute-done.24.came = bf16[272,384]{1,0:T(8,128)(2,1)S(1)} collective-permute-done((bf16[272,384]{1,0:T(8,128)(2,1)S(1)}, bf16[272,384]{1,0:T(8,128)(2,1)S(1)}, u32[]{:S(2)}, u32[]{:S(2)}) %collective-permute-start.24) | collective-permute-done | bytes 208928 | tf_op jit(solution)/shard_map/ppermute | solution.py:220
  87.1 1.5 %shard_map.156 = (bf16[128,384]{1,0:T(8,128)(2,1)S(1)}, bf16[128,384]{1,0:T(8,128)(2,1)S(1)}, bf16[128,384]{1,0:T(8,128)(2,1)S(1)}, bf16[128,384]{1,0:T(8,128)(2...) custom-call(s32[8]{0:T(128)S(1)} %copy-done.9, f32[256,384]{1,0:T(8,128)S(1)} %get-tuple-element.115.gap, ...), custom_call_target="tpu_custom_call" | custom-call | flops 301989888 | bytes 3297312 | tf_op jit(solution)/shard_map/pallas_call | solution.py:233
  88.8 2.6 %collective-permute-start.27 = (bf16[128,384]{1,0:T(8,128)(2,1)S(1)}, bf16[128,384]{1,0:T(8,128)(2,1)S(1)}, u32[]{:S(2)}, u32[]{:S(2)}) collective-permute-start(bf16[128,384]{1,0:T(8,128)(2,1)S(1)} %get-tuple-element.123), channel_id=1, source_target_pairs={{0,6},{2,4},{4,2},{6,0},{8,14},{10,12},{12,10},{14,8},{1,7},{3,5},... | collective-permute-start | bytes 294920 | tf_op jit(solution)/shard_map/ppermute | solution.py:217
  91.4 1.3 %shard_map.159 = (bf16[80,384]{1,0:T(8,128)(2,1)S(1)}, bf16[80,384]{1,0:T(8,128)(2,1)S(1)}, bf16[80,384]{1,0:T(8,128)(2,1)S(1)}, bf16[80,384]{1,0:T(8,128)(2,1)S(1)}) custom-call(s32[8]{0:T(128)S(1)} %copy-done.9, f32[256,384]{1,0:T(8,128)S(1)} %get-tuple-element.137.gap, bf16[256,384]{1,0:T(8,128)(2,1)S(1)} %collective-permute-done.29.came, ...), custom_call_target="tpu_custom_call" | custom-call | flops 301989888 | bytes 3223584 | tf_op jit(solution)/shard_map/pallas_call | solution.py:233
  93.1 2.4 %collective-permute-start.32 = (bf16[80,384]{1,0:T(8,128)(2,1)S(1)}, bf16[80,384]{1,0:T(8,128)(2,1)S(1)}, u32[]{:S(2)}, u32[]{:S(2)}) collective-permute-start(bf16[80,384]{1,0:T(8,128)(2,1)S(1)} %get-tuple-element.144), channel_id=1, source_target_pairs={{0,6},{2,4},{4,2},{6,0},{8,14},{10,12},{12,10},{14,8},{1,7},{3,5},... | collective-permute-start | bytes 184328 | tf_op jit(solution)/shard_map/ppermute | solution.py:217
  96.9 1.7 %collective-permute-done.32.refs_7_ = bf16[80,384]{1,0:T(8,128)(2,1)S(1)} collective-permute-done((bf16[80,384]{1,0:T(8,128)(2,1)S(1)}, bf16[80,384]{1,0:T(8,128)(2,1)S(1)}, u32[]{:S(2)}, u32[]{:S(2)}) %collective-permute-start.32) | collective-permute-done | bytes 61472 | tf_op jit(solution)/shard_map/ppermute | solution.py:217
  99.3 3.5 %collective-permute-start.33 = (bf16[80,1536]{1,0:T(8,128)(2,1)S(1)}, bf16[80,1536]{1,0:T(8,128)(2,1)S(1)}, u32[]{:S(2)}, u32[]{:S(2)}) collective-permute-start(bf16[80,1536]{1,0:T(8,128)(2,1)S(1)} %get-tuple-element.148), channel_id=1, source_target_pairs={{0,1},{1,0},{2,3},{3,2},{4,5},{5,4},{6,7},{7,6},{8,9},{9,8},{10,11... | collective-permute-start | bytes 737288 | tf_op jit(solution)/shard_map/ppermute | solution.py:223
  (82 shorter events, 22.9 us)
Async XLA Ops:
  2.0 18.3 %collective-permute-start = (bf16[192,384]{1,0:T(8,128)(2,1)S(1)}, bf16[192,384]{1,0:T(8,128)(2,1)S(1)}, u32[]{:S(2)}, u32[]{:S(2)}) collective-permute-start(bf16[192,384]{1,0:T(8,128)(2,1)S(1)} %get-tuple-element.77), channel_id=1, source_target_pairs={{0,4},{2,6},{4,0},{6,2},{8,12},{10,14},{12,8},{14,10},{1,5},{3,7},... | collective-permute-start | bytes 442376 | tf_op jit(solution)/shard_map/ppermute | solution.py:217
  4.2 16.1 %collective-permute-start.1 = (bf16[192,384]{1,0:T(8,128)(2,1)S(1)}, bf16[192,384]{1,0:T(8,128)(2,1)S(1)}, u32[]{:S(2)}, u32[]{:S(2)}) collective-permute-start(bf16[192,384]{1,0:T(8,128)(2,1)S(1)} %get-tuple-element.78), channel_id=1, source_target_pairs={{0,6},{2,4},{4,2},{6,0},{8,14},{10,12},{12,10},{14,8},{1,7},{3,5},... | collective-permute-start | bytes 442376 | tf_op jit(solution)/shard_map/ppermute | solution.py:217
  5.3 11.0 %collective-permute-start.2 = (bf16[64,1536]{1,0:T(8,128)(2,1)}, bf16[64,1536]{1,0:T(8,128)(2,1)S(1)}, u32[]{:S(2)}, u32[]{:S(2)}) collective-permute-start(bf16[64,1536]{1,0:T(8,128)(2,1)} %param.13), channel_id=1, source_target_pairs={{0,0},{1,8},{2,2},{3,10},{4,4},{5,12},{6,6},{7,14},{8,1},{9,9},{10... | collective-permute-start | bytes 589832 | tf_op jit(solution)/shard_map/ppermute | solution.py:226
  10.7 9.6 %collective-permute-start.3 = (bf16[64,1536]{1,0:T(8,128)(2,1)}, bf16[64,1536]{1,0:T(8,128)(2,1)S(1)}, u32[]{:S(2)}, u32[]{:S(2)}) collective-permute-start(bf16[64,1536]{1,0:T(8,128)(2,1)} %param.14), channel_id=1, source_target_pairs={{0,0},{1,8},{2,2},{3,10},{4,4},{5,12},{6,6},{7,14},{8,1},{9,9},{10... | collective-permute-start | bytes 589832 | tf_op jit(solution)/shard_map/ppermute | solution.py:226
  12.6 14.9 %collective-permute-start.4 = (bf16[384,384]{1,0:T(8,128)(2,1)S(1)}, bf16[384,384]{1,0:T(8,128)(2,1)S(1)}, u32[]{:S(2)}, u32[]{:S(2)}) collective-permute-start(bf16[384,384]{1,0:T(8,128)(2,1)S(1)} %get-tuple-element.82), channel_id=1, source_target_pairs={{0,2},{2,0},{4,6},{6,4},{8,10},{10,8},{12,14},{14,12},{1,3},{3,1},... | collective-permute-start | bytes 884744 | tf_op jit(solution)/shard_map/ppermute | solution.py:217
  21.6 5.8 %collective-permute-start.6 = (bf16[192,384]{1,0:T(8,128)(2,1)S(1)}, bf16[192,384]{1,0:T(8,128)(2,1)S(1)}, u32[]{:S(2)}, u32[]{:S(2)}) collective-permute-start(bf16[192,384]{1,0:T(8,128)(2,1)S(1)} %collective-permute-done.1.refs_1_), channel_id=1, source_target_pairs={{0,16},{16,0},{1,17},{17,1},{2,18},{18,2},{3,19},{19,3},{4,20},{20... | collective-permute-start | bytes 442376 | tf_op jit(solution)/shard_map/ppermute | solution.py:379
  21.8 7.7 %collective-permute-start.7 = (bf16[80,1536]{1,0:T(8,128)(2,1)S(1)}, bf16[80,1536]{1,0:T(8,128)(2,1)S(1)}, u32[]{:S(2)}, u32[]{:S(2)}) collective-permute-start(bf16[80,1536]{1,0:T(8,128)(2,1)S(1)} %get-tuple-element.87), channel_id=1, source_target_pairs={{0,2},{2,0},{4,6},{6,4},{8,10},{10,8},{12,14},{14,12},{1,3},{3,1},... | collective-permute-start | bytes 737288 | tf_op jit(solution)/shard_map/ppermute | solution.py:217
  22.9 7.2 %collective-permute-start.8 = (bf16[80,1536]{1,0:T(8,128)(2,1)S(1)}, bf16[80,1536]{1,0:T(8,128)(2,1)S(1)}, u32[]{:S(2)}, u32[]{:S(2)}) collective-permute-start(bf16[80,1536]{1,0:T(8,128)(2,1)S(1)} %get-tuple-element.89), channel_id=1, source_target_pairs={{0,4},{2,6},{4,0},{6,2},{8,12},{10,14},{12,8},{14,10},{1,5},{3,7},... | collective-permute-start | bytes 737288 | tf_op jit(solution)/shard_map/ppermute | solution.py:217
  24.4 8.1 %collective-permute-start.9 = (bf16[80,1536]{1,0:T(8,128)(2,1)S(1)}, bf16[80,1536]{1,0:T(8,128)(2,1)S(1)}, u32[]{:S(2)}, u32[]{:S(2)}) collective-permute-start(bf16[80,1536]{1,0:T(8,128)(2,1)S(1)} %get-tuple-element.90), channel_id=1, source_target_pairs={{0,6},{2,4},{4,2},{6,0},{8,14},{10,12},{12,10},{14,8},{1,7},{3,5},... | collective-permute-start | bytes 737288 | tf_op jit(solution)/shard_map/ppermute | solution.py:217
  32.4 22.5 %collective-permute-start.19 = (bf16[2,384,384]{2,1,0:T(8,128)(2,1)S(1)}, bf16[2,384,384]{2,1,0:T(8,128)(2,1)S(1)}, u32[]{:S(2)}, u32[]{:S(2)}) collective-permute-start(bf16[2,384,384]{2,1,0:T(8,128)(2,1)S(1)} %get-tuple-element.108), channel_id=1, source_target_pairs={{0,2},{2,0},{4,6},{6,4},{8,10},{10,8},{12,14},{14,12},{1,3},{3,1},... | collective-permute-start | bytes 1769480 | tf_op jit(solution)/shard_map/ppermute | solution.py:217
  32.4 13.5 %collective-permute-start.15 = (bf16[384,384]{1,0:T(8,128)(2,1)S(1)}, bf16[384,384]{1,0:T(8,128)(2,1)S(1)}, u32[]{:S(2)}, u32[]{:S(2)}) collective-permute-start(bf16[384,384]{1,0:T(8,128)(2,1)S(1)} %get-tuple-element.100), channel_id=1, source_target_pairs={{0,4},{2,6},{4,0},{6,2},{8,12},{10,14},{12,8},{14,10},{1,5},{3,7},... | collective-permute-start | bytes 884744 | tf_op jit(solution)/shard_map/ppermute | solution.py:217
  32.9 19.5 %collective-permute-start.16 = (bf16[384,384]{1,0:T(8,128)(2,1)S(1)}, bf16[384,384]{1,0:T(8,128)(2,1)S(1)}, u32[]{:S(2)}, u32[]{:S(2)}) collective-permute-start(bf16[384,384]{1,0:T(8,128)(2,1)S(1)} %get-tuple-element.101), channel_id=1, source_target_pairs={{0,6},{2,4},{4,2},{6,0},{8,14},{10,12},{12,10},{14,8},{1,7},{3,5},... | collective-permute-start | bytes 884744 | tf_op jit(solution)/shard_map/ppermute | solution.py:217
  37.1 15.3 %collective-permute-start.14 = (bf16[272,384]{1,0:T(8,128)(2,1)S(1)}, bf16[272,384]{1,0:T(8,128)(2,1)S(1)}, u32[]{:S(2)}, u32[]{:S(2)}) collective-permute-start(bf16[272,384]{1,0:T(8,128)(2,1)S(1)} %get-tuple-element.97), channel_id=1, source_target_pairs={{0,8},{2,10},{4,12},{6,14},{8,0},{10,2},{12,4},{14,6},{1,9},{3,11}... | collective-permute-start | bytes 626696 | tf_op jit(solution)/shard_map/ppermute | solution.py:220
  53.3 7.6 %collective-permute-start.17 = (bf16[256,384]{1,0:T(8,128)(2,1)S(1)}, bf16[256,384]{1,0:T(8,128)(2,1)S(1)}, u32[]{:S(2)}, u32[]{:S(2)}) collective-permute-start(bf16[256,384]{1,0:T(8,128)(2,1)S(1)} %get-tuple-element.112.refs_0_), channel_id=1, source_target_pairs={{0,6},{2,4},{4,2},{6,0},{8,14},{10,12},{12,10},{14,8},{1,7},{3,5},... | collective-permute-start | bytes 589832 | tf_op jit(solution)/shard_map/ppermute | solution.py:217
  53.4 11.9 %collective-permute-start.20 = (bf16[384,384]{1,0:T(8,128)(2,1)S(1)}, bf16[384,384]{1,0:T(8,128)(2,1)S(1)}, u32[]{:S(2)}, u32[]{:S(2)}) collective-permute-start(bf16[384,384]{1,0:T(8,128)(2,1)S(1)} %collective-permute-done.15.refs_7_.refs_2_), channel_id=1, source_target_pairs={{0,16},{16,0},{1,17},{17,1},{2,18},{18,2},{3,19},{19,3},{4,20},{20... | collective-permute-start | bytes 884744 | tf_op jit(solution)/shard_map/ppermute | solution.py:452
  54.7 11.4 %collective-permute-start.21 = (bf16[384,384]{1,0:T(8,128)(2,1)S(1)}, bf16[384,384]{1,0:T(8,128)(2,1)S(1)}, u32[]{:S(2)}, u32[]{:S(2)}) collective-permute-start(bf16[384,384]{1,0:T(8,128)(2,1)S(1)} %collective-permute-done.16.refs_8_.refs_3_), channel_id=1, source_target_pairs={{0,16},{16,0},{1,17},{17,1},{2,18},{18,2},{3,19},{19,3},{4,20},{20... | collective-permute-start | bytes 884744 | tf_op jit(solution)/shard_map/ppermute | solution.py:452
  54.9 10.4 %collective-permute-start.22 = (bf16[256,384]{1,0:T(8,128)(2,1)S(1)}, bf16[256,384]{1,0:T(8,128)(2,1)S(1)}, u32[]{:S(2)}, u32[]{:S(2)}) collective-permute-start(bf16[256,384]{1,0:T(8,128)(2,1)S(1)} %get-tuple-element.112.refs_0_), channel_id=1, source_target_pairs={{0,2},{2,0},{4,6},{6,4},{8,10},{10,8},{12,14},{14,12},{1,3},{3,1},... | collective-permute-start | bytes 589832 | tf_op jit(solution)/shard_map/ppermute | solution.py:217
  55.0 10.3 %collective-permute-start.23 = (bf16[256,384]{1,0:T(8,128)(2,1)S(1)}, bf16[256,384]{1,0:T(8,128)(2,1)S(1)}, u32[]{:S(2)}, u32[]{:S(2)}) collective-permute-start(bf16[256,384]{1,0:T(8,128)(2,1)S(1)} %get-tuple-element.112.refs_0_), channel_id=1, source_target_pairs={{0,4},{2,6},{4,0},{6,2},{8,12},{10,14},{12,8},{14,10},{1,5},{3,7},... | collective-permute-start | bytes 589832 | tf_op jit(solution)/shard_map/ppermute | solution.py:217
  60.9 10.0 %collective-permute-start.18 = (bf16[256,384]{1,0:T(8,128)(2,1)S(1)}, bf16[256,384]{1,0:T(8,128)(2,1)S(1)}, u32[]{:S(2)}, u32[]{:S(2)}) collective-permute-start(bf16[256,384]{1,0:T(8,128)(2,1)S(1)} %get-tuple-element.112.refs_0_), channel_id=1, source_target_pairs={{0,0},{1,8},{2,2},{3,10},{4,4},{5,12},{6,6},{7,14},{8,1},{9,9},{10... | collective-permute-start | bytes 589832 | tf_op jit(solution)/shard_map/ppermute | solution.py:226
  71.2 16.0 %collective-permute-start.24 = (bf16[272,384]{1,0:T(8,128)(2,1)S(1)}, bf16[272,384]{1,0:T(8,128)(2,1)S(1)}, u32[]{:S(2)}, u32[]{:S(2)}) collective-permute-start(bf16[272,384]{1,0:T(8,128)(2,1)S(1)} %get-tuple-element.116), channel_id=1, source_target_pairs={{0,8},{2,10},{4,12},{6,14},{8,0},{10,2},{12,4},{14,6},{1,9},{3,11}... | collective-permute-start | bytes 626696 | tf_op jit(solution)/shard_map/ppermute | solution.py:220
  76.8 14.6 %collective-permute-start.29 = (bf16[256,384]{1,0:T(8,128)(2,1)S(1)}, bf16[256,384]{1,0:T(8,128)(2,1)S(1)}, u32[]{:S(2)}, u32[]{:S(2)}) collective-permute-start(bf16[256,384]{1,0:T(8,128)(2,1)S(1)} %get-tuple-element.138), channel_id=1, source_target_pairs={{0,8},{2,10},{4,12},{6,14},{8,0},{10,2},{12,4},{14,6},{1,9},{3,11}... | collective-permute-start | bytes 589832 | tf_op jit(solution)/shard_map/ppermute | solution.py:220
  88.8 6.7 %collective-permute-start.26 = (bf16[128,384]{1,0:T(8,128)(2,1)S(1)}, bf16[128,384]{1,0:T(8,128)(2,1)S(1)}, u32[]{:S(2)}, u32[]{:S(2)}) collective-permute-start(bf16[128,384]{1,0:T(8,128)(2,1)S(1)} %get-tuple-element.122), channel_id=1, source_target_pairs={{0,4},{2,6},{4,0},{6,2},{8,12},{10,14},{12,8},{14,10},{1,5},{3,7},... | collective-permute-start | bytes 294920 | tf_op jit(solution)/shard_map/ppermute | solution.py:217
  88.8 6.6 %collective-permute-start.27 = (bf16[128,384]{1,0:T(8,128)(2,1)S(1)}, bf16[128,384]{1,0:T(8,128)(2,1)S(1)}, u32[]{:S(2)}, u32[]{:S(2)}) collective-permute-start(bf16[128,384]{1,0:T(8,128)(2,1)S(1)} %get-tuple-element.123), channel_id=1, source_target_pairs={{0,6},{2,4},{4,2},{6,0},{8,14},{10,12},{12,10},{14,8},{1,7},{3,5},... | collective-permute-start | bytes 294920 | tf_op jit(solution)/shard_map/ppermute | solution.py:217
  93.1 5.5 %collective-permute-start.32 = (bf16[80,384]{1,0:T(8,128)(2,1)S(1)}, bf16[80,384]{1,0:T(8,128)(2,1)S(1)}, u32[]{:S(2)}, u32[]{:S(2)}) collective-permute-start(bf16[80,384]{1,0:T(8,128)(2,1)S(1)} %get-tuple-element.144), channel_id=1, source_target_pairs={{0,6},{2,4},{4,2},{6,0},{8,14},{10,12},{12,10},{14,8},{1,7},{3,5},... | collective-permute-start | bytes 184328 | tf_op jit(solution)/shard_map/ppermute | solution.py:217
  (20 other events, 178.0 us)

commit v9 on v8

--- a/solution.py
+++ b/solution.py
@@ -446,8 +446,8 @@
             made = keep[band(j), :] + came[band(j), :].astype(f32)
             noised[band(j), :] = (base[band(j), :] + (stay * inverse[band(j), :]) * made).astype(bf16)
 
-    came, *fetched = lax.optimization_barrier((across(away), *score_mine[shared:g]))
-    score_mine[shared:g] = fetched
+    came, *fetched = lax.optimization_barrier((across(away), *score_mine[shared : g - 1]))
+    score_mine[shared : g - 1] = fetched
     for k in range(shared, g):
         score_mine.append(lax.ppermute(score_mine[k], "rep", [(0, 1), (1, 0)]))
     noised_mine, x_root = call(
@@ -501,7 +501,7 @@
 
         pack(rows, store)
 
-    noised_home, noised[3] = lax.optimization_barrier((noised_mine, noised[3]))
+    noised_home, noised[2] = lax.optimization_barrier((noised_mine, noised[2]))
     gap_here, away_here, noised_sums, lifts = call(
         score_kernel,
         noised + [scales] + score_mine,

time: 105 us -> 103 us (0.981)
  waiting for transfers between devices: 52.6 us -> 44.5 us
  starting transfers between devices: 37.1 us -> 43.2 us
    ppermute x18, waiting for transfers between devices: 25.3 us -> 15.5 us  [in_square(): return lax.ppermute(value, 'fsdp', [(i, i ^ k) for i in range(2 * g)])]
    ppermute x3, starting transfers between devices: 11.4 us -> 15.2 us  [turned(): lax.ppermute(value, ('fsdp', 'mp'), [(flat(*i), flat(i[2], i[1], i[0])) f...]
    ppermute x3, waiting for transfers between devices: 10.3 us -> 13.9 us  [across(): return lax.ppermute(value, 'fsdp', [(i, i ^ g) for i in range(2 * g)])]
    ppermute x3, starting transfers between devices: 1.01 us -> 3.51 us  [across(): return lax.ppermute(value, 'fsdp', [(i, i ^ g) for i in range(2 * g)])]
    ppermute x6, waiting for transfers between devices: 5.35 us -> 3.89 us  [cores(): return lax.ppermute(value, 'mp', [(0, 1), (1, 0)])]
  transfers between devices with their start and end apart: 34 -> 34, of which waited for: 17 -> 16; matrix products, arithmetic and copies ran while one was open for 1% -> 1% of each run, Pallas kernels for 8% -> 9%
where the time goes in v9:
time: 103 us
  waiting for transfers between devices  44.5 us (43%)
  starting transfers between devices  43.2 us (42%)
  Pallas kernels  10.6 us (10%)
  local copies, waits for them, and re-layouts  2.42 us (2%)
    ppermute x18, starting transfers between devices, in_square(): return lax.ppermute(value, 'fsdp', [(i, i ^ k) for i in range(2 * g)])  16.6 us
    ppermute x18, waiting for transfers between devices, in_square(): return lax.ppermute(value, 'fsdp', [(i, i ^ k) for i in range(2 * g)])  15.5 us
    ppermute x3, starting transfers between devices, turned(): lax.ppermute(value, ('fsdp', 'mp'), [(flat(*i), flat(i[2], i[1], i[0])) f...  15.2 us
    ppermute x3, waiting for transfers between devices, across(): return lax.ppermute(value, 'fsdp', [(i, i ^ g) for i in range(2 * g)])  13.9 us
    pallas_call x13, Pallas kernels, call(): pl.pallas_call(kernel, in_specs=[scalars] * in_scalars + [whole] * (len(o...  10.1 us
    ppermute x3, waiting for transfers between devices, turned(): lax.ppermute(value, ('fsdp', 'mp'), [(flat(*i), flat(i[2], i[1], i[0])) f...  9.7 us
    ppermute x6, starting transfers between devices, cores(): return lax.ppermute(value, 'mp', [(0, 1), (1, 0)])  4.88 us
    ppermute x6, waiting for transfers between devices, cores(): return lax.ppermute(value, 'mp', [(0, 1), (1, 0)])  3.89 us
  transfers between devices with their start and end apart: 34, of which 16 were waited for; matrix products, arithmetic and copies ran while one was open for 1% of the time, Pallas kernels for 9%

profile of v9, /device:TPU:1, one launch (start us, length us, event | category | flops | bytes accessed | tf_op | source)
XLA Modules:
  0.0 102.6 jit_solution(8765847889547694954)
XLA Ops:
  2.0 2.2 %collective-permute-start = (bf16[192,384]{1,0:T(8,128)(2,1)S(1)}, bf16[192,384]{1,0:T(8,128)(2,1)S(1)}, u32[]{:S(2)}, u32[]{:S(2)}) collective-permute-start(bf16[192,384]{1,0:T(8,128)(2,1)S(1)} %get-tuple-element.76), channel_id=1, source_target_pairs={{0,4},{2,6},{4,0},{6,2},{8,12},{10,14},{12,8},{14,10},{1,5},{3,7},... | collective-permute-start | bytes 442376 | tf_op jit(solution)/shard_map/ppermute | solution.py:217
  5.3 5.3 %collective-permute-start.2 = (bf16[64,1536]{1,0:T(8,128)(2,1)}, bf16[64,1536]{1,0:T(8,128)(2,1)S(1)}, u32[]{:S(2)}, u32[]{:S(2)}) collective-permute-start(bf16[64,1536]{1,0:T(8,128)(2,1)} %param.13), channel_id=1, source_target_pairs={{0,0},{1,8},{2,2},{3,10},{4,4},{5,12},{6,6},{7,14},{8,1},{9,9},{10... | collective-permute-start | bytes 589832 | tf_op jit(solution)/shard_map/ppermute | solution.py:226
  10.7 1.9 %collective-permute-start.3 = (bf16[64,1536]{1,0:T(8,128)(2,1)}, bf16[64,1536]{1,0:T(8,128)(2,1)S(1)}, u32[]{:S(2)}, u32[]{:S(2)}) collective-permute-start(bf16[64,1536]{1,0:T(8,128)(2,1)} %param.14), channel_id=1, source_target_pairs={{0,0},{1,8},{2,2},{3,10},{4,4},{5,12},{6,6},{7,14},{8,1},{9,9},{10... | collective-permute-start | bytes 589832 | tf_op jit(solution)/shard_map/ppermute | solution.py:226
  13.7 2.6 %collective-permute-done.2.rows = bf16[64,1536]{1,0:T(8,128)(2,1)S(1)} collective-permute-done((bf16[64,1536]{1,0:T(8,128)(2,1)}, bf16[64,1536]{1,0:T(8,128)(2,1)S(1)}, u32[]{:S(2)}, u32[]{:S(2)}) %collective-permute-start.2) | collective-permute-done | bytes 196640 | tf_op jit(solution)/shard_map/ppermute | solution.py:226
  16.3 3.9 %collective-permute-done.3.fresh = bf16[64,1536]{1,0:T(8,128)(2,1)S(1)} collective-permute-done((bf16[64,1536]{1,0:T(8,128)(2,1)}, bf16[64,1536]{1,0:T(8,128)(2,1)S(1)}, u32[]{:S(2)}, u32[]{:S(2)}) %collective-permute-start.3) | collective-permute-done | bytes 196640 | tf_op jit(solution)/shard_map/ppermute | solution.py:226
  20.3 1.3 %collective-permute-start.5 = (bf16[192,384]{1,0:T(8,128)(2,1)S(1)}, bf16[192,384]{1,0:T(8,128)(2,1)S(1)}, u32[]{:S(2)}, u32[]{:S(2)}) collective-permute-start(bf16[192,384]{1,0:T(8,128)(2,1)S(1)} %collective-permute-done.refs_0_), channel_id=1, source_target_pairs={{0,16},{16,0},{1,17},{17,1},{2,18},{18,2},{3,19},{19,3},{4,20},{20... | collective-permute-start | bytes 442376 | tf_op jit(solution)/shard_map/ppermute | solution.py:379
  27.5 2.1 %collective-permute-done.7.refs_1_ = bf16[80,1536]{1,0:T(8,128)(2,1)S(1)} collective-permute-done((bf16[80,1536]{1,0:T(8,128)(2,1)S(1)}, bf16[80,1536]{1,0:T(8,128)(2,1)S(1)}, u32[]{:S(2)}, u32[]{:S(2)}) %collective-permute-start.7) | collective-permute-done | bytes 245792 | tf_op jit(solution)/shard_map/ppermute | solution.py:217
  30.7 1.7 %collective-permute-done.9.refs_3_ = bf16[80,1536]{1,0:T(8,128)(2,1)S(1)} collective-permute-done((bf16[80,1536]{1,0:T(8,128)(2,1)S(1)}, bf16[80,1536]{1,0:T(8,128)(2,1)S(1)}, u32[]{:S(2)}, u32[]{:S(2)}) %collective-permute-start.9) | collective-permute-done | bytes 245792 | tf_op jit(solution)/shard_map/ppermute | solution.py:217
  32.9 2.2 %collective-permute-start.19 = (bf16[384,384]{1,0:T(8,128)(2,1)S(1)}, bf16[384,384]{1,0:T(8,128)(2,1)S(1)}, u32[]{:S(2)}, u32[]{:S(2)}) collective-permute-start(bf16[384,384]{1,0:T(8,128)(2,1)S(1)} %get-tuple-element.109), channel_id=1, source_target_pairs={{0,6},{2,4},{4,2},{6,0},{8,14},{10,12},{12,10},{14,8},{1,7},{3,5},... | collective-permute-start | bytes 884744 | tf_op jit(solution)/shard_map/ppermute | solution.py:217
  35.1 2.0 %shard_map.152 = (f32[256,384]{1,0:T(8,128)S(1)}, bf16[272,384]{1,0:T(8,128)(2,1)S(1)}, f32[8,256]{1,0:T(8,128)S(1)}, f32[256,384]{1,0:T(8,128)S(1)}) custom-call(s32[8]{0:T(128)S(1)} %copy-done.9, bf16[80,1536]{1,0:T(8,128)(2,1)S(1)} %get-tuple-element.79.refs_0_, bf16[80,1536]{1,0:T(8,128)(2,1)S(1)} %collective-permute-done.7.refs_1_, ...), custom_call_target="tpu_custom_call" | custom-call | flops 603979776 | bytes 3538976 | tf_op jit(solution)/shard_map/pallas_call | solution.py:233
  37.7 8.2 %collective-permute-done.15.refs_7_.refs_2_ = bf16[384,384]{1,0:T(8,128)(2,1)S(1)} collective-permute-done((bf16[384,384]{1,0:T(8,128)(2,1)S(1)}, bf16[384,384]{1,0:T(8,128)(2,1)S(1)}, u32[]{:S(2)}, u32[]{:S(2)}) %collective-permute-start.15) | collective-permute-done | bytes 294944 | tf_op jit(solution)/shard_map/ppermute | solution.py:217
  45.9 4.1 %collective-permute-done.14.came = bf16[272,384]{1,0:T(8,128)(2,1)S(1)} collective-permute-done((bf16[272,384]{1,0:T(8,128)(2,1)S(1)}, bf16[272,384]{1,0:T(8,128)(2,1)S(1)}, u32[]{:S(2)}, u32[]{:S(2)}) %collective-permute-start.14) | collective-permute-done | bytes 208928 | tf_op jit(solution)/shard_map/ppermute | solution.py:220
  55.4 7.9 %collective-permute-start.17 = (bf16[256,384]{1,0:T(8,128)(2,1)S(1)}, bf16[256,384]{1,0:T(8,128)(2,1)S(1)}, u32[]{:S(2)}, u32[]{:S(2)}) collective-permute-start(bf16[256,384]{1,0:T(8,128)(2,1)S(1)} %get-tuple-element.110.refs_0_), channel_id=1, source_target_pairs={{0,0},{1,8},{2,2},{3,10},{4,4},{5,12},{6,6},{7,14},{8,1},{9,9},{10... | collective-permute-start | bytes 589832 | tf_op jit(solution)/shard_map/ppermute | solution.py:226
  65.4 3.2 %collective-permute-done.17.owned = bf16[256,384]{1,0:T(8,128)(2,1)S(1)} collective-permute-done((bf16[256,384]{1,0:T(8,128)(2,1)S(1)}, bf16[256,384]{1,0:T(8,128)(2,1)S(1)}, u32[]{:S(2)}, u32[]{:S(2)}) %collective-permute-start.17) | collective-permute-done | bytes 196640 | tf_op jit(solution)/shard_map/ppermute | solution.py:226
  69.7 1.4 %collective-permute-start.24 = (bf16[272,384]{1,0:T(8,128)(2,1)S(1)}, bf16[272,384]{1,0:T(8,128)(2,1)S(1)}, u32[]{:S(2)}, u32[]{:S(2)}) collective-permute-start(bf16[272,384]{1,0:T(8,128)(2,1)S(1)} %get-tuple-element.114), channel_id=1, source_target_pairs={{0,8},{2,10},{4,12},{6,14},{8,0},{10,2},{12,4},{14,6},{1,9},{3,11}... | collective-permute-start | bytes 626696 | tf_op jit(solution)/shard_map/ppermute | solution.py:220
  71.1 2.7 %collective-permute-done.28.other = bf16[8,384,384]{2,1,0:T(8,128)(2,1)S(1)} collective-permute-done((bf16[8,384,384]{2,1,0:T(8,128)(2,1)S(1)}, bf16[8,384,384]{2,1,0:T(8,128)(2,1)S(1)}, u32[]{:S(2)}, u32[]{:S(2)}) %collective-permute-start.28) | collective-permute-done | bytes 2359328 | tf_op jit(solution)/shard_map/ppermute | solution.py:223
  75.0 1.5 %collective-permute-start.29 = (bf16[256,384]{1,0:T(8,128)(2,1)S(1)}, bf16[256,384]{1,0:T(8,128)(2,1)S(1)}, u32[]{:S(2)}, u32[]{:S(2)}) collective-permute-start(bf16[256,384]{1,0:T(8,128)(2,1)S(1)} %get-tuple-element.136), channel_id=1, source_target_pairs={{0,8},{2,10},{4,12},{6,14},{8,0},{10,2},{12,4},{14,6},{1,9},{3,11}... | collective-permute-start | bytes 589832 | tf_op jit(solution)/shard_map/ppermute | solution.py:220
  76.5 9.8 %collective-permute-done.24.came = bf16[272,384]{1,0:T(8,128)(2,1)S(1)} collective-permute-done((bf16[272,384]{1,0:T(8,128)(2,1)S(1)}, bf16[272,384]{1,0:T(8,128)(2,1)S(1)}, u32[]{:S(2)}, u32[]{:S(2)}) %collective-permute-start.24) | collective-permute-done | bytes 208928 | tf_op jit(solution)/shard_map/ppermute | solution.py:220
  86.3 1.5 %shard_map.156 = (bf16[128,384]{1,0:T(8,128)(2,1)S(1)}, bf16[128,384]{1,0:T(8,128)(2,1)S(1)}, bf16[128,384]{1,0:T(8,128)(2,1)S(1)}, bf16[128,384]{1,0:T(8,128)(2...) custom-call(s32[8]{0:T(128)S(1)} %copy-done.9, f32[256,384]{1,0:T(8,128)S(1)} %get-tuple-element.113.gap, ...), custom_call_target="tpu_custom_call" | custom-call | flops 301989888 | bytes 3297312 | tf_op jit(solution)/shard_map/pallas_call | solution.py:233
  88.2 2.3 %collective-permute-start.27 = (bf16[128,384]{1,0:T(8,128)(2,1)S(1)}, bf16[128,384]{1,0:T(8,128)(2,1)S(1)}, u32[]{:S(2)}, u32[]{:S(2)}) collective-permute-start(bf16[128,384]{1,0:T(8,128)(2,1)S(1)} %get-tuple-element.121), channel_id=1, source_target_pairs={{0,6},{2,4},{4,2},{6,0},{8,14},{10,12},{12,10},{14,8},{1,7},{3,5},... | collective-permute-start | bytes 294920 | tf_op jit(solution)/shard_map/ppermute | solution.py:217
  90.5 1.3 %shard_map.159 = (bf16[80,384]{1,0:T(8,128)(2,1)S(1)}, bf16[80,384]{1,0:T(8,128)(2,1)S(1)}, bf16[80,384]{1,0:T(8,128)(2,1)S(1)}, bf16[80,384]{1,0:T(8,128)(2,1)S(1)}) custom-call(s32[8]{0:T(128)S(1)} %copy-done.9, f32[256,384]{1,0:T(8,128)S(1)} %get-tuple-element.135.gap, bf16[256,384]{1,0:T(8,128)(2,1)S(1)} %collective-permute-done.29.came, ...), custom_call_target="tpu_custom_call" | custom-call | flops 301989888 | bytes 3223584 | tf_op jit(solution)/shard_map/pallas_call | solution.py:233
  92.3 2.3 %collective-permute-start.32 = (bf16[80,384]{1,0:T(8,128)(2,1)S(1)}, bf16[80,384]{1,0:T(8,128)(2,1)S(1)}, u32[]{:S(2)}, u32[]{:S(2)}) collective-permute-start(bf16[80,384]{1,0:T(8,128)(2,1)S(1)} %get-tuple-element.142), channel_id=1, source_target_pairs={{0,6},{2,4},{4,2},{6,0},{8,14},{10,12},{12,10},{14,8},{1,7},{3,5},... | collective-permute-start | bytes 184328 | tf_op jit(solution)/shard_map/ppermute | solution.py:217
  94.6 1.5 %collective-permute-done.30.refs_5_ = bf16[80,384]{1,0:T(8,128)(2,1)S(1)} collective-permute-done((bf16[80,384]{1,0:T(8,128)(2,1)S(1)}, bf16[80,384]{1,0:T(8,128)(2,1)S(1)}, u32[]{:S(2)}, u32[]{:S(2)}) %collective-permute-start.30) | collective-permute-done | bytes 61472 | tf_op jit(solution)/shard_map/ppermute | solution.py:217
  97.8 2.9 %collective-permute-start.33 = (bf16[80,1536]{1,0:T(8,128)(2,1)S(1)}, bf16[80,1536]{1,0:T(8,128)(2,1)S(1)}, u32[]{:S(2)}, u32[]{:S(2)}) collective-permute-start(bf16[80,1536]{1,0:T(8,128)(2,1)S(1)} %get-tuple-element.146), channel_id=1, source_target_pairs={{0,1},{1,0},{2,3},{3,2},{4,5},{5,4},{6,7},{7,6},{8,9},{9,8},{10,11... | collective-permute-start | bytes 737288 | tf_op jit(solution)/shard_map/ppermute | solution.py:223
  (82 shorter events, 25.8 us)
Async XLA Ops:
  2.0 18.3 %collective-permute-start = (bf16[192,384]{1,0:T(8,128)(2,1)S(1)}, bf16[192,384]{1,0:T(8,128)(2,1)S(1)}, u32[]{:S(2)}, u32[]{:S(2)}) collective-permute-start(bf16[192,384]{1,0:T(8,128)(2,1)S(1)} %get-tuple-element.76), channel_id=1, source_target_pairs={{0,4},{2,6},{4,0},{6,2},{8,12},{10,14},{12,8},{14,10},{1,5},{3,7},... | collective-permute-start | bytes 442376 | tf_op jit(solution)/shard_map/ppermute | solution.py:217
  4.2 16.1 %collective-permute-start.1 = (bf16[192,384]{1,0:T(8,128)(2,1)S(1)}, bf16[192,384]{1,0:T(8,128)(2,1)S(1)}, u32[]{:S(2)}, u32[]{:S(2)}) collective-permute-start(bf16[192,384]{1,0:T(8,128)(2,1)S(1)} %get-tuple-element.77), channel_id=1, source_target_pairs={{0,6},{2,4},{4,2},{6,0},{8,14},{10,12},{12,10},{14,8},{1,7},{3,5},... | collective-permute-start | bytes 442376 | tf_op jit(solution)/shard_map/ppermute | solution.py:217
  5.3 11.0 %collective-permute-start.2 = (bf16[64,1536]{1,0:T(8,128)(2,1)}, bf16[64,1536]{1,0:T(8,128)(2,1)S(1)}, u32[]{:S(2)}, u32[]{:S(2)}) collective-permute-start(bf16[64,1536]{1,0:T(8,128)(2,1)} %param.13), channel_id=1, source_target_pairs={{0,0},{1,8},{2,2},{3,10},{4,4},{5,12},{6,6},{7,14},{8,1},{9,9},{10... | collective-permute-start | bytes 589832 | tf_op jit(solution)/shard_map/ppermute | solution.py:226
  10.7 9.6 %collective-permute-start.3 = (bf16[64,1536]{1,0:T(8,128)(2,1)}, bf16[64,1536]{1,0:T(8,128)(2,1)S(1)}, u32[]{:S(2)}, u32[]{:S(2)}) collective-permute-start(bf16[64,1536]{1,0:T(8,128)(2,1)} %param.14), channel_id=1, source_target_pairs={{0,0},{1,8},{2,2},{3,10},{4,4},{5,12},{6,6},{7,14},{8,1},{9,9},{10... | collective-permute-start | bytes 589832 | tf_op jit(solution)/shard_map/ppermute | solution.py:226
  12.6 14.9 %collective-permute-start.4 = (bf16[384,384]{1,0:T(8,128)(2,1)S(1)}, bf16[384,384]{1,0:T(8,128)(2,1)S(1)}, u32[]{:S(2)}, u32[]{:S(2)}) collective-permute-start(bf16[384,384]{1,0:T(8,128)(2,1)S(1)} %get-tuple-element.81), channel_id=1, source_target_pairs={{0,2},{2,0},{4,6},{6,4},{8,10},{10,8},{12,14},{14,12},{1,3},{3,1},... | collective-permute-start | bytes 884744 | tf_op jit(solution)/shard_map/ppermute | solution.py:217
  21.6 5.8 %collective-permute-start.6 = (bf16[192,384]{1,0:T(8,128)(2,1)S(1)}, bf16[192,384]{1,0:T(8,128)(2,1)S(1)}, u32[]{:S(2)}, u32[]{:S(2)}) collective-permute-start(bf16[192,384]{1,0:T(8,128)(2,1)S(1)} %collective-permute-done.1.refs_1_), channel_id=1, source_target_pairs={{0,16},{16,0},{1,17},{17,1},{2,18},{18,2},{3,19},{19,3},{4,20},{20... | collective-permute-start | bytes 442376 | tf_op jit(solution)/shard_map/ppermute | solution.py:379
  21.8 7.7 %collective-permute-start.7 = (bf16[80,1536]{1,0:T(8,128)(2,1)S(1)}, bf16[80,1536]{1,0:T(8,128)(2,1)S(1)}, u32[]{:S(2)}, u32[]{:S(2)}) collective-permute-start(bf16[80,1536]{1,0:T(8,128)(2,1)S(1)} %get-tuple-element.86), channel_id=1, source_target_pairs={{0,2},{2,0},{4,6},{6,4},{8,10},{10,8},{12,14},{14,12},{1,3},{3,1},... | collective-permute-start | bytes 737288 | tf_op jit(solution)/shard_map/ppermute | solution.py:217
  22.9 7.2 %collective-permute-start.8 = (bf16[80,1536]{1,0:T(8,128)(2,1)S(1)}, bf16[80,1536]{1,0:T(8,128)(2,1)S(1)}, u32[]{:S(2)}, u32[]{:S(2)}) collective-permute-start(bf16[80,1536]{1,0:T(8,128)(2,1)S(1)} %get-tuple-element.88), channel_id=1, source_target_pairs={{0,4},{2,6},{4,0},{6,2},{8,12},{10,14},{12,8},{14,10},{1,5},{3,7},... | collective-permute-start | bytes 737288 | tf_op jit(solution)/shard_map/ppermute | solution.py:217
  24.4 8.1 %collective-permute-start.9 = (bf16[80,1536]{1,0:T(8,128)(2,1)S(1)}, bf16[80,1536]{1,0:T(8,128)(2,1)S(1)}, u32[]{:S(2)}, u32[]{:S(2)}) collective-permute-start(bf16[80,1536]{1,0:T(8,128)(2,1)S(1)} %get-tuple-element.89), channel_id=1, source_target_pairs={{0,6},{2,4},{4,2},{6,0},{8,14},{10,12},{12,10},{14,8},{1,7},{3,5},... | collective-permute-start | bytes 737288 | tf_op jit(solution)/shard_map/ppermute | solution.py:217
  30.0 5.1 %collective-permute-start.12 = (bf16[384,384]{1,0:T(8,128)(2,1)S(1)}, bf16[384,384]{1,0:T(8,128)(2,1)S(1)}, u32[]{:S(2)}, u32[]{:S(2)}) collective-permute-start(bf16[384,384]{1,0:T(8,128)(2,1)S(1)} %get-tuple-element.93.refs_7_.refs_6_), channel_id=1, source_target_pairs={{0,1},{1,0},{2,3},{3,2},{4,5},{5,4},{6,7},{7,6},{8,9},{9,8},{10,11... | collective-permute-start | bytes 884744 | tf_op jit(solution)/shard_map/ppermute | solution.py:223
  32.4 21.4 %collective-permute-start.18 = (bf16[2,384,384]{2,1,0:T(8,128)(2,1)S(1)}, bf16[2,384,384]{2,1,0:T(8,128)(2,1)S(1)}, u32[]{:S(2)}, u32[]{:S(2)}) collective-permute-start(bf16[2,384,384]{2,1,0:T(8,128)(2,1)S(1)} %get-tuple-element.106), channel_id=1, source_target_pairs={{0,2},{2,0},{4,6},{6,4},{8,10},{10,8},{12,14},{14,12},{1,3},{3,1},... | collective-permute-start | bytes 1769480 | tf_op jit(solution)/shard_map/ppermute | solution.py:217
  32.4 13.5 %collective-permute-start.15 = (bf16[384,384]{1,0:T(8,128)(2,1)S(1)}, bf16[384,384]{1,0:T(8,128)(2,1)S(1)}, u32[]{:S(2)}, u32[]{:S(2)}) collective-permute-start(bf16[384,384]{1,0:T(8,128)(2,1)S(1)} %get-tuple-element.99), channel_id=1, source_target_pairs={{0,4},{2,6},{4,0},{6,2},{8,12},{10,14},{12,8},{14,10},{1,5},{3,7},... | collective-permute-start | bytes 884744 | tf_op jit(solution)/shard_map/ppermute | solution.py:217
  32.9 19.5 %collective-permute-start.19 = (bf16[384,384]{1,0:T(8,128)(2,1)S(1)}, bf16[384,384]{1,0:T(8,128)(2,1)S(1)}, u32[]{:S(2)}, u32[]{:S(2)}) collective-permute-start(bf16[384,384]{1,0:T(8,128)(2,1)S(1)} %get-tuple-element.109), channel_id=1, source_target_pairs={{0,6},{2,4},{4,2},{6,0},{8,14},{10,12},{12,10},{14,8},{1,7},{3,5},... | collective-permute-start | bytes 884744 | tf_op jit(solution)/shard_map/ppermute | solution.py:217
  37.1 12.9 %collective-permute-start.14 = (bf16[272,384]{1,0:T(8,128)(2,1)S(1)}, bf16[272,384]{1,0:T(8,128)(2,1)S(1)}, u32[]{:S(2)}, u32[]{:S(2)}) collective-permute-start(bf16[272,384]{1,0:T(8,128)(2,1)S(1)} %get-tuple-element.96), channel_id=1, source_target_pairs={{0,8},{2,10},{4,12},{6,14},{8,0},{10,2},{12,4},{14,6},{1,9},{3,11}... | collective-permute-start | bytes 626696 | tf_op jit(solution)/shard_map/ppermute | solution.py:220
  52.4 11.0 %collective-permute-start.21 = (bf16[384,384]{1,0:T(8,128)(2,1)S(1)}, bf16[384,384]{1,0:T(8,128)(2,1)S(1)}, u32[]{:S(2)}, u32[]{:S(2)}) collective-permute-start(bf16[384,384]{1,0:T(8,128)(2,1)S(1)} %collective-permute-done.19.refs_8_.refs_3_), channel_id=1, source_target_pairs={{0,16},{16,0},{1,17},{17,1},{2,18},{18,2},{3,19},{19,3},{4,20},{20... | collective-permute-start | bytes 884744 | tf_op jit(solution)/shard_map/ppermute | solution.py:452
  53.6 10.4 %collective-permute-start.20 = (bf16[384,384]{1,0:T(8,128)(2,1)S(1)}, bf16[384,384]{1,0:T(8,128)(2,1)S(1)}, u32[]{:S(2)}, u32[]{:S(2)}) collective-permute-start(bf16[384,384]{1,0:T(8,128)(2,1)S(1)} %collective-permute-done.15.refs_7_.refs_2_), channel_id=1, source_target_pairs={{0,16},{16,0},{1,17},{17,1},{2,18},{18,2},{3,19},{19,3},{4,20},{20... | collective-permute-start | bytes 884744 | tf_op jit(solution)/shard_map/ppermute | solution.py:452
  53.9 9.5 %collective-permute-start.22 = (bf16[256,384]{1,0:T(8,128)(2,1)S(1)}, bf16[256,384]{1,0:T(8,128)(2,1)S(1)}, u32[]{:S(2)}, u32[]{:S(2)}) collective-permute-start(bf16[256,384]{1,0:T(8,128)(2,1)S(1)} %get-tuple-element.110.refs_0_), channel_id=1, source_target_pairs={{0,2},{2,0},{4,6},{6,4},{8,10},{10,8},{12,14},{14,12},{1,3},{3,1},... | collective-permute-start | bytes 589832 | tf_op jit(solution)/shard_map/ppermute | solution.py:217
  54.0 9.4 %collective-permute-start.23 = (bf16[256,384]{1,0:T(8,128)(2,1)S(1)}, bf16[256,384]{1,0:T(8,128)(2,1)S(1)}, u32[]{:S(2)}, u32[]{:S(2)}) collective-permute-start(bf16[256,384]{1,0:T(8,128)(2,1)S(1)} %get-tuple-element.110.refs_0_), channel_id=1, source_target_pairs={{0,6},{2,4},{4,2},{6,0},{8,14},{10,12},{12,10},{14,8},{1,7},{3,5},... | collective-permute-start | bytes 589832 | tf_op jit(solution)/shard_map/ppermute | solution.py:217
  55.4 13.1 %collective-permute-start.17 = (bf16[256,384]{1,0:T(8,128)(2,1)S(1)}, bf16[256,384]{1,0:T(8,128)(2,1)S(1)}, u32[]{:S(2)}, u32[]{:S(2)}) collective-permute-start(bf16[256,384]{1,0:T(8,128)(2,1)S(1)} %get-tuple-element.110.refs_0_), channel_id=1, source_target_pairs={{0,0},{1,8},{2,2},{3,10},{4,4},{5,12},{6,6},{7,14},{8,1},{9,9},{10... | collective-permute-start | bytes 589832 | tf_op jit(solution)/shard_map/ppermute | solution.py:226
  68.7 5.2 %collective-permute-start.28 = (bf16[8,384,384]{2,1,0:T(8,128)(2,1)S(1)}, bf16[8,384,384]{2,1,0:T(8,128)(2,1)S(1)}, u32[]{:S(2)}, u32[]{:S(2)}) collective-permute-start(bf16[8,384,384]{2,1,0:T(8,128)(2,1)S(1)} %shard_map.157), channel_id=1, source_target_pairs={{0,1},{1,0},{2,3},{3,2},{4,5},{5,4},{6,7},{7,6},{8,9},{9,8},{10,11... | collective-permute-start | bytes 7077896 | tf_op jit(solution)/shard_map/ppermute | solution.py:223
  69.7 16.6 %collective-permute-start.24 = (bf16[272,384]{1,0:T(8,128)(2,1)S(1)}, bf16[272,384]{1,0:T(8,128)(2,1)S(1)}, u32[]{:S(2)}, u32[]{:S(2)}) collective-permute-start(bf16[272,384]{1,0:T(8,128)(2,1)S(1)} %get-tuple-element.114), channel_id=1, source_target_pairs={{0,8},{2,10},{4,12},{6,14},{8,0},{10,2},{12,4},{14,6},{1,9},{3,11}... | collective-permute-start | bytes 626696 | tf_op jit(solution)/shard_map/ppermute | solution.py:220
  75.0 15.5 %collective-permute-start.29 = (bf16[256,384]{1,0:T(8,128)(2,1)S(1)}, bf16[256,384]{1,0:T(8,128)(2,1)S(1)}, u32[]{:S(2)}, u32[]{:S(2)}) collective-permute-start(bf16[256,384]{1,0:T(8,128)(2,1)S(1)} %get-tuple-element.136), channel_id=1, source_target_pairs={{0,8},{2,10},{4,12},{6,14},{8,0},{10,2},{12,4},{14,6},{1,9},{3,11}... | collective-permute-start | bytes 589832 | tf_op jit(solution)/shard_map/ppermute | solution.py:220
  87.9 6.7 %collective-permute-start.26 = (bf16[128,384]{1,0:T(8,128)(2,1)S(1)}, bf16[128,384]{1,0:T(8,128)(2,1)S(1)}, u32[]{:S(2)}, u32[]{:S(2)}) collective-permute-start(bf16[128,384]{1,0:T(8,128)(2,1)S(1)} %get-tuple-element.120), channel_id=1, source_target_pairs={{0,4},{2,6},{4,0},{6,2},{8,12},{10,14},{12,8},{14,10},{1,5},{3,7},... | collective-permute-start | bytes 294920 | tf_op jit(solution)/shard_map/ppermute | solution.py:217
  88.2 6.4 %collective-permute-start.27 = (bf16[128,384]{1,0:T(8,128)(2,1)S(1)}, bf16[128,384]{1,0:T(8,128)(2,1)S(1)}, u32[]{:S(2)}, u32[]{:S(2)}) collective-permute-start(bf16[128,384]{1,0:T(8,128)(2,1)S(1)} %get-tuple-element.121), channel_id=1, source_target_pairs={{0,6},{2,4},{4,2},{6,0},{8,14},{10,12},{12,10},{14,8},{1,7},{3,5},... | collective-permute-start | bytes 294920 | tf_op jit(solution)/shard_map/ppermute | solution.py:217
  (20 other events, 178.1 us)

commit v10 on v9

--- a/solution.py
+++ b/solution.py
@@ -446,10 +446,8 @@
             made = keep[band(j), :] + came[band(j), :].astype(f32)
             noised[band(j), :] = (base[band(j), :] + (stay * inverse[band(j), :]) * made).astype(bf16)
 
-    came, *fetched = lax.optimization_barrier((across(away), *score_mine[shared : g - 1]))
-    score_mine[shared : g - 1] = fetched
-    for k in range(shared, g):
-        score_mine.append(lax.ppermute(score_mine[k], "rep", [(0, 1), (1, 0)]))
+    score_mine += [lax.ppermute(v, "rep", [(0, 1), (1, 0)]) for v in score_mine[shared:g]]
+    came, score_mine[shared] = lax.optimization_barrier((across(away), score_mine[shared]))
     noised_mine, x_root = call(
         blend_kernel,
         [noise_step, keep, came, x_sums, base],

time: 103 us -> 103 us (level)
  waiting for transfers between devices: 44.5 us -> 42.5 us
  starting transfers between devices: 43.2 us -> 44.9 us
    ppermute x3, starting transfers between devices: 3.51 us -> 4.66 us  [across(): return lax.ppermute(value, 'fsdp', [(i, i ^ g) for i in range(2 * g)])]
  transfers between devices with their start and end apart: 34 -> 34, of which waited for: 16 -> 14; matrix products, arithmetic and copies ran while one was open for 1% -> 1% of each run, Pallas kernels for 9% -> 9%
where the time goes in v10:
time: 103 us; the launch traced here: 102 us
  starting transfers between devices  44.9 us (44%)
  waiting for transfers between devices  42.5 us (41%)
  Pallas kernels  10.6 us (10%)
  local copies, waits for them, and re-layouts  2.42 us (2%)
    ppermute x18, starting transfers between devices, in_square(): return lax.ppermute(value, 'fsdp', [(i, i ^ k) for i in range(2 * g)])  16.8 us
    ppermute x3, starting transfers between devices, turned(): lax.ppermute(value, ('fsdp', 'mp'), [(flat(*i), flat(i[2], i[1], i[0])) f...  15.2 us
    ppermute x18, waiting for transfers between devices, in_square(): return lax.ppermute(value, 'fsdp', [(i, i ^ k) for i in range(2 * g)])  15 us
    ppermute x3, waiting for transfers between devices, across(): return lax.ppermute(value, 'fsdp', [(i, i ^ g) for i in range(2 * g)])  12.9 us
    ppermute x3, waiting for transfers between devices, turned(): lax.ppermute(value, ('fsdp', 'mp'), [(flat(*i), flat(i[2], i[1], i[0])) f...  10.3 us
    pallas_call x13, Pallas kernels, call(): pl.pallas_call(kernel, in_specs=[scalars] * in_scalars + [whole] * (len(o...  10.1 us
    ppermute x6, starting transfers between devices, cores(): return lax.ppermute(value, 'mp', [(0, 1), (1, 0)])  4.86 us
    ppermute x3, starting transfers between devices, across(): return lax.ppermute(value, 'fsdp', [(i, i ^ g) for i in range(2 * g)])  4.66 us
  transfers between devices with their start and end apart: 34, of which 14 were waited for; matrix products, arithmetic and copies ran while one was open for 1% of the time, Pallas kernels for 9%

profile of v10, /device:TPU:1, one launch (start us, length us, event | category | flops | bytes accessed | tf_op | source)
XLA Modules:
  0.0 102.3 jit_solution(6314194674827664333)
XLA Ops:
  2.0 2.2 %collective-permute-start = (bf16[192,384]{1,0:T(8,128)(2,1)S(1)}, bf16[192,384]{1,0:T(8,128)(2,1)S(1)}, u32[]{:S(2)}, u32[]{:S(2)}) collective-permute-start(bf16[192,384]{1,0:T(8,128)(2,1)S(1)} %get-tuple-element.76), channel_id=1, source_target_pairs={{0,4},{2,6},{4,0},{6,2},{8,12},{10,14},{12,8},{14,10},{1,5},{3,7},... | collective-permute-start | bytes 442376 | tf_op jit(solution)/shard_map/ppermute | solution.py:217
  5.3 5.3 %collective-permute-start.2 = (bf16[64,1536]{1,0:T(8,128)(2,1)}, bf16[64,1536]{1,0:T(8,128)(2,1)S(1)}, u32[]{:S(2)}, u32[]{:S(2)}) collective-permute-start(bf16[64,1536]{1,0:T(8,128)(2,1)} %param.13), channel_id=1, source_target_pairs={{0,0},{1,8},{2,2},{3,10},{4,4},{5,12},{6,6},{7,14},{8,1},{9,9},{10... | collective-permute-start | bytes 589832 | tf_op jit(solution)/shard_map/ppermute | solution.py:226
  10.7 1.9 %collective-permute-start.3 = (bf16[64,1536]{1,0:T(8,128)(2,1)}, bf16[64,1536]{1,0:T(8,128)(2,1)S(1)}, u32[]{:S(2)}, u32[]{:S(2)}) collective-permute-start(bf16[64,1536]{1,0:T(8,128)(2,1)} %param.14), channel_id=1, source_target_pairs={{0,0},{1,8},{2,2},{3,10},{4,4},{5,12},{6,6},{7,14},{8,1},{9,9},{10... | collective-permute-start | bytes 589832 | tf_op jit(solution)/shard_map/ppermute | solution.py:226
  13.7 2.6 %collective-permute-done.2.rows = bf16[64,1536]{1,0:T(8,128)(2,1)S(1)} collective-permute-done((bf16[64,1536]{1,0:T(8,128)(2,1)}, bf16[64,1536]{1,0:T(8,128)(2,1)S(1)}, u32[]{:S(2)}, u32[]{:S(2)}) %collective-permute-start.2) | collective-permute-done | bytes 196640 | tf_op jit(solution)/shard_map/ppermute | solution.py:226
  16.3 3.9 %collective-permute-done.3.fresh = bf16[64,1536]{1,0:T(8,128)(2,1)S(1)} collective-permute-done((bf16[64,1536]{1,0:T(8,128)(2,1)}, bf16[64,1536]{1,0:T(8,128)(2,1)S(1)}, u32[]{:S(2)}, u32[]{:S(2)}) %collective-permute-start.3) | collective-permute-done | bytes 196640 | tf_op jit(solution)/shard_map/ppermute | solution.py:226
  20.3 1.3 %collective-permute-start.5 = (bf16[192,384]{1,0:T(8,128)(2,1)S(1)}, bf16[192,384]{1,0:T(8,128)(2,1)S(1)}, u32[]{:S(2)}, u32[]{:S(2)}) collective-permute-start(bf16[192,384]{1,0:T(8,128)(2,1)S(1)} %collective-permute-done.refs_0_), channel_id=1, source_target_pairs={{0,16},{16,0},{1,17},{17,1},{2,18},{18,2},{3,19},{19,3},{4,20},{20... | collective-permute-start | bytes 442376 | tf_op jit(solution)/shard_map/ppermute | solution.py:379
  27.5 2.1 %collective-permute-done.7.refs_1_ = bf16[80,1536]{1,0:T(8,128)(2,1)S(1)} collective-permute-done((bf16[80,1536]{1,0:T(8,128)(2,1)S(1)}, bf16[80,1536]{1,0:T(8,128)(2,1)S(1)}, u32[]{:S(2)}, u32[]{:S(2)}) %collective-permute-start.7) | collective-permute-done | bytes 245792 | tf_op jit(solution)/shard_map/ppermute | solution.py:217
  30.7 1.7 %collective-permute-done.9.refs_3_ = bf16[80,1536]{1,0:T(8,128)(2,1)S(1)} collective-permute-done((bf16[80,1536]{1,0:T(8,128)(2,1)S(1)}, bf16[80,1536]{1,0:T(8,128)(2,1)S(1)}, u32[]{:S(2)}, u32[]{:S(2)}) %collective-permute-start.9) | collective-permute-done | bytes 245792 | tf_op jit(solution)/shard_map/ppermute | solution.py:217
  32.9 2.2 %collective-permute-start.19 = (bf16[384,384]{1,0:T(8,128)(2,1)S(1)}, bf16[384,384]{1,0:T(8,128)(2,1)S(1)}, u32[]{:S(2)}, u32[]{:S(2)}) collective-permute-start(bf16[384,384]{1,0:T(8,128)(2,1)S(1)} %get-tuple-element.109), channel_id=1, source_target_pairs={{0,6},{2,4},{4,2},{6,0},{8,14},{10,12},{12,10},{14,8},{1,7},{3,5},... | collective-permute-start | bytes 884744 | tf_op jit(solution)/shard_map/ppermute | solution.py:217
  35.1 2.0 %shard_map.152 = (f32[256,384]{1,0:T(8,128)S(1)}, bf16[272,384]{1,0:T(8,128)(2,1)S(1)}, f32[8,256]{1,0:T(8,128)S(1)}, f32[256,384]{1,0:T(8,128)S(1)}) custom-call(s32[8]{0:T(128)S(1)} %copy-done.9, bf16[80,1536]{1,0:T(8,128)(2,1)S(1)} %get-tuple-element.79.refs_0_, bf16[80,1536]{1,0:T(8,128)(2,1)S(1)} %collective-permute-done.7.refs_1_, ...), custom_call_target="tpu_custom_call" | custom-call | flops 603979776 | bytes 3538976 | tf_op jit(solution)/shard_map/pallas_call | solution.py:233
  37.7 8.2 %collective-permute-done.15.refs_7_.refs_2_ = bf16[384,384]{1,0:T(8,128)(2,1)S(1)} collective-permute-done((bf16[384,384]{1,0:T(8,128)(2,1)S(1)}, bf16[384,384]{1,0:T(8,128)(2,1)S(1)}, u32[]{:S(2)}, u32[]{:S(2)}) %collective-permute-start.15) | collective-permute-done | bytes 294944 | tf_op jit(solution)/shard_map/ppermute | solution.py:217
  45.9 4.1 %collective-permute-done.14.came = bf16[272,384]{1,0:T(8,128)(2,1)S(1)} collective-permute-done((bf16[272,384]{1,0:T(8,128)(2,1)S(1)}, bf16[272,384]{1,0:T(8,128)(2,1)S(1)}, u32[]{:S(2)}, u32[]{:S(2)}) %collective-permute-start.14) | collective-permute-done | bytes 208928 | tf_op jit(solution)/shard_map/ppermute | solution.py:220
  55.4 7.9 %collective-permute-start.17 = (bf16[256,384]{1,0:T(8,128)(2,1)S(1)}, bf16[256,384]{1,0:T(8,128)(2,1)S(1)}, u32[]{:S(2)}, u32[]{:S(2)}) collective-permute-start(bf16[256,384]{1,0:T(8,128)(2,1)S(1)} %get-tuple-element.110.refs_0_), channel_id=1, source_target_pairs={{0,0},{1,8},{2,2},{3,10},{4,4},{5,12},{6,6},{7,14},{8,1},{9,9},{10... | collective-permute-start | bytes 589832 | tf_op jit(solution)/shard_map/ppermute | solution.py:226
  64.7 3.8 %collective-permute-done.17.owned = bf16[256,384]{1,0:T(8,128)(2,1)S(1)} collective-permute-done((bf16[256,384]{1,0:T(8,128)(2,1)S(1)}, bf16[256,384]{1,0:T(8,128)(2,1)S(1)}, u32[]{:S(2)}, u32[]{:S(2)}) %collective-permute-start.17) | collective-permute-done | bytes 196640 | tf_op jit(solution)/shard_map/ppermute | solution.py:226
  69.1 2.0 %collective-permute-start.24 = (bf16[272,384]{1,0:T(8,128)(2,1)S(1)}, bf16[272,384]{1,0:T(8,128)(2,1)S(1)}, u32[]{:S(2)}, u32[]{:S(2)}) collective-permute-start(bf16[272,384]{1,0:T(8,128)(2,1)S(1)} %get-tuple-element.114), channel_id=1, source_target_pairs={{0,8},{2,10},{4,12},{6,14},{8,0},{10,2},{12,4},{14,6},{1,9},{3,11}... | collective-permute-start | bytes 626696 | tf_op jit(solution)/shard_map/ppermute | solution.py:220
  71.1 2.2 %collective-permute-done.28.other = bf16[8,384,384]{2,1,0:T(8,128)(2,1)S(1)} collective-permute-done((bf16[8,384,384]{2,1,0:T(8,128)(2,1)S(1)}, bf16[8,384,384]{2,1,0:T(8,128)(2,1)S(1)}, u32[]{:S(2)}, u32[]{:S(2)}) %collective-permute-start.28) | collective-permute-done | bytes 2359328 | tf_op jit(solution)/shard_map/ppermute | solution.py:223
  74.4 2.0 %collective-permute-start.29 = (bf16[256,384]{1,0:T(8,128)(2,1)S(1)}, bf16[256,384]{1,0:T(8,128)(2,1)S(1)}, u32[]{:S(2)}, u32[]{:S(2)}) collective-permute-start(bf16[256,384]{1,0:T(8,128)(2,1)S(1)} %get-tuple-element.136), channel_id=1, source_target_pairs={{0,8},{2,10},{4,12},{6,14},{8,0},{10,2},{12,4},{14,6},{1,9},{3,11}... | collective-permute-start | bytes 589832 | tf_op jit(solution)/shard_map/ppermute | solution.py:220
  76.5 8.8 %collective-permute-done.24.came = bf16[272,384]{1,0:T(8,128)(2,1)S(1)} collective-permute-done((bf16[272,384]{1,0:T(8,128)(2,1)S(1)}, bf16[272,384]{1,0:T(8,128)(2,1)S(1)}, u32[]{:S(2)}, u32[]{:S(2)}) %collective-permute-start.24) | collective-permute-done | bytes 208928 | tf_op jit(solution)/shard_map/ppermute | solution.py:220
  85.3 1.5 %shard_map.156 = (bf16[128,384]{1,0:T(8,128)(2,1)S(1)}, bf16[128,384]{1,0:T(8,128)(2,1)S(1)}, bf16[128,384]{1,0:T(8,128)(2,1)S(1)}, bf16[128,384]{1,0:T(8,128)(2...) custom-call(s32[8]{0:T(128)S(1)} %copy-done.9, f32[256,384]{1,0:T(8,128)S(1)} %get-tuple-element.113.gap, ...), custom_call_target="tpu_custom_call" | custom-call | flops 301989888 | bytes 3297312 | tf_op jit(solution)/shard_map/pallas_call | solution.py:233
  88.2 1.3 %collective-permute-start.27 = (bf16[128,384]{1,0:T(8,128)(2,1)S(1)}, bf16[128,384]{1,0:T(8,128)(2,1)S(1)}, u32[]{:S(2)}, u32[]{:S(2)}) collective-permute-start(bf16[128,384]{1,0:T(8,128)(2,1)S(1)} %get-tuple-element.121), channel_id=1, source_target_pairs={{0,6},{2,4},{4,2},{6,0},{8,14},{10,12},{12,10},{14,8},{1,7},{3,5},... | collective-permute-start | bytes 294920 | tf_op jit(solution)/shard_map/ppermute | solution.py:217
  89.6 1.3 %shard_map.159 = (bf16[80,384]{1,0:T(8,128)(2,1)S(1)}, bf16[80,384]{1,0:T(8,128)(2,1)S(1)}, bf16[80,384]{1,0:T(8,128)(2,1)S(1)}, bf16[80,384]{1,0:T(8,128)(2,1)S(1)}) custom-call(s32[8]{0:T(128)S(1)} %copy-done.9, f32[256,384]{1,0:T(8,128)S(1)} %get-tuple-element.135.gap, bf16[256,384]{1,0:T(8,128)(2,1)S(1)} %collective-permute-done.29.came, ...), custom_call_target="tpu_custom_call" | custom-call | flops 301989888 | bytes 3223584 | tf_op jit(solution)/shard_map/pallas_call | solution.py:233
  92.3 1.3 %collective-permute-start.32 = (bf16[80,384]{1,0:T(8,128)(2,1)S(1)}, bf16[80,384]{1,0:T(8,128)(2,1)S(1)}, u32[]{:S(2)}, u32[]{:S(2)}) collective-permute-start(bf16[80,384]{1,0:T(8,128)(2,1)S(1)} %get-tuple-element.142), channel_id=1, source_target_pairs={{0,6},{2,4},{4,2},{6,0},{8,14},{10,12},{12,10},{14,8},{1,7},{3,5},... | collective-permute-start | bytes 184328 | tf_op jit(solution)/shard_map/ppermute | solution.py:217
  93.6 1.8 %collective-permute-done.30.refs_5_ = bf16[80,384]{1,0:T(8,128)(2,1)S(1)} collective-permute-done((bf16[80,384]{1,0:T(8,128)(2,1)S(1)}, bf16[80,384]{1,0:T(8,128)(2,1)S(1)}, u32[]{:S(2)}, u32[]{:S(2)}) %collective-permute-start.30) | collective-permute-done | bytes 61472 | tf_op jit(solution)/shard_map/ppermute | solution.py:217
  97.0 3.4 %collective-permute-start.33 = (bf16[80,1536]{1,0:T(8,128)(2,1)S(1)}, bf16[80,1536]{1,0:T(8,128)(2,1)S(1)}, u32[]{:S(2)}, u32[]{:S(2)}) collective-permute-start(bf16[80,1536]{1,0:T(8,128)(2,1)S(1)} %get-tuple-element.146), channel_id=1, source_target_pairs={{0,1},{1,0},{2,3},{3,2},{4,5},{5,4},{6,7},{7,6},{8,9},{9,8},{10,11... | collective-permute-start | bytes 737288 | tf_op jit(solution)/shard_map/ppermute | solution.py:223
  (82 shorter events, 26.3 us)
Async XLA Ops:
  2.0 18.3 %collective-permute-start = (bf16[192,384]{1,0:T(8,128)(2,1)S(1)}, bf16[192,384]{1,0:T(8,128)(2,1)S(1)}, u32[]{:S(2)}, u32[]{:S(2)}) collective-permute-start(bf16[192,384]{1,0:T(8,128)(2,1)S(1)} %get-tuple-element.76), channel_id=1, source_target_pairs={{0,4},{2,6},{4,0},{6,2},{8,12},{10,14},{12,8},{14,10},{1,5},{3,7},... | collective-permute-start | bytes 442376 | tf_op jit(solution)/shard_map/ppermute | solution.py:217
  4.2 16.1 %collective-permute-start.1 = (bf16[192,384]{1,0:T(8,128)(2,1)S(1)}, bf16[192,384]{1,0:T(8,128)(2,1)S(1)}, u32[]{:S(2)}, u32[]{:S(2)}) collective-permute-start(bf16[192,384]{1,0:T(8,128)(2,1)S(1)} %get-tuple-element.77), channel_id=1, source_target_pairs={{0,6},{2,4},{4,2},{6,0},{8,14},{10,12},{12,10},{14,8},{1,7},{3,5},... | collective-permute-start | bytes 442376 | tf_op jit(solution)/shard_map/ppermute | solution.py:217
  5.3 11.0 %collective-permute-start.2 = (bf16[64,1536]{1,0:T(8,128)(2,1)}, bf16[64,1536]{1,0:T(8,128)(2,1)S(1)}, u32[]{:S(2)}, u32[]{:S(2)}) collective-permute-start(bf16[64,1536]{1,0:T(8,128)(2,1)} %param.13), channel_id=1, source_target_pairs={{0,0},{1,8},{2,2},{3,10},{4,4},{5,12},{6,6},{7,14},{8,1},{9,9},{10... | collective-permute-start | bytes 589832 | tf_op jit(solution)/shard_map/ppermute | solution.py:226
  10.7 9.6 %collective-permute-start.3 = (bf16[64,1536]{1,0:T(8,128)(2,1)}, bf16[64,1536]{1,0:T(8,128)(2,1)S(1)}, u32[]{:S(2)}, u32[]{:S(2)}) collective-permute-start(bf16[64,1536]{1,0:T(8,128)(2,1)} %param.14), channel_id=1, source_target_pairs={{0,0},{1,8},{2,2},{3,10},{4,4},{5,12},{6,6},{7,14},{8,1},{9,9},{10... | collective-permute-start | bytes 589832 | tf_op jit(solution)/shard_map/ppermute | solution.py:226
  12.6 14.9 %collective-permute-start.4 = (bf16[384,384]{1,0:T(8,128)(2,1)S(1)}, bf16[384,384]{1,0:T(8,128)(2,1)S(1)}, u32[]{:S(2)}, u32[]{:S(2)}) collective-permute-start(bf16[384,384]{1,0:T(8,128)(2,1)S(1)} %get-tuple-element.81), channel_id=1, source_target_pairs={{0,2},{2,0},{4,6},{6,4},{8,10},{10,8},{12,14},{14,12},{1,3},{3,1},... | collective-permute-start | bytes 884744 | tf_op jit(solution)/shard_map/ppermute | solution.py:217
  21.6 5.8 %collective-permute-start.6 = (bf16[192,384]{1,0:T(8,128)(2,1)S(1)}, bf16[192,384]{1,0:T(8,128)(2,1)S(1)}, u32[]{:S(2)}, u32[]{:S(2)}) collective-permute-start(bf16[192,384]{1,0:T(8,128)(2,1)S(1)} %collective-permute-done.1.refs_1_), channel_id=1, source_target_pairs={{0,16},{16,0},{1,17},{17,1},{2,18},{18,2},{3,19},{19,3},{4,20},{20... | collective-permute-start | bytes 442376 | tf_op jit(solution)/shard_map/ppermute | solution.py:379
  21.8 7.7 %collective-permute-start.7 = (bf16[80,1536]{1,0:T(8,128)(2,1)S(1)}, bf16[80,1536]{1,0:T(8,128)(2,1)S(1)}, u32[]{:S(2)}, u32[]{:S(2)}) collective-permute-start(bf16[80,1536]{1,0:T(8,128)(2,1)S(1)} %get-tuple-element.86), channel_id=1, source_target_pairs={{0,2},{2,0},{4,6},{6,4},{8,10},{10,8},{12,14},{14,12},{1,3},{3,1},... | collective-permute-start | bytes 737288 | tf_op jit(solution)/shard_map/ppermute | solution.py:217
  22.9 7.2 %collective-permute-start.8 = (bf16[80,1536]{1,0:T(8,128)(2,1)S(1)}, bf16[80,1536]{1,0:T(8,128)(2,1)S(1)}, u32[]{:S(2)}, u32[]{:S(2)}) collective-permute-start(bf16[80,1536]{1,0:T(8,128)(2,1)S(1)} %get-tuple-element.88), channel_id=1, source_target_pairs={{0,4},{2,6},{4,0},{6,2},{8,12},{10,14},{12,8},{14,10},{1,5},{3,7},... | collective-permute-start | bytes 737288 | tf_op jit(solution)/shard_map/ppermute | solution.py:217
  24.4 8.1 %collective-permute-start.9 = (bf16[80,1536]{1,0:T(8,128)(2,1)S(1)}, bf16[80,1536]{1,0:T(8,128)(2,1)S(1)}, u32[]{:S(2)}, u32[]{:S(2)}) collective-permute-start(bf16[80,1536]{1,0:T(8,128)(2,1)S(1)} %get-tuple-element.89), channel_id=1, source_target_pairs={{0,6},{2,4},{4,2},{6,0},{8,14},{10,12},{12,10},{14,8},{1,7},{3,5},... | collective-permute-start | bytes 737288 | tf_op jit(solution)/shard_map/ppermute | solution.py:217
  30.0 5.1 %collective-permute-start.12 = (bf16[384,384]{1,0:T(8,128)(2,1)S(1)}, bf16[384,384]{1,0:T(8,128)(2,1)S(1)}, u32[]{:S(2)}, u32[]{:S(2)}) collective-permute-start(bf16[384,384]{1,0:T(8,128)(2,1)S(1)} %get-tuple-element.93.refs_7_.refs_6_), channel_id=1, source_target_pairs={{0,1},{1,0},{2,3},{3,2},{4,5},{5,4},{6,7},{7,6},{8,9},{9,8},{10,11... | collective-permute-start | bytes 884744 | tf_op jit(solution)/shard_map/ppermute | solution.py:223
  32.4 21.2 %collective-permute-start.18 = (bf16[2,384,384]{2,1,0:T(8,128)(2,1)S(1)}, bf16[2,384,384]{2,1,0:T(8,128)(2,1)S(1)}, u32[]{:S(2)}, u32[]{:S(2)}) collective-permute-start(bf16[2,384,384]{2,1,0:T(8,128)(2,1)S(1)} %get-tuple-element.106), channel_id=1, source_target_pairs={{0,2},{2,0},{4,6},{6,4},{8,10},{10,8},{12,14},{14,12},{1,3},{3,1},... | collective-permute-start | bytes 1769480 | tf_op jit(solution)/shard_map/ppermute | solution.py:217
  32.4 13.5 %collective-permute-start.15 = (bf16[384,384]{1,0:T(8,128)(2,1)S(1)}, bf16[384,384]{1,0:T(8,128)(2,1)S(1)}, u32[]{:S(2)}, u32[]{:S(2)}) collective-permute-start(bf16[384,384]{1,0:T(8,128)(2,1)S(1)} %get-tuple-element.99), channel_id=1, source_target_pairs={{0,4},{2,6},{4,0},{6,2},{8,12},{10,14},{12,8},{14,10},{1,5},{3,7},... | collective-permute-start | bytes 884744 | tf_op jit(solution)/shard_map/ppermute | solution.py:217
  32.9 20.2 %collective-permute-start.19 = (bf16[384,384]{1,0:T(8,128)(2,1)S(1)}, bf16[384,384]{1,0:T(8,128)(2,1)S(1)}, u32[]{:S(2)}, u32[]{:S(2)}) collective-permute-start(bf16[384,384]{1,0:T(8,128)(2,1)S(1)} %get-tuple-element.109), channel_id=1, source_target_pairs={{0,6},{2,4},{4,2},{6,0},{8,14},{10,12},{12,10},{14,8},{1,7},{3,5},... | collective-permute-start | bytes 884744 | tf_op jit(solution)/shard_map/ppermute | solution.py:217
  37.1 12.9 %collective-permute-start.14 = (bf16[272,384]{1,0:T(8,128)(2,1)S(1)}, bf16[272,384]{1,0:T(8,128)(2,1)S(1)}, u32[]{:S(2)}, u32[]{:S(2)}) collective-permute-start(bf16[272,384]{1,0:T(8,128)(2,1)S(1)} %get-tuple-element.96), channel_id=1, source_target_pairs={{0,8},{2,10},{4,12},{6,14},{8,0},{10,2},{12,4},{14,6},{1,9},{3,11}... | collective-permute-start | bytes 626696 | tf_op jit(solution)/shard_map/ppermute | solution.py:220
  51.8 11.6 %collective-permute-start.20 = (bf16[384,384]{1,0:T(8,128)(2,1)S(1)}, bf16[384,384]{1,0:T(8,128)(2,1)S(1)}, u32[]{:S(2)}, u32[]{:S(2)}) collective-permute-start(bf16[384,384]{1,0:T(8,128)(2,1)S(1)} %collective-permute-done.15.refs_7_.refs_2_), channel_id=1, source_target_pairs={{0,16},{16,0},{1,17},{17,1},{2,18},{18,2},{3,19},{19,3},{4,20},{20... | collective-permute-start | bytes 884744 | tf_op jit(solution)/shard_map/ppermute | solution.py:449
  53.0 10.4 %collective-permute-start.21 = (bf16[384,384]{1,0:T(8,128)(2,1)S(1)}, bf16[384,384]{1,0:T(8,128)(2,1)S(1)}, u32[]{:S(2)}, u32[]{:S(2)}) collective-permute-start(bf16[384,384]{1,0:T(8,128)(2,1)S(1)} %collective-permute-done.19.refs_8_.refs_3_), channel_id=1, source_target_pairs={{0,16},{16,0},{1,17},{17,1},{2,18},{18,2},{3,19},{19,3},{4,20},{20... | collective-permute-start | bytes 884744 | tf_op jit(solution)/shard_map/ppermute | solution.py:449
  53.6 9.8 %collective-permute-start.22 = (bf16[256,384]{1,0:T(8,128)(2,1)S(1)}, bf16[256,384]{1,0:T(8,128)(2,1)S(1)}, u32[]{:S(2)}, u32[]{:S(2)}) collective-permute-start(bf16[256,384]{1,0:T(8,128)(2,1)S(1)} %get-tuple-element.110.refs_0_), channel_id=1, source_target_pairs={{0,2},{2,0},{4,6},{6,4},{8,10},{10,8},{12,14},{14,12},{1,3},{3,1},... | collective-permute-start | bytes 589832 | tf_op jit(solution)/shard_map/ppermute | solution.py:217
  53.8 9.6 %collective-permute-start.23 = (bf16[256,384]{1,0:T(8,128)(2,1)S(1)}, bf16[256,384]{1,0:T(8,128)(2,1)S(1)}, u32[]{:S(2)}, u32[]{:S(2)}) collective-permute-start(bf16[256,384]{1,0:T(8,128)(2,1)S(1)} %get-tuple-element.110.refs_0_), channel_id=1, source_target_pairs={{0,6},{2,4},{4,2},{6,0},{8,14},{10,12},{12,10},{14,8},{1,7},{3,5},... | collective-permute-start | bytes 589832 | tf_op jit(solution)/shard_map/ppermute | solution.py:217
  55.4 13.1 %collective-permute-start.17 = (bf16[256,384]{1,0:T(8,128)(2,1)S(1)}, bf16[256,384]{1,0:T(8,128)(2,1)S(1)}, u32[]{:S(2)}, u32[]{:S(2)}) collective-permute-start(bf16[256,384]{1,0:T(8,128)(2,1)S(1)} %get-tuple-element.110.refs_0_), channel_id=1, source_target_pairs={{0,0},{1,8},{2,2},{3,10},{4,4},{5,12},{6,6},{7,14},{8,1},{9,9},{10... | collective-permute-start | bytes 589832 | tf_op jit(solution)/shard_map/ppermute | solution.py:226
  69.1 16.2 %collective-permute-start.24 = (bf16[272,384]{1,0:T(8,128)(2,1)S(1)}, bf16[272,384]{1,0:T(8,128)(2,1)S(1)}, u32[]{:S(2)}, u32[]{:S(2)}) collective-permute-start(bf16[272,384]{1,0:T(8,128)(2,1)S(1)} %get-tuple-element.114), channel_id=1, source_target_pairs={{0,8},{2,10},{4,12},{6,14},{8,0},{10,2},{12,4},{14,6},{1,9},{3,11}... | collective-permute-start | bytes 626696 | tf_op jit(solution)/shard_map/ppermute | solution.py:220
  74.4 15.1 %collective-permute-start.29 = (bf16[256,384]{1,0:T(8,128)(2,1)S(1)}, bf16[256,384]{1,0:T(8,128)(2,1)S(1)}, u32[]{:S(2)}, u32[]{:S(2)}) collective-permute-start(bf16[256,384]{1,0:T(8,128)(2,1)S(1)} %get-tuple-element.136), channel_id=1, source_target_pairs={{0,8},{2,10},{4,12},{6,14},{8,0},{10,2},{12,4},{14,6},{1,9},{3,11}... | collective-permute-start | bytes 589832 | tf_op jit(solution)/shard_map/ppermute | solution.py:220
  86.8 5.5 %collective-permute-start.25 = (bf16[128,384]{1,0:T(8,128)(2,1)S(1)}, bf16[128,384]{1,0:T(8,128)(2,1)S(1)}, u32[]{:S(2)}, u32[]{:S(2)}) collective-permute-start(bf16[128,384]{1,0:T(8,128)(2,1)S(1)} %get-tuple-element.119), channel_id=1, source_target_pairs={{0,2},{2,0},{4,6},{6,4},{8,10},{10,8},{12,14},{14,12},{1,3},{3,1},... | collective-permute-start | bytes 294920 | tf_op jit(solution)/shard_map/ppermute | solution.py:217
  87.0 6.6 %collective-permute-start.26 = (bf16[128,384]{1,0:T(8,128)(2,1)S(1)}, bf16[128,384]{1,0:T(8,128)(2,1)S(1)}, u32[]{:S(2)}, u32[]{:S(2)}) collective-permute-start(bf16[128,384]{1,0:T(8,128)(2,1)S(1)} %get-tuple-element.120), channel_id=1, source_target_pairs={{0,4},{2,6},{4,0},{6,2},{8,12},{10,14},{12,8},{14,10},{1,5},{3,7},... | collective-permute-start | bytes 294920 | tf_op jit(solution)/shard_map/ppermute | solution.py:217
  88.2 5.4 %collective-permute-start.27 = (bf16[128,384]{1,0:T(8,128)(2,1)S(1)}, bf16[128,384]{1,0:T(8,128)(2,1)S(1)}, u32[]{:S(2)}, u32[]{:S(2)}) collective-permute-start(bf16[128,384]{1,0:T(8,128)(2,1)S(1)} %get-tuple-element.121), channel_id=1, source_target_pairs={{0,6},{2,4},{4,2},{6,0},{8,14},{10,12},{12,10},{14,8},{1,7},{3,5},... | collective-permute-start | bytes 294920 | tf_op jit(solution)/shard_map/ppermute | solution.py:217
  (20 other events, 178.5 us)

commit v11 on v10

--- a/solution.py
+++ b/solution.py
@@ -372,13 +372,13 @@
 
     x_turned, fresh_turned = turned(noise_in), turned(renoise)
     gen_sent = call(cut_gen_kernel, [gen_weight], [((depth, w), bf16)] * shared + [((part_rows, w), bf16)] * (g - shared), depth * h)
-    gen_mine = [gen_sent[0]] + [in_square(gen_sent[k], k) for k in range(1, g)]
+    gen_mine = [gen_sent[0]] + [in_square(gen_sent[k], k) for k in range(g - 1, 0, -1)][::-1]
     x_sent = call(cut_rows_kernel, [x_turned, fresh_turned], [((r + fold, h), bf16)] * g, r * h)
     x_sent = list(x_sent)
     *fetched, x_sent[0] = lax.optimization_barrier((*gen_mine[shared:], x_sent[0]))
     given = [lax.ppermute(v, "rep", [(0, 1), (1, 0)]) for v in fetched]
     gen_mine[shared:] = call(join_gen_kernel, fetched + given, [((depth, w), bf16)] * (g - shared), depth * w)
-    x = [x_sent[0]] + [in_square(x_sent[k], k) for k in range(1, g)]
+    x = [x_sent[0]] + [in_square(x_sent[k], k) for k in range(g - 1, 0, -1)][::-1]
     gen_swap, x[1], scales = lax.optimization_barrier((gen_mine, x[1], scales))
     gen_other = [cores(v) for v in gen_swap]
     real_weight, fake_weight, _ = lax.optimization_barrier((real_weight, fake_weight, x_turned))

time: 103 us -> 103 us (level)
  no operation moved by 1% of the time
where the time goes in v11:
time: 103 us; the launch traced here: 102 us
  starting transfers between devices  44.9 us (44%)
  waiting for transfers between devices  42.5 us (41%)
  Pallas kernels  10.6 us (10%)
  local copies, waits for them, and re-layouts  2.42 us (2%)
    ppermute x18, starting transfers between devices, in_square(): return lax.ppermute(value, 'fsdp', [(i, i ^ k) for i in range(2 * g)])  16.8 us
    ppermute x3, starting transfers between devices, turned(): lax.ppermute(value, ('fsdp', 'mp'), [(flat(*i), flat(i[2], i[1], i[0])) f...  15.2 us
    ppermute x18, waiting for transfers between devices, in_square(): return lax.ppermute(value, 'fsdp', [(i, i ^ k) for i in range(2 * g)])  15 us
    ppermute x3, waiting for transfers between devices, across(): return lax.ppermute(value, 'fsdp', [(i, i ^ g) for i in range(2 * g)])  12.9 us
    ppermute x3, waiting for transfers between devices, turned(): lax.ppermute(value, ('fsdp', 'mp'), [(flat(*i), flat(i[2], i[1], i[0])) f...  10.3 us
    pallas_call x13, Pallas kernels, call(): pl.pallas_call(kernel, in_specs=[scalars] * in_scalars + [whole] * (len(o...  10.1 us
    ppermute x6, starting transfers between devices, cores(): return lax.ppermute(value, 'mp', [(0, 1), (1, 0)])  4.86 us
    ppermute x3, starting transfers between devices, across(): return lax.ppermute(value, 'fsdp', [(i, i ^ g) for i in range(2 * g)])  4.66 us
  transfers between devices with their start and end apart: 34, of which 14 were waited for; matrix products, arithmetic and copies ran while one was open for 1% of the time, Pallas kernels for 9%

profile of v11, /device:TPU:1, one launch (start us, length us, event | category | flops | bytes accessed | tf_op | source)
XLA Modules:
  0.0 102.3 jit_solution(6314194674827664333)
XLA Ops:
  2.0 2.2 %collective-permute-start = (bf16[192,384]{1,0:T(8,128)(2,1)S(1)}, bf16[192,384]{1,0:T(8,128)(2,1)S(1)}, u32[]{:S(2)}, u32[]{:S(2)}) collective-permute-start(bf16[192,384]{1,0:T(8,128)(2,1)S(1)} %get-tuple-element.76), channel_id=1, source_target_pairs={{0,4},{2,6},{4,0},{6,2},{8,12},{10,14},{12,8},{14,10},{1,5},{3,7},... | collective-permute-start | bytes 442376 | tf_op jit(solution)/shard_map/ppermute | solution.py:217
  5.3 5.3 %collective-permute-start.2 = (bf16[64,1536]{1,0:T(8,128)(2,1)}, bf16[64,1536]{1,0:T(8,128)(2,1)S(1)}, u32[]{:S(2)}, u32[]{:S(2)}) collective-permute-start(bf16[64,1536]{1,0:T(8,128)(2,1)} %param.13), channel_id=1, source_target_pairs={{0,0},{1,8},{2,2},{3,10},{4,4},{5,12},{6,6},{7,14},{8,1},{9,9},{10... | collective-permute-start | bytes 589832 | tf_op jit(solution)/shard_map/ppermute | solution.py:226
  10.7 1.9 %collective-permute-start.3 = (bf16[64,1536]{1,0:T(8,128)(2,1)}, bf16[64,1536]{1,0:T(8,128)(2,1)S(1)}, u32[]{:S(2)}, u32[]{:S(2)}) collective-permute-start(bf16[64,1536]{1,0:T(8,128)(2,1)} %param.14), channel_id=1, source_target_pairs={{0,0},{1,8},{2,2},{3,10},{4,4},{5,12},{6,6},{7,14},{8,1},{9,9},{10... | collective-permute-start | bytes 589832 | tf_op jit(solution)/shard_map/ppermute | solution.py:226
  13.7 2.6 %collective-permute-done.2.rows = bf16[64,1536]{1,0:T(8,128)(2,1)S(1)} collective-permute-done((bf16[64,1536]{1,0:T(8,128)(2,1)}, bf16[64,1536]{1,0:T(8,128)(2,1)S(1)}, u32[]{:S(2)}, u32[]{:S(2)}) %collective-permute-start.2) | collective-permute-done | bytes 196640 | tf_op jit(solution)/shard_map/ppermute | solution.py:226
  16.3 3.9 %collective-permute-done.3.fresh = bf16[64,1536]{1,0:T(8,128)(2,1)S(1)} collective-permute-done((bf16[64,1536]{1,0:T(8,128)(2,1)}, bf16[64,1536]{1,0:T(8,128)(2,1)S(1)}, u32[]{:S(2)}, u32[]{:S(2)}) %collective-permute-start.3) | collective-permute-done | bytes 196640 | tf_op jit(solution)/shard_map/ppermute | solution.py:226
  20.3 1.3 %collective-permute-start.5 = (bf16[192,384]{1,0:T(8,128)(2,1)S(1)}, bf16[192,384]{1,0:T(8,128)(2,1)S(1)}, u32[]{:S(2)}, u32[]{:S(2)}) collective-permute-start(bf16[192,384]{1,0:T(8,128)(2,1)S(1)} %collective-permute-done.refs_0_), channel_id=1, source_target_pairs={{0,16},{16,0},{1,17},{17,1},{2,18},{18,2},{3,19},{19,3},{4,20},{20... | collective-permute-start | bytes 442376 | tf_op jit(solution)/shard_map/ppermute | solution.py:379
  27.5 2.1 %collective-permute-done.7.refs_1_ = bf16[80,1536]{1,0:T(8,128)(2,1)S(1)} collective-permute-done((bf16[80,1536]{1,0:T(8,128)(2,1)S(1)}, bf16[80,1536]{1,0:T(8,128)(2,1)S(1)}, u32[]{:S(2)}, u32[]{:S(2)}) %collective-permute-start.7) | collective-permute-done | bytes 245792 | tf_op jit(solution)/shard_map/ppermute | solution.py:217
  30.7 1.7 %collective-permute-done.9.refs_3_ = bf16[80,1536]{1,0:T(8,128)(2,1)S(1)} collective-permute-done((bf16[80,1536]{1,0:T(8,128)(2,1)S(1)}, bf16[80,1536]{1,0:T(8,128)(2,1)S(1)}, u32[]{:S(2)}, u32[]{:S(2)}) %collective-permute-start.9) | collective-permute-done | bytes 245792 | tf_op jit(solution)/shard_map/ppermute | solution.py:217
  32.9 2.2 %collective-permute-start.19 = (bf16[384,384]{1,0:T(8,128)(2,1)S(1)}, bf16[384,384]{1,0:T(8,128)(2,1)S(1)}, u32[]{:S(2)}, u32[]{:S(2)}) collective-permute-start(bf16[384,384]{1,0:T(8,128)(2,1)S(1)} %get-tuple-element.109), channel_id=1, source_target_pairs={{0,6},{2,4},{4,2},{6,0},{8,14},{10,12},{12,10},{14,8},{1,7},{3,5},... | collective-permute-start | bytes 884744 | tf_op jit(solution)/shard_map/ppermute | solution.py:217
  35.1 2.0 %shard_map.152 = (f32[256,384]{1,0:T(8,128)S(1)}, bf16[272,384]{1,0:T(8,128)(2,1)S(1)}, f32[8,256]{1,0:T(8,128)S(1)}, f32[256,384]{1,0:T(8,128)S(1)}) custom-call(s32[8]{0:T(128)S(1)} %copy-done.9, bf16[80,1536]{1,0:T(8,128)(2,1)S(1)} %get-tuple-element.79.refs_0_, bf16[80,1536]{1,0:T(8,128)(2,1)S(1)} %collective-permute-done.7.refs_1_, ...), custom_call_target="tpu_custom_call" | custom-call | flops 603979776 | bytes 3538976 | tf_op jit(solution)/shard_map/pallas_call | solution.py:233
  37.7 8.2 %collective-permute-done.15.refs_7_.refs_2_ = bf16[384,384]{1,0:T(8,128)(2,1)S(1)} collective-permute-done((bf16[384,384]{1,0:T(8,128)(2,1)S(1)}, bf16[384,384]{1,0:T(8,128)(2,1)S(1)}, u32[]{:S(2)}, u32[]{:S(2)}) %collective-permute-start.15) | collective-permute-done | bytes 294944 | tf_op jit(solution)/shard_map/ppermute | solution.py:217
  45.9 4.1 %collective-permute-done.14.came = bf16[272,384]{1,0:T(8,128)(2,1)S(1)} collective-permute-done((bf16[272,384]{1,0:T(8,128)(2,1)S(1)}, bf16[272,384]{1,0:T(8,128)(2,1)S(1)}, u32[]{:S(2)}, u32[]{:S(2)}) %collective-permute-start.14) | collective-permute-done | bytes 208928 | tf_op jit(solution)/shard_map/ppermute | solution.py:220
  55.4 7.9 %collective-permute-start.17 = (bf16[256,384]{1,0:T(8,128)(2,1)S(1)}, bf16[256,384]{1,0:T(8,128)(2,1)S(1)}, u32[]{:S(2)}, u32[]{:S(2)}) collective-permute-start(bf16[256,384]{1,0:T(8,128)(2,1)S(1)} %get-tuple-element.110.refs_0_), channel_id=1, source_target_pairs={{0,0},{1,8},{2,2},{3,10},{4,4},{5,12},{6,6},{7,14},{8,1},{9,9},{10... | collective-permute-start | bytes 589832 | tf_op jit(solution)/shard_map/ppermute | solution.py:226
  64.7 3.8 %collective-permute-done.17.owned = bf16[256,384]{1,0:T(8,128)(2,1)S(1)} collective-permute-done((bf16[256,384]{1,0:T(8,128)(2,1)S(1)}, bf16[256,384]{1,0:T(8,128)(2,1)S(1)}, u32[]{:S(2)}, u32[]{:S(2)}) %collective-permute-start.17) | collective-permute-done | bytes 196640 | tf_op jit(solution)/shard_map/ppermute | solution.py:226
  69.1 2.0 %collective-permute-start.24 = (bf16[272,384]{1,0:T(8,128)(2,1)S(1)}, bf16[272,384]{1,0:T(8,128)(2,1)S(1)}, u32[]{:S(2)}, u32[]{:S(2)}) collective-permute-start(bf16[272,384]{1,0:T(8,128)(2,1)S(1)} %get-tuple-element.114), channel_id=1, source_target_pairs={{0,8},{2,10},{4,12},{6,14},{8,0},{10,2},{12,4},{14,6},{1,9},{3,11}... | collective-permute-start | bytes 626696 | tf_op jit(solution)/shard_map/ppermute | solution.py:220
  71.1 2.2 %collective-permute-done.28.other = bf16[8,384,384]{2,1,0:T(8,128)(2,1)S(1)} collective-permute-done((bf16[8,384,384]{2,1,0:T(8,128)(2,1)S(1)}, bf16[8,384,384]{2,1,0:T(8,128)(2,1)S(1)}, u32[]{:S(2)}, u32[]{:S(2)}) %collective-permute-start.28) | collective-permute-done | bytes 2359328 | tf_op jit(solution)/shard_map/ppermute | solution.py:223
  74.4 2.0 %collective-permute-start.29 = (bf16[256,384]{1,0:T(8,128)(2,1)S(1)}, bf16[256,384]{1,0:T(8,128)(2,1)S(1)}, u32[]{:S(2)}, u32[]{:S(2)}) collective-permute-start(bf16[256,384]{1,0:T(8,128)(2,1)S(1)} %get-tuple-element.136), channel_id=1, source_target_pairs={{0,8},{2,10},{4,12},{6,14},{8,0},{10,2},{12,4},{14,6},{1,9},{3,11}... | collective-permute-start | bytes 589832 | tf_op jit(solution)/shard_map/ppermute | solution.py:220
  76.5 8.8 %collective-permute-done.24.came = bf16[272,384]{1,0:T(8,128)(2,1)S(1)} collective-permute-done((bf16[272,384]{1,0:T(8,128)(2,1)S(1)}, bf16[272,384]{1,0:T(8,128)(2,1)S(1)}, u32[]{:S(2)}, u32[]{:S(2)}) %collective-permute-start.24) | collective-permute-done | bytes 208928 | tf_op jit(solution)/shard_map/ppermute | solution.py:220
  85.3 1.5 %shard_map.156 = (bf16[128,384]{1,0:T(8,128)(2,1)S(1)}, bf16[128,384]{1,0:T(8,128)(2,1)S(1)}, bf16[128,384]{1,0:T(8,128)(2,1)S(1)}, bf16[128,384]{1,0:T(8,128)(2...) custom-call(s32[8]{0:T(128)S(1)} %copy-done.9, f32[256,384]{1,0:T(8,128)S(1)} %get-tuple-element.113.gap, ...), custom_call_target="tpu_custom_call" | custom-call | flops 301989888 | bytes 3297312 | tf_op jit(solution)/shard_map/pallas_call | solution.py:233
  88.2 1.3 %collective-permute-start.27 = (bf16[128,384]{1,0:T(8,128)(2,1)S(1)}, bf16[128,384]{1,0:T(8,128)(2,1)S(1)}, u32[]{:S(2)}, u32[]{:S(2)}) collective-permute-start(bf16[128,384]{1,0:T(8,128)(2,1)S(1)} %get-tuple-element.121), channel_id=1, source_target_pairs={{0,6},{2,4},{4,2},{6,0},{8,14},{10,12},{12,10},{14,8},{1,7},{3,5},... | collective-permute-start | bytes 294920 | tf_op jit(solution)/shard_map/ppermute | solution.py:217
  89.6 1.3 %shard_map.159 = (bf16[80,384]{1,0:T(8,128)(2,1)S(1)}, bf16[80,384]{1,0:T(8,128)(2,1)S(1)}, bf16[80,384]{1,0:T(8,128)(2,1)S(1)}, bf16[80,384]{1,0:T(8,128)(2,1)S(1)}) custom-call(s32[8]{0:T(128)S(1)} %copy-done.9, f32[256,384]{1,0:T(8,128)S(1)} %get-tuple-element.135.gap, bf16[256,384]{1,0:T(8,128)(2,1)S(1)} %collective-permute-done.29.came, ...), custom_call_target="tpu_custom_call" | custom-call | flops 301989888 | bytes 3223584 | tf_op jit(solution)/shard_map/pallas_call | solution.py:233
  92.3 1.3 %collective-permute-start.32 = (bf16[80,384]{1,0:T(8,128)(2,1)S(1)}, bf16[80,384]{1,0:T(8,128)(2,1)S(1)}, u32[]{:S(2)}, u32[]{:S(2)}) collective-permute-start(bf16[80,384]{1,0:T(8,128)(2,1)S(1)} %get-tuple-element.142), channel_id=1, source_target_pairs={{0,6},{2,4},{4,2},{6,0},{8,14},{10,12},{12,10},{14,8},{1,7},{3,5},... | collective-permute-start | bytes 184328 | tf_op jit(solution)/shard_map/ppermute | solution.py:217
  93.6 1.8 %collective-permute-done.30.refs_5_ = bf16[80,384]{1,0:T(8,128)(2,1)S(1)} collective-permute-done((bf16[80,384]{1,0:T(8,128)(2,1)S(1)}, bf16[80,384]{1,0:T(8,128)(2,1)S(1)}, u32[]{:S(2)}, u32[]{:S(2)}) %collective-permute-start.30) | collective-permute-done | bytes 61472 | tf_op jit(solution)/shard_map/ppermute | solution.py:217
  97.0 3.4 %collective-permute-start.33 = (bf16[80,1536]{1,0:T(8,128)(2,1)S(1)}, bf16[80,1536]{1,0:T(8,128)(2,1)S(1)}, u32[]{:S(2)}, u32[]{:S(2)}) collective-permute-start(bf16[80,1536]{1,0:T(8,128)(2,1)S(1)} %get-tuple-element.146), channel_id=1, source_target_pairs={{0,1},{1,0},{2,3},{3,2},{4,5},{5,4},{6,7},{7,6},{8,9},{9,8},{10,11... | collective-permute-start | bytes 737288 | tf_op jit(solution)/shard_map/ppermute | solution.py:223
  (82 shorter events, 26.3 us)
Async XLA Ops:
  2.0 18.3 %collective-permute-start = (bf16[192,384]{1,0:T(8,128)(2,1)S(1)}, bf16[192,384]{1,0:T(8,128)(2,1)S(1)}, u32[]{:S(2)}, u32[]{:S(2)}) collective-permute-start(bf16[192,384]{1,0:T(8,128)(2,1)S(1)} %get-tuple-element.76), channel_id=1, source_target_pairs={{0,4},{2,6},{4,0},{6,2},{8,12},{10,14},{12,8},{14,10},{1,5},{3,7},... | collective-permute-start | bytes 442376 | tf_op jit(solution)/shard_map/ppermute | solution.py:217
  4.2 16.1 %collective-permute-start.1 = (bf16[192,384]{1,0:T(8,128)(2,1)S(1)}, bf16[192,384]{1,0:T(8,128)(2,1)S(1)}, u32[]{:S(2)}, u32[]{:S(2)}) collective-permute-start(bf16[192,384]{1,0:T(8,128)(2,1)S(1)} %get-tuple-element.77), channel_id=1, source_target_pairs={{0,6},{2,4},{4,2},{6,0},{8,14},{10,12},{12,10},{14,8},{1,7},{3,5},... | collective-permute-start | bytes 442376 | tf_op jit(solution)/shard_map/ppermute | solution.py:217
  5.3 11.0 %collective-permute-start.2 = (bf16[64,1536]{1,0:T(8,128)(2,1)}, bf16[64,1536]{1,0:T(8,128)(2,1)S(1)}, u32[]{:S(2)}, u32[]{:S(2)}) collective-permute-start(bf16[64,1536]{1,0:T(8,128)(2,1)} %param.13), channel_id=1, source_target_pairs={{0,0},{1,8},{2,2},{3,10},{4,4},{5,12},{6,6},{7,14},{8,1},{9,9},{10... | collective-permute-start | bytes 589832 | tf_op jit(solution)/shard_map/ppermute | solution.py:226
  10.7 9.6 %collective-permute-start.3 = (bf16[64,1536]{1,0:T(8,128)(2,1)}, bf16[64,1536]{1,0:T(8,128)(2,1)S(1)}, u32[]{:S(2)}, u32[]{:S(2)}) collective-permute-start(bf16[64,1536]{1,0:T(8,128)(2,1)} %param.14), channel_id=1, source_target_pairs={{0,0},{1,8},{2,2},{3,10},{4,4},{5,12},{6,6},{7,14},{8,1},{9,9},{10... | collective-permute-start | bytes 589832 | tf_op jit(solution)/shard_map/ppermute | solution.py:226
  12.6 14.9 %collective-permute-start.4 = (bf16[384,384]{1,0:T(8,128)(2,1)S(1)}, bf16[384,384]{1,0:T(8,128)(2,1)S(1)}, u32[]{:S(2)}, u32[]{:S(2)}) collective-permute-start(bf16[384,384]{1,0:T(8,128)(2,1)S(1)} %get-tuple-element.81), channel_id=1, source_target_pairs={{0,2},{2,0},{4,6},{6,4},{8,10},{10,8},{12,14},{14,12},{1,3},{3,1},... | collective-permute-start | bytes 884744 | tf_op jit(solution)/shard_map/ppermute | solution.py:217
  21.6 5.8 %collective-permute-start.6 = (bf16[192,384]{1,0:T(8,128)(2,1)S(1)}, bf16[192,384]{1,0:T(8,128)(2,1)S(1)}, u32[]{:S(2)}, u32[]{:S(2)}) collective-permute-start(bf16[192,384]{1,0:T(8,128)(2,1)S(1)} %collective-permute-done.1.refs_1_), channel_id=1, source_target_pairs={{0,16},{16,0},{1,17},{17,1},{2,18},{18,2},{3,19},{19,3},{4,20},{20... | collective-permute-start | bytes 442376 | tf_op jit(solution)/shard_map/ppermute | solution.py:379
  21.8 7.7 %collective-permute-start.7 = (bf16[80,1536]{1,0:T(8,128)(2,1)S(1)}, bf16[80,1536]{1,0:T(8,128)(2,1)S(1)}, u32[]{:S(2)}, u32[]{:S(2)}) collective-permute-start(bf16[80,1536]{1,0:T(8,128)(2,1)S(1)} %get-tuple-element.86), channel_id=1, source_target_pairs={{0,2},{2,0},{4,6},{6,4},{8,10},{10,8},{12,14},{14,12},{1,3},{3,1},... | collective-permute-start | bytes 737288 | tf_op jit(solution)/shard_map/ppermute | solution.py:217
  22.9 7.2 %collective-permute-start.8 = (bf16[80,1536]{1,0:T(8,128)(2,1)S(1)}, bf16[80,1536]{1,0:T(8,128)(2,1)S(1)}, u32[]{:S(2)}, u32[]{:S(2)}) collective-permute-start(bf16[80,1536]{1,0:T(8,128)(2,1)S(1)} %get-tuple-element.88), channel_id=1, source_target_pairs={{0,4},{2,6},{4,0},{6,2},{8,12},{10,14},{12,8},{14,10},{1,5},{3,7},... | collective-permute-start | bytes 737288 | tf_op jit(solution)/shard_map/ppermute | solution.py:217
  24.4 8.1 %collective-permute-start.9 = (bf16[80,1536]{1,0:T(8,128)(2,1)S(1)}, bf16[80,1536]{1,0:T(8,128)(2,1)S(1)}, u32[]{:S(2)}, u32[]{:S(2)}) collective-permute-start(bf16[80,1536]{1,0:T(8,128)(2,1)S(1)} %get-tuple-element.89), channel_id=1, source_target_pairs={{0,6},{2,4},{4,2},{6,0},{8,14},{10,12},{12,10},{14,8},{1,7},{3,5},... | collective-permute-start | bytes 737288 | tf_op jit(solution)/shard_map/ppermute | solution.py:217
  30.0 5.1 %collective-permute-start.12 = (bf16[384,384]{1,0:T(8,128)(2,1)S(1)}, bf16[384,384]{1,0:T(8,128)(2,1)S(1)}, u32[]{:S(2)}, u32[]{:S(2)}) collective-permute-start(bf16[384,384]{1,0:T(8,128)(2,1)S(1)} %get-tuple-element.93.refs_7_.refs_6_), channel_id=1, source_target_pairs={{0,1},{1,0},{2,3},{3,2},{4,5},{5,4},{6,7},{7,6},{8,9},{9,8},{10,11... | collective-permute-start | bytes 884744 | tf_op jit(solution)/shard_map/ppermute | solution.py:223
  32.4 21.2 %collective-permute-start.18 = (bf16[2,384,384]{2,1,0:T(8,128)(2,1)S(1)}, bf16[2,384,384]{2,1,0:T(8,128)(2,1)S(1)}, u32[]{:S(2)}, u32[]{:S(2)}) collective-permute-start(bf16[2,384,384]{2,1,0:T(8,128)(2,1)S(1)} %get-tuple-element.106), channel_id=1, source_target_pairs={{0,2},{2,0},{4,6},{6,4},{8,10},{10,8},{12,14},{14,12},{1,3},{3,1},... | collective-permute-start | bytes 1769480 | tf_op jit(solution)/shard_map/ppermute | solution.py:217
  32.4 13.5 %collective-permute-start.15 = (bf16[384,384]{1,0:T(8,128)(2,1)S(1)}, bf16[384,384]{1,0:T(8,128)(2,1)S(1)}, u32[]{:S(2)}, u32[]{:S(2)}) collective-permute-start(bf16[384,384]{1,0:T(8,128)(2,1)S(1)} %get-tuple-element.99), channel_id=1, source_target_pairs={{0,4},{2,6},{4,0},{6,2},{8,12},{10,14},{12,8},{14,10},{1,5},{3,7},... | collective-permute-start | bytes 884744 | tf_op jit(solution)/shard_map/ppermute | solution.py:217
  32.9 20.2 %collective-permute-start.19 = (bf16[384,384]{1,0:T(8,128)(2,1)S(1)}, bf16[384,384]{1,0:T(8,128)(2,1)S(1)}, u32[]{:S(2)}, u32[]{:S(2)}) collective-permute-start(bf16[384,384]{1,0:T(8,128)(2,1)S(1)} %get-tuple-element.109), channel_id=1, source_target_pairs={{0,6},{2,4},{4,2},{6,0},{8,14},{10,12},{12,10},{14,8},{1,7},{3,5},... | collective-permute-start | bytes 884744 | tf_op jit(solution)/shard_map/ppermute | solution.py:217
  37.1 12.9 %collective-permute-start.14 = (bf16[272,384]{1,0:T(8,128)(2,1)S(1)}, bf16[272,384]{1,0:T(8,128)(2,1)S(1)}, u32[]{:S(2)}, u32[]{:S(2)}) collective-permute-start(bf16[272,384]{1,0:T(8,128)(2,1)S(1)} %get-tuple-element.96), channel_id=1, source_target_pairs={{0,8},{2,10},{4,12},{6,14},{8,0},{10,2},{12,4},{14,6},{1,9},{3,11}... | collective-permute-start | bytes 626696 | tf_op jit(solution)/shard_map/ppermute | solution.py:220
  51.8 11.6 %collective-permute-start.20 = (bf16[384,384]{1,0:T(8,128)(2,1)S(1)}, bf16[384,384]{1,0:T(8,128)(2,1)S(1)}, u32[]{:S(2)}, u32[]{:S(2)}) collective-permute-start(bf16[384,384]{1,0:T(8,128)(2,1)S(1)} %collective-permute-done.15.refs_7_.refs_2_), channel_id=1, source_target_pairs={{0,16},{16,0},{1,17},{17,1},{2,18},{18,2},{3,19},{19,3},{4,20},{20... | collective-permute-start | bytes 884744 | tf_op jit(solution)/shard_map/ppermute | solution.py:449
  53.0 10.4 %collective-permute-start.21 = (bf16[384,384]{1,0:T(8,128)(2,1)S(1)}, bf16[384,384]{1,0:T(8,128)(2,1)S(1)}, u32[]{:S(2)}, u32[]{:S(2)}) collective-permute-start(bf16[384,384]{1,0:T(8,128)(2,1)S(1)} %collective-permute-done.19.refs_8_.refs_3_), channel_id=1, source_target_pairs={{0,16},{16,0},{1,17},{17,1},{2,18},{18,2},{3,19},{19,3},{4,20},{20... | collective-permute-start | bytes 884744 | tf_op jit(solution)/shard_map/ppermute | solution.py:449
  53.6 9.8 %collective-permute-start.22 = (bf16[256,384]{1,0:T(8,128)(2,1)S(1)}, bf16[256,384]{1,0:T(8,128)(2,1)S(1)}, u32[]{:S(2)}, u32[]{:S(2)}) collective-permute-start(bf16[256,384]{1,0:T(8,128)(2,1)S(1)} %get-tuple-element.110.refs_0_), channel_id=1, source_target_pairs={{0,2},{2,0},{4,6},{6,4},{8,10},{10,8},{12,14},{14,12},{1,3},{3,1},... | collective-permute-start | bytes 589832 | tf_op jit(solution)/shard_map/ppermute | solution.py:217
  53.8 9.6 %collective-permute-start.23 = (bf16[256,384]{1,0:T(8,128)(2,1)S(1)}, bf16[256,384]{1,0:T(8,128)(2,1)S(1)}, u32[]{:S(2)}, u32[]{:S(2)}) collective-permute-start(bf16[256,384]{1,0:T(8,128)(2,1)S(1)} %get-tuple-element.110.refs_0_), channel_id=1, source_target_pairs={{0,6},{2,4},{4,2},{6,0},{8,14},{10,12},{12,10},{14,8},{1,7},{3,5},... | collective-permute-start | bytes 589832 | tf_op jit(solution)/shard_map/ppermute | solution.py:217
  55.4 13.1 %collective-permute-start.17 = (bf16[256,384]{1,0:T(8,128)(2,1)S(1)}, bf16[256,384]{1,0:T(8,128)(2,1)S(1)}, u32[]{:S(2)}, u32[]{:S(2)}) collective-permute-start(bf16[256,384]{1,0:T(8,128)(2,1)S(1)} %get-tuple-element.110.refs_0_), channel_id=1, source_target_pairs={{0,0},{1,8},{2,2},{3,10},{4,4},{5,12},{6,6},{7,14},{8,1},{9,9},{10... | collective-permute-start | bytes 589832 | tf_op jit(solution)/shard_map/ppermute | solution.py:226
  69.1 16.2 %collective-permute-start.24 = (bf16[272,384]{1,0:T(8,128)(2,1)S(1)}, bf16[272,384]{1,0:T(8,128)(2,1)S(1)}, u32[]{:S(2)}, u32[]{:S(2)}) collective-permute-start(bf16[272,384]{1,0:T(8,128)(2,1)S(1)} %get-tuple-element.114), channel_id=1, source_target_pairs={{0,8},{2,10},{4,12},{6,14},{8,0},{10,2},{12,4},{14,6},{1,9},{3,11}... | collective-permute-start | bytes 626696 | tf_op jit(solution)/shard_map/ppermute | solution.py:220
  74.4 15.1 %collective-permute-start.29 = (bf16[256,384]{1,0:T(8,128)(2,1)S(1)}, bf16[256,384]{1,0:T(8,128)(2,1)S(1)}, u32[]{:S(2)}, u32[]{:S(2)}) collective-permute-start(bf16[256,384]{1,0:T(8,128)(2,1)S(1)} %get-tuple-element.136), channel_id=1, source_target_pairs={{0,8},{2,10},{4,12},{6,14},{8,0},{10,2},{12,4},{14,6},{1,9},{3,11}... | collective-permute-start | bytes 589832 | tf_op jit(solution)/shard_map/ppermute | solution.py:220
  86.8 5.5 %collective-permute-start.25 = (bf16[128,384]{1,0:T(8,128)(2,1)S(1)}, bf16[128,384]{1,0:T(8,128)(2,1)S(1)}, u32[]{:S(2)}, u32[]{:S(2)}) collective-permute-start(bf16[128,384]{1,0:T(8,128)(2,1)S(1)} %get-tuple-element.119), channel_id=1, source_target_pairs={{0,2},{2,0},{4,6},{6,4},{8,10},{10,8},{12,14},{14,12},{1,3},{3,1},... | collective-permute-start | bytes 294920 | tf_op jit(solution)/shard_map/ppermute | solution.py:217
  87.0 6.6 %collective-permute-start.26 = (bf16[128,384]{1,0:T(8,128)(2,1)S(1)}, bf16[128,384]{1,0:T(8,128)(2,1)S(1)}, u32[]{:S(2)}, u32[]{:S(2)}) collective-permute-start(bf16[128,384]{1,0:T(8,128)(2,1)S(1)} %get-tuple-element.120), channel_id=1, source_target_pairs={{0,4},{2,6},{4,0},{6,2},{8,12},{10,14},{12,8},{14,10},{1,5},{3,7},... | collective-permute-start | bytes 294920 | tf_op jit(solution)/shard_map/ppermute | solution.py:217
  88.2 5.4 %collective-permute-start.27 = (bf16[128,384]{1,0:T(8,128)(2,1)S(1)}, bf16[128,384]{1,0:T(8,128)(2,1)S(1)}, u32[]{:S(2)}, u32[]{:S(2)}) collective-permute-start(bf16[128,384]{1,0:T(8,128)(2,1)S(1)} %get-tuple-element.121), channel_id=1, source_target_pairs={{0,6},{2,4},{4,2},{6,0},{8,14},{10,12},{12,10},{14,8},{1,7},{3,5},... | collective-permute-start | bytes 294920 | tf_op jit(solution)/shard_map/ppermute | solution.py:217
  (20 other events, 178.5 us)
